TPU v7x, 32 devices: a whole 2x2x4 slice. The times are simulated.
32 devices in a mesh: rows: 8 (over y, x, core), cols: 4 (over z).
Axes of the slice: x: 2, y: 2, z: 4, core: 2. Of those that a mesh axis runs over, the one named last changes fastest.
Arguments:
- local_weights: bfloat16 [8, 4, 48, 256, 256], P('rows', 'cols'), may hold values from -6 to 6
- local_gains: float32 [8, 4, 48, 2, 256], P('rows', 'cols'), may hold values from 1 to 48
- local_coords: int32 [8, 4, 48, 2], P('rows', 'cols'), may hold values from 0 to 15, as said below
- remote_weights: bfloat16 [8, 4, 8, 256, 256], P('rows', 'cols'), may hold values from -6 to 6
- remote_gains: float32 [8, 4, 8, 2, 256], P('rows', 'cols'), may hold values from 1 to 48
- remote_groups: int32 [8, 4, 8], P('rows', 'cols'), may hold values from 0 to 7, as said below
- remote_coords: int32 [8, 4, 8, 2], P('rows', 'cols'), may hold values from 0 to 15
- start_block: float32 [16, 32768], P(None, 'rows'), may hold values from -20 to 20
Outputs:
- embedding: float32 [16, 32768], P(None, ('rows', 'cols'))
Inputs may be any that keep to these rules, and one draw needn't show every extreme that they name: For each [r, c], the row tiles local_coords[r, c, :, 0] take every value 0 to 15. For each [r, c], every group named in remote_groups[r, c, :] is named exactly 2 times; one group is named 2 times in every [r, c].
All inputs are finite; a program needn't handle non-finite values.
Results may differ from a plain program's by a relative error of at most 0.0046.
Values may be sent and summed in bfloat16 or wider, within the bound.
No kernel may reach another device: no remote copies, remote signals or barrier semaphores. Data moves between devices by JAX's collectives and lax.ppermute only.
A program may use at most 128 MiB of HBM per device.

v0:
```python
import jax
import jax.numpy as jnp
from jax import lax
from jax.sharding import PartitionSpec as P

TILE = 256
WIDTH = 16
BR = 16
MOST = 2
ITERS = 2


def dequantize(weights, gain_pair):
    return (
        gain_pair[:, 0, :, None] * weights.astype(jnp.float32) * gain_pair[:, 1, None, :]
    ).astype(jnp.bfloat16)


def add_tiles(totals, targets, products, is_live):
    one_hot = jnp.where(
        (targets[None, :] == jnp.arange(totals.shape[0])[:, None]) & is_live[None, :], 1.0, 0.0
    ).astype(jnp.float32)
    flattened = products.reshape(products.shape[0], -1)
    added = jnp.dot(
        one_hot, flattened, precision=lax.Precision.HIGHEST, preferred_element_type=jnp.float32
    )
    return totals + added.reshape(totals.shape)


def per_device(
    local_weights,
    local_gains,
    local_coords,
    remote_weights,
    remote_gains,
    remote_groups,
    remote_coords,
    start_block,
):
    groups = lax.axis_size("rows")
    splits = lax.axis_size("cols")
    my_group = lax.axis_index("rows")
    my_split = lax.axis_index("cols")
    vertices = groups * BR * TILE
    quarter = BR // splits
    slot_count = groups * MOST
    local_eff = dequantize(local_weights[0, 0], local_gains[0, 0])
    remote_eff = dequantize(remote_weights[0, 0], remote_gains[0, 0])
    local_rows = local_coords[0, 0, :, 0]
    local_cols = local_coords[0, 0, :, 1]
    dest_groups = remote_groups[0, 0]
    remote_rows = remote_coords[0, 0, :, 0]
    remote_cols = remote_coords[0, 0, :, 1]
    tile_count = dest_groups.shape[0]
    listing = jnp.stack([dest_groups, remote_rows, remote_cols])[None]
    listing = lax.all_gather(listing, "rows", axis=0, tiled=True)
    all_dest = listing[:, 0]
    all_cols = listing[:, 2]
    positions = jnp.arange(tile_count)
    earlier = positions[None, :] < positions[:, None]
    all_ranks = jnp.sum((all_dest[:, :, None] == all_dest[:, None, :]) & earlier[None], axis=2)
    own_ranks = jnp.sum((dest_groups[:, None] == dest_groups[None, :]) & earlier, axis=1)
    slot_ids = dest_groups * MOST + own_ranks
    send_match = slot_ids[None, :] == jnp.arange(slot_count)[:, None]
    send_src = jnp.sum(jnp.where(send_match, positions[None, :] + 1, 0), axis=1) - 1
    send_live = send_src >= 0
    send_src = jnp.maximum(send_src, 0)
    recv_match = (all_dest == my_group)[:, None, :] & (
        all_ranks[:, None, :] == jnp.arange(MOST)[None, :, None]
    )
    recv_src = jnp.sum(jnp.where(recv_match, positions[None, None, :] + 1, 0), axis=2) - 1
    recv_live = (recv_src >= 0).reshape(slot_count)
    recv_src = jnp.maximum(recv_src, 0)
    recv_target = jnp.take_along_axis(all_cols, recv_src, axis=1).reshape(slot_count)
    local_live = jnp.ones((local_rows.shape[0],), bool)
    remote_live = jnp.ones((tile_count,), bool)
    degree = jnp.zeros((BR, TILE), jnp.float32)
    send_tiles = jnp.where(send_live[:, None, None], jnp.take(remote_eff, send_src, axis=0), 0)
    mirrored = lax.all_to_all(
        send_tiles.reshape(groups, MOST, TILE, TILE),
        "rows",
        split_axis=0,
        concat_axis=0,
        tiled=True,
    ).reshape(slot_count, TILE, TILE)
    column_part = jnp.sum(jnp.abs(mirrored), axis=1, dtype=jnp.float32)
    degree = add_tiles(
        degree, local_rows, jnp.sum(jnp.abs(local_eff), axis=2, dtype=jnp.float32), local_live
    )
    degree = add_tiles(
        degree, local_cols, jnp.sum(jnp.abs(local_eff), axis=1, dtype=jnp.float32), local_live
    )
    degree = add_tiles(
        degree, remote_rows, jnp.sum(jnp.abs(remote_eff), axis=2, dtype=jnp.float32), remote_live
    )
    degree = add_tiles(degree, recv_target, column_part, recv_live)
    vectors = start_block.reshape(WIDTH, BR, TILE).transpose(1, 0, 2)
    degree = lax.psum(degree, "cols")
    inv_root = 1.0 / jnp.sqrt(degree)
    for iteration in range(ITERS):
        scaled_block = (vectors * inv_root[:, None, :]).astype(jnp.bfloat16)
        answer = jnp.where(recv_live[:, None, None], jnp.take(scaled_block, recv_target, axis=0), 0)
        answer = answer.reshape(groups, MOST, WIDTH, TILE)
        outgoing = jnp.where(
            send_live[:, None, None],
            jnp.take(scaled_block, jnp.take(remote_rows, send_src), axis=0),
            0,
        )
        stacked = jnp.stack([answer, outgoing.reshape(groups, MOST, WIDTH, TILE)])
        arrived = lax.all_to_all(stacked, "rows", split_axis=1, concat_axis=1, tiled=True)
        fetched = arrived[0].reshape(slot_count, WIDTH, TILE)
        mirror_in = arrived[1].reshape(slot_count, WIDTH, TILE)
        far_terms = jnp.einsum(
            "sij,ski->skj", mirrored, mirror_in, preferred_element_type=jnp.float32
        )
        partial_value = jnp.zeros((BR, WIDTH, TILE), jnp.float32)
        forward = jnp.einsum(
            "tij,tkj->tki",
            local_eff,
            jnp.take(scaled_block, local_cols, axis=0),
            preferred_element_type=jnp.float32,
        )
        backward = jnp.einsum(
            "tij,tki->tkj",
            local_eff,
            jnp.take(scaled_block, local_rows, axis=0),
            preferred_element_type=jnp.float32,
        )
        partial_value = add_tiles(partial_value, local_rows, forward, local_live)
        partial_value = add_tiles(partial_value, local_cols, backward, local_live)
        remote_forward = jnp.einsum(
            "tij,tkj->tki",
            remote_eff,
            jnp.take(fetched, slot_ids, axis=0),
            preferred_element_type=jnp.float32,
        )
        partial_value = add_tiles(partial_value, remote_rows, remote_forward, remote_live)
        partial_value = add_tiles(partial_value, recv_target, far_terms, recv_live)
        summed = lax.psum(partial_value, "cols")
        image = summed * inv_root[:, None, :]
        gram_local = jnp.einsum("bki,bli->kl", image, image, precision=lax.Precision.HIGHEST)
        gram_all = lax.psum(gram_local, "rows")
        gram_all = gram_all / vertices
        factor = jnp.linalg.cholesky(gram_all)
        inverse = jax.scipy.linalg.solve_triangular(
            factor, jnp.eye(WIDTH, dtype=jnp.float32), lower=True
        )
        vectors = jnp.einsum("kl,bli->bki", inverse, image, precision=lax.Precision.HIGHEST)
    vectors = lax.dynamic_slice_in_dim(vectors, my_split * quarter, quarter, 0)
    return vectors.transpose(1, 0, 2).reshape(WIDTH, quarter * TILE)


def solution(mesh):
    in_specs = (
        P("rows", "cols", None, None, None),
        P("rows", "cols", None, None, None),
        P("rows", "cols", None, None),
        P("rows", "cols", None, None, None),
        P("rows", "cols", None, None, None),
        P("rows", "cols", None),
        P("rows", "cols", None, None),
        P(None, "rows"),
    )
    out_specs = P(None, ("rows", "cols"))
    return jax.shard_map(
        per_device, mesh=mesh, in_specs=in_specs, out_specs=out_specs, check_vma=False
    )
```

profile of v0, /device:TPU:0, one launch (start us, length us, event | category | flops | bytes accessed | tf_op | source)
XLA Modules:
  0.0 264.3 jit_solution(4237792836947261862)
XLA Ops:
  7.4 1.2 compare_and_fusion.1
  12.1 1.9 convert_reduce_fusion.3
  14.7 1.6 select_select_fusion
  16.4 5.2 %all-to-all-start = ((bf16[8,2,256,256]{3,2,1,0:T(8,128)(2,1)}), bf16[8,2,256,256]{3,2,1,0:T(8,128)(2,1)S(1)}, u32[]{:S(2)}, u32[]{:S(2)}) async-start(bf16[8,2,256,256]{3,2,1,0:T(8,128)(2,1)} %select_select_fusion), calls=%async_computation | async-start | bytes 4194304 | tf_op jit(solution)/shard_map/all_to_all | solution.py:79
  21.6 29.7 %all-gather.1 = s32[8,3,8]{2,1,0:T(4,128)S(1)} all-gather(s32[1,3,8]{2,1,0:T(4,128)S(1)} %add_bitcast_fusion), channel_id=2, replica_groups=mesh['rows'=8,'cols'=4] {'rows'}, dimensions={0}, use_global_device_ids=true | all-gather | bytes 864 | tf_op jit(solution)/shard_map/all_gather | solution.py:56
  56.5 1.2 pad_clamp_fusion.1
  60.7 7.2 %convert_reduce_fusion = (f32[48,256]{1,0:T(8,128)S(1)}, f32[48,256]{1,0:T(8,128)S(1)}) fusion(f32[48,256]{1,0:T(8,128)S(1)} %get-tuple-element.42, bf16[1,1,48,256,256]{4,3,2,1,0:T(8,128)(2,1)} %param.19, f32[48,256]{1,0:T(8,128)S(1)} %get-tuple-element.43), kind=kLoop, calls=%fused_computation.13 | loop fusion | flops 25141248 | bytes 6488064 | tf_op jit(solution)/shard_map/reduce_sum | solution.py:91
  69.2 19.0 %psum.35 = f32[16,256]{1,0:T(8,128)S(1)} all-reduce(f32[16,256]{1,0:T(8,128)S(1)} %convolution_add_fusion.6), channel_id=1, replica_groups=mesh['rows'=8,'cols'=4] {'cols'}, use_global_device_ids=true, to_apply=%region_8.9 | all-reduce | flops 4096 | bytes 32768 | tf_op jit(solution)/shard_map/psum | solution.py:98
  92.4 4.0 %all-to-all-start.1 = ((bf16[2,8,2,16,256]{4,3,2,0,1:T(8,128)(2,1)}), bf16[2,8,2,16,256]{4,3,2,0,1:T(8,128)(2,1)}, u32[]{:S(2)}, u32[]{:S(2)}) async-start(bf16[2,8,2,16,256]{4,3,2,0,1:T(8,128)(2,1)} %pad_maximum_fusion), calls=%async_computation.1 | async-start | bytes 524288 | tf_op jit(solution)/shard_map/all_to_all | solution.py:110
  96.5 1.4 gather_fusion.2
  98.0 4.8 %fusion.22 = f32[48,16,256]{2,1,0:T(8,128)S(1)} fusion(bf16[48,16,256]{2,1,0:T(8,128)(2,1)} %gather_fusion.2, pred[48]{0:T(512)(128)(4,1)} %get-tuple-element.33, bf16[1,1,48,256,256]{4,3,2,1,0:T(8,128)(2,1)} %param.19, f32[48,256]{1,0:T(8,128)} %copy-done.6, f32[48,256]{1,0:T(8,128)} %copy-done.9), kind=kOutput, calls=%fused_computation.58 | convolution fusion | flops 113442816 | bytes 7569456 | tf_op jit(solution)/shard_map/tij,tkj->tki/dot_general | solution.py:117
  102.8 1.6 fusion.13
  104.4 1.6 gather_fusion.3
  106.0 4.2 %fusion.20 = f32[48,16,256]{2,1,0:T(8,128)S(1)} fusion(bf16[48,16,256]{2,1,0:T(8,128)(2,1)} %gather_fusion.3, pred[48]{0:T(512)(128)(4,1)S(1)} %copy-done.24, bf16[1,1,48,256,256]{4,3,2,1,0:T(8,128)(2,1)} %param.19, f32[48,256]{1,0:T(8,128)S(1)} %copy-done.7, f32[48,256]{1,0:T(8,128)S(1)} %copy-done.10), kind=kOutput, calls=%fused_computation.56 | convolution fusion | flops 113442816 | bytes 7569456 | tf_op jit(solution)/shard_map/tij,tki->tkj/dot_general | solution.py:123
  111.2 1.6 fusion.142
  113.9 1.6 gather_fusion.7
  116.4 2.1 convolution_add_fusion.3
  118.6 34.1 %all-reduce.3.cloned.1.call-done = f32[16,16,256]{2,0,1:T(8,128)} async-done(((f32[16,16,256]{2,0,1:T(8,128)}), f32[16,16,256]{2,0,1:T(8,128)}) %all-reduce.3.cloned.1.call-update) | async-done | bytes 262160 | tf_op jit(solution)/shard_map/psum | solution.py:139
  154.2 12.7 %psum.37 = f32[16,16]{0,1:T(8,128)S(1)} all-reduce(f32[16,16]{0,1:T(8,128)S(1)} %convolution_bitcast_fusion.5), channel_id=1, replica_groups=mesh['rows'=8,'cols'=4] {'rows'}, use_global_device_ids=true, to_apply=%region_10.15 | all-reduce | flops 256 | bytes 2048 | tf_op jit(solution)/shard_map/psum | solution.py:142
  167.0 1.5 cholesky.44
  171.2 1.2 fusion.5
  173.8 1.4 gather_fusion.9
  175.2 1.4 gather_fusion.8
  178.9 4.2 %all-to-all-start.2 = ((bf16[2,8,2,16,256]{4,3,2,0,1:T(8,128)(2,1)}), bf16[2,8,2,16,256]{4,3,2,0,1:T(8,128)(2,1)}, u32[]{:S(2)}, u32[]{:S(2)}) async-start(bf16[2,8,2,16,256]{4,3,2,0,1:T(8,128)(2,1)} %pad_maximum_fusion.1), calls=%async_computation.2 | async-start | bytes 524288 | tf_op jit(solution)/shard_map/all_to_all | solution.py:110
  183.2 4.9 %fusion.16 = f32[48,16,256]{2,1,0:T(8,128)S(1)} fusion(bf16[48,16,256]{2,1,0:T(8,128)(2,1)} %gather_fusion.9, pred[48]{0:T(512)(128)(4,1)} %get-tuple-element.17, bf16[1,1,48,256,256]{4,3,2,1,0:T(8,128)(2,1)} %param.19, f32[48,256]{1,0:T(8,128)} %copy-done.6, f32[48,256]{1,0:T(8,128)} %copy-done.9), kind=kOutput, calls=%fused_computation.52 | convolution fusion | flops 113442816 | bytes 7569456 | tf_op jit(solution)/shard_map/tij,tki->tkj/dot_general | solution.py:123
  188.1 4.8 %fusion.18 = f32[48,16,256]{2,1,0:T(8,128)S(1)} fusion(bf16[48,16,256]{2,1,0:T(8,128)(2,1)S(1)} %copy-done.4, pred[48]{0:T(512)(128)(4,1)} %get-tuple-element.33, bf16[1,1,48,256,256]{4,3,2,1,0:T(8,128)(2,1)} %param.19, f32[48,256]{1,0:T(8,128)S(1)} %copy-done.8, f32[48,256]{1,0:T(8,128)S(1)} %copy-done.11), kind=kOutput, calls=%fused_computation.54 | convolution fusion | flops 113442816 | bytes 7569456 | tf_op jit(solution)/shard_map/tij,tkj->tki/dot_general | solution.py:117
  194.7 1.6 fusion.141
  197.4 1.6 gather_fusion.12
  200.6 2.1 convolution_add_fusion
  202.7 35.2 %all-reduce.5.cloned.1.call-done = f32[16,16,256]{2,0,1:T(8,128)} async-done(((f32[16,16,256]{2,0,1:T(8,128)}), f32[16,16,256]{2,0,1:T(8,128)}) %all-reduce.5.cloned.1.call-update) | async-done | bytes 262160 | tf_op jit(solution)/shard_map/psum | solution.py:139
  239.5 12.5 %psum.39 = f32[16,16]{0,1:T(8,128)S(1)} all-reduce(f32[16,16]{0,1:T(8,128)S(1)} %convolution_bitcast_fusion.4), channel_id=1, replica_groups=mesh['rows'=8,'cols'=4] {'rows'}, use_global_device_ids=true, to_apply=%region_14.21 | all-reduce | flops 256 | bytes 2048 | tf_op jit(solution)/shard_map/psum | solution.py:142
  252.1 1.5 cholesky.55
  (148 shorter events, 39.4 us)
Async XLA Ops:
  10.8 0.5 copy-start.21
  14.0 7.6 %copy-start.23 = (s32[1,1,8]{2,1,0:T(1,128)S(1)}, s32[1,1,8]{2,1,0:T(1,128)}, u32[]{:S(2)}) copy-start(s32[1,1,8]{2,1,0:T(1,128)} %param.24) | copy-start | bytes 100
  14.0 38.7 %copy-start.22 = (s32[1,1,48,2]{2,3,1,0:T(2,128)S(1)}, s32[1,1,48,2]{2,3,1,0:T(2,128)}, u32[]{:S(2)}) copy-start(s32[1,1,48,2]{2,3,1,0:T(2,128)} %param.21) | copy-start | bytes 1156
  14.0 39.9 %copy-start.12 = (f32[1,1,48,2,256]{4,3,2,1,0:T(2,128)S(1)}, f32[1,1,48,2,256]{4,3,2,1,0:T(2,128)}, u32[]{:S(2)}) copy-start(f32[1,1,48,2,256]{4,3,2,1,0:T(2,128)} %param.20) | copy-start | bytes 294916
  16.4 52.2 %all-to-all-start = ((bf16[8,2,256,256]{3,2,1,0:T(8,128)(2,1)}), bf16[8,2,256,256]{3,2,1,0:T(8,128)(2,1)S(1)}, u32[]{:S(2)}, u32[]{:S(2)}) async-start(bf16[8,2,256,256]{3,2,1,0:T(8,128)(2,1)} %select_select_fusion), calls=%async_computation | async-start | bytes 4194304 | tf_op jit(solution)/shard_map/all_to_all | solution.py:79
  54.0 14.0 %copy-start.17 = (s32[48]{0:T(128)S(1)}, s32[48]{0:T(128)}, u32[]{:S(2)}) copy-start(s32[48]{0:T(128)} %get-tuple-element.39) | copy-start | bytes 580
  54.0 14.1 %copy-start.15 = (s32[48]{0:T(128)S(1)}, s32[48]{0:T(128)}, u32[]{:S(2)}) copy-start(s32[48]{0:T(128)} %get-tuple-element.38) | copy-start | bytes 580
  54.2 34.6 %copy-start.5 = (f32[16,4096]{1,0:T(8,128)S(1)}, f32[16,4096]{1,0:T(8,128)}, u32[]{:S(2)}) copy-start(f32[16,4096]{1,0:T(8,128)} %param.26) | copy-start | bytes 786436
  55.2 33.1 %copy-start.13 = (s32[16]{0:T(128)}, s32[16]{0:T(128)S(1)}, u32[]{:S(2)}) copy-start(s32[16]{0:T(128)S(1)} %select_n.108) | copy-start | bytes 196
  60.7 7.6 %copy-start.6 = (f32[48,256]{1,0:T(8,128)}, f32[48,256]{1,0:T(8,128)S(1)}, u32[]{:S(2)}) copy-start(f32[48,256]{1,0:T(8,128)S(1)} %get-tuple-element.42) | copy-start | bytes 147460
  60.7 7.6 %copy-start.9 = (f32[48,256]{1,0:T(8,128)}, f32[48,256]{1,0:T(8,128)S(1)}, u32[]{:S(2)}) copy-start(f32[48,256]{1,0:T(8,128)S(1)} %get-tuple-element.43) | copy-start | bytes 147460
  88.2 0.6 copy-start.1
  92.4 18.8 %all-to-all-start.1 = ((bf16[2,8,2,16,256]{4,3,2,0,1:T(8,128)(2,1)}), bf16[2,8,2,16,256]{4,3,2,0,1:T(8,128)(2,1)}, u32[]{:S(2)}, u32[]{:S(2)}) async-start(bf16[2,8,2,16,256]{4,3,2,0,1:T(8,128)(2,1)} %pad_maximum_fusion), calls=%async_computation.1 | async-start | bytes 524288 | tf_op jit(solution)/shard_map/all_to_all | solution.py:110
  96.5 56.2 %all-reduce.3.cloned.1.call-start = ((), (), s32[]{:S(2)}) async-start(), calls=%async_computation.3 | async-start | bytes 524288 | tf_op jit(solution)/shard_map/psum | solution.py:139
  96.5 6.3 %copy-start.18 = (s32[48]{0:T(128)S(1)}, s32[48]{0:T(128)}, u32[]{:S(2)}) copy-start(s32[48]{0:T(128)} %get-tuple-element.39) | copy-start | bytes 580
  98.0 8.0 %copy-start.7 = (f32[48,256]{1,0:T(8,128)S(1)}, f32[48,256]{1,0:T(8,128)}, u32[]{:S(2)}) copy-start(f32[48,256]{1,0:T(8,128)} %copy-done.6) | copy-start | bytes 147460
  98.0 8.0 %copy-start.10 = (f32[48,256]{1,0:T(8,128)S(1)}, f32[48,256]{1,0:T(8,128)}, u32[]{:S(2)}) copy-start(f32[48,256]{1,0:T(8,128)} %copy-done.9) | copy-start | bytes 147460
  98.0 8.0 %copy-start.24 = (pred[48]{0:T(512)(128)(4,1)S(1)}, pred[48]{0:T(512)(128)(4,1)}, u32[]{:S(2)}) copy-start(pred[48]{0:T(512)(128)(4,1)} %get-tuple-element.17) | copy-start | bytes 148
  104.4 5.8 %copy-start.16 = (s32[48]{0:T(128)S(1)}, s32[48]{0:T(128)}, u32[]{:S(2)}) copy-start(s32[48]{0:T(128)} %get-tuple-element.38) | copy-start | bytes 580
  106.0 4.3 %copy-start = (f32[16,16,256]{2,0,1:T(8,128)S(1)}, f32[16,16,256]{2,0,1:T(8,128)}, u32[]{:S(2)}) copy-start(f32[16,16,256]{2,0,1:T(8,128)} %fusion.13) | copy-start | bytes 786436
  106.0 9.5 %copy-start.20 = (pred[8]{0:T(512)(128)(4,1)S(1)}, pred[8]{0:T(512)(128)(4,1)}, u32[]{:S(2)}) copy-start(pred[8]{0:T(512)(128)(4,1)} %get-tuple-element.10) | copy-start | bytes 28
  106.0 10.4 %copy-start.14 = (s32[16]{0:T(128)S(1)}, s32[16]{0:T(128)}, u32[]{:S(2)}) copy-start(s32[16]{0:T(128)} %copy-done.13) | copy-start | bytes 196
  110.3 42.5 %copy-start.2 = (f32[16,256]{1,0:T(8,128)S(1)}, f32[16,256]{1,0:T(8,128)}, u32[]{:S(2)}) copy-start(f32[16,256]{1,0:T(8,128)} %copy-done.1) | copy-start | bytes 49156
  178.9 9.1 %copy-start.4 = (bf16[48,16,256]{2,1,0:T(8,128)(2,1)S(1)}, bf16[48,16,256]{2,1,0:T(8,128)(2,1)}, u32[]{:S(2)}) copy-start(bf16[48,16,256]{2,1,0:T(8,128)(2,1)} %gather_fusion.8) | copy-start | bytes 1179652
  178.9 15.8 %all-to-all-start.2 = ((bf16[2,8,2,16,256]{4,3,2,0,1:T(8,128)(2,1)}), bf16[2,8,2,16,256]{4,3,2,0,1:T(8,128)(2,1)}, u32[]{:S(2)}, u32[]{:S(2)}) async-start(bf16[2,8,2,16,256]{4,3,2,0,1:T(8,128)(2,1)} %pad_maximum_fusion.1), calls=%async_computation.2 | async-start | bytes 524288 | tf_op jit(solution)/shard_map/all_to_all | solution.py:110
  183.1 54.9 %all-reduce.5.cloned.1.call-start = ((), (), s32[]{:S(2)}) async-start(), calls=%async_computation.4 | async-start | bytes 524288 | tf_op jit(solution)/shard_map/psum | solution.py:139
  183.1 4.9 %copy-start.8 = (f32[48,256]{1,0:T(8,128)S(1)}, f32[48,256]{1,0:T(8,128)}, u32[]{:S(2)}) copy-start(f32[48,256]{1,0:T(8,128)} %copy-done.6) | copy-start | bytes 147460
  183.1 4.9 %copy-start.11 = (f32[48,256]{1,0:T(8,128)S(1)}, f32[48,256]{1,0:T(8,128)}, u32[]{:S(2)}) copy-start(f32[48,256]{1,0:T(8,128)} %copy-done.9) | copy-start | bytes 147460
  188.1 4.8 %copy-start.19 = (s32[48]{0:T(128)S(1)}, s32[48]{0:T(128)}, u32[]{:S(2)}) copy-start(s32[48]{0:T(128)} %get-tuple-element.39) | copy-start | bytes 580
  192.9 45.1 %copy-start.3 = (f32[16,256]{1,0:T(8,128)S(1)}, f32[16,256]{1,0:T(8,128)}, u32[]{:S(2)}) copy-start(f32[16,256]{1,0:T(8,128)} %copy-done.1) | copy-start | bytes 49156
Sparse Core Ops, SparseCore 0:
  118.7 33.9 all-reduce.2
  202.9 35.0 all-reduce.4
where the time goes:
time: 265 us; the launch traced here: 264 us
  blocking collectives  73.8 us (28%)
  waiting for transfers between devices  69.4 us (26%)
  matrix products  35.8 us (14%)
  other arithmetic  35.2 us (13%)
  local copies, waits for them, and re-layouts  22.6 us (9%)
  between operations  14 us (5%)
  starting transfers between devices  13.5 us (5%)
    psum x2, waiting for transfers between devices, per_device(): summed = lax.psum(partial_value, 'cols')  69.4 us
    all_gather x1, blocking collectives, per_device(): listing = lax.all_gather(listing, 'rows', axis=0, tiled=True)  29.7 us
    psum x2, blocking collectives, per_device(): gram_all = lax.psum(gram_local, 'rows')  25.1 us
    psum x1, blocking collectives, per_device(): degree = lax.psum(degree, 'cols')  19 us
    dot_general x12, matrix products, add_tiles(): jnp.dot(one_hot, flattened, precision=lax.Precision.HIGHEST, preferred_el...  10.3 us
    dot_general x2, matrix products, per_device(): jnp.einsum('tij,tkj->tki', local_eff, jnp.take(scaled_block, local_cols,...  9.61 us
    dot_general x2, matrix products, per_device(): jnp.einsum('tij,tki->tkj', local_eff, jnp.take(scaled_block, local_rows,...  9.09 us
    all_to_all x2, starting transfers between devices, per_device(): lax.all_to_all(stacked, 'rows', split_axis=1, concat_axis=1, tiled=True)  8.21 us
  transfers between devices with their start and end apart: 5, of which 2 were waited for; matrix products, arithmetic and copies ran while one was open for 16% of the time, Pallas kernels for 0%

commit v1 on v0

v1 whole, which is shorter than its diff:
```python
import functools

import jax
import jax.numpy as jnp
from jax import lax
from jax.experimental import pallas as pl
from jax.experimental.pallas import tpu as pltpu
from jax.sharding import PartitionSpec as P

TILE = 256
WIDTH = 16
BR = 16
MOST = 2
CHUNK = 8
F32 = jnp.float32
BF16 = jnp.bfloat16
HIGHEST = lax.Precision.HIGHEST
VMEM_LIMIT = 48 * 1024 * 1024

vmem = pl.BlockSpec(memory_space=pltpu.VMEM)
smem = pl.BlockSpec(memory_space=pltpu.SMEM)
hbm = pl.BlockSpec(memory_space=pl.ANY)


def shape(dims, dtype=F32):
    return jax.ShapeDtypeStruct(dims, dtype)


def call(kernel, out_shape, in_specs, scratch_shapes=(), flops=10**6, moved=10**6, name=None):
    return pl.pallas_call(
        kernel,
        out_shape=out_shape,
        in_specs=in_specs,
        out_specs=jax.tree.map(lambda _: vmem, out_shape),
        scratch_shapes=scratch_shapes,
        cost_estimate=pl.CostEstimate(flops=flops, bytes_accessed=moved, transcendentals=0),
        compiler_params=pltpu.CompilerParams(vmem_limit_bytes=VMEM_LIMIT),
        name=name,
    )


def times(left, right):
    return lax.dot_general(left, right, (((1,), (0,)), ((), ())), preferred_element_type=F32)


def times_t(left, right):
    return lax.dot_general(left, right, (((1,), (1,)), ((), ())), preferred_element_type=F32)


def slots_of(groups_ref, count_ref, tile_count, group_count):
    for g in range(group_count):
        count_ref[g] = 0
    for t in range(tile_count):
        g = groups_ref[t]
        m = count_ref[g]
        count_ref[g] = m + 1
        yield t, g, m


def scale_chunk(raw, gains):
    row_gain = jnp.transpose(gains[:, 0, :])
    return [
        (row_gain[:, k : k + 1] * raw[k].astype(F32) * gains[k, 1:2, :]).astype(BF16)
        for k in range(CHUNK)
    ]


def remote_degree_kernel(
    group_count, weights, gains, groups, coords, scaled, payload, row_degree, count
):
    tiles = weights.shape[0]
    sub = lax.broadcasted_iota(jnp.int32, (8, TILE), 0)
    blank = jnp.where((sub >= MOST) & (sub < 2 * MOST), -1.0, 0.0).astype(F32)
    for g in range(group_count):
        payload[g] = blank
    row_degree[...] = jnp.zeros(row_degree.shape, F32)
    ones = jnp.ones((16, TILE), BF16)
    places = slots_of(groups, count, tiles, group_count)
    for first in range(0, tiles, CHUNK):
        pieces = scale_chunk(weights[first : first + CHUNK], gains[first : first + CHUNK])
        for piece in pieces:
            t, g, m = next(places)
            scaled[t] = piece
            size = jnp.abs(piece)
            r, c = coords[t, 0], coords[t, 1]
            row_degree[pl.ds(r, 1), :] += times_t(ones, size)[:1]
            payload[g, pl.ds(m, 1), :] = times(ones, size)[:1]
            payload[g, pl.ds(MOST + m, 1), :] = jnp.full((1, TILE), c, jnp.int32).astype(F32)


def local_degree_kernel(weights, gains, coords, scaled, degree, sems):
    chunks = weights.shape[0] // CHUNK
    copies = [
        pltpu.make_async_copy(
            weights.at[pl.ds(n * CHUNK, CHUNK)], scaled.at[pl.ds(n * CHUNK, CHUNK)], sems.at[n]
        )
        for n in range(chunks)
    ]
    for copy in copies:
        copy.start()
    degree[...] = jnp.zeros(degree.shape, F32)
    ones = jnp.ones((16, TILE), BF16)

    def step(n, _):
        pltpu.make_async_copy(
            weights.at[pl.ds(n * CHUNK, CHUNK)], scaled.at[pl.ds(n * CHUNK, CHUNK)], sems.at[n]
        ).wait()
        base = pl.multiple_of(n * CHUNK, CHUNK)
        pieces = scale_chunk(scaled[pl.ds(base, CHUNK)], gains[pl.ds(base, CHUNK)])
        for k, piece in enumerate(pieces):
            scaled[base + k] = piece
            size = jnp.abs(piece)
            r, c = coords[base + k, 0], coords[base + k, 1]
            degree[pl.ds(r, 1), :] += times_t(ones, size)[:1]
            degree[pl.ds(c, 1), :] += times(ones, size)[:1]
        return 0

    lax.fori_loop(0, chunks, step, 0)


def join_degree_kernel(arrived, row_degree, local_degree, joined):
    total = row_degree[...] + local_degree[...]
    sub = lax.broadcasted_iota(jnp.int32, total.shape, 0).astype(F32)
    for g in range(arrived.shape[0]):
        block = arrived[g]
        for m in range(MOST):
            hit = sub == block[MOST + m : MOST + m + 1, :]
            total += jnp.where(hit, block[m : m + 1, :], 0.0)
    joined[...] = total


def outgoing(x, scaled, groups, coords, targets, payload, count):
    group_count = payload.shape[0]
    for g in range(group_count):
        payload[g, MOST : 2 * MOST] = jnp.zeros((MOST, WIDTH, TILE), BF16)
    for t, g, m in slots_of(groups, count, scaled.shape[0], group_count):
        payload[g, MOST + m] = times(x[coords[t, 0]], scaled[t]).astype(BF16)
    for g in range(group_count):
        for m in range(MOST):
            payload[g, m] = x[jnp.maximum(targets[g, m], 0)]


def first_block_kernel(
    splits, start, scaled, groups, coords, targets, *refs
):
    degrees, (inv_root, x, payload, count) = refs[:splits], refs[splits:]
    degree = degrees[0][...]
    for other in degrees[1:]:
        degree += other[...]
    inv = 1.0 / jnp.sqrt(degree)
    inv_root[...] = inv
    for k in range(BR):
        x[k] = (start[:, k * TILE : (k + 1) * TILE] * inv[k : k + 1, :]).astype(BF16)
    outgoing(x, scaled, groups, coords, targets, payload, count)


def next_block_kernel(
    splits, vertices, scaled, inv_root, groups, coords, targets, *refs
):
    quarters, (x, payload, gram_out, count) = refs[:splits], refs[splits:]
    me = lax.axis_index("cols")
    quarter = BR // splits
    for k, part in enumerate(quarters):
        base = pl.multiple_of((me ^ k) * quarter, quarter)
        x[pl.ds(base, quarter)] = part[...]
    outgoing(x, scaled, groups, coords, targets, payload, count)
    gram = jnp.zeros((WIDTH, WIDTH), F32)
    for k in range(BR):
        image = x[k].astype(F32) / inv_root[k : k + 1, :]
        gram += lax.dot_general(
            image, image, (((1,), (1,)), ((), ())), precision=HIGHEST, preferred_element_type=F32
        )
    gram = gram / vertices
    high = gram.astype(BF16)
    middle = (gram - high.astype(F32)).astype(BF16)
    low = (gram - high.astype(F32) - middle.astype(F32)).astype(BF16)
    block = jnp.concatenate(
        [high, middle, low, jnp.zeros((WIDTH, TILE - 3 * WIDTH), BF16)], axis=1
    )
    for g in range(payload.shape[0]):
        payload[g, 2 * MOST] = block
    gram_out[...] = gram


def local_products_kernel(x, scaled, coords, partial):
    partial[...] = jnp.zeros(partial.shape, F32)
    unroll = 4

    def step(n, _):
        places, results = [], []
        for k in range(unroll):
            t = n * unroll + k
            r, c = coords[t, 0], coords[t, 1]
            tile = scaled[t]
            results.append((times_t(x[c], tile), times(x[r], tile)))
            places.append((r, c))
        for (r, c), (forward, backward) in zip(places, results):
            partial[r] += forward
            partial[c] += backward
        return 0

    lax.fori_loop(0, scaled.shape[0] // unroll, step, 0)


def remote_products_kernel(
    splits, arrived, scaled, partial, groups, coords, targets, *refs
):
    outs, (total, count) = refs[:splits], refs[splits:]
    group_count = arrived.shape[0]
    total[...] = partial[...]
    for t, g, m in slots_of(groups, count, scaled.shape[0], group_count):
        total[coords[t, 0]] += times_t(arrived[g, m], scaled[t])
    for g in range(group_count):
        for m in range(MOST):
            total[jnp.maximum(targets[g, m], 0)] += arrived[g, MOST + m].astype(F32)
    me = lax.axis_index("cols")
    quarter = BR // splits
    for k, out in enumerate(outs):
        base = pl.multiple_of((me ^ k) * quarter, quarter)
        out[...] = total[pl.ds(base, quarter)].astype(out.dtype)


def quarter_sum(pieces, inv_root, me):
    quarter = pieces[0].shape[0]
    images, roots = [], []
    for k in range(quarter):
        value = pieces[0][k]
        for piece in pieces[1:]:
            value += piece[k].astype(F32)
        root = inv_root[pl.ds(me * quarter + k, 1), :]
        images.append(value * root)
        roots.append(root)
    return images, roots


def middle_quarter_kernel(splits, inv_root, *refs):
    pieces, (x,) = refs[:splits], refs[splits:]
    images, roots = quarter_sum(pieces, inv_root, lax.axis_index("cols"))
    for k, (image, root) in enumerate(zip(images, roots)):
        x[k] = (image * root).astype(BF16)


def inverse_factor(gram):
    row = lax.broadcasted_iota(jnp.int32, (WIDTH, 2 * WIDTH), 0)
    col = lax.broadcasted_iota(jnp.int32, (WIDTH, 2 * WIDTH), 1)
    eye = jnp.where(
        lax.broadcasted_iota(jnp.int32, (WIDTH, WIDTH), 0)
        == lax.broadcasted_iota(jnp.int32, (WIDTH, WIDTH), 1),
        1.0,
        0.0,
    ).astype(F32)
    work = jnp.concatenate([gram, eye], axis=1)
    for k in range(WIDTH - 1):
        pivot = work[k : k + 1, :]
        factor = work[:, k : k + 1] / work[k : k + 1, k : k + 1]
        work = work - jnp.where(row > k, factor * pivot, 0.0)
    diagonal = jnp.sum(jnp.where(row == col, work, 0.0), axis=1, keepdims=True)
    return work[:, WIDTH:] / jnp.sqrt(diagonal)


def middle_factor_kernel(arrived, inverse):
    gram = jnp.zeros((WIDTH, WIDTH), F32)
    for g in range(arrived.shape[0]):
        block = arrived[g, 2 * MOST].astype(F32)
        gram += (block[:, 2 * WIDTH : 3 * WIDTH] + block[:, WIDTH : 2 * WIDTH]) + block[:, :WIDTH]
    inverse[...] = inverse_factor(gram)


def last_quarter_kernel(splits, vertices, inv_root, inverse, *refs):
    pieces, (image_out, grams) = refs[:splits], refs[splits:]
    images, _ = quarter_sum(pieces, inv_root, lax.axis_index("cols"))
    first = inverse[...]
    gram = jnp.zeros((WIDTH, WIDTH), F32)
    for k, image in enumerate(images):
        value = jnp.dot(first, image, precision=HIGHEST, preferred_element_type=F32)
        image_out[:, k * TILE : (k + 1) * TILE] = value
        gram += lax.dot_general(
            value, value, (((1,), (1,)), ((), ())), precision=HIGHEST, preferred_element_type=F32
        )
    gram = gram / vertices
    half = WIDTH // 2
    block = jnp.concatenate(
        [gram[:half], gram[half:], jnp.zeros((half, 128 - 2 * WIDTH), F32)], axis=1
    )
    for n in range(grams.shape[0]):
        grams[n] = block


def finish_kernel(grams, image, out):
    block = grams[0]
    for n in range(1, grams.shape[0]):
        block = block + grams[n]
    gram = jnp.concatenate([block[:, :WIDTH], block[:, WIDTH : 2 * WIDTH]], axis=0)
    out[...] = jnp.dot(
        inverse_factor(gram), image[...], precision=HIGHEST, preferred_element_type=F32
    )


def per_device(
    local_weights,
    local_gains,
    local_coords,
    remote_weights,
    remote_gains,
    remote_groups,
    remote_coords,
    start_block,
):
    groups = lax.axis_size("rows")
    splits = lax.axis_size("cols")
    vertices = groups * BR * TILE
    quarter = BR // splits
    local_tiles, remote_tiles = local_weights.shape[2], remote_weights.shape[2]
    listed, coords, near = remote_groups[0, 0], remote_coords[0, 0], local_coords[0, 0]
    count = pltpu.SMEM((groups,), jnp.int32)

    def swap(value, k):
        return lax.ppermute(value, "cols", [(j, j ^ k) for j in range(splits)])

    def trade(value):
        return lax.all_to_all(value, "rows", split_axis=0, concat_axis=0, tiled=True)

    remote_scaled, sums, row_degree = call(
        functools.partial(remote_degree_kernel, groups),
        (
            shape((remote_tiles, TILE, TILE), BF16),
            shape((groups, 8, TILE)),
            shape((BR, TILE)),
        ),
        [vmem, vmem, smem, smem],
        [count],
        name="remote_degree",
    )(remote_weights[0, 0], remote_gains[0, 0], listed, coords)
    sums_in = trade(sums)
    local_scaled, local_degree = call(
        local_degree_kernel,
        (shape((local_tiles, TILE, TILE), BF16), shape((BR, TILE))),
        [hbm, vmem, smem],
        [pltpu.SemaphoreType.DMA((local_tiles // CHUNK,))],
        moved=10**7,
        name="local_degree",
    )(local_weights[0, 0], local_gains[0, 0], near)
    targets = sums_in[:, MOST : 2 * MOST, 0].astype(jnp.int32)
    joined = call(
        join_degree_kernel, shape((BR, TILE)), [vmem, vmem, vmem], name="join_degree"
    )(sums_in, row_degree, local_degree)
    degrees = [joined] + [swap(joined, k) for k in range(1, splits)]
    inv_root, x, payload = call(
        functools.partial(first_block_kernel, splits),
        (
            shape((BR, TILE)),
            shape((BR, WIDTH, TILE), BF16),
            shape((groups, 2 * MOST, WIDTH, TILE), BF16),
        ),
        [vmem, vmem, smem, smem, smem] + [vmem] * splits,
        [count],
        name="first_block",
    )(start_block, remote_scaled, listed, coords, targets, *degrees)

    def product(x, payload):
        arrived = trade(payload)
        partial = call(
            local_products_kernel,
            shape((BR, WIDTH, TILE)),
            [vmem, vmem, smem],
            moved=10**7,
            name="local_products",
        )(x, local_scaled, near)
        pieces = call(
            functools.partial(remote_products_kernel, splits),
            tuple(
                shape((quarter, WIDTH, TILE), BF16 if k else F32) for k in range(splits)
            ),
            [vmem, vmem, vmem, smem, smem, smem],
            [pltpu.VMEM((BR, WIDTH, TILE), F32), count],
            name="remote_products",
        )(arrived, remote_scaled, partial, listed, coords, targets)
        return arrived, [pieces[0]] + [swap(pieces[k], k) for k in range(1, splits)]

    _, pieces = product(x, payload)
    x_quarter = call(
        functools.partial(middle_quarter_kernel, splits),
        shape((quarter, WIDTH, TILE), BF16),
        [vmem] * (1 + splits),
        name="middle_quarter",
    )(inv_root, *pieces)
    quarters = [x_quarter] + [swap(x_quarter, k) for k in range(1, splits)]
    x, payload, _ = call(
        functools.partial(next_block_kernel, splits, vertices),
        (
            shape((BR, WIDTH, TILE), BF16),
            shape((groups, 2 * MOST + 1, WIDTH, TILE), BF16),
            shape((WIDTH, WIDTH)),
        ),
        [vmem, vmem, smem, smem, smem] + [vmem] * splits,
        [count],
        name="next_block",
    )(remote_scaled, inv_root, listed, coords, targets, *quarters)
    arrived, pieces = product(x, payload)
    inverse = call(
        middle_factor_kernel, shape((WIDTH, WIDTH)), [vmem], name="middle_factor"
    )(arrived)
    image, grams = call(
        functools.partial(last_quarter_kernel, splits, vertices),
        (shape((WIDTH, quarter * TILE)), shape((groups * splits, 8, 128))),
        [vmem] * (2 + splits),
        name="last_quarter",
    )(inv_root, inverse, *pieces)
    grams = lax.all_to_all(
        grams, ("rows", "cols"), split_axis=0, concat_axis=0, tiled=True
    )
    return call(finish_kernel, shape((WIDTH, quarter * TILE)), [vmem, vmem], name="finish")(
        grams, image
    )


def solution(mesh):
    in_specs = (
        P("rows", "cols", None, None, None),
        P("rows", "cols", None, None, None),
        P("rows", "cols", None, None),
        P("rows", "cols", None, None, None),
        P("rows", "cols", None, None, None),
        P("rows", "cols", None),
        P("rows", "cols", None, None),
        P(None, "rows"),
    )
    out_specs = P(None, ("rows", "cols"))
    return jax.shard_map(
        per_device, mesh=mesh, in_specs=in_specs, out_specs=out_specs, check_vma=False
    )
```

time: 265 us -> 97.9 us (0.37)
  blocking collectives: 73.8 us -> 12.1 us
  waiting for transfers between devices: 69.4 us -> 13.1 us
  matrix products: 35.8 us -> 0 us
  Pallas kernels: 0 us -> 35.5 us
  other arithmetic: 35.2 us -> 0.01 us
  starting transfers between devices: 13.5 us -> 31.3 us
  local copies, waits for them, and re-layouts: 22.6 us -> 5.2 us
  between operations: 14 us -> 0.13 us
    psum x2 -> x0, waiting for transfers between devices: 69.4 us -> none  [per_device(): summed = lax.psum(partial_value, 'cols')]
    psum x3 -> x0, blocking collectives: 44.1 us -> none  [the longest x2 25.1 us: per_device(): gram_all = lax.psum(gram_local, 'rows')]
    pallas_call x0 -> x13, Pallas kernels: none -> 35.5 us  [the longest x2 13.5 us: product(): call(local_products_kernel, shape((BR, WIDTH, TILE)), [vmem, vmem, smem],...]
    dot_general x24 -> x0, matrix products: 35.4 us -> none  [the longest x12 10.3 us: add_tiles(): jnp.dot(one_hot, flattened, precision=lax.Precision.HIGHEST, preferred_el...]
    all_gather x1 -> x0, blocking collectives: 29.7 us -> none  [per_device(): listing = lax.all_gather(listing, 'rows', axis=0, tiled=True)]
    ppermute x0 -> x12, starting transfers between devices: none -> 17.8 us  [swap(): return lax.ppermute(value, 'cols', [(j, j ^ k) for j in range(splits)])]
    gather x17 -> x0, local copies, waits for them, and re-layouts: 14.1 us -> none  [the longest x2 3.15 us: per_device(): jnp.take(fetched, slot_ids, axis=0)]
    all_to_all x0 -> x1, blocking collectives: none -> 12.1 us  [per_device(): lax.all_to_all(grams, ('rows', 'cols'), split_axis=0, concat_axis=0, tile...]
  transfers between devices with their start and end apart: 5 -> 15, of which waited for: 2 -> 10; matrix products, arithmetic and copies ran while one was open for 16% -> 1% of each run, Pallas kernels for 0% -> 25%
where the time goes in v1:
time: 97.9 us; the launch traced here: 97.2 us
  Pallas kernels  35.5 us (36%)
  starting transfers between devices  31.3 us (32%)
  waiting for transfers between devices  13.1 us (13%)
  blocking collectives  12.1 us (12%)
  local copies, waits for them, and re-layouts  5.2 us (5%)
    ppermute x12, starting transfers between devices, swap(): return lax.ppermute(value, 'cols', [(j, j ^ k) for j in range(splits)])  17.8 us
    pallas_call x2, Pallas kernels, product(): call(local_products_kernel, shape((BR, WIDTH, TILE)), [vmem, vmem, smem],...  13.5 us
    all_to_all x3, starting transfers between devices, trade(): lax.all_to_all(value, 'rows', split_axis=0, concat_axis=0, tiled=True)  13.4 us
    all_to_all x1, blocking collectives, per_device(): lax.all_to_all(grams, ('rows', 'cols'), split_axis=0, concat_axis=0, tile...  12.1 us
    ppermute x12, waiting for transfers between devices, swap(): return lax.ppermute(value, 'cols', [(j, j ^ k) for j in range(splits)])  12.1 us
    pallas_call x1, Pallas kernels, per_device(): call(local_degree_kernel, (shape((local_tiles, TILE, TILE), BF16), shape(...  9.41 us
    unnamed x12, local copies, waits for them, and re-layouts  3.5 us
    pallas_call x2, Pallas kernels, product(): call(functools.partial(remote_products_kernel, splits), tuple((shape((qua...  2.27 us
  transfers between devices with their start and end apart: 15, of which 10 were waited for; matrix products, arithmetic and copies ran while one was open for 1% of the time, Pallas kernels for 25%

profile of v1, /device:TPU:0, one launch (start us, length us, event | category | flops | bytes accessed | tf_op | source)
XLA Modules:
  0.0 97.2 jit_solution(1455448783001687619)
XLA Ops:
  0.8 1.2 %copy-done = bf16[1,1,8,256,256]{4,3,2,1,0:T(8,128)(2,1)S(1)} copy-done((bf16[1,1,8,256,256]{4,3,2,1,0:T(8,128)(2,1)S(1)}, bf16[1,1,8,256,256]{4,3,2,1,0:T(8,128)(2,1)}, u32[]{:S(2)}) %copy-start) | copy-done | bytes 1048600
  3.4 2.0 %remote_degree.1 = (bf16[8,256,256]{2,1,0:T(8,128)(2,1)S(1)}, f32[8,8,256]{2,1,0:T(8,128)}, f32[16,256]{1,0:T(8,128)S(1)}) custom-call(bf16[8,256,256]{2,1,0:T(8,128)(2,1)S(1)} %bitcast.8, f32[8,2,256]{2,1,0:T(2,128)S(1)} %bitcast.10, s32[8]{0:T(128)S(1)} %bitcast.11, s32[8,2]{1,0:T(8,128)S(1)} %copy.22.coords), custom_call_target="tpu_custom_call" | custom-call | flops 1000000 | bytes 1000000 | tf_op jit(solution)/shard_map/remote_degree/pallas_call | solution.py:323
  5.4 5.2 %all-to-all-start = ((f32[8,8,256]{2,1,0:T(8,128)}), f32[8,8,256]{2,1,0:T(8,128)S(1)}, u32[]{:S(2)}, u32[]{:S(2)}) async-start(f32[8,8,256]{2,1,0:T(8,128)} %get-tuple-element.26), calls=%async_computation | async-start | bytes 131072 | tf_op jit(solution)/shard_map/all_to_all | solution.py:321
  11.3 0.9 copy-done.2
  12.2 9.4 %local_degree.1 = (bf16[48,256,256]{2,1,0:T(8,128)(2,1)}, f32[16,256]{1,0:T(8,128)S(1)}) custom-call(bf16[48,256,256]{2,1,0:T(8,128)(2,1)} %bitcast.16, f32[48,2,256]{2,1,0:T(2,128)S(1)} %bitcast.9, s32[48,2]{1,0:T(8,128)S(1)} %copy.24.coords), custom_call_target="tpu_custom_call" | custom-call | flops 1000000 | bytes 10000000 | tf_op jit(solution)/shard_map/local_degree/pallas_call | solution.py:335
  21.7 3.7 %collective-permute-start.2 = (f32[16,256]{1,0:T(8,128)S(1)}, f32[16,256]{1,0:T(8,128)S(1)}, u32[]{:S(2)}, u32[]{:S(2)}) collective-permute-start(f32[16,256]{1,0:T(8,128)S(1)} %join_degree.1.refs_0_), channel_id=1, source_target_pairs={{0,3},{1,2},{2,1},{3,0},{4,7},{5,6},{6,5},{7,4},{8,11},{9,10},{10,... | collective-permute-start | bytes 49160 | tf_op jit(solution)/shard_map/ppermute | solution.py:318
  26.3 0.9 collective-permute-done.2.refs_3_
  27.3 2.7 %collective-permute-done.1.refs_2_ = f32[16,256]{1,0:T(8,128)S(1)} collective-permute-done((f32[16,256]{1,0:T(8,128)S(1)}, f32[16,256]{1,0:T(8,128)S(1)}, u32[]{:S(2)}, u32[]{:S(2)}) %collective-permute-start.1) | collective-permute-done | bytes 16416 | tf_op jit(solution)/shard_map/ppermute | solution.py:318
  30.0 1.7 %first_block.1 = (f32[16,256]{1,0:T(8,128)S(1)}, bf16[16,16,256]{2,1,0:T(8,128)(2,1)S(1)}, bf16[8,4,16,256]{3,2,1,0:T(8,128)(2,1)}) custom-call(f32[16,4096]{1,0:T(8,128)S(1)} %copy-done.1, bf16[8,256,256]{2,1,0:T(8,128)(2,1)S(1)} %get-tuple-element.25.scaled, s32[8]{0:T(128)S(1)} %bitcast.12, s32[8,2]{1,0:T(8,128)S(1)} %copy.22.coords, ...), custom_call_target="tpu_custom_call" | custom-call | flops 1000000 | bytes 1000000 | tf_op jit(solution)/shard_map/first_block/pallas_call | solution.py:348
  31.7 4.2 %all-to-all-start.1 = ((bf16[8,4,16,256]{3,2,1,0:T(8,128)(2,1)}), bf16[8,4,16,256]{3,2,1,0:T(8,128)(2,1)S(1)}, u32[]{:S(2)}, u32[]{:S(2)}) async-start(bf16[8,4,16,256]{3,2,1,0:T(8,128)(2,1)} %get-tuple-element.30), calls=%async_computation.1 | async-start | bytes 524288 | tf_op jit(solution)/shard_map/all_to_all | solution.py:321
  35.9 6.8 %local_products.2.partial = f32[16,16,256]{2,1,0:T(8,128)S(1)} custom-call(bf16[16,16,256]{2,1,0:T(8,128)(2,1)S(1)} %get-tuple-element.31.x, bf16[48,256,256]{2,1,0:T(8,128)(2,1)} %get-tuple-element.32.scaled, s32[48,2]{1,0:T(8,128)S(1)} %copy.24.coords), custom_call_target="tpu_custom_call" | custom-call | flops 1000000 | bytes 10000000 | tf_op jit(solution)/shard_map/local_products/pallas_call | solution.py:362
  42.8 1.1 %remote_products.2 = (f32[4,16,256]{2,1,0:T(8,128)S(1)}, bf16[4,16,256]{2,1,0:T(8,128)(2,1)S(1)}, bf16[4,16,256]{2,1,0:T(8,128)(2,1)S(1)}, bf16[4,16,256]{2,1,0:T(8,128)(2,1)S(1)}) custom-call(bf16[8,4,16,256]{3,2,1,0:T(8,128)(2,1)S(1)} %all-to-all-done.1.arrived, bf16[8,256,256]{2,1,0:T(8,128)(2,1)S(1)} %get-tuple-element.25.scaled, ...), custom_call_target="tpu_custom_call" | custom-call | flops 1000000 | bytes 1000000 | tf_op jit(solution)/shard_map/remote_products/pallas_call | solution.py:369
  44.0 2.1 %collective-permute-start.4 = (bf16[4,16,256]{2,1,0:T(8,128)(2,1)S(1)}, bf16[4,16,256]{2,1,0:T(8,128)(2,1)S(1)}, u32[]{:S(2)}, u32[]{:S(2)}) collective-permute-start(bf16[4,16,256]{2,1,0:T(8,128)(2,1)S(1)} %get-tuple-element.35), channel_id=1, source_target_pairs={{0,2},{1,3},{2,0},{3,1},{4,6},{5,7},{6,4},{7,5},{8,10},{9,11},{10,... | collective-permute-start | bytes 98312 | tf_op jit(solution)/shard_map/ppermute | solution.py:318
  46.1 2.3 %collective-permute-start.5 = (bf16[4,16,256]{2,1,0:T(8,128)(2,1)S(1)}, bf16[4,16,256]{2,1,0:T(8,128)(2,1)S(1)}, u32[]{:S(2)}, u32[]{:S(2)}) collective-permute-start(bf16[4,16,256]{2,1,0:T(8,128)(2,1)S(1)} %get-tuple-element.36), channel_id=1, source_target_pairs={{0,3},{1,2},{2,1},{3,0},{4,7},{5,6},{6,5},{7,4},{8,11},{9,10},{10,... | collective-permute-start | bytes 98312 | tf_op jit(solution)/shard_map/ppermute | solution.py:318
  48.9 2.9 %collective-permute-done.5.refs_3_ = bf16[4,16,256]{2,1,0:T(8,128)(2,1)S(1)} collective-permute-done((bf16[4,16,256]{2,1,0:T(8,128)(2,1)S(1)}, bf16[4,16,256]{2,1,0:T(8,128)(2,1)S(1)}, u32[]{:S(2)}, u32[]{:S(2)}) %collective-permute-start.5) | collective-permute-done | bytes 32800 | tf_op jit(solution)/shard_map/ppermute | solution.py:318
  51.9 2.3 %collective-permute-start.8 = (bf16[4,16,256]{2,1,0:T(8,128)(2,1)S(1)}, bf16[4,16,256]{2,1,0:T(8,128)(2,1)S(1)}, u32[]{:S(2)}, u32[]{:S(2)}) collective-permute-start(bf16[4,16,256]{2,1,0:T(8,128)(2,1)S(1)} %middle_quarter.1.refs_0_), channel_id=1, source_target_pairs={{0,3},{1,2},{2,1},{3,0},{4,7},{5,6},{6,5},{7,4},{8,11},{9,10},{10,... | collective-permute-start | bytes 98312 | tf_op jit(solution)/shard_map/ppermute | solution.py:318
  54.2 2.1 %collective-permute-start.6 = (bf16[4,16,256]{2,1,0:T(8,128)(2,1)S(1)}, bf16[4,16,256]{2,1,0:T(8,128)(2,1)S(1)}, u32[]{:S(2)}, u32[]{:S(2)}) collective-permute-start(bf16[4,16,256]{2,1,0:T(8,128)(2,1)S(1)} %middle_quarter.1.refs_0_), channel_id=1, source_target_pairs={{0,1},{1,0},{2,3},{3,2},{4,5},{5,4},{6,7},{7,6},{8,9},{9,8},{10,11... | collective-permute-start | bytes 98312 | tf_op jit(solution)/shard_map/ppermute | solution.py:318
  56.3 1.6 %collective-permute-done.8.refs_3_ = bf16[4,16,256]{2,1,0:T(8,128)(2,1)S(1)} collective-permute-done((bf16[4,16,256]{2,1,0:T(8,128)(2,1)S(1)}, bf16[4,16,256]{2,1,0:T(8,128)(2,1)S(1)}, u32[]{:S(2)}, u32[]{:S(2)}) %collective-permute-start.8) | collective-permute-done | bytes 32800 | tf_op jit(solution)/shard_map/ppermute | solution.py:318
  57.9 1.1 %collective-permute-done.7.refs_2_ = bf16[4,16,256]{2,1,0:T(8,128)(2,1)S(1)} collective-permute-done((bf16[4,16,256]{2,1,0:T(8,128)(2,1)S(1)}, bf16[4,16,256]{2,1,0:T(8,128)(2,1)S(1)}, u32[]{:S(2)}, u32[]{:S(2)}) %collective-permute-start.7) | collective-permute-done | bytes 32800 | tf_op jit(solution)/shard_map/ppermute | solution.py:318
  59.0 2.2 %next_block.1 = (bf16[16,16,256]{2,1,0:T(8,128)(2,1)S(1)}, bf16[8,5,16,256]{3,2,1,0:T(8,128)(2,1)}, f32[16,16]{1,0:T(8,128)}) custom-call(bf16[8,256,256]{2,1,0:T(8,128)(2,1)S(1)} %get-tuple-element.25.scaled, f32[16,256]{1,0:T(8,128)S(1)} %get-tuple-element.29.inv_root, s32[8]{0:T(128)S(1)} %bitcast.14, s32[8,2]{1,0:T(8,128)S(1)} %copy.22.coords, ...), custom_call_target="tpu_custom_call" | custom-call | flops 1000000 | bytes 1000000 | tf_op jit(solution)/shard_map/next_block/pallas_call | solution.py:388
  61.2 4.1 %all-to-all-start.2 = ((bf16[8,5,16,256]{3,2,1,0:T(8,128)(2,1)}), bf16[8,5,16,256]{3,2,1,0:T(8,128)(2,1)S(1)}, u32[]{:S(2)}, u32[]{:S(2)}) async-start(bf16[8,5,16,256]{3,2,1,0:T(8,128)(2,1)} %get-tuple-element.37), calls=%async_computation.2 | async-start | bytes 655360 | tf_op jit(solution)/shard_map/all_to_all | solution.py:321
  65.3 6.8 %local_products.3.partial = f32[16,16,256]{2,1,0:T(8,128)S(1)} custom-call(bf16[16,16,256]{2,1,0:T(8,128)(2,1)S(1)} %get-tuple-element.38.x, bf16[48,256,256]{2,1,0:T(8,128)(2,1)} %get-tuple-element.32.scaled, s32[48,2]{1,0:T(8,128)S(1)} %copy.24.coords), custom_call_target="tpu_custom_call" | custom-call | flops 1000000 | bytes 10000000 | tf_op jit(solution)/shard_map/local_products/pallas_call | solution.py:362
  72.1 0.8 all-to-all-done.2.arrived
  72.9 1.1 %remote_products.3 = (f32[4,16,256]{2,1,0:T(8,128)S(1)}, bf16[4,16,256]{2,1,0:T(8,128)(2,1)S(1)}, bf16[4,16,256]{2,1,0:T(8,128)(2,1)S(1)}, bf16[4,16,256]{2,1,0:T(8,128)(2,1)S(1)}) custom-call(bf16[8,5,16,256]{3,2,1,0:T(8,128)(2,1)S(1)} %all-to-all-done.2.arrived, bf16[8,256,256]{2,1,0:T(8,128)(2,1)S(1)} %get-tuple-element.25.scaled, ...), custom_call_target="tpu_custom_call" | custom-call | flops 1000000 | bytes 1000000 | tf_op jit(solution)/shard_map/remote_products/pallas_call | solution.py:369
  74.1 1.3 %collective-permute-start.9 = (bf16[4,16,256]{2,1,0:T(8,128)(2,1)S(1)}, bf16[4,16,256]{2,1,0:T(8,128)(2,1)S(1)}, u32[]{:S(2)}, u32[]{:S(2)}) collective-permute-start(bf16[4,16,256]{2,1,0:T(8,128)(2,1)S(1)} %get-tuple-element.40), channel_id=1, source_target_pairs={{0,1},{1,0},{2,3},{3,2},{4,5},{5,4},{6,7},{7,6},{8,9},{9,8},{10,11... | collective-permute-start | bytes 98312 | tf_op jit(solution)/shard_map/ppermute | solution.py:318
  75.3 1.2 %collective-permute-start.10 = (bf16[4,16,256]{2,1,0:T(8,128)(2,1)S(1)}, bf16[4,16,256]{2,1,0:T(8,128)(2,1)S(1)}, u32[]{:S(2)}, u32[]{:S(2)}) collective-permute-start(bf16[4,16,256]{2,1,0:T(8,128)(2,1)S(1)} %get-tuple-element.41), channel_id=1, source_target_pairs={{0,2},{1,3},{2,0},{3,1},{4,6},{5,7},{6,4},{7,5},{8,10},{9,11},{10,... | collective-permute-start | bytes 98312 | tf_op jit(solution)/shard_map/ppermute | solution.py:318
  76.5 2.0 %collective-permute-start.11 = (bf16[4,16,256]{2,1,0:T(8,128)(2,1)S(1)}, bf16[4,16,256]{2,1,0:T(8,128)(2,1)S(1)}, u32[]{:S(2)}, u32[]{:S(2)}) collective-permute-start(bf16[4,16,256]{2,1,0:T(8,128)(2,1)S(1)} %get-tuple-element.42), channel_id=1, source_target_pairs={{0,3},{1,2},{2,1},{3,0},{4,7},{5,6},{6,5},{7,4},{8,11},{9,10},{10,... | collective-permute-start | bytes 98312 | tf_op jit(solution)/shard_map/ppermute | solution.py:318
  78.5 1.5 %middle_factor.1.inverse = f32[16,16]{1,0:T(8,128)S(1)} custom-call(bf16[8,5,16,256]{3,2,1,0:T(8,128)(2,1)S(1)} %all-to-all-done.2.arrived), custom_call_target="tpu_custom_call" | custom-call | flops 1000000 | bytes 1000000 | tf_op jit(solution)/shard_map/middle_factor/pallas_call | solution.py:400
  80.0 0.9 collective-permute-done.10.refs_2_
  80.9 1.4 %collective-permute-done.11.refs_3_ = bf16[4,16,256]{2,1,0:T(8,128)(2,1)S(1)} collective-permute-done((bf16[4,16,256]{2,1,0:T(8,128)(2,1)S(1)}, bf16[4,16,256]{2,1,0:T(8,128)(2,1)S(1)}, u32[]{:S(2)}, u32[]{:S(2)}) %collective-permute-start.11) | collective-permute-done | bytes 32800 | tf_op jit(solution)/shard_map/ppermute | solution.py:318
  82.9 12.1 %all_to_all.20.grams = f32[32,8,128]{2,1,0:T(8,128)S(1)} all-to-all(f32[32,8,128]{2,1,0:T(8,128)S(1)} %get-tuple-element.43), channel_id=1, replica_groups=mesh['rows'=8,'cols'=4] {'rows','cols'}, dimensions={0} | all-to-all | bytes 262144 | tf_op jit(solution)/shard_map/all_to_all | solution.py:409
  95.0 2.2 %finish.1 = f32[16,1024]{1,0:T(8,128)} custom-call(f32[32,8,128]{2,1,0:T(8,128)S(1)} %all_to_all.20.grams, f32[16,1024]{1,0:T(8,128)S(1)} %get-tuple-element.44.image), custom_call_target="tpu_custom_call" | custom-call | flops 1000000 | bytes 1000000 | tf_op jit(solution)/shard_map/finish/pallas_call | solution.py:412
  (29 shorter events, 5.4 us)
Async XLA Ops:
  0.0 30.0 %copy-start.5 = (s32[1,1,8]{2,1,0:T(1,128)S(1)}, s32[1,1,8]{2,1,0:T(1,128)}, u32[]{:S(2)}) copy-start(s32[1,1,8]{2,1,0:T(1,128)} %param.13) | copy-start | bytes 100
  0.8 1.2 %copy-start = (bf16[1,1,8,256,256]{4,3,2,1,0:T(8,128)(2,1)S(1)}, bf16[1,1,8,256,256]{4,3,2,1,0:T(8,128)(2,1)}, u32[]{:S(2)}) copy-start(bf16[1,1,8,256,256]{4,3,2,1,0:T(8,128)(2,1)} %param.11) | copy-start | bytes 3145732
  2.0 0.7 copy-start.3
  2.7 0.7 copy-start.4
  3.4 26.6 %copy-start.1 = (f32[16,4096]{1,0:T(8,128)S(1)}, f32[16,4096]{1,0:T(8,128)}, u32[]{:S(2)}) copy-start(f32[16,4096]{1,0:T(8,128)} %start.1) | copy-start | bytes 786436
  5.4 16.2 %all-to-all-start = ((f32[8,8,256]{2,1,0:T(8,128)}), f32[8,8,256]{2,1,0:T(8,128)S(1)}, u32[]{:S(2)}, u32[]{:S(2)}) async-start(f32[8,8,256]{2,1,0:T(8,128)} %get-tuple-element.26), calls=%async_computation | async-start | bytes 131072 | tf_op jit(solution)/shard_map/all_to_all | solution.py:321
  11.3 0.9 copy-start.2
  21.7 5.6 %collective-permute-start.2 = (f32[16,256]{1,0:T(8,128)S(1)}, f32[16,256]{1,0:T(8,128)S(1)}, u32[]{:S(2)}, u32[]{:S(2)}) collective-permute-start(f32[16,256]{1,0:T(8,128)S(1)} %join_degree.1.refs_0_), channel_id=1, source_target_pairs={{0,3},{1,2},{2,1},{3,0},{4,7},{5,6},{6,5},{7,4},{8,11},{9,10},{10,... | collective-permute-start | bytes 49160 | tf_op jit(solution)/shard_map/ppermute | solution.py:318
  25.4 4.6 %collective-permute-start.1 = (f32[16,256]{1,0:T(8,128)S(1)}, f32[16,256]{1,0:T(8,128)S(1)}, u32[]{:S(2)}, u32[]{:S(2)}) collective-permute-start(f32[16,256]{1,0:T(8,128)S(1)} %join_degree.1.refs_0_), channel_id=1, source_target_pairs={{0,2},{1,3},{2,0},{3,1},{4,6},{5,7},{6,4},{7,5},{8,10},{9,11},{10,... | collective-permute-start | bytes 49160 | tf_op jit(solution)/shard_map/ppermute | solution.py:318
  25.4 4.6 %collective-permute-start = (f32[16,256]{1,0:T(8,128)S(1)}, f32[16,256]{1,0:T(8,128)S(1)}, u32[]{:S(2)}, u32[]{:S(2)}) collective-permute-start(f32[16,256]{1,0:T(8,128)S(1)} %join_degree.1.refs_0_), channel_id=1, source_target_pairs={{0,1},{1,0},{2,3},{3,2},{4,5},{5,4},{6,7},{7,6},{8,9},{9,8},{10,11... | collective-permute-start | bytes 49160 | tf_op jit(solution)/shard_map/ppermute | solution.py:318
  31.7 11.1 %all-to-all-start.1 = ((bf16[8,4,16,256]{3,2,1,0:T(8,128)(2,1)}), bf16[8,4,16,256]{3,2,1,0:T(8,128)(2,1)S(1)}, u32[]{:S(2)}, u32[]{:S(2)}) async-start(bf16[8,4,16,256]{3,2,1,0:T(8,128)(2,1)} %get-tuple-element.30), calls=%async_computation.1 | async-start | bytes 524288 | tf_op jit(solution)/shard_map/all_to_all | solution.py:321
  43.9 4.5 %collective-permute-start.3 = (bf16[4,16,256]{2,1,0:T(8,128)(2,1)S(1)}, bf16[4,16,256]{2,1,0:T(8,128)(2,1)S(1)}, u32[]{:S(2)}, u32[]{:S(2)}) collective-permute-start(bf16[4,16,256]{2,1,0:T(8,128)(2,1)S(1)} %get-tuple-element.34), channel_id=1, source_target_pairs={{0,1},{1,0},{2,3},{3,2},{4,5},{5,4},{6,7},{7,6},{8,9},{9,8},{10,11... | collective-permute-start | bytes 98312 | tf_op jit(solution)/shard_map/ppermute | solution.py:318
  44.0 4.9 %collective-permute-start.4 = (bf16[4,16,256]{2,1,0:T(8,128)(2,1)S(1)}, bf16[4,16,256]{2,1,0:T(8,128)(2,1)S(1)}, u32[]{:S(2)}, u32[]{:S(2)}) collective-permute-start(bf16[4,16,256]{2,1,0:T(8,128)(2,1)S(1)} %get-tuple-element.35), channel_id=1, source_target_pairs={{0,2},{1,3},{2,0},{3,1},{4,6},{5,7},{6,4},{7,5},{8,10},{9,11},{10,... | collective-permute-start | bytes 98312 | tf_op jit(solution)/shard_map/ppermute | solution.py:318
  46.1 5.7 %collective-permute-start.5 = (bf16[4,16,256]{2,1,0:T(8,128)(2,1)S(1)}, bf16[4,16,256]{2,1,0:T(8,128)(2,1)S(1)}, u32[]{:S(2)}, u32[]{:S(2)}) collective-permute-start(bf16[4,16,256]{2,1,0:T(8,128)(2,1)S(1)} %get-tuple-element.36), channel_id=1, source_target_pairs={{0,3},{1,2},{2,1},{3,0},{4,7},{5,6},{6,5},{7,4},{8,11},{9,10},{10,... | collective-permute-start | bytes 98312 | tf_op jit(solution)/shard_map/ppermute | solution.py:318
  51.9 6.1 %collective-permute-start.8 = (bf16[4,16,256]{2,1,0:T(8,128)(2,1)S(1)}, bf16[4,16,256]{2,1,0:T(8,128)(2,1)S(1)}, u32[]{:S(2)}, u32[]{:S(2)}) collective-permute-start(bf16[4,16,256]{2,1,0:T(8,128)(2,1)S(1)} %middle_quarter.1.refs_0_), channel_id=1, source_target_pairs={{0,3},{1,2},{2,1},{3,0},{4,7},{5,6},{6,5},{7,4},{8,11},{9,10},{10,... | collective-permute-start | bytes 98312 | tf_op jit(solution)/shard_map/ppermute | solution.py:318
  54.2 4.8 %collective-permute-start.7 = (bf16[4,16,256]{2,1,0:T(8,128)(2,1)S(1)}, bf16[4,16,256]{2,1,0:T(8,128)(2,1)S(1)}, u32[]{:S(2)}, u32[]{:S(2)}) collective-permute-start(bf16[4,16,256]{2,1,0:T(8,128)(2,1)S(1)} %middle_quarter.1.refs_0_), channel_id=1, source_target_pairs={{0,2},{1,3},{2,0},{3,1},{4,6},{5,7},{6,4},{7,5},{8,10},{9,11},{10,... | collective-permute-start | bytes 98312 | tf_op jit(solution)/shard_map/ppermute | solution.py:318
  54.2 4.8 %collective-permute-start.6 = (bf16[4,16,256]{2,1,0:T(8,128)(2,1)S(1)}, bf16[4,16,256]{2,1,0:T(8,128)(2,1)S(1)}, u32[]{:S(2)}, u32[]{:S(2)}) collective-permute-start(bf16[4,16,256]{2,1,0:T(8,128)(2,1)S(1)} %middle_quarter.1.refs_0_), channel_id=1, source_target_pairs={{0,1},{1,0},{2,3},{3,2},{4,5},{5,4},{6,7},{7,6},{8,9},{9,8},{10,11... | collective-permute-start | bytes 98312 | tf_op jit(solution)/shard_map/ppermute | solution.py:318
  61.2 11.7 %all-to-all-start.2 = ((bf16[8,5,16,256]{3,2,1,0:T(8,128)(2,1)}), bf16[8,5,16,256]{3,2,1,0:T(8,128)(2,1)S(1)}, u32[]{:S(2)}, u32[]{:S(2)}) async-start(bf16[8,5,16,256]{3,2,1,0:T(8,128)(2,1)} %get-tuple-element.37), calls=%async_computation.2 | async-start | bytes 655360 | tf_op jit(solution)/shard_map/all_to_all | solution.py:321
  74.1 5.9 %collective-permute-start.9 = (bf16[4,16,256]{2,1,0:T(8,128)(2,1)S(1)}, bf16[4,16,256]{2,1,0:T(8,128)(2,1)S(1)}, u32[]{:S(2)}, u32[]{:S(2)}) collective-permute-start(bf16[4,16,256]{2,1,0:T(8,128)(2,1)S(1)} %get-tuple-element.40), channel_id=1, source_target_pairs={{0,1},{1,0},{2,3},{3,2},{4,5},{5,4},{6,7},{7,6},{8,9},{9,8},{10,11... | collective-permute-start | bytes 98312 | tf_op jit(solution)/shard_map/ppermute | solution.py:318
  75.3 5.5 %collective-permute-start.10 = (bf16[4,16,256]{2,1,0:T(8,128)(2,1)S(1)}, bf16[4,16,256]{2,1,0:T(8,128)(2,1)S(1)}, u32[]{:S(2)}, u32[]{:S(2)}) collective-permute-start(bf16[4,16,256]{2,1,0:T(8,128)(2,1)S(1)} %get-tuple-element.41), channel_id=1, source_target_pairs={{0,2},{1,3},{2,0},{3,1},{4,6},{5,7},{6,4},{7,5},{8,10},{9,11},{10,... | collective-permute-start | bytes 98312 | tf_op jit(solution)/shard_map/ppermute | solution.py:318
  76.5 5.7 %collective-permute-start.11 = (bf16[4,16,256]{2,1,0:T(8,128)(2,1)S(1)}, bf16[4,16,256]{2,1,0:T(8,128)(2,1)S(1)}, u32[]{:S(2)}, u32[]{:S(2)}) collective-permute-start(bf16[4,16,256]{2,1,0:T(8,128)(2,1)S(1)} %get-tuple-element.42), channel_id=1, source_target_pairs={{0,3},{1,2},{2,1},{3,0},{4,7},{5,6},{6,5},{7,4},{8,11},{9,10},{10,... | collective-permute-start | bytes 98312 | tf_op jit(solution)/shard_map/ppermute | solution.py:318

commit v2 on v1

v2 whole, which is shorter than its diff:
```python
import functools

import jax
import jax.numpy as jnp
from jax import lax
from jax.experimental import pallas as pl
from jax.experimental.pallas import tpu as pltpu
from jax.sharding import PartitionSpec as P

TILE = 256
WIDTH = 16
BR = 16
MOST = 2
CHUNK = 8
F32 = jnp.float32
BF16 = jnp.bfloat16
HIGHEST = lax.Precision.HIGHEST
VMEM_LIMIT = 48 * 1024 * 1024

vmem = pl.BlockSpec(memory_space=pltpu.VMEM)
smem = pl.BlockSpec(memory_space=pltpu.SMEM)
hbm = pl.BlockSpec(memory_space=pltpu.HBM)


def shape(dims, dtype=F32):
    return jax.ShapeDtypeStruct(dims, dtype)


def call(kernel, out_shape, in_specs, scratch_shapes=(), flops=10**6, moved=10**6, name=None):
    return pl.pallas_call(
        kernel,
        out_shape=out_shape,
        in_specs=in_specs,
        out_specs=jax.tree.map(lambda _: vmem, out_shape),
        scratch_shapes=scratch_shapes,
        cost_estimate=pl.CostEstimate(flops=flops, bytes_accessed=moved, transcendentals=0),
        compiler_params=pltpu.CompilerParams(vmem_limit_bytes=VMEM_LIMIT),
        name=name,
    )


def times(left, right):
    return lax.dot_general(left, right, (((1,), (0,)), ((), ())), preferred_element_type=F32)


def times_t(left, right):
    return lax.dot_general(left, right, (((1,), (1,)), ((), ())), preferred_element_type=F32)


def in_hbm(value):
    return pltpu.with_memory_space_constraint(value, pltpu.HBM)


def slots_of(groups_ref, count_ref, tile_count, group_count):
    for g in range(group_count):
        count_ref[g] = 0
    for t in range(tile_count):
        g = groups_ref[0, 0, t]
        m = count_ref[g]
        count_ref[g] = m + 1
        yield t, g, m


def weighted_sums(size, gains):
    sub = lax.broadcasted_iota(jnp.int32, (8, TILE), 0)
    gains = jnp.abs(gains)
    left = jnp.where(sub == 0, gains[0:1, :], jnp.where(sub == 1, gains[1:2, :], 0.0))
    high = left.astype(BF16).astype(F32)
    halves = jnp.concatenate([high, left - high], axis=0).astype(BF16)
    rows, cols = times_t(halves, size), times(halves, size)
    return (rows[1:2] + rows[9:10]) * gains[0:1, :], (cols[0:1] + cols[8:9]) * gains[1:2, :]


def remote_degree_kernel(
    group_count,
    weights,
    gains,
    groups,
    coords,
    payload,
    row_degree,
    tiles,
    tile_gains,
    tile_groups,
    tile_coords,
    count,
    sems,
):
    copies = [
        pltpu.make_async_copy(source, target, sems.at[n])
        for n, (source, target) in enumerate(
            [(groups, tile_groups), (coords, tile_coords), (gains, tile_gains), (weights, tiles)]
        )
    ]
    for copy in copies:
        copy.start()
    sub = lax.broadcasted_iota(jnp.int32, (8, TILE), 0)
    blank = jnp.where((sub >= MOST) & (sub < 2 * MOST), -1.0, 0.0).astype(F32)
    for g in range(group_count):
        payload[g] = blank
    row_degree[...] = jnp.zeros(row_degree.shape, F32)
    for copy in copies:
        copy.wait()
    places = slots_of(tile_groups, count, weights.shape[2], group_count)
    for t, g, m in places:
        r, c = tile_coords[0, 0, 0, t], tile_coords[0, 0, 1, t]
        by_row, by_col = weighted_sums(jnp.abs(tiles[0, 0, t]), tile_gains[0, 0, t])
        row_degree[pl.ds(r, 1), :] += by_row
        payload[g, pl.ds(m, 1), :] = by_col
        payload[g, pl.ds(MOST + m, 1), :] = jnp.full((1, TILE), c, jnp.int32).astype(F32)


def local_degree_kernel(
    weights, gains, coords, degree, tiles, tile_gains, tile_coords, sems, small_sems
):
    chunks = weights.shape[2] // CHUNK

    def copy_of(n):
        part = pl.ds(n * CHUNK, CHUNK)
        return pltpu.make_async_copy(weights.at[0, 0, part], tiles.at[part], sems.at[n])

    small = [
        pltpu.make_async_copy(coords, tile_coords, small_sems.at[0]),
        pltpu.make_async_copy(gains, tile_gains, small_sems.at[1]),
    ]
    for copy in small:
        copy.start()
    for n in range(chunks):
        copy_of(n).start()
    degree[...] = jnp.zeros(degree.shape, F32)
    for copy in small:
        copy.wait()

    def step(n, _):
        copy_of(n).wait()
        for k in range(CHUNK):
            t = n * CHUNK + k
            r, c = tile_coords[0, 0, 0, t], tile_coords[0, 0, 1, t]
            by_row, by_col = weighted_sums(jnp.abs(tiles[t]), tile_gains[0, 0, t])
            degree[pl.ds(r, 1), :] += by_row
            degree[pl.ds(c, 1), :] += by_col
        return 0

    lax.fori_loop(0, chunks, step, 0)


def scale_kernel(raw, gains, scaled):
    row_gain = jnp.transpose(gains[0, 0, :, 0, :])
    for k in range(raw.shape[2]):
        scaled[k] = (
            row_gain[:, k : k + 1] * raw[0, 0, k].astype(F32) * gains[0, 0, k, 1:2, :]
        ).astype(BF16)


def scale(weights, gains, name):
    count = weights.shape[2]
    return pl.pallas_call(
        scale_kernel,
        out_shape=shape((count, TILE, TILE), BF16),
        grid=(count // CHUNK,),
        in_specs=[
            pl.BlockSpec((1, 1, CHUNK, TILE, TILE), lambda n: (0, 0, n, 0, 0)),
            pl.BlockSpec((1, 1, CHUNK, 2, TILE), lambda n: (0, 0, n, 0, 0)),
        ],
        out_specs=pl.BlockSpec((CHUNK, TILE, TILE), lambda n: (n, 0, 0)),
        cost_estimate=pl.CostEstimate(
            flops=2 * count * TILE * TILE, bytes_accessed=4 * count * TILE * TILE, transcendentals=0
        ),
        compiler_params=pltpu.CompilerParams(vmem_limit_bytes=VMEM_LIMIT),
        name=name,
    )(weights, gains)


def join_degree_kernel(arrived, row_degree, local_degree, joined):
    total = row_degree[...] + local_degree[...]
    sub = lax.broadcasted_iota(jnp.int32, total.shape, 0).astype(F32)
    for g in range(arrived.shape[0]):
        block = arrived[g]
        for m in range(MOST):
            hit = sub == block[MOST + m : MOST + m + 1, :]
            total += jnp.where(hit, block[m : m + 1, :], 0.0)
    joined[...] = total


def outgoing(x, scaled, groups, coords, targets, payload, count):
    group_count = payload.shape[0]
    for g in range(group_count):
        payload[g, MOST : 2 * MOST] = jnp.zeros((MOST, WIDTH, TILE), BF16)
    for t, g, m in slots_of(groups, count, scaled.shape[0], group_count):
        payload[g, MOST + m] = times(x[coords[0, 0, 0, t]], scaled[t]).astype(BF16)
    for g in range(group_count):
        for m in range(MOST):
            payload[g, m] = x[jnp.maximum(targets[g, m], 0)]


def first_block_kernel(
    start, scaled, groups, coords, targets, mine, theirs, inv_root, x, payload, count
):
    inv = 1.0 / jnp.sqrt(mine[...] + theirs[...])
    inv_root[...] = inv
    for k in range(BR):
        x[k] = (start[:, k * TILE : (k + 1) * TILE] * inv[k : k + 1, :]).astype(BF16)
    outgoing(x, scaled, groups, coords, targets, payload, count)


def pair_sum_kernel(mine, theirs, total, sent):
    value = mine[...] + theirs[...].astype(F32)
    total[...] = value
    sent[...] = value.astype(BF16)


def next_block_kernel(
    vertices, scaled, inv_root, groups, coords, targets, mine, theirs, x, payload, count
):
    gram = jnp.zeros((2 * WIDTH, 2 * WIDTH), F32)
    for k in range(BR):
        value = mine[k] + theirs[k].astype(F32)
        root = inv_root[k : k + 1, :]
        image = value * root
        x[k] = (image * root).astype(BF16)
        high = image.astype(BF16)
        halves = jnp.concatenate([high, (image - high.astype(F32)).astype(BF16)], axis=0)
        gram += times_t(halves, halves)
    outgoing(x, scaled, groups, coords, targets, payload, count)
    low = gram[:WIDTH, WIDTH:] + gram[WIDTH:, :WIDTH] + gram[WIDTH:, WIDTH:]
    gram = (gram[:WIDTH, :WIDTH] + low) / vertices
    high = gram.astype(BF16)
    middle = (gram - high.astype(F32)).astype(BF16)
    low = (gram - high.astype(F32) - middle.astype(F32)).astype(BF16)
    block = jnp.concatenate(
        [high, middle, low, jnp.zeros((WIDTH, TILE - 3 * WIDTH), BF16)], axis=1
    )
    for g in range(payload.shape[0]):
        payload[g, 2 * MOST] = block


def local_products_kernel(x, weights, gains, coords, partial, tiles, sems):
    count, chunk = weights.shape[2], tiles.shape[0] // sems.shape[0]
    batch = 2 * CHUNK if count % (2 * CHUNK) == 0 else CHUNK

    def copy_of(n):
        part = pl.ds(n * chunk, chunk)
        return pltpu.make_async_copy(weights.at[0, 0, part], tiles.at[part], sems.at[n])

    for n in range(count // chunk):
        copy_of(n).start()
    partial[...] = jnp.zeros(partial.shape, F32)

    def step(n, _):
        for k in range(batch // chunk):
            copy_of(n * (batch // chunk) + k).wait()
        base = n * batch
        row_gains = [
            jnp.transpose(gains[0, 0, pl.ds(base + k, CHUNK), 0, :]) for k in range(0, batch, CHUNK)
        ]
        places, results = [], []
        for k in range(batch):
            t = base + k
            r, c = coords[0, 0, 0, t], coords[0, 0, 1, t]
            row_gain = row_gains[k // CHUNK][:, k % CHUNK : k % CHUNK + 1]
            tile = (row_gain * tiles[t].astype(F32) * gains[0, 0, t, 1:2, :]).astype(BF16)
            results.append((times_t(x[c], tile), times(x[r], tile)))
            places.append((r, c))
        for (r, c), (forward, backward) in zip(places, results):
            partial[r] += forward
            partial[c] += backward
        return 0

    lax.fori_loop(0, count // batch, step, 0)


def remote_products_kernel(
    splits, whole, arrived, scaled, partial, groups, coords, targets, *refs
):
    outs, (total, count) = refs[:-2], refs[-2:]
    group_count = arrived.shape[0]
    total[...] = partial[...]
    for t, g, m in slots_of(groups, count, scaled.shape[0], group_count):
        total[coords[0, 0, 0, t]] += times_t(arrived[g, m], scaled[t])
    for g in range(group_count):
        for m in range(MOST):
            total[jnp.maximum(targets[g, m], 0)] += arrived[g, MOST + m].astype(F32)
    if whole:
        for out in outs:
            out[...] = total[...].astype(out.dtype)
        return
    me = lax.axis_index("cols")
    quarter = BR // splits
    for k, out in enumerate(outs):
        base = pl.multiple_of((me ^ k) * quarter, quarter)
        out[...] = total[pl.ds(base, quarter)].astype(out.dtype)


def quarter_sum(pieces, inv_root, me):
    quarter = pieces[0].shape[0]
    images, roots = [], []
    for k in range(quarter):
        value = pieces[0][k]
        for piece in pieces[1:]:
            value += piece[k].astype(F32)
        root = inv_root[pl.ds(me * quarter + k, 1), :]
        images.append(value * root)
        roots.append(root)
    return images, roots


def inverse_factor(gram):
    row = lax.broadcasted_iota(jnp.int32, (WIDTH, 2 * WIDTH), 0)
    col = lax.broadcasted_iota(jnp.int32, (WIDTH, 2 * WIDTH), 1)
    eye = jnp.where(
        lax.broadcasted_iota(jnp.int32, (WIDTH, WIDTH), 0)
        == lax.broadcasted_iota(jnp.int32, (WIDTH, WIDTH), 1),
        1.0,
        0.0,
    ).astype(F32)
    work = jnp.concatenate([gram, eye], axis=1)
    for k in range(WIDTH - 1):
        pivot = work[k : k + 1, :]
        factor = work[:, k : k + 1] / work[k : k + 1, k : k + 1]
        work = work - jnp.where(row > k, factor * pivot, 0.0)
    diagonal = jnp.sum(jnp.where(row == col, work, 0.0), axis=1, keepdims=True)
    return work[:, WIDTH:] / jnp.sqrt(diagonal)


def middle_factor_kernel(arrived, inverse):
    gram = jnp.zeros((WIDTH, WIDTH), F32)
    for g in range(arrived.shape[0]):
        block = arrived[g, 2 * MOST].astype(F32)
        gram += (block[:, 2 * WIDTH : 3 * WIDTH] + block[:, WIDTH : 2 * WIDTH]) + block[:, :WIDTH]
    inverse[...] = inverse_factor(gram)


def last_quarter_kernel(splits, vertices, inv_root, inverse, *refs):
    pieces, (image_out, grams) = refs[:splits], refs[splits:]
    images, _ = quarter_sum(pieces, inv_root, lax.axis_index("cols"))
    first = inverse[...]
    gram = jnp.zeros((WIDTH, WIDTH), F32)
    for k, image in enumerate(images):
        value = jnp.dot(first, image, precision=HIGHEST, preferred_element_type=F32)
        image_out[:, k * TILE : (k + 1) * TILE] = value
        gram += lax.dot_general(
            value, value, (((1,), (1,)), ((), ())), precision=HIGHEST, preferred_element_type=F32
        )
    gram = gram / vertices
    block = jnp.concatenate(
        [gram[4 * n : 4 * n + 4] for n in range(4)] + [jnp.zeros((4, 128 - 4 * WIDTH), F32)], axis=1
    )
    for n in range(grams.shape[0]):
        grams[n] = block


def finish_kernel(grams, image, out):
    block = grams[0]
    for n in range(1, grams.shape[0]):
        block = block + grams[n]
    gram = jnp.concatenate([block[:, WIDTH * n : WIDTH * (n + 1)] for n in range(4)], axis=0)
    out[...] = jnp.dot(
        inverse_factor(gram), image[...], precision=HIGHEST, preferred_element_type=F32
    )


def per_device(
    local_weights,
    local_gains,
    local_coords,
    remote_weights,
    remote_gains,
    remote_groups,
    remote_coords,
    start_block,
):
    groups = lax.axis_size("rows")
    splits = lax.axis_size("cols")
    vertices = groups * BR * TILE
    quarter = BR // splits
    local_coords, remote_coords = jnp.swapaxes(local_coords, 2, 3), jnp.swapaxes(remote_coords, 2, 3)
    local_tiles, remote_tiles = local_weights.shape[2], remote_weights.shape[2]
    count = pltpu.SMEM((groups,), jnp.int32)

    def swap(value, k):
        return lax.ppermute(value, "cols", [(j, j ^ k) for j in range(splits)])

    def trade(value):
        return lax.all_to_all(value, "rows", split_axis=0, concat_axis=0, tiled=True)

    listing = (remote_weights, remote_gains, remote_groups, remote_coords)
    sums, row_degree = call(
        functools.partial(remote_degree_kernel, groups),
        (shape((groups, 8, TILE)), shape((BR, TILE))),
        [hbm, hbm, hbm, hbm],
        [
            pltpu.VMEM(remote_weights.shape, BF16),
            pltpu.VMEM(remote_gains.shape, F32),
            pltpu.SMEM(remote_groups.shape, jnp.int32),
            pltpu.SMEM(remote_coords.shape, jnp.int32),
            count,
            pltpu.SemaphoreType.DMA((4,)),
        ],
        name="remote_degree",
    )(*[in_hbm(value) for value in listing])
    sums_in = trade(sums)
    local_degree = call(
        local_degree_kernel,
        shape((BR, TILE)),
        [hbm, hbm, hbm],
        [
            pltpu.VMEM((local_tiles, TILE, TILE), BF16),
            pltpu.VMEM(local_gains.shape, F32),
            pltpu.SMEM(local_coords.shape, jnp.int32),
            pltpu.SemaphoreType.DMA((local_tiles // CHUNK,)),
            pltpu.SemaphoreType.DMA((2,)),
        ],
        moved=10**7,
        name="local_degree",
    )(*[in_hbm(value) for value in (local_weights, local_gains, local_coords)])
    targets = sums_in[:, MOST : 2 * MOST, 0].astype(jnp.int32)
    joined = call(
        join_degree_kernel, shape((BR, TILE)), [vmem, vmem, vmem], name="join_degree"
    )(sums_in, row_degree, local_degree)
    step = 1
    while 2 * step < splits:
        joined = joined + swap(joined, step)
        step *= 2
    degrees = [joined, swap(joined, step)]
    remote_scaled = scale(remote_weights, remote_gains, "remote_scale")
    inv_root, x, payload = call(
        first_block_kernel,
        (
            shape((BR, TILE)),
            shape((BR, WIDTH, TILE), BF16),
            shape((groups, 2 * MOST, WIDTH, TILE), BF16),
        ),
        [vmem, vmem, smem, smem, smem, vmem, vmem],
        [count],
        name="first_block",
    )(start_block, remote_scaled, remote_groups, remote_coords, targets, *degrees)

    def product(x, payload, out_shape, whole):
        arrived = trade(payload)
        partial = call(
            local_products_kernel,
            shape((BR, WIDTH, TILE)),
            [vmem, hbm, vmem, smem],
            [
                pltpu.VMEM((local_tiles, TILE, TILE), BF16),
                pltpu.SemaphoreType.DMA((local_tiles // 4,)),
            ],
            moved=10**7,
            name="local_products",
        )(x, local_weights, local_gains, local_coords)
        return arrived, call(
            functools.partial(remote_products_kernel, splits, whole),
            out_shape,
            [vmem, vmem, vmem, smem, smem, smem],
            [pltpu.VMEM((BR, WIDTH, TILE), F32), count],
            name="remote_products",
        )(arrived, remote_scaled, partial, remote_groups, remote_coords, targets)

    _, (own, sent) = product(
        x, payload, (shape((BR, WIDTH, TILE)), shape((BR, WIDTH, TILE), BF16)), True
    )
    step = 1
    while 2 * step < splits:
        own, sent = call(
            pair_sum_kernel,
            (shape((BR, WIDTH, TILE)), shape((BR, WIDTH, TILE), BF16)),
            [vmem, vmem],
            name="pair_sum",
        )(own, swap(sent, step))
        step *= 2
    pieces = [own, swap(sent, step)]
    x, payload = call(
        functools.partial(next_block_kernel, vertices),
        (
            shape((BR, WIDTH, TILE), BF16),
            shape((groups, 2 * MOST + 1, WIDTH, TILE), BF16),
        ),
        [vmem, vmem, smem, smem, smem, vmem, vmem],
        [count],
        name="next_block",
    )(remote_scaled, inv_root, remote_groups, remote_coords, targets, *pieces)
    arrived, sent = product(
        x,
        payload,
        tuple(shape((quarter, WIDTH, TILE), BF16 if k else F32) for k in range(splits)),
        False,
    )
    pieces = [sent[0]] + [swap(sent[k], k) for k in range(1, splits)]
    inverse = call(
        middle_factor_kernel, shape((WIDTH, WIDTH)), [vmem], name="middle_factor"
    )(arrived)
    image, grams = call(
        functools.partial(last_quarter_kernel, splits, vertices),
        (shape((WIDTH, quarter * TILE)), shape((groups * splits, 4, 128))),
        [vmem] * (2 + splits),
        name="last_quarter",
    )(inv_root, inverse, *pieces)
    grams = lax.all_to_all(
        grams, ("rows", "cols"), split_axis=0, concat_axis=0, tiled=True
    )
    return call(finish_kernel, shape((WIDTH, quarter * TILE)), [vmem, vmem], name="finish")(
        grams, image
    )


def solution(mesh):
    in_specs = (
        P("rows", "cols", None, None, None),
        P("rows", "cols", None, None, None),
        P("rows", "cols", None, None),
        P("rows", "cols", None, None, None),
        P("rows", "cols", None, None, None),
        P("rows", "cols", None),
        P("rows", "cols", None, None),
        P(None, "rows"),
    )
    out_specs = P(None, ("rows", "cols"))
    return jax.shard_map(
        per_device, mesh=mesh, in_specs=in_specs, out_specs=out_specs, check_vma=False
    )
```

time: 97.9 us -> 86.2 us (0.88)
  waiting for transfers between devices: 13.1 us -> 18.7 us
  Pallas kernels: 35.5 us -> 30.4 us
  local copies, waits for them, and re-layouts: 5.2 us -> 0.21 us
  starting transfers between devices: 31.3 us -> 27.1 us
  blocking collectives: 12.1 us -> 9.19 us
    pallas_call x9 -> x10, Pallas kernels: 31.1 us -> 26 us  [the longest x2 11.4 us: product(): call(local_products_kernel, shape((BR, WIDTH, TILE)), [vmem, hbm, vmem, s...]
    ppermute x12 -> x7, starting transfers between devices: 17.8 us -> 13 us  [swap(): return lax.ppermute(value, 'cols', [(j, j ^ k) for j in range(splits)])]
    unnamed x12 -> x14, local copies, waits for them, and re-layouts: 3.5 us -> 0.03 us
    ppermute x12 -> x7, waiting for transfers between devices: 12.1 us -> 15.5 us  [swap(): return lax.ppermute(value, 'cols', [(j, j ^ k) for j in range(splits)])]
    all_to_all x1, blocking collectives: 12.1 us -> 9.19 us  [per_device(): lax.all_to_all(grams, ('rows', 'cols'), split_axis=0, concat_axis=0, tile...]
    all_to_all x3, waiting for transfers between devices: 1 us -> 3.19 us  [trade(): lax.all_to_all(value, 'rows', split_axis=0, concat_axis=0, tiled=True)]
    squeeze x2 -> x0, local copies, waits for them, and re-layouts: 1.53 us -> none  [the longest x1 0.77 us: per_device(): remote_coords[0, 0]]
  transfers between devices with their start and end apart: 15 -> 10, of which waited for: 10 -> 8; matrix products, arithmetic and copies ran while one was open for 1% -> 0% of each run, Pallas kernels for 25% -> 22%
where the time goes in v2:
time: 86.2 us; the launch traced here: 85.7 us
  Pallas kernels  30.4 us (35%)
  starting transfers between devices  27.1 us (31%)
  waiting for transfers between devices  18.7 us (22%)
  blocking collectives  9.19 us (11%)
    ppermute x7, waiting for transfers between devices, swap(): return lax.ppermute(value, 'cols', [(j, j ^ k) for j in range(splits)])  15.5 us
    all_to_all x3, starting transfers between devices, trade(): lax.all_to_all(value, 'rows', split_axis=0, concat_axis=0, tiled=True)  14.1 us
    ppermute x7, starting transfers between devices, swap(): return lax.ppermute(value, 'cols', [(j, j ^ k) for j in range(splits)])  13 us
    pallas_call x2, Pallas kernels, product(): call(local_products_kernel, shape((BR, WIDTH, TILE)), [vmem, hbm, vmem, s...  11.4 us
    all_to_all x1, blocking collectives, per_device(): lax.all_to_all(grams, ('rows', 'cols'), split_axis=0, concat_axis=0, tile...  9.19 us
    pallas_call x1, Pallas kernels, per_device(): call(local_degree_kernel, shape((BR, TILE)), [hbm, hbm, hbm], [pltpu.VMEM...  5.83 us
    all_to_all x3, waiting for transfers between devices, trade(): lax.all_to_all(value, 'rows', split_axis=0, concat_axis=0, tiled=True)  3.19 us
    pallas_call x1, Pallas kernels, per_device(): call(functools.partial(remote_degree_kernel, groups), (shape((groups, 8,...  2.55 us
  transfers between devices with their start and end apart: 10, of which 8 were waited for; matrix products, arithmetic and copies ran while one was open for 0% of the time, Pallas kernels for 22%

profile of v2, /device:TPU:0, one launch (start us, length us, event | category | flops | bytes accessed | tf_op | source)
XLA Modules:
  0.0 85.7 jit_solution(11533520334289236970)
XLA Ops:
  0.0 2.6 %remote_degree.1 = (f32[8,8,256]{2,1,0:T(8,128)}, f32[16,256]{1,0:T(8,128)S(1)}) custom-call(bf16[1,1,8,256,256]{4,3,2,1,0:T(8,128)(2,1)} %weights.4, f32[1,1,8,2,256]{4,3,2,1,0:T(2,128)} %gains.6, s32[1,1,8]{2,1,0:T(1,128)} %groups.9, s32[1,1,2,8]{3,2,1,0:T(2,128)} %bitcast.3), custom_call_target="tpu_custom_call" | custom-call | flops 1000000 | bytes 1000000 | tf_op jit(solution)/shard_map/remote_degree/pallas_call | solution.py:387
  2.6 5.2 %all-to-all-start = ((f32[8,8,256]{2,1,0:T(8,128)}), f32[8,8,256]{2,1,0:T(8,128)S(1)}, u32[]{:S(2)}, u32[]{:S(2)}) async-start(f32[8,8,256]{2,1,0:T(8,128)} %get-tuple-element.22), calls=%async_computation | async-start | bytes 131072 | tf_op jit(solution)/shard_map/all_to_all | solution.py:384
  7.8 5.8 %local_degree.1 = f32[16,256]{1,0:T(8,128)S(1)} custom-call(bf16[1,1,48,256,256]{4,3,2,1,0:T(8,128)(2,1)} %weights.7, f32[1,1,48,2,256]{4,3,2,1,0:T(2,128)} %gains.9, s32[1,1,2,48]{3,2,1,0:T(2,128)} %bitcast.8), custom_call_target="tpu_custom_call" | custom-call | flops 1000000 | bytes 10000000 | tf_op jit(solution)/shard_map/local_degree/pallas_call | solution.py:402
  13.7 1.6 %collective-permute-start = (f32[16,256]{1,0:T(8,128)S(1)}, f32[16,256]{1,0:T(8,128)S(1)}, u32[]{:S(2)}, u32[]{:S(2)}) collective-permute-start(f32[16,256]{1,0:T(8,128)S(1)} %join_degree.1), channel_id=1, source_target_pairs={{0,1},{1,0},{2,3},{3,2},{4,5},{5,4},{6,7},{7,6},{8,9},{9,8},{10,11... | collective-permute-start | bytes 49160 | tf_op jit(solution)/shard_map/ppermute | solution.py:381
  15.3 0.5 remote_scale.1.scaled
  15.9 1.6 %collective-permute-done = f32[16,256]{1,0:T(8,128)S(1)} collective-permute-done((f32[16,256]{1,0:T(8,128)S(1)}, f32[16,256]{1,0:T(8,128)S(1)}, u32[]{:S(2)}, u32[]{:S(2)}) %collective-permute-start) | collective-permute-done | bytes 16416 | tf_op jit(solution)/shard_map/ppermute | solution.py:381
  17.5 2.6 %collective-permute-start.1 = (f32[16,256]{1,0:T(8,128)S(1)}, f32[16,256]{1,0:T(8,128)S(1)}, u32[]{:S(2)}, u32[]{:S(2)}) collective-permute-start(f32[16,256]{1,0:T(8,128)S(1)} %add.3.mine), channel_id=1, source_target_pairs={{0,2},{1,3},{2,0},{3,1},{4,6},{5,7},{6,4},{7,5},{8,10},{9,11},{10,... | collective-permute-start | bytes 49160 | tf_op jit(solution)/shard_map/ppermute | solution.py:381
  20.1 0.1 copy.14
  20.3 1.9 %collective-permute-done.1.theirs = f32[16,256]{1,0:T(8,128)S(1)} collective-permute-done((f32[16,256]{1,0:T(8,128)S(1)}, f32[16,256]{1,0:T(8,128)S(1)}, u32[]{:S(2)}, u32[]{:S(2)}) %collective-permute-start.1) | collective-permute-done | bytes 16416 | tf_op jit(solution)/shard_map/ppermute | solution.py:381
  22.1 1.6 %first_block.1 = (f32[16,256]{1,0:T(8,128)S(1)}, bf16[16,16,256]{2,1,0:T(8,128)(2,1)S(1)}, bf16[8,4,16,256]{3,2,1,0:T(8,128)(2,1)}) custom-call(f32[16,4096]{1,0:T(8,128)S(1)} %copy-done.2, bf16[8,256,256]{2,1,0:T(8,128)(2,1)S(1)} %remote_scale.1.scaled, s32[1,1,8]{2,1,0:T(1,128)S(1)} %copy-done.5, s32[1,1,2,8]{3,2,1,0:T(2,128)S(1)} %bitcast.4, ...), custom_call_target="tpu_custom_call" | custom-call | flops 1000000 | bytes 1000000 | tf_op jit(solution)/shard_map/first_block/pallas_call | solution.py:426
  23.7 4.2 %all-to-all-start.1 = ((bf16[8,4,16,256]{3,2,1,0:T(8,128)(2,1)}), bf16[8,4,16,256]{3,2,1,0:T(8,128)(2,1)S(1)}, u32[]{:S(2)}, u32[]{:S(2)}) async-start(bf16[8,4,16,256]{3,2,1,0:T(8,128)(2,1)} %get-tuple-element.25), calls=%async_computation.1 | async-start | bytes 524288 | tf_op jit(solution)/shard_map/all_to_all | solution.py:384
  28.0 5.7 %local_products.2.partial = f32[16,16,256]{2,1,0:T(8,128)S(1)} custom-call(bf16[16,16,256]{2,1,0:T(8,128)(2,1)S(1)} %get-tuple-element.26.x, bf16[1,1,48,256,256]{4,3,2,1,0:T(8,128)(2,1)} %weights.7, f32[1,1,48,2,256]{4,3,2,1,0:T(2,128)S(1)} %copy-done.1, s32[1,1,2,48]{3,2,1,0:T(2,128)S(1)} %bitcast.9), custom_call_target="tpu_custom_call" | custom-call | flops 1000000 | bytes 10000000 | tf_op jit(solution)/shard_map/local_products/pallas_call | solution.py:440
  33.6 1.2 %all-to-all-done.1.arrived = bf16[8,4,16,256]{3,2,1,0:T(8,128)(2,1)S(1)} async-done(((bf16[8,4,16,256]{3,2,1,0:T(8,128)(2,1)}), bf16[8,4,16,256]{3,2,1,0:T(8,128)(2,1)S(1)}, u32[]{:S(2)}, u32[]{:S(2)}) %all-to-all-start.1) | async-done | bytes 262176 | tf_op jit(solution)/shard_map/all_to_all | solution.py:384
  34.9 1.1 %remote_products.2 = (f32[16,16,256]{2,1,0:T(8,128)S(1)}, bf16[16,16,256]{2,1,0:T(8,128)(2,1)S(1)}) custom-call(bf16[8,4,16,256]{3,2,1,0:T(8,128)(2,1)S(1)} %all-to-all-done.1.arrived, bf16[8,256,256]{2,1,0:T(8,128)(2,1)S(1)} %remote_scale.1.scaled, f32[16,16,256]{2,1,0:T(8,128)S(1)} %local_products.2.partial, s32[1,1,8]{2,1,0:T(1,128)S(1)} %copy-done.5, ...), custom_call_target="tpu_custom_call" | custom-call | flops 1000000 | bytes 1000000 | tf_op jit(solution)/shard_map/remote_products/pallas_call | solution.py:451
  36.0 1.7 %collective-permute-start.2 = (bf16[16,16,256]{2,1,0:T(8,128)(2,1)S(1)}, bf16[16,16,256]{2,1,0:T(8,128)(2,1)S(1)}, u32[]{:S(2)}, u32[]{:S(2)}) collective-permute-start(bf16[16,16,256]{2,1,0:T(8,128)(2,1)S(1)} %get-tuple-element.28), channel_id=1, source_target_pairs={{0,1},{1,0},{2,3},{3,2},{4,5},{5,4},{6,7},{7,6},{8,9},{9,8},{10,11... | collective-permute-start | bytes 393224 | tf_op jit(solution)/shard_map/ppermute | solution.py:381
  37.7 3.4 %collective-permute-done.2.theirs = bf16[16,16,256]{2,1,0:T(8,128)(2,1)S(1)} collective-permute-done((bf16[16,16,256]{2,1,0:T(8,128)(2,1)S(1)}, bf16[16,16,256]{2,1,0:T(8,128)(2,1)S(1)}, u32[]{:S(2)}, u32[]{:S(2)}) %collective-permute-start.2) | collective-permute-done | bytes 131104 | tf_op jit(solution)/shard_map/ppermute | solution.py:381
  41.1 2.7 %collective-permute-start.3 = (bf16[16,16,256]{2,1,0:T(8,128)(2,1)S(1)}, bf16[16,16,256]{2,1,0:T(8,128)(2,1)S(1)}, u32[]{:S(2)}, u32[]{:S(2)}) collective-permute-start(bf16[16,16,256]{2,1,0:T(8,128)(2,1)S(1)} %get-tuple-element.30), channel_id=1, source_target_pairs={{0,2},{1,3},{2,0},{3,1},{4,6},{5,7},{6,4},{7,5},{8,10},{9,11},{10,... | collective-permute-start | bytes 393224 | tf_op jit(solution)/shard_map/ppermute | solution.py:381
  43.7 4.7 %collective-permute-done.3.theirs = bf16[16,16,256]{2,1,0:T(8,128)(2,1)S(1)} collective-permute-done((bf16[16,16,256]{2,1,0:T(8,128)(2,1)S(1)}, bf16[16,16,256]{2,1,0:T(8,128)(2,1)S(1)}, u32[]{:S(2)}, u32[]{:S(2)}) %collective-permute-start.3) | collective-permute-done | bytes 131104 | tf_op jit(solution)/shard_map/ppermute | solution.py:381
  48.4 1.8 %next_block.1 = (bf16[16,16,256]{2,1,0:T(8,128)(2,1)S(1)}, bf16[8,5,16,256]{3,2,1,0:T(8,128)(2,1)}) custom-call(bf16[8,256,256]{2,1,0:T(8,128)(2,1)S(1)} %remote_scale.1.scaled, f32[16,256]{1,0:T(8,128)S(1)} %get-tuple-element.24.inv_root, s32[1,1,8]{2,1,0:T(1,128)S(1)} %copy-done.5, s32[1,1,2,8]{3,2,1,0:T(2,128)S(1)} %bitcast.6, s32[8,2]{1,0:T(8,128)S(1)} %copy.15.targets, ...), custom_call_target="tpu_custom_call" | custom-call | flops 1000000 | bytes 1000000 | tf_op jit(solution)/shard_map/next_block/pallas_call | solution.py:472
  50.3 4.7 %all-to-all-start.2 = ((bf16[8,5,16,256]{3,2,1,0:T(8,128)(2,1)}), bf16[8,5,16,256]{3,2,1,0:T(8,128)(2,1)S(1)}, u32[]{:S(2)}, u32[]{:S(2)}) async-start(bf16[8,5,16,256]{3,2,1,0:T(8,128)(2,1)} %get-tuple-element.31), calls=%async_computation.2 | async-start | bytes 655360 | tf_op jit(solution)/shard_map/all_to_all | solution.py:384
  54.9 5.7 %local_products.3.partial = f32[16,16,256]{2,1,0:T(8,128)S(1)} custom-call(bf16[16,16,256]{2,1,0:T(8,128)(2,1)S(1)} %get-tuple-element.32.x, bf16[1,1,48,256,256]{4,3,2,1,0:T(8,128)(2,1)} %weights.7, f32[1,1,48,2,256]{4,3,2,1,0:T(2,128)S(1)} %copy-done.1, s32[1,1,2,48]{3,2,1,0:T(2,128)S(1)} %bitcast.10), custom_call_target="tpu_custom_call" | custom-call | flops 1000000 | bytes 10000000 | tf_op jit(solution)/shard_map/local_products/pallas_call | solution.py:440
  60.6 2.0 %all-to-all-done.2.arrived = bf16[8,5,16,256]{3,2,1,0:T(8,128)(2,1)S(1)} async-done(((bf16[8,5,16,256]{3,2,1,0:T(8,128)(2,1)}), bf16[8,5,16,256]{3,2,1,0:T(8,128)(2,1)S(1)}, u32[]{:S(2)}, u32[]{:S(2)}) %all-to-all-start.2) | async-done | bytes 327712 | tf_op jit(solution)/shard_map/all_to_all | solution.py:384
  62.6 1.1 %remote_products.3 = (f32[4,16,256]{2,1,0:T(8,128)S(1)}, bf16[4,16,256]{2,1,0:T(8,128)(2,1)S(1)}, bf16[4,16,256]{2,1,0:T(8,128)(2,1)S(1)}, bf16[4,16,256]{2,1,0:T(8,128)(2,1)S(1)}) custom-call(bf16[8,5,16,256]{3,2,1,0:T(8,128)(2,1)S(1)} %all-to-all-done.2.arrived, bf16[8,256,256]{2,1,0:T(8,128)(2,1)S(1)} %remote_scale.1.scaled, ...), custom_call_target="tpu_custom_call" | custom-call | flops 1000000 | bytes 1000000 | tf_op jit(solution)/shard_map/remote_products/pallas_call | solution.py:451
  63.7 0.8 collective-permute-start.4
  64.5 3.4 %collective-permute-start.5 = (bf16[4,16,256]{2,1,0:T(8,128)(2,1)S(1)}, bf16[4,16,256]{2,1,0:T(8,128)(2,1)S(1)}, u32[]{:S(2)}, u32[]{:S(2)}) collective-permute-start(bf16[4,16,256]{2,1,0:T(8,128)(2,1)S(1)} %get-tuple-element.35), channel_id=1, source_target_pairs={{0,2},{1,3},{2,0},{3,1},{4,6},{5,7},{6,4},{7,5},{8,10},{9,11},{10,... | collective-permute-start | bytes 98312 | tf_op jit(solution)/shard_map/ppermute | solution.py:381
  67.8 0.3 collective-permute-start.6
  68.1 1.5 %middle_factor.1.inverse = f32[16,16]{1,0:T(8,128)S(1)} custom-call(bf16[8,5,16,256]{3,2,1,0:T(8,128)(2,1)S(1)} %all-to-all-done.2.arrived), custom_call_target="tpu_custom_call" | custom-call | flops 1000000 | bytes 1000000 | tf_op jit(solution)/shard_map/middle_factor/pallas_call | solution.py:489
  69.6 0.1 collective-permute-done.5.refs_2_
  69.7 3.8 %collective-permute-done.6.refs_3_ = bf16[4,16,256]{2,1,0:T(8,128)(2,1)S(1)} collective-permute-done((bf16[4,16,256]{2,1,0:T(8,128)(2,1)S(1)}, bf16[4,16,256]{2,1,0:T(8,128)(2,1)S(1)}, u32[]{:S(2)}, u32[]{:S(2)}) %collective-permute-start.6) | collective-permute-done | bytes 32800 | tf_op jit(solution)/shard_map/ppermute | solution.py:381
  73.5 0.7 last_quarter.1
  74.2 9.2 %all_to_all.20.grams = f32[32,4,128]{2,1,0:T(4,128)S(1)} all-to-all(f32[32,4,128]{2,1,0:T(4,128)S(1)} %get-tuple-element.37), channel_id=1, replica_groups=mesh['rows'=8,'cols'=4] {'rows','cols'}, dimensions={0} | all-to-all | bytes 131072 | tf_op jit(solution)/shard_map/all_to_all | solution.py:498
  83.4 2.3 %finish.1 = f32[16,1024]{1,0:T(8,128)} custom-call(f32[32,4,128]{2,1,0:T(4,128)S(1)} %all_to_all.20.grams, f32[16,1024]{1,0:T(8,128)S(1)} %get-tuple-element.38.image), custom_call_target="tpu_custom_call" | custom-call | flops 1000000 | bytes 1000000 | tf_op jit(solution)/shard_map/finish/pallas_call | solution.py:501
  (21 shorter events, 0.2 us)
Async XLA Ops:
  0.0 22.1 %copy-start.5 = (s32[1,1,8]{2,1,0:T(1,128)S(1)}, s32[1,1,8]{2,1,0:T(1,128)}, u32[]{:S(2)}) copy-start(s32[1,1,8]{2,1,0:T(1,128)} %groups.9) | copy-start | bytes 100
  0.0 15.3 %copy-start.3 = (f32[1,1,8,2,256]{4,3,2,1,0:T(2,128)S(1)}, f32[1,1,8,2,256]{4,3,2,1,0:T(2,128)}, u32[]{:S(2)}) copy-start(f32[1,1,8,2,256]{4,3,2,1,0:T(2,128)} %gains.6) | copy-start | bytes 49156
  0.0 15.3 %copy-start = (bf16[1,1,8,256,256]{4,3,2,1,0:T(8,128)(2,1)S(1)}, bf16[1,1,8,256,256]{4,3,2,1,0:T(8,128)(2,1)}, u32[]{:S(2)}) copy-start(bf16[1,1,8,256,256]{4,3,2,1,0:T(8,128)(2,1)} %weights.4) | copy-start | bytes 3145732
  0.0 22.1 %copy-start.4 = (s32[1,1,8,2]{2,3,1,0:T(2,128)S(1)}, s32[1,1,8,2]{2,3,1,0:T(2,128)}, u32[]{:S(2)}) copy-start(s32[1,1,8,2]{2,3,1,0:T(2,128)} %param.14) | copy-start | bytes 196
  0.0 27.9 %copy-start.1 = (f32[1,1,48,2,256]{4,3,2,1,0:T(2,128)S(1)}, f32[1,1,48,2,256]{4,3,2,1,0:T(2,128)}, u32[]{:S(2)}) copy-start(f32[1,1,48,2,256]{4,3,2,1,0:T(2,128)} %gains.9) | copy-start | bytes 294916
  0.0 27.9 %copy-start.6 = (s32[1,1,48,2]{2,3,1,0:T(2,128)S(1)}, s32[1,1,48,2]{2,3,1,0:T(2,128)}, u32[]{:S(2)}) copy-start(s32[1,1,48,2]{2,3,1,0:T(2,128)} %param.10) | copy-start | bytes 1156
  0.0 22.1 %copy-start.2 = (f32[16,4096]{1,0:T(8,128)S(1)}, f32[16,4096]{1,0:T(8,128)}, u32[]{:S(2)}) copy-start(f32[16,4096]{1,0:T(8,128)} %start.1) | copy-start | bytes 786436
  2.6 11.0 %all-to-all-start = ((f32[8,8,256]{2,1,0:T(8,128)}), f32[8,8,256]{2,1,0:T(8,128)S(1)}, u32[]{:S(2)}, u32[]{:S(2)}) async-start(f32[8,8,256]{2,1,0:T(8,128)} %get-tuple-element.22), calls=%async_computation | async-start | bytes 131072 | tf_op jit(solution)/shard_map/all_to_all | solution.py:384
  13.7 3.8 %collective-permute-start = (f32[16,256]{1,0:T(8,128)S(1)}, f32[16,256]{1,0:T(8,128)S(1)}, u32[]{:S(2)}, u32[]{:S(2)}) collective-permute-start(f32[16,256]{1,0:T(8,128)S(1)} %join_degree.1), channel_id=1, source_target_pairs={{0,1},{1,0},{2,3},{3,2},{4,5},{5,4},{6,7},{7,6},{8,9},{9,8},{10,11... | collective-permute-start | bytes 49160 | tf_op jit(solution)/shard_map/ppermute | solution.py:381
  17.5 4.6 %collective-permute-start.1 = (f32[16,256]{1,0:T(8,128)S(1)}, f32[16,256]{1,0:T(8,128)S(1)}, u32[]{:S(2)}, u32[]{:S(2)}) collective-permute-start(f32[16,256]{1,0:T(8,128)S(1)} %add.3.mine), channel_id=1, source_target_pairs={{0,2},{1,3},{2,0},{3,1},{4,6},{5,7},{6,4},{7,5},{8,10},{9,11},{10,... | collective-permute-start | bytes 49160 | tf_op jit(solution)/shard_map/ppermute | solution.py:381
  23.7 11.1 %all-to-all-start.1 = ((bf16[8,4,16,256]{3,2,1,0:T(8,128)(2,1)}), bf16[8,4,16,256]{3,2,1,0:T(8,128)(2,1)S(1)}, u32[]{:S(2)}, u32[]{:S(2)}) async-start(bf16[8,4,16,256]{3,2,1,0:T(8,128)(2,1)} %get-tuple-element.25), calls=%async_computation.1 | async-start | bytes 524288 | tf_op jit(solution)/shard_map/all_to_all | solution.py:384
  36.0 5.0 %collective-permute-start.2 = (bf16[16,16,256]{2,1,0:T(8,128)(2,1)S(1)}, bf16[16,16,256]{2,1,0:T(8,128)(2,1)S(1)}, u32[]{:S(2)}, u32[]{:S(2)}) collective-permute-start(bf16[16,16,256]{2,1,0:T(8,128)(2,1)S(1)} %get-tuple-element.28), channel_id=1, source_target_pairs={{0,1},{1,0},{2,3},{3,2},{4,5},{5,4},{6,7},{7,6},{8,9},{9,8},{10,11... | collective-permute-start | bytes 393224 | tf_op jit(solution)/shard_map/ppermute | solution.py:381
  41.1 7.3 %collective-permute-start.3 = (bf16[16,16,256]{2,1,0:T(8,128)(2,1)S(1)}, bf16[16,16,256]{2,1,0:T(8,128)(2,1)S(1)}, u32[]{:S(2)}, u32[]{:S(2)}) collective-permute-start(bf16[16,16,256]{2,1,0:T(8,128)(2,1)S(1)} %get-tuple-element.30), channel_id=1, source_target_pairs={{0,2},{1,3},{2,0},{3,1},{4,6},{5,7},{6,4},{7,5},{8,10},{9,11},{10,... | collective-permute-start | bytes 393224 | tf_op jit(solution)/shard_map/ppermute | solution.py:381
  50.3 12.3 %all-to-all-start.2 = ((bf16[8,5,16,256]{3,2,1,0:T(8,128)(2,1)}), bf16[8,5,16,256]{3,2,1,0:T(8,128)(2,1)S(1)}, u32[]{:S(2)}, u32[]{:S(2)}) async-start(bf16[8,5,16,256]{3,2,1,0:T(8,128)(2,1)} %get-tuple-element.31), calls=%async_computation.2 | async-start | bytes 655360 | tf_op jit(solution)/shard_map/all_to_all | solution.py:384
  63.7 5.9 %collective-permute-start.4 = (bf16[4,16,256]{2,1,0:T(8,128)(2,1)S(1)}, bf16[4,16,256]{2,1,0:T(8,128)(2,1)S(1)}, u32[]{:S(2)}, u32[]{:S(2)}) collective-permute-start(bf16[4,16,256]{2,1,0:T(8,128)(2,1)S(1)} %get-tuple-element.34), channel_id=1, source_target_pairs={{0,1},{1,0},{2,3},{3,2},{4,5},{5,4},{6,7},{7,6},{8,9},{9,8},{10,11... | collective-permute-start | bytes 98312 | tf_op jit(solution)/shard_map/ppermute | solution.py:381
  64.5 5.3 %collective-permute-start.5 = (bf16[4,16,256]{2,1,0:T(8,128)(2,1)S(1)}, bf16[4,16,256]{2,1,0:T(8,128)(2,1)S(1)}, u32[]{:S(2)}, u32[]{:S(2)}) collective-permute-start(bf16[4,16,256]{2,1,0:T(8,128)(2,1)S(1)} %get-tuple-element.35), channel_id=1, source_target_pairs={{0,2},{1,3},{2,0},{3,1},{4,6},{5,7},{6,4},{7,5},{8,10},{9,11},{10,... | collective-permute-start | bytes 98312 | tf_op jit(solution)/shard_map/ppermute | solution.py:381
  67.8 5.7 %collective-permute-start.6 = (bf16[4,16,256]{2,1,0:T(8,128)(2,1)S(1)}, bf16[4,16,256]{2,1,0:T(8,128)(2,1)S(1)}, u32[]{:S(2)}, u32[]{:S(2)}) collective-permute-start(bf16[4,16,256]{2,1,0:T(8,128)(2,1)S(1)} %get-tuple-element.36), channel_id=1, source_target_pairs={{0,3},{1,2},{2,1},{3,0},{4,7},{5,6},{6,5},{7,4},{8,11},{9,10},{10,... | collective-permute-start | bytes 98312 | tf_op jit(solution)/shard_map/ppermute | solution.py:381

commit v3 on v2

--- a/solution.py
+++ b/solution.py
@@ -12,6 +12,7 @@
 BR = 16
 MOST = 2
 CHUNK = 8
+LANES = 128
 F32 = jnp.float32
 BF16 = jnp.bfloat16
 HIGHEST = lax.Precision.HIGHEST
@@ -20,6 +21,7 @@
 vmem = pl.BlockSpec(memory_space=pltpu.VMEM)
 smem = pl.BlockSpec(memory_space=pltpu.SMEM)
 hbm = pl.BlockSpec(memory_space=pltpu.HBM)
+anywhere = pl.BlockSpec(memory_space=pl.ANY)
 
 
 def shape(dims, dtype=F32):
@@ -49,6 +51,21 @@
 
 def in_hbm(value):
     return pltpu.with_memory_space_constraint(value, pltpu.HBM)
+
+
+def fetch(sources, targets, sems):
+    copies = [
+        pltpu.make_async_copy(source, target, sems.at[n])
+        for n, (source, target) in enumerate(zip(sources, targets))
+    ]
+    for copy in copies:
+        copy.start()
+
+    def wait():
+        for copy in copies:
+            copy.wait()
+
+    return wait
 
 
 def slots_of(groups_ref, count_ref, tile_count, group_count):
@@ -86,21 +103,15 @@
     count,
     sems,
 ):
-    copies = [
-        pltpu.make_async_copy(source, target, sems.at[n])
-        for n, (source, target) in enumerate(
-            [(groups, tile_groups), (coords, tile_coords), (gains, tile_gains), (weights, tiles)]
-        )
-    ]
-    for copy in copies:
-        copy.start()
+    wait = fetch(
+        (groups, coords, gains, weights), (tile_groups, tile_coords, tile_gains, tiles), sems
+    )
     sub = lax.broadcasted_iota(jnp.int32, (8, TILE), 0)
     blank = jnp.where((sub >= MOST) & (sub < 2 * MOST), -1.0, 0.0).astype(F32)
     for g in range(group_count):
         payload[g] = blank
     row_degree[...] = jnp.zeros(row_degree.shape, F32)
-    for copy in copies:
-        copy.wait()
+    wait()
     places = slots_of(tile_groups, count, weights.shape[2], group_count)
     for t, g, m in places:
         r, c = tile_coords[0, 0, 0, t], tile_coords[0, 0, 1, t]
@@ -113,10 +124,12 @@
 def local_degree_kernel(
     weights, gains, coords, degree, tiles, tile_gains, tile_coords, sems, small_sems
 ):
-    chunks = weights.shape[2] // CHUNK
+    chunk = CHUNK
+    chunks = weights.shape[2] // chunk
+    batch = 2 * chunk if chunks % 2 == 0 else chunk
 
     def copy_of(n):
-        part = pl.ds(n * CHUNK, CHUNK)
+        part = pl.ds(n * chunk, chunk)
         return pltpu.make_async_copy(weights.at[0, 0, part], tiles.at[part], sems.at[n])
 
     small = [
@@ -132,16 +145,17 @@
         copy.wait()
 
     def step(n, _):
-        copy_of(n).wait()
-        for k in range(CHUNK):
-            t = n * CHUNK + k
+        for k in range(batch // chunk):
+            copy_of(n * (batch // chunk) + k).wait()
+        for k in range(batch):
+            t = n * batch + k
             r, c = tile_coords[0, 0, 0, t], tile_coords[0, 0, 1, t]
             by_row, by_col = weighted_sums(jnp.abs(tiles[t]), tile_gains[0, 0, t])
             degree[pl.ds(r, 1), :] += by_row
             degree[pl.ds(c, 1), :] += by_col
         return 0
 
-    lax.fori_loop(0, chunks, step, 0)
+    lax.fori_loop(0, chunks * chunk // batch, step, 0)
 
 
 def scale_kernel(raw, gains, scaled):
@@ -182,25 +196,69 @@
     joined[...] = total
 
 
-def outgoing(x, scaled, groups, coords, targets, payload, count):
-    group_count = payload.shape[0]
+def by_chips(groups):
+    return groups // 2 <= 4
+
+
+def place_of(group, group_count, core):
+    if not by_chips(group_count):
+        return group
+    return ((group + core) % 2) * (group_count // 2) + group // 2
+
+
+def outgoing(x, scaled, groups, coords, targets, staged, count, gram=None):
+    group_count = staged.shape[0]
+    core = lax.axis_index("rows") % 2
     for g in range(group_count):
-        payload[g, MOST : 2 * MOST] = jnp.zeros((MOST, WIDTH, TILE), BF16)
+        staged[g, MOST : 2 * MOST] = jnp.zeros((MOST, WIDTH, TILE), BF16)
+        if gram is not None:
+            staged[g, 2 * MOST] = gram
     for t, g, m in slots_of(groups, count, scaled.shape[0], group_count):
-        payload[g, MOST + m] = times(x[coords[0, 0, 0, t]], scaled[t]).astype(BF16)
+        place = place_of(g, group_count, core)
+        staged[place, MOST + m] = times(x[coords[0, 0, 0, t]], scaled[t]).astype(BF16)
     for g in range(group_count):
+        place = place_of(g, group_count, core)
         for m in range(MOST):
-            payload[g, m] = x[jnp.maximum(targets[g, m], 0)]
+            staged[place, m] = x[jnp.maximum(targets[g, m], 0)]
+
+
+def split_out(staged, outs):
+    size = outs[0].shape[0]
+    for k, out in enumerate(outs):
+        out[...] = staged[k * size : (k + 1) * size]
+
+
+def forward_kernel(near, passed, *pieces):
+    chips = near.shape[0]
+    me = lax.axis_index("rows")
+    chip, core = me // 2, me % 2
+    for k, piece in enumerate(pieces):
+        piece[core] = near[chip ^ k]
+        piece[1 - core] = passed[chip ^ k]
+
+
+def by_group(arrived, joined):
+    if len(arrived) == 1:
+        joined[...] = arrived[0][...]
+        return
+    chip = lax.axis_index("rows") // 2
+    for k, piece in enumerate(arrived):
+        joined[pl.ds((chip ^ k) * 2, 2)] = piece[...]
 
 
 def first_block_kernel(
-    start, scaled, groups, coords, targets, mine, theirs, inv_root, x, payload, count
+    start, scaled, groups, coords, targets, mine, theirs, inv_root, x, *refs
 ):
+    *outs, tile_groups, tile_coords, tile_targets, count, sems, staged = refs
+    routes = (tile_groups, tile_coords, tile_targets)
+    wait = fetch((groups, coords, targets), routes, sems)
     inv = 1.0 / jnp.sqrt(mine[...] + theirs[...])
     inv_root[...] = inv
     for k in range(BR):
         x[k] = (start[:, k * TILE : (k + 1) * TILE] * inv[k : k + 1, :]).astype(BF16)
-    outgoing(x, scaled, groups, coords, targets, payload, count)
+    wait()
+    outgoing(x, scaled, *routes, staged, count)
+    split_out(staged, outs)
 
 
 def pair_sum_kernel(mine, theirs, total, sent):
@@ -210,8 +268,11 @@
 
 
 def next_block_kernel(
-    vertices, scaled, inv_root, groups, coords, targets, mine, theirs, x, payload, count
+    vertices, scaled, inv_root, groups, coords, targets, mine, theirs, x, *refs
 ):
+    *outs, tile_groups, tile_coords, tile_targets, count, sems, staged = refs
+    routes = (tile_groups, tile_coords, tile_targets)
+    wait = fetch((groups, coords, targets), routes, sems)
     gram = jnp.zeros((2 * WIDTH, 2 * WIDTH), F32)
     for k in range(BR):
         value = mine[k] + theirs[k].astype(F32)
@@ -221,7 +282,6 @@
         high = image.astype(BF16)
         halves = jnp.concatenate([high, (image - high.astype(F32)).astype(BF16)], axis=0)
         gram += times_t(halves, halves)
-    outgoing(x, scaled, groups, coords, targets, payload, count)
     low = gram[:WIDTH, WIDTH:] + gram[WIDTH:, :WIDTH] + gram[WIDTH:, WIDTH:]
     gram = (gram[:WIDTH, :WIDTH] + low) / vertices
     high = gram.astype(BF16)
@@ -230,21 +290,26 @@
     block = jnp.concatenate(
         [high, middle, low, jnp.zeros((WIDTH, TILE - 3 * WIDTH), BF16)], axis=1
     )
-    for g in range(payload.shape[0]):
-        payload[g, 2 * MOST] = block
-
-
-def local_products_kernel(x, weights, gains, coords, partial, tiles, sems):
-    count, chunk = weights.shape[2], tiles.shape[0] // sems.shape[0]
-    batch = 2 * CHUNK if count % (2 * CHUNK) == 0 else CHUNK
+    wait()
+    outgoing(x, scaled, *routes, staged, count, block)
+    split_out(staged, outs)
+
+
+def local_products_kernel(
+    x, weights, gains, coords, partial, tiles, sems, tile_coords, coord_sems
+):
+    count, chunk = tiles.shape[0], CHUNK
+    batch = 2 * chunk if count % (2 * chunk) == 0 else chunk
 
     def copy_of(n):
         part = pl.ds(n * chunk, chunk)
         return pltpu.make_async_copy(weights.at[0, 0, part], tiles.at[part], sems.at[n])
 
+    wait = fetch((coords,), (tile_coords,), coord_sems)
     for n in range(count // chunk):
         copy_of(n).start()
     partial[...] = jnp.zeros(partial.shape, F32)
+    wait()
 
     def step(n, _):
         for k in range(batch // chunk):
@@ -256,7 +321,7 @@
         places, results = [], []
         for k in range(batch):
             t = base + k
-            r, c = coords[0, 0, 0, t], coords[0, 0, 1, t]
+            r, c = tile_coords[0, 0, 0, t], tile_coords[0, 0, 1, t]
             row_gain = row_gains[k // CHUNK][:, k % CHUNK : k % CHUNK + 1]
             tile = (row_gain * tiles[t].astype(F32) * gains[0, 0, t, 1:2, :]).astype(BF16)
             results.append((times_t(x[c], tile), times(x[r], tile)))
@@ -269,17 +334,19 @@
     lax.fori_loop(0, count // batch, step, 0)
 
 
-def remote_products_kernel(
-    splits, whole, arrived, scaled, partial, groups, coords, targets, *refs
-):
-    outs, (total, count) = refs[:-2], refs[-2:]
-    group_count = arrived.shape[0]
+def remote_products_kernel(splits, whole, pieces, scaled, partial, groups, coords, targets, *refs):
+    arrived, refs = refs[:pieces], refs[pieces:]
+    *outs, total, tile_groups, tile_coords, tile_targets, count, sems, joined = refs
+    wait = fetch((groups, coords, targets), (tile_groups, tile_coords, tile_targets), sems)
+    group_count = joined.shape[0]
+    by_group(arrived, joined)
     total[...] = partial[...]
-    for t, g, m in slots_of(groups, count, scaled.shape[0], group_count):
-        total[coords[0, 0, 0, t]] += times_t(arrived[g, m], scaled[t])
+    wait()
+    for t, g, m in slots_of(tile_groups, count, scaled.shape[0], group_count):
+        total[tile_coords[0, 0, 0, t]] += times_t(joined[g, m], scaled[t])
     for g in range(group_count):
         for m in range(MOST):
-            total[jnp.maximum(targets[g, m], 0)] += arrived[g, MOST + m].astype(F32)
+            total[jnp.maximum(tile_targets[g, m], 0)] += joined[g, MOST + m].astype(F32)
     if whole:
         for out in outs:
             out[...] = total[...].astype(out.dtype)
@@ -304,30 +371,41 @@
     return images, roots
 
 
-def inverse_factor(gram):
-    row = lax.broadcasted_iota(jnp.int32, (WIDTH, 2 * WIDTH), 0)
-    col = lax.broadcasted_iota(jnp.int32, (WIDTH, 2 * WIDTH), 1)
-    eye = jnp.where(
-        lax.broadcasted_iota(jnp.int32, (WIDTH, WIDTH), 0)
-        == lax.broadcasted_iota(jnp.int32, (WIDTH, WIDTH), 1),
-        1.0,
-        0.0,
-    ).astype(F32)
-    work = jnp.concatenate([gram, eye], axis=1)
-    for k in range(WIDTH - 1):
-        pivot = work[k : k + 1, :]
-        factor = work[:, k : k + 1] / work[k : k + 1, k : k + 1]
-        work = work - jnp.where(row > k, factor * pivot, 0.0)
-    diagonal = jnp.sum(jnp.where(row == col, work, 0.0), axis=1, keepdims=True)
-    return work[:, WIDTH:] / jnp.sqrt(diagonal)
-
-
-def middle_factor_kernel(arrived, inverse):
+def eliminate(gram, right):
+    shape = (WIDTH, LANES)
+    row = lax.broadcasted_iota(jnp.int32, shape, 0)
+    lane = lax.broadcasted_iota(jnp.int32, shape, 1)
+    gram = jnp.concatenate([gram, jnp.zeros((WIDTH, LANES - WIDTH), F32)], axis=1)
+    for k in range(0, WIDTH, 2):
+        first = jnp.broadcast_to(gram[:, k : k + 1], shape)
+        second = jnp.broadcast_to(gram[:, k + 1 : k + 2], shape)
+        factor = first / first[k : k + 1]
+        second = second - factor * second[k : k + 1]
+        then = jnp.where(row > k + 1, second / second[k + 1 : k + 2], 0.0)
+        link = factor[k + 1 : k + 2]
+        factor = jnp.where(row > k, factor, 0.0)
+
+        def step(work):
+            top = work[k : k + 1, :]
+            return work - factor * top - then * (work[k + 1 : k + 2, :] - link * top)
+
+        gram, right = step(gram), [step(block) for block in right]
+    pivots = jnp.sum(jnp.where(row == lane, gram, 0.0), axis=1, keepdims=True)
+    root = jnp.broadcast_to(1.0 / jnp.sqrt(pivots), shape)
+    return [block * root for block in right]
+
+
+def middle_factor_kernel(*refs):
+    *arrived, inverse = refs
     gram = jnp.zeros((WIDTH, WIDTH), F32)
-    for g in range(arrived.shape[0]):
-        block = arrived[g, 2 * MOST].astype(F32)
+    for block in [piece[g, 2 * MOST] for piece in arrived for g in range(piece.shape[0])]:
+        block = block.astype(F32)
         gram += (block[:, 2 * WIDTH : 3 * WIDTH] + block[:, WIDTH : 2 * WIDTH]) + block[:, :WIDTH]
-    inverse[...] = inverse_factor(gram)
+    eye = lax.broadcasted_iota(jnp.int32, (WIDTH, LANES), 0) == lax.broadcasted_iota(
+        jnp.int32, (WIDTH, LANES), 1
+    )
+    (result,) = eliminate(gram, [eye.astype(F32)])
+    inverse[...] = result[:, :WIDTH]
 
 
 def last_quarter_kernel(splits, vertices, inv_root, inverse, *refs):
@@ -343,7 +421,7 @@
         )
     gram = gram / vertices
     block = jnp.concatenate(
-        [gram[4 * n : 4 * n + 4] for n in range(4)] + [jnp.zeros((4, 128 - 4 * WIDTH), F32)], axis=1
+        [gram[4 * n : 4 * n + 4] for n in range(4)] + [jnp.zeros((4, LANES - 4 * WIDTH), F32)], axis=1
     )
     for n in range(grams.shape[0]):
         grams[n] = block
@@ -354,9 +432,9 @@
     for n in range(1, grams.shape[0]):
         block = block + grams[n]
     gram = jnp.concatenate([block[:, WIDTH * n : WIDTH * (n + 1)] for n in range(4)], axis=0)
-    out[...] = jnp.dot(
-        inverse_factor(gram), image[...], precision=HIGHEST, preferred_element_type=F32
-    )
+    starts = range(0, out.shape[1], LANES)
+    for n, block in zip(starts, eliminate(gram, [image[:, n : n + LANES] for n in starts])):
+        out[:, n : n + LANES] = block
 
 
 def per_device(
@@ -376,6 +454,15 @@
     local_coords, remote_coords = jnp.swapaxes(local_coords, 2, 3), jnp.swapaxes(remote_coords, 2, 3)
     local_tiles, remote_tiles = local_weights.shape[2], remote_weights.shape[2]
     count = pltpu.SMEM((groups,), jnp.int32)
+    routes = [
+        pltpu.SMEM(remote_groups.shape, jnp.int32),
+        pltpu.SMEM(remote_coords.shape, jnp.int32),
+        pltpu.SMEM((groups, MOST), jnp.int32),
+        count,
+        pltpu.SemaphoreType.DMA((3,)),
+    ]
+
+    partners = [2 * 2**k - 1 for k in range(splits.bit_length() - 1)]
 
     def swap(value, k):
         return lax.ppermute(value, "cols", [(j, j ^ k) for j in range(splits)])
@@ -417,81 +504,110 @@
     joined = call(
         join_degree_kernel, shape((BR, TILE)), [vmem, vmem, vmem], name="join_degree"
     )(sums_in, row_degree, local_degree)
-    step = 1
-    while 2 * step < splits:
-        joined = joined + swap(joined, step)
-        step *= 2
-    degrees = [joined, swap(joined, step)]
+    for k in partners[:-1]:
+        joined = joined + swap(joined, k)
+    degrees = [joined, swap(joined, partners[-1])]
     remote_scaled = scale(remote_weights, remote_gains, "remote_scale")
-    inv_root, x, payload = call(
+    def sent_blocks(blocks):
+        if by_chips(groups):
+            return (shape((groups // 2, blocks, WIDTH, TILE), BF16),) * 2
+        return (shape((groups, blocks, WIDTH, TILE), BF16),)
+
+    def staging(blocks):
+        return pltpu.VMEM((groups, blocks, WIDTH, TILE), BF16)
+
+    inv_root, x, *sent = call(
         first_block_kernel,
-        (
-            shape((BR, TILE)),
-            shape((BR, WIDTH, TILE), BF16),
-            shape((groups, 2 * MOST, WIDTH, TILE), BF16),
-        ),
-        [vmem, vmem, smem, smem, smem, vmem, vmem],
-        [count],
+        (shape((BR, TILE)), shape((BR, WIDTH, TILE), BF16)) + sent_blocks(2 * MOST),
+        [vmem, vmem, anywhere, anywhere, anywhere, vmem, vmem],
+        routes + [staging(2 * MOST)],
         name="first_block",
     )(start_block, remote_scaled, remote_groups, remote_coords, targets, *degrees)
 
-    def product(x, payload, out_shape, whole):
-        arrived = trade(payload)
-        partial = call(
+    def local_products(x):
+        return call(
             local_products_kernel,
             shape((BR, WIDTH, TILE)),
-            [vmem, hbm, vmem, smem],
+            [vmem, hbm, vmem, anywhere],
             [
                 pltpu.VMEM((local_tiles, TILE, TILE), BF16),
-                pltpu.SemaphoreType.DMA((local_tiles // 4,)),
+                pltpu.SemaphoreType.DMA((local_tiles // CHUNK,)),
+                pltpu.SMEM(local_coords.shape, jnp.int32),
+                pltpu.SemaphoreType.DMA((1,)),
             ],
-            moved=10**7,
+            flops=4 * local_tiles * TILE * TILE * WIDTH,
+            moved=2 * local_tiles * TILE * TILE,
             name="local_products",
         )(x, local_weights, local_gains, local_coords)
+
+    def product(x, sent, out_shape, whole):
+        blocks = sent[0].shape[1]
+        if by_chips(groups):
+            near, far = sent
+            passed = lax.ppermute(far, "rows", [(j, j ^ 1) for j in range(groups)])
+            own, *others = call(
+                forward_kernel,
+                (shape((2, blocks, WIDTH, TILE), BF16),) * (groups // 2),
+                [vmem, vmem],
+                name="forward",
+            )(near, passed)
+            arrived = [own] + [
+                lax.ppermute(piece, "rows", [(j, j ^ (2 * k)) for j in range(groups)])
+                for k, piece in enumerate(others, 1)
+            ]
+            partial = local_products(x)
+        else:
+            arrived = [trade(sent[0])]
+            partial = local_products(x)
         return arrived, call(
-            functools.partial(remote_products_kernel, splits, whole),
+            functools.partial(remote_products_kernel, splits, whole, len(arrived)),
             out_shape,
-            [vmem, vmem, vmem, smem, smem, smem],
-            [pltpu.VMEM((BR, WIDTH, TILE), F32), count],
+            [vmem, vmem, anywhere, anywhere, anywhere] + [vmem] * len(arrived),
+            [pltpu.VMEM((BR, WIDTH, TILE), F32)] + routes + [staging(blocks)],
             name="remote_products",
-        )(arrived, remote_scaled, partial, remote_groups, remote_coords, targets)
+        )(remote_scaled, partial, remote_groups, remote_coords, targets, *arrived)
 
     _, (own, sent) = product(
-        x, payload, (shape((BR, WIDTH, TILE)), shape((BR, WIDTH, TILE), BF16)), True
-    )
-    step = 1
-    while 2 * step < splits:
+        x, sent, (shape((BR, WIDTH, TILE)), shape((BR, WIDTH, TILE), BF16)), True
+    )
+    for k in partners[:-1]:
         own, sent = call(
             pair_sum_kernel,
             (shape((BR, WIDTH, TILE)), shape((BR, WIDTH, TILE), BF16)),
             [vmem, vmem],
             name="pair_sum",
-        )(own, swap(sent, step))
-        step *= 2
-    pieces = [own, swap(sent, step)]
-    x, payload = call(
+        )(own, swap(sent, k))
+    x, *sent = call(
         functools.partial(next_block_kernel, vertices),
-        (
-            shape((BR, WIDTH, TILE), BF16),
-            shape((groups, 2 * MOST + 1, WIDTH, TILE), BF16),
-        ),
-        [vmem, vmem, smem, smem, smem, vmem, vmem],
-        [count],
+        (shape((BR, WIDTH, TILE), BF16),) + sent_blocks(2 * MOST + 1),
+        [vmem, vmem, anywhere, anywhere, anywhere, vmem, vmem],
+        routes + [staging(2 * MOST + 1)],
         name="next_block",
-    )(remote_scaled, inv_root, remote_groups, remote_coords, targets, *pieces)
+    )(
+        remote_scaled,
+        inv_root,
+        remote_groups,
+        remote_coords,
+        targets,
+        own,
+        swap(sent, partners[-1]),
+    )
     arrived, sent = product(
         x,
-        payload,
+        sent,
         tuple(shape((quarter, WIDTH, TILE), BF16 if k else F32) for k in range(splits)),
         False,
     )
     pieces = [sent[0]] + [swap(sent[k], k) for k in range(1, splits)]
     inverse = call(
-        middle_factor_kernel, shape((WIDTH, WIDTH)), [vmem], name="middle_factor"
-    )(arrived)
+        middle_factor_kernel,
+        shape((WIDTH, WIDTH)),
+        [vmem] * len(arrived),
+        name="middle_factor",
+    )(*arrived)
     image, grams = call(
         functools.partial(last_quarter_kernel, splits, vertices),
-        (shape((WIDTH, quarter * TILE)), shape((groups * splits, 4, 128))),
+        (shape((WIDTH, quarter * TILE)), shape((groups * splits, 4, LANES))),
         [vmem] * (2 + splits),
         name="last_quarter",
     )(inv_root, inverse, *pieces)

time: 86.2 us -> 82.4 us (0.956)
  Pallas kernels: 30.4 us -> 26.8 us
  blocking collectives: 9.19 us -> 10.4 us
  starting transfers between devices: 27.1 us -> 26.1 us
    all_to_all x3 -> x1, starting transfers between devices: 14.1 us -> 5.19 us  [trade(): lax.all_to_all(value, 'rows', split_axis=0, concat_axis=0, tiled=True)]
    ppermute x0 -> x8, starting transfers between devices: none -> 7.32 us  [the longest x6 7.18 us: product(): lax.ppermute(piece, 'rows', [(j, j ^ 2 * k) for j in range(groups)])]
    all_to_all x3 -> x1, waiting for transfers between devices: 3.19 us -> 0.01 us  [trade(): lax.all_to_all(value, 'rows', split_axis=0, concat_axis=0, tiled=True)]
    ppermute x0 -> x8, waiting for transfers between devices: none -> 2.87 us  [the longest x2 2.72 us: product(): passed = lax.ppermute(far, 'rows', [(j, j ^ 1) for j in range(groups)])]
    pallas_call x5 -> x7, Pallas kernels: 15 us -> 13.8 us  [the longest x2 10.2 us: local_products(): call(local_products_kernel, shape((BR, WIDTH, TILE)), [vmem, hbm, vmem, a...]
    all_to_all x1, blocking collectives: 9.19 us -> 10.4 us  [per_device(): lax.all_to_all(grams, ('rows', 'cols'), split_axis=0, concat_axis=0, tile...]
  transfers between devices with their start and end apart: 10 -> 16, of which waited for: 8 -> 9; matrix products, arithmetic and copies ran while one was open for 0% -> 0% of each run, Pallas kernels for 22% -> 21%
where the time goes in v3:
time: 82.4 us; the launch traced here: 82.2 us
  Pallas kernels  26.8 us (33%)
  starting transfers between devices  26.1 us (32%)
  waiting for transfers between devices  18.5 us (22%)
  blocking collectives  10.4 us (13%)
    ppermute x7, waiting for transfers between devices, swap(): return lax.ppermute(value, 'cols', [(j, j ^ k) for j in range(splits)])  15.6 us
    ppermute x7, starting transfers between devices, swap(): return lax.ppermute(value, 'cols', [(j, j ^ k) for j in range(splits)])  13.6 us
    all_to_all x1, blocking collectives, per_device(): lax.all_to_all(grams, ('rows', 'cols'), split_axis=0, concat_axis=0, tile...  10.4 us
    pallas_call x2, Pallas kernels, local_products(): call(local_products_kernel, shape((BR, WIDTH, TILE)), [vmem, hbm, vmem, a...  10.2 us
    ppermute x6, starting transfers between devices, product(): lax.ppermute(piece, 'rows', [(j, j ^ 2 * k) for j in range(groups)])  7.18 us
    pallas_call x1, Pallas kernels, per_device(): call(local_degree_kernel, shape((BR, TILE)), [hbm, hbm, hbm], [pltpu.VMEM...  5.45 us
    all_to_all x1, starting transfers between devices, trade(): lax.all_to_all(value, 'rows', split_axis=0, concat_axis=0, tiled=True)  5.19 us
    ppermute x2, waiting for transfers between devices, product(): passed = lax.ppermute(far, 'rows', [(j, j ^ 1) for j in range(groups)])  2.72 us
  transfers between devices with their start and end apart: 16, of which 9 were waited for; matrix products, arithmetic and copies ran while one was open for 0% of the time, Pallas kernels for 21%

profile of v3, /device:TPU:0, one launch (start us, length us, event | category | flops | bytes accessed | tf_op | source)
XLA Modules:
  0.0 82.2 jit_solution(15934428982607589344)
XLA Ops:
  0.0 2.6 %remote_degree.1 = (f32[8,8,256]{2,1,0:T(8,128)}, f32[16,256]{1,0:T(8,128)S(1)}) custom-call(bf16[1,1,8,256,256]{4,3,2,1,0:T(8,128)(2,1)} %weights.4, f32[1,1,8,2,256]{4,3,2,1,0:T(2,128)} %gains.6, s32[1,1,8]{2,1,0:T(1,128)} %groups.9, s32[1,1,2,8]{3,2,1,0:T(2,128)} %bitcast.3), custom_call_target="tpu_custom_call" | custom-call | flops 1000000 | bytes 1000000 | tf_op jit(solution)/shard_map/remote_degree/pallas_call | solution.py:474
  2.6 5.2 %all-to-all-start = ((f32[8,8,256]{2,1,0:T(8,128)}), f32[8,8,256]{2,1,0:T(8,128)S(1)}, u32[]{:S(2)}, u32[]{:S(2)}) async-start(f32[8,8,256]{2,1,0:T(8,128)} %get-tuple-element.32), calls=%async_computation | async-start | bytes 131072 | tf_op jit(solution)/shard_map/all_to_all | solution.py:471
  7.8 5.5 %local_degree.1 = f32[16,256]{1,0:T(8,128)S(1)} custom-call(bf16[1,1,48,256,256]{4,3,2,1,0:T(8,128)(2,1)} %weights.7, f32[1,1,48,2,256]{4,3,2,1,0:T(2,128)} %gains.9, s32[1,1,2,48]{3,2,1,0:T(2,128)} %bitcast.8), custom_call_target="tpu_custom_call" | custom-call | flops 1000000 | bytes 10000000 | tf_op jit(solution)/shard_map/local_degree/pallas_call | solution.py:489
  13.3 1.6 %collective-permute-start = (f32[16,256]{1,0:T(8,128)S(1)}, f32[16,256]{1,0:T(8,128)S(1)}, u32[]{:S(2)}, u32[]{:S(2)}) collective-permute-start(f32[16,256]{1,0:T(8,128)S(1)} %join_degree.1), channel_id=1, source_target_pairs={{0,1},{1,0},{2,3},{3,2},{4,5},{5,4},{6,7},{7,6},{8,9},{9,8},{10,11... | collective-permute-start | bytes 49160 | tf_op jit(solution)/shard_map/ppermute | solution.py:468
  15.0 0.5 remote_scale.1.scaled
  15.5 1.6 %collective-permute-done = f32[16,256]{1,0:T(8,128)S(1)} collective-permute-done((f32[16,256]{1,0:T(8,128)S(1)}, f32[16,256]{1,0:T(8,128)S(1)}, u32[]{:S(2)}, u32[]{:S(2)}) %collective-permute-start) | collective-permute-done | bytes 16416 | tf_op jit(solution)/shard_map/ppermute | solution.py:468
  17.1 3.6 %collective-permute-start.1 = (f32[16,256]{1,0:T(8,128)S(1)}, f32[16,256]{1,0:T(8,128)S(1)}, u32[]{:S(2)}, u32[]{:S(2)}) collective-permute-start(f32[16,256]{1,0:T(8,128)S(1)} %add.3.mine), channel_id=1, source_target_pairs={{0,3},{1,2},{2,1},{3,0},{4,7},{5,6},{6,5},{7,4},{8,11},{9,10},{10,... | collective-permute-start | bytes 49160 | tf_op jit(solution)/shard_map/ppermute | solution.py:468
  20.9 1.7 %collective-permute-done.1.theirs = f32[16,256]{1,0:T(8,128)S(1)} collective-permute-done((f32[16,256]{1,0:T(8,128)S(1)}, f32[16,256]{1,0:T(8,128)S(1)}, u32[]{:S(2)}, u32[]{:S(2)}) %collective-permute-start.1) | collective-permute-done | bytes 16416 | tf_op jit(solution)/shard_map/ppermute | solution.py:468
  22.7 0.9 %first_block.1 = (f32[16,256]{1,0:T(8,128)S(1)}, bf16[16,16,256]{2,1,0:T(8,128)(2,1)S(1)}, bf16[4,4,16,256]{3,2,1,0:T(8,128)(2,1)S(1)}, bf16[4,4,16,256]{3,2,1,0:T(8,128)(2,1)S(1)}) custom-call(f32[16,4096]{1,0:T(8,128)S(1)} %copy-done.2, bf16[8,256,256]{2,1,0:T(8,128)(2,1)S(1)} %remote_scale.1.scaled, s32[1,1,8]{2,1,0:T(1,128)S(1)} %copy-done.5, ...), custom_call_target="tpu_custom_call" | custom-call | flops 1000000 | bytes 1000000 | tf_op jit(solution)/shard_map/first_block/pallas_call | solution.py:519
  23.7 1.3 %collective-permute-done.2.passed = bf16[4,4,16,256]{3,2,1,0:T(8,128)(2,1)S(1)} collective-permute-done((bf16[4,4,16,256]{3,2,1,0:T(8,128)(2,1)S(1)}, bf16[4,4,16,256]{3,2,1,0:T(8,128)(2,1)S(1)}, u32[]{:S(2)}, u32[]{:S(2)}) %collective-permute-start.2) | collective-permute-done | bytes 131104 | tf_op jit(solution)/shard_map/ppermute | solution.py:547
  25.0 2.1 %collective-permute-start.3 = (bf16[2,4,16,256]{3,2,1,0:T(8,128)(2,1)S(1)}, bf16[2,4,16,256]{3,2,1,0:T(8,128)(2,1)S(1)}, u32[]{:S(2)}, u32[]{:S(2)}) collective-permute-start(bf16[2,4,16,256]{3,2,1,0:T(8,128)(2,1)S(1)} %get-tuple-element.39), channel_id=1, source_target_pairs={{0,8},{4,12},{8,0},{12,4},{16,24},{20,28},{24,16},{28,20},{1,9},{5... | collective-permute-start | bytes 196616 | tf_op jit(solution)/shard_map/ppermute | solution.py:555
  27.1 1.5 %collective-permute-start.4 = (bf16[2,4,16,256]{3,2,1,0:T(8,128)(2,1)S(1)}, bf16[2,4,16,256]{3,2,1,0:T(8,128)(2,1)S(1)}, u32[]{:S(2)}, u32[]{:S(2)}) collective-permute-start(bf16[2,4,16,256]{3,2,1,0:T(8,128)(2,1)S(1)} %get-tuple-element.40), channel_id=1, source_target_pairs={{0,16},{4,20},{8,24},{12,28},{16,0},{20,4},{24,8},{28,12},{1,17},{... | collective-permute-start | bytes 196616 | tf_op jit(solution)/shard_map/ppermute | solution.py:555
  28.7 5.1 %local_products.2.partial = f32[16,16,256]{2,1,0:T(8,128)S(1)} custom-call(bf16[16,16,256]{2,1,0:T(8,128)(2,1)S(1)} %get-tuple-element.35.x, bf16[1,1,48,256,256]{4,3,2,1,0:T(8,128)(2,1)} %weights.7, f32[1,1,48,2,256]{4,3,2,1,0:T(2,128)S(1)} %copy-done.1, s32[1,1,2,48]{3,2,1,0:T(2,128)S(1)} %bitcast.9), custom_call_target="tpu_custom_call" | custom-call | flops 201326592 | bytes 6291456 | tf_op jit(solution)/shard_map/local_products/pallas_call | solution.py:528
  33.8 1.1 %remote_products.2 = (f32[16,16,256]{2,1,0:T(8,128)S(1)}, bf16[16,16,256]{2,1,0:T(8,128)(2,1)S(1)}) custom-call(bf16[8,256,256]{2,1,0:T(8,128)(2,1)S(1)} %remote_scale.1.scaled, f32[16,16,256]{2,1,0:T(8,128)S(1)} %local_products.2.partial, s32[1,1,8]{2,1,0:T(1,128)S(1)} %copy-done.5, s32[1,1,2,8]{3,2,1,0:T(2,128)S(1)} %bitcast.5, s32[8,2]{1,0:T(8,128)S(1)} %copy.15.targets, ...), custom_call_target="tpu_custom_call" | custom-call | flops 1000000 | bytes 1000000 | tf_op jit(solution)/shard_map/remote_products/pallas_call | solution.py:562
  35.0 5.0 %collective-permute-done.6.theirs = bf16[16,16,256]{2,1,0:T(8,128)(2,1)S(1)} collective-permute-done((bf16[16,16,256]{2,1,0:T(8,128)(2,1)S(1)}, bf16[16,16,256]{2,1,0:T(8,128)(2,1)S(1)}, u32[]{:S(2)}, u32[]{:S(2)}) %collective-permute-start.6) | collective-permute-done | bytes 131104 | tf_op jit(solution)/shard_map/ppermute | solution.py:468
  40.1 3.7 %collective-permute-start.7 = (bf16[16,16,256]{2,1,0:T(8,128)(2,1)S(1)}, bf16[16,16,256]{2,1,0:T(8,128)(2,1)S(1)}, u32[]{:S(2)}, u32[]{:S(2)}) collective-permute-start(bf16[16,16,256]{2,1,0:T(8,128)(2,1)S(1)} %get-tuple-element.45), channel_id=1, source_target_pairs={{0,3},{1,2},{2,1},{3,0},{4,7},{5,6},{6,5},{7,4},{8,11},{9,10},{10,... | collective-permute-start | bytes 393224 | tf_op jit(solution)/shard_map/ppermute | solution.py:468
  43.7 3.3 %collective-permute-done.7.theirs = bf16[16,16,256]{2,1,0:T(8,128)(2,1)S(1)} collective-permute-done((bf16[16,16,256]{2,1,0:T(8,128)(2,1)S(1)}, bf16[16,16,256]{2,1,0:T(8,128)(2,1)S(1)}, u32[]{:S(2)}, u32[]{:S(2)}) %collective-permute-start.7) | collective-permute-done | bytes 131104 | tf_op jit(solution)/shard_map/ppermute | solution.py:468
  47.0 1.0 %next_block.1 = (bf16[16,16,256]{2,1,0:T(8,128)(2,1)S(1)}, bf16[4,5,16,256]{3,2,1,0:T(8,128)(2,1)S(1)}, bf16[4,5,16,256]{3,2,1,0:T(8,128)(2,1)S(1)}) custom-call(bf16[8,256,256]{2,1,0:T(8,128)(2,1)S(1)} %remote_scale.1.scaled, f32[16,256]{1,0:T(8,128)S(1)} %get-tuple-element.34.inv_root, s32[1,1,8]{2,1,0:T(1,128)S(1)} %copy-done.5, ...), custom_call_target="tpu_custom_call" | custom-call | flops 1000000 | bytes 1000000 | tf_op jit(solution)/shard_map/next_block/pallas_call | solution.py:580
  48.1 1.4 %collective-permute-done.8.passed = bf16[4,5,16,256]{3,2,1,0:T(8,128)(2,1)S(1)} collective-permute-done((bf16[4,5,16,256]{3,2,1,0:T(8,128)(2,1)S(1)}, bf16[4,5,16,256]{3,2,1,0:T(8,128)(2,1)S(1)}, u32[]{:S(2)}, u32[]{:S(2)}) %collective-permute-start.8) | collective-permute-done | bytes 163872 | tf_op jit(solution)/shard_map/ppermute | solution.py:547
  49.5 2.0 %collective-permute-start.9 = (bf16[2,5,16,256]{3,2,1,0:T(8,128)(2,1)S(1)}, bf16[2,5,16,256]{3,2,1,0:T(8,128)(2,1)S(1)}, u32[]{:S(2)}, u32[]{:S(2)}) collective-permute-start(bf16[2,5,16,256]{3,2,1,0:T(8,128)(2,1)S(1)} %get-tuple-element.49), channel_id=1, source_target_pairs={{0,8},{4,12},{8,0},{12,4},{16,24},{20,28},{24,16},{28,20},{1,9},{5... | collective-permute-start | bytes 245768 | tf_op jit(solution)/shard_map/ppermute | solution.py:555
  51.5 1.5 %collective-permute-start.10 = (bf16[2,5,16,256]{3,2,1,0:T(8,128)(2,1)S(1)}, bf16[2,5,16,256]{3,2,1,0:T(8,128)(2,1)S(1)}, u32[]{:S(2)}, u32[]{:S(2)}) collective-permute-start(bf16[2,5,16,256]{3,2,1,0:T(8,128)(2,1)S(1)} %get-tuple-element.50), channel_id=1, source_target_pairs={{0,16},{4,20},{8,24},{12,28},{16,0},{20,4},{24,8},{28,12},{1,17},{... | collective-permute-start | bytes 245768 | tf_op jit(solution)/shard_map/ppermute | solution.py:555
  53.1 5.1 %local_products.3.partial = f32[16,16,256]{2,1,0:T(8,128)S(1)} custom-call(bf16[16,16,256]{2,1,0:T(8,128)(2,1)S(1)} %get-tuple-element.52.x, bf16[1,1,48,256,256]{4,3,2,1,0:T(8,128)(2,1)} %weights.7, f32[1,1,48,2,256]{4,3,2,1,0:T(2,128)S(1)} %copy-done.1, s32[1,1,2,48]{3,2,1,0:T(2,128)S(1)} %bitcast.10), custom_call_target="tpu_custom_call" | custom-call | flops 201326592 | bytes 6291456 | tf_op jit(solution)/shard_map/local_products/pallas_call | solution.py:528
  58.3 1.1 %remote_products.3 = (f32[4,16,256]{2,1,0:T(8,128)S(1)}, bf16[4,16,256]{2,1,0:T(8,128)(2,1)S(1)}, bf16[4,16,256]{2,1,0:T(8,128)(2,1)S(1)}, bf16[4,16,256]{2,1,0:T(8,128)(2,1)S(1)}) custom-call(bf16[8,256,256]{2,1,0:T(8,128)(2,1)S(1)} %remote_scale.1.scaled, f32[16,16,256]{2,1,0:T(8,128)S(1)} %local_products.3.partial, s32[1,1,8]{2,1,0:T(1,128)S(1)} %copy-done.5, ...), custom_call_target="tpu_custom_call" | custom-call | flops 1000000 | bytes 1000000 | tf_op jit(solution)/shard_map/remote_products/pallas_call | solution.py:562
  59.5 1.6 %collective-permute-start.12 = (bf16[4,16,256]{2,1,0:T(8,128)(2,1)S(1)}, bf16[4,16,256]{2,1,0:T(8,128)(2,1)S(1)}, u32[]{:S(2)}, u32[]{:S(2)}) collective-permute-start(bf16[4,16,256]{2,1,0:T(8,128)(2,1)S(1)} %get-tuple-element.54), channel_id=1, source_target_pairs={{0,1},{1,0},{2,3},{3,2},{4,5},{5,4},{6,7},{7,6},{8,9},{9,8},{10,11... | collective-permute-start | bytes 98312 | tf_op jit(solution)/shard_map/ppermute | solution.py:468
  61.0 2.5 %collective-permute-start.13 = (bf16[4,16,256]{2,1,0:T(8,128)(2,1)S(1)}, bf16[4,16,256]{2,1,0:T(8,128)(2,1)S(1)}, u32[]{:S(2)}, u32[]{:S(2)}) collective-permute-start(bf16[4,16,256]{2,1,0:T(8,128)(2,1)S(1)} %get-tuple-element.55), channel_id=1, source_target_pairs={{0,2},{1,3},{2,0},{3,1},{4,6},{5,7},{6,4},{7,5},{8,10},{9,11},{10,... | collective-permute-start | bytes 98312 | tf_op jit(solution)/shard_map/ppermute | solution.py:468
  63.6 0.5 collective-permute-start.14
  64.0 1.3 %middle_factor.1.inverse = f32[16,16]{1,0:T(8,128)S(1)} custom-call(bf16[2,5,16,256]{3,2,1,0:T(8,128)(2,1)S(1)} %get-tuple-element.48.refs_0_, bf16[2,5,16,256]{3,2,1,0:T(8,128)(2,1)S(1)} %collective-permute-done.9.refs_1_, bf16[2,5,16,256]{3,2,1,0:T(8,128)(2,1)S(1)} %collective-permute-done.10.refs_2_, ...), custom_call_target="tpu_custom_call" | custom-call | flops 1000000 | bytes 1000000 | tf_op jit(solution)/shard_map/middle_factor/pallas_call | solution.py:602
  65.3 1.1 %collective-permute-done.13.refs_2_ = bf16[4,16,256]{2,1,0:T(8,128)(2,1)S(1)} collective-permute-done((bf16[4,16,256]{2,1,0:T(8,128)(2,1)S(1)}, bf16[4,16,256]{2,1,0:T(8,128)(2,1)S(1)}, u32[]{:S(2)}, u32[]{:S(2)}) %collective-permute-start.13) | collective-permute-done | bytes 32800 | tf_op jit(solution)/shard_map/ppermute | solution.py:468
  66.4 2.8 %collective-permute-done.14.refs_3_ = bf16[4,16,256]{2,1,0:T(8,128)(2,1)S(1)} collective-permute-done((bf16[4,16,256]{2,1,0:T(8,128)(2,1)S(1)}, bf16[4,16,256]{2,1,0:T(8,128)(2,1)S(1)}, u32[]{:S(2)}, u32[]{:S(2)}) %collective-permute-start.14) | collective-permute-done | bytes 32800 | tf_op jit(solution)/shard_map/ppermute | solution.py:468
  69.3 0.7 last_quarter.1
  69.9 10.4 %all_to_all.10.grams = f32[32,4,128]{2,1,0:T(4,128)S(1)} all-to-all(f32[32,4,128]{2,1,0:T(4,128)S(1)} %get-tuple-element.57), channel_id=1, replica_groups=mesh['rows'=8,'cols'=4] {'rows','cols'}, dimensions={0} | all-to-all | bytes 131072 | tf_op jit(solution)/shard_map/all_to_all | solution.py:614
  80.4 1.8 %finish.1 = f32[16,1024]{1,0:T(8,128)} custom-call(f32[32,4,128]{2,1,0:T(4,128)S(1)} %all_to_all.10.grams, f32[16,1024]{1,0:T(8,128)S(1)} %get-tuple-element.58.image), custom_call_target="tpu_custom_call" | custom-call | flops 1000000 | bytes 1000000 | tf_op jit(solution)/shard_map/finish/pallas_call | solution.py:617
  (35 shorter events, 0.8 us)
Async XLA Ops:
  0.0 22.7 %copy-start.5 = (s32[1,1,8]{2,1,0:T(1,128)S(1)}, s32[1,1,8]{2,1,0:T(1,128)}, u32[]{:S(2)}) copy-start(s32[1,1,8]{2,1,0:T(1,128)} %groups.9) | copy-start | bytes 100
  0.0 15.0 %copy-start.3 = (f32[1,1,8,2,256]{4,3,2,1,0:T(2,128)S(1)}, f32[1,1,8,2,256]{4,3,2,1,0:T(2,128)}, u32[]{:S(2)}) copy-start(f32[1,1,8,2,256]{4,3,2,1,0:T(2,128)} %gains.6) | copy-start | bytes 49156
  0.0 15.0 %copy-start = (bf16[1,1,8,256,256]{4,3,2,1,0:T(8,128)(2,1)S(1)}, bf16[1,1,8,256,256]{4,3,2,1,0:T(8,128)(2,1)}, u32[]{:S(2)}) copy-start(bf16[1,1,8,256,256]{4,3,2,1,0:T(8,128)(2,1)} %weights.4) | copy-start | bytes 3145732
  0.0 22.7 %copy-start.4 = (s32[1,1,8,2]{2,3,1,0:T(2,128)S(1)}, s32[1,1,8,2]{2,3,1,0:T(2,128)}, u32[]{:S(2)}) copy-start(s32[1,1,8,2]{2,3,1,0:T(2,128)} %param.14) | copy-start | bytes 196
  0.0 28.7 %copy-start.1 = (f32[1,1,48,2,256]{4,3,2,1,0:T(2,128)S(1)}, f32[1,1,48,2,256]{4,3,2,1,0:T(2,128)}, u32[]{:S(2)}) copy-start(f32[1,1,48,2,256]{4,3,2,1,0:T(2,128)} %gains.9) | copy-start | bytes 294916
  0.0 28.7 %copy-start.6 = (s32[1,1,48,2]{2,3,1,0:T(2,128)S(1)}, s32[1,1,48,2]{2,3,1,0:T(2,128)}, u32[]{:S(2)}) copy-start(s32[1,1,48,2]{2,3,1,0:T(2,128)} %param.10) | copy-start | bytes 1156
  0.0 22.6 %copy-start.2 = (f32[16,4096]{1,0:T(8,128)S(1)}, f32[16,4096]{1,0:T(8,128)}, u32[]{:S(2)}) copy-start(f32[16,4096]{1,0:T(8,128)} %start.1) | copy-start | bytes 786436
  2.6 10.7 %all-to-all-start = ((f32[8,8,256]{2,1,0:T(8,128)}), f32[8,8,256]{2,1,0:T(8,128)S(1)}, u32[]{:S(2)}, u32[]{:S(2)}) async-start(f32[8,8,256]{2,1,0:T(8,128)} %get-tuple-element.32), calls=%async_computation | async-start | bytes 131072 | tf_op jit(solution)/shard_map/all_to_all | solution.py:471
  13.3 3.8 %collective-permute-start = (f32[16,256]{1,0:T(8,128)S(1)}, f32[16,256]{1,0:T(8,128)S(1)}, u32[]{:S(2)}, u32[]{:S(2)}) collective-permute-start(f32[16,256]{1,0:T(8,128)S(1)} %join_degree.1), channel_id=1, source_target_pairs={{0,1},{1,0},{2,3},{3,2},{4,5},{5,4},{6,7},{7,6},{8,9},{9,8},{10,11... | collective-permute-start | bytes 49160 | tf_op jit(solution)/shard_map/ppermute | solution.py:468
  17.1 5.5 %collective-permute-start.1 = (f32[16,256]{1,0:T(8,128)S(1)}, f32[16,256]{1,0:T(8,128)S(1)}, u32[]{:S(2)}, u32[]{:S(2)}) collective-permute-start(f32[16,256]{1,0:T(8,128)S(1)} %add.3.mine), channel_id=1, source_target_pairs={{0,3},{1,2},{2,1},{3,0},{4,7},{5,6},{6,5},{7,4},{8,11},{9,10},{10,... | collective-permute-start | bytes 49160 | tf_op jit(solution)/shard_map/ppermute | solution.py:468
  23.6 1.4 %collective-permute-start.2 = (bf16[4,4,16,256]{3,2,1,0:T(8,128)(2,1)S(1)}, bf16[4,4,16,256]{3,2,1,0:T(8,128)(2,1)S(1)}, u32[]{:S(2)}, u32[]{:S(2)}) collective-permute-start(bf16[4,4,16,256]{3,2,1,0:T(8,128)(2,1)S(1)} %get-tuple-element.37), channel_id=1, source_target_pairs={{0,4},{4,0},{8,12},{12,8},{16,20},{20,16},{24,28},{28,24},{1,5},{5... | collective-permute-start | bytes 393224 | tf_op jit(solution)/shard_map/ppermute | solution.py:547
  25.0 8.8 %collective-permute-start.3 = (bf16[2,4,16,256]{3,2,1,0:T(8,128)(2,1)S(1)}, bf16[2,4,16,256]{3,2,1,0:T(8,128)(2,1)S(1)}, u32[]{:S(2)}, u32[]{:S(2)}) collective-permute-start(bf16[2,4,16,256]{3,2,1,0:T(8,128)(2,1)S(1)} %get-tuple-element.39), channel_id=1, source_target_pairs={{0,8},{4,12},{8,0},{12,4},{16,24},{20,28},{24,16},{28,20},{1,9},{5... | collective-permute-start | bytes 196616 | tf_op jit(solution)/shard_map/ppermute | solution.py:555
  27.1 6.7 %collective-permute-start.4 = (bf16[2,4,16,256]{3,2,1,0:T(8,128)(2,1)S(1)}, bf16[2,4,16,256]{3,2,1,0:T(8,128)(2,1)S(1)}, u32[]{:S(2)}, u32[]{:S(2)}) collective-permute-start(bf16[2,4,16,256]{3,2,1,0:T(8,128)(2,1)S(1)} %get-tuple-element.40), channel_id=1, source_target_pairs={{0,16},{4,20},{8,24},{12,28},{16,0},{20,4},{24,8},{28,12},{1,17},{... | collective-permute-start | bytes 196616 | tf_op jit(solution)/shard_map/ppermute | solution.py:555
  28.6 5.2 %collective-permute-start.5 = (bf16[2,4,16,256]{3,2,1,0:T(8,128)(2,1)S(1)}, bf16[2,4,16,256]{3,2,1,0:T(8,128)(2,1)S(1)}, u32[]{:S(2)}, u32[]{:S(2)}) collective-permute-start(bf16[2,4,16,256]{3,2,1,0:T(8,128)(2,1)S(1)} %get-tuple-element.41), channel_id=1, source_target_pairs={{0,24},{4,28},{8,16},{12,20},{16,8},{20,12},{24,0},{28,4},{1,25},{... | collective-permute-start | bytes 196616 | tf_op jit(solution)/shard_map/ppermute | solution.py:555
  34.9 5.1 %collective-permute-start.6 = (bf16[16,16,256]{2,1,0:T(8,128)(2,1)S(1)}, bf16[16,16,256]{2,1,0:T(8,128)(2,1)S(1)}, u32[]{:S(2)}, u32[]{:S(2)}) collective-permute-start(bf16[16,16,256]{2,1,0:T(8,128)(2,1)S(1)} %get-tuple-element.43), channel_id=1, source_target_pairs={{0,1},{1,0},{2,3},{3,2},{4,5},{5,4},{6,7},{7,6},{8,9},{9,8},{10,11... | collective-permute-start | bytes 393224 | tf_op jit(solution)/shard_map/ppermute | solution.py:468
  40.1 6.9 %collective-permute-start.7 = (bf16[16,16,256]{2,1,0:T(8,128)(2,1)S(1)}, bf16[16,16,256]{2,1,0:T(8,128)(2,1)S(1)}, u32[]{:S(2)}, u32[]{:S(2)}) collective-permute-start(bf16[16,16,256]{2,1,0:T(8,128)(2,1)S(1)} %get-tuple-element.45), channel_id=1, source_target_pairs={{0,3},{1,2},{2,1},{3,0},{4,7},{5,6},{6,5},{7,4},{8,11},{9,10},{10,... | collective-permute-start | bytes 393224 | tf_op jit(solution)/shard_map/ppermute | solution.py:468
  48.0 1.5 %collective-permute-start.8 = (bf16[4,5,16,256]{3,2,1,0:T(8,128)(2,1)S(1)}, bf16[4,5,16,256]{3,2,1,0:T(8,128)(2,1)S(1)}, u32[]{:S(2)}, u32[]{:S(2)}) collective-permute-start(bf16[4,5,16,256]{3,2,1,0:T(8,128)(2,1)S(1)} %get-tuple-element.47), channel_id=1, source_target_pairs={{0,4},{4,0},{8,12},{12,8},{16,20},{20,16},{24,28},{28,24},{1,5},{5... | collective-permute-start | bytes 491528 | tf_op jit(solution)/shard_map/ppermute | solution.py:547
  49.5 8.7 %collective-permute-start.9 = (bf16[2,5,16,256]{3,2,1,0:T(8,128)(2,1)S(1)}, bf16[2,5,16,256]{3,2,1,0:T(8,128)(2,1)S(1)}, u32[]{:S(2)}, u32[]{:S(2)}) collective-permute-start(bf16[2,5,16,256]{3,2,1,0:T(8,128)(2,1)S(1)} %get-tuple-element.49), channel_id=1, source_target_pairs={{0,8},{4,12},{8,0},{12,4},{16,24},{20,28},{24,16},{28,20},{1,9},{5... | collective-permute-start | bytes 245768 | tf_op jit(solution)/shard_map/ppermute | solution.py:555
  51.5 6.7 %collective-permute-start.10 = (bf16[2,5,16,256]{3,2,1,0:T(8,128)(2,1)S(1)}, bf16[2,5,16,256]{3,2,1,0:T(8,128)(2,1)S(1)}, u32[]{:S(2)}, u32[]{:S(2)}) collective-permute-start(bf16[2,5,16,256]{3,2,1,0:T(8,128)(2,1)S(1)} %get-tuple-element.50), channel_id=1, source_target_pairs={{0,16},{4,20},{8,24},{12,28},{16,0},{20,4},{24,8},{28,12},{1,17},{... | collective-permute-start | bytes 245768 | tf_op jit(solution)/shard_map/ppermute | solution.py:555
  53.0 5.3 %collective-permute-start.11 = (bf16[2,5,16,256]{3,2,1,0:T(8,128)(2,1)S(1)}, bf16[2,5,16,256]{3,2,1,0:T(8,128)(2,1)S(1)}, u32[]{:S(2)}, u32[]{:S(2)}) collective-permute-start(bf16[2,5,16,256]{3,2,1,0:T(8,128)(2,1)S(1)} %get-tuple-element.51), channel_id=1, source_target_pairs={{0,24},{4,28},{8,16},{12,20},{16,8},{20,12},{24,0},{28,4},{1,25},{... | collective-permute-start | bytes 245768 | tf_op jit(solution)/shard_map/ppermute | solution.py:555
  59.5 5.8 %collective-permute-start.12 = (bf16[4,16,256]{2,1,0:T(8,128)(2,1)S(1)}, bf16[4,16,256]{2,1,0:T(8,128)(2,1)S(1)}, u32[]{:S(2)}, u32[]{:S(2)}) collective-permute-start(bf16[4,16,256]{2,1,0:T(8,128)(2,1)S(1)} %get-tuple-element.54), channel_id=1, source_target_pairs={{0,1},{1,0},{2,3},{3,2},{4,5},{5,4},{6,7},{7,6},{8,9},{9,8},{10,11... | collective-permute-start | bytes 98312 | tf_op jit(solution)/shard_map/ppermute | solution.py:468
  61.0 5.4 %collective-permute-start.13 = (bf16[4,16,256]{2,1,0:T(8,128)(2,1)S(1)}, bf16[4,16,256]{2,1,0:T(8,128)(2,1)S(1)}, u32[]{:S(2)}, u32[]{:S(2)}) collective-permute-start(bf16[4,16,256]{2,1,0:T(8,128)(2,1)S(1)} %get-tuple-element.55), channel_id=1, source_target_pairs={{0,2},{1,3},{2,0},{3,1},{4,6},{5,7},{6,4},{7,5},{8,10},{9,11},{10,... | collective-permute-start | bytes 98312 | tf_op jit(solution)/shard_map/ppermute | solution.py:468
  63.6 5.7 %collective-permute-start.14 = (bf16[4,16,256]{2,1,0:T(8,128)(2,1)S(1)}, bf16[4,16,256]{2,1,0:T(8,128)(2,1)S(1)}, u32[]{:S(2)}, u32[]{:S(2)}) collective-permute-start(bf16[4,16,256]{2,1,0:T(8,128)(2,1)S(1)} %get-tuple-element.56), channel_id=1, source_target_pairs={{0,3},{1,2},{2,1},{3,0},{4,7},{5,6},{6,5},{7,4},{8,11},{9,10},{10,... | collective-permute-start | bytes 98312 | tf_op jit(solution)/shard_map/ppermute | solution.py:468

commit v4 on v3

--- a/solution.py
+++ b/solution.py
@@ -12,6 +12,7 @@
 BR = 16
 MOST = 2
 CHUNK = 8
+HELD = 16
 LANES = 128
 F32 = jnp.float32
 BF16 = jnp.bfloat16
@@ -121,41 +122,59 @@
         payload[g, pl.ds(MOST + m, 1), :] = jnp.full((1, TILE), c, jnp.int32).astype(F32)
 
 
+def halves_of(value):
+    high = value.astype(BF16)
+    return high, (value - high.astype(F32)).astype(BF16)
+
+
+def add_by_place(places, values):
+    shape = (BR, places.shape[1])
+    chosen = (lax.broadcasted_iota(jnp.int32, shape, 0) == places).astype(BF16)
+    high, low = halves_of(values)
+    return times(chosen, high) + times(chosen, low)
+
+
 def local_degree_kernel(
-    weights, gains, coords, degree, tiles, tile_gains, tile_coords, sems, small_sems
+    weights, gains, coords, degree, ready, tiles, tile_gains, places, by_row, by_col, sems, small_sems
 ):
-    chunk = CHUNK
-    chunks = weights.shape[2] // chunk
-    batch = 2 * chunk if chunks % 2 == 0 else chunk
-
-    def copy_of(n):
-        part = pl.ds(n * chunk, chunk)
-        return pltpu.make_async_copy(weights.at[0, 0, part], tiles.at[part], sems.at[n])
-
-    small = [
-        pltpu.make_async_copy(coords, tile_coords, small_sems.at[0]),
-        pltpu.make_async_copy(gains, tile_gains, small_sems.at[1]),
-    ]
-    for copy in small:
-        copy.start()
-    for n in range(chunks):
-        copy_of(n).start()
-    degree[...] = jnp.zeros(degree.shape, F32)
-    for copy in small:
-        copy.wait()
-
-    def step(n, _):
-        for k in range(batch // chunk):
-            copy_of(n * (batch // chunk) + k).wait()
-        for k in range(batch):
-            t = n * batch + k
-            r, c = tile_coords[0, 0, 0, t], tile_coords[0, 0, 1, t]
-            by_row, by_col = weighted_sums(jnp.abs(tiles[t]), tile_gains[0, 0, t])
-            degree[pl.ds(r, 1), :] += by_row
-            degree[pl.ds(c, 1), :] += by_col
+    count, held = weights.shape[2], ready.shape[0]
+
+    def copy_of(n, base, target):
+        source = weights.at[0, 0, pl.ds(base + n * CHUNK, CHUNK)]
+        return pltpu.make_async_copy(
+            source, target.at[pl.ds(n * CHUNK, CHUNK)], sems.at[base // CHUNK + n]
+        )
+
+    wait = fetch((gains, coords), (tile_gains, places), small_sems)
+    parts = ((0, ready), (held, tiles))
+    for base, target in parts:
+        for n in range(target.shape[0] // CHUNK):
+            copy_of(n, base, target).start()
+    by_row[...] = jnp.zeros(by_row.shape, F32)
+    first = lax.broadcasted_iota(jnp.int32, (8, TILE), 0) == 0
+    lane = lax.broadcasted_iota(jnp.int32, by_row.shape, 1)
+    wait()
+
+    def step(base, target, n, _):
+        copy_of(n, base, target).wait()
+        for k in range(CHUNK):
+            t = base + n * CHUNK + k
+            size = jnp.abs(target[n * CHUNK + k])
+            pair = jnp.abs(tile_gains[0, 0, t])
+            left = jnp.where(first, pair[0:1, :], 0.0)
+            high = left.astype(BF16).astype(F32)
+            sums = times(jnp.concatenate([high, left - high], axis=0).astype(BF16), size)
+            by_col[pl.ds(t, 1), :] = (sums[0:1] + sums[8:9]) * pair[1:2, :]
+            sums = jnp.sum(size.astype(F32) * pair[1:2, :], axis=1, keepdims=True)
+            by_row[...] = jnp.where(lane == t, sums, by_row[...])
         return 0
 
-    lax.fori_loop(0, chunks * chunk // batch, step, 0)
+    for base, target in parts:
+        lax.fori_loop(0, target.shape[0] // CHUNK, functools.partial(step, base, target), 0)
+    row_sums = jnp.transpose(by_row[...])[:count] * jnp.abs(tile_gains[0, 0, :, 0, :])
+    degree[...] = add_by_place(places[0, 0, 0:1, :], row_sums) + add_by_place(
+        places[0, 0, 1:2, :], by_col[...]
+    )
 
 
 def scale_kernel(raw, gains, scaled):
@@ -182,7 +201,7 @@
         ),
         compiler_params=pltpu.CompilerParams(vmem_limit_bytes=VMEM_LIMIT),
         name=name,
-    )(weights, gains)
+    )(in_hbm(weights), gains)
 
 
 def join_degree_kernel(arrived, row_degree, local_degree, joined):
@@ -246,13 +265,15 @@
         joined[pl.ds((chip ^ k) * 2, 2)] = piece[...]
 
 
-def first_block_kernel(
-    start, scaled, groups, coords, targets, mine, theirs, inv_root, x, *refs
-):
+def first_block_kernel(splits, start, scaled, groups, coords, targets, *refs):
+    parts, (inv_root, x, *refs) = refs[:splits], refs[splits:]
     *outs, tile_groups, tile_coords, tile_targets, count, sems, staged = refs
     routes = (tile_groups, tile_coords, tile_targets)
     wait = fetch((groups, coords, targets), routes, sems)
-    inv = 1.0 / jnp.sqrt(mine[...] + theirs[...])
+    degree = parts[0][...]
+    for part in parts[1:]:
+        degree += part[...]
+    inv = 1.0 / jnp.sqrt(degree)
     inv_root[...] = inv
     for k in range(BR):
         x[k] = (start[:, k * TILE : (k + 1) * TILE] * inv[k : k + 1, :]).astype(BF16)
@@ -296,14 +317,14 @@
 
 
 def local_products_kernel(
-    x, weights, gains, coords, partial, tiles, sems, tile_coords, coord_sems
+    x, ready, weights, gains, coords, partial, tiles, sems, tile_coords, coord_sems
 ):
-    count, chunk = tiles.shape[0], CHUNK
+    held, count, chunk = ready.shape[0], tiles.shape[0], CHUNK
     batch = 2 * chunk if count % (2 * chunk) == 0 else chunk
 
     def copy_of(n):
-        part = pl.ds(n * chunk, chunk)
-        return pltpu.make_async_copy(weights.at[0, 0, part], tiles.at[part], sems.at[n])
+        source = weights.at[0, 0, pl.ds(held + n * chunk, chunk)]
+        return pltpu.make_async_copy(source, tiles.at[pl.ds(n * chunk, chunk)], sems.at[n])
 
     wait = fetch((coords,), (tile_coords,), coord_sems)
     for n in range(count // chunk):
@@ -311,24 +332,29 @@
     partial[...] = jnp.zeros(partial.shape, F32)
     wait()
 
-    def step(n, _):
-        for k in range(batch // chunk):
-            copy_of(n * (batch // chunk) + k).wait()
-        base = n * batch
+    def add(base, raw):
         row_gains = [
-            jnp.transpose(gains[0, 0, pl.ds(base + k, CHUNK), 0, :]) for k in range(0, batch, CHUNK)
+            jnp.transpose(gains[0, 0, pl.ds(base + k, CHUNK), 0, :])
+            for k in range(0, len(raw), CHUNK)
         ]
         places, results = [], []
-        for k in range(batch):
+        for k, tile in enumerate(raw):
             t = base + k
             r, c = tile_coords[0, 0, 0, t], tile_coords[0, 0, 1, t]
             row_gain = row_gains[k // CHUNK][:, k % CHUNK : k % CHUNK + 1]
-            tile = (row_gain * tiles[t].astype(F32) * gains[0, 0, t, 1:2, :]).astype(BF16)
+            tile = (row_gain * tile().astype(F32) * gains[0, 0, t, 1:2, :]).astype(BF16)
             results.append((times_t(x[c], tile), times(x[r], tile)))
             places.append((r, c))
         for (r, c), (forward, backward) in zip(places, results):
             partial[r] += forward
             partial[c] += backward
+
+    add(0, [lambda k=k: ready[k] for k in range(held)])
+
+    def step(n, _):
+        for k in range(batch // chunk):
+            copy_of(n * (batch // chunk) + k).wait()
+        add(held + n * batch, [lambda k=k: tiles[n * batch + k] for k in range(batch)])
         return 0
 
     lax.fori_loop(0, count // batch, step, 0)
@@ -486,14 +512,16 @@
         name="remote_degree",
     )(*[in_hbm(value) for value in listing])
     sums_in = trade(sums)
-    local_degree = call(
+    local_degree, ready = call(
         local_degree_kernel,
-        shape((BR, TILE)),
+        (shape((BR, TILE)), shape((HELD, TILE, TILE), BF16)),
         [hbm, hbm, hbm],
         [
-            pltpu.VMEM((local_tiles, TILE, TILE), BF16),
+            pltpu.VMEM((local_tiles - HELD, TILE, TILE), BF16),
             pltpu.VMEM(local_gains.shape, F32),
-            pltpu.SMEM(local_coords.shape, jnp.int32),
+            pltpu.VMEM(local_coords.shape, jnp.int32),
+            pltpu.VMEM((TILE, -(-local_tiles // LANES) * LANES), F32),
+            pltpu.VMEM((local_tiles, TILE), F32),
             pltpu.SemaphoreType.DMA((local_tiles // CHUNK,)),
             pltpu.SemaphoreType.DMA((2,)),
         ],
@@ -504,9 +532,8 @@
     joined = call(
         join_degree_kernel, shape((BR, TILE)), [vmem, vmem, vmem], name="join_degree"
     )(sums_in, row_degree, local_degree)
-    for k in partners[:-1]:
-        joined = joined + swap(joined, k)
-    degrees = [joined, swap(joined, partners[-1])]
+    joined, remote_gains = lax.optimization_barrier((joined, remote_gains))
+    degrees = [joined] + [swap(joined, k) for k in range(1, splits)]
     remote_scaled = scale(remote_weights, remote_gains, "remote_scale")
     def sent_blocks(blocks):
         if by_chips(groups):
@@ -517,9 +544,9 @@
         return pltpu.VMEM((groups, blocks, WIDTH, TILE), BF16)
 
     inv_root, x, *sent = call(
-        first_block_kernel,
+        functools.partial(first_block_kernel, splits),
         (shape((BR, TILE)), shape((BR, WIDTH, TILE), BF16)) + sent_blocks(2 * MOST),
-        [vmem, vmem, anywhere, anywhere, anywhere, vmem, vmem],
+        [vmem, vmem, anywhere, anywhere, anywhere] + [vmem] * splits,
         routes + [staging(2 * MOST)],
         name="first_block",
     )(start_block, remote_scaled, remote_groups, remote_coords, targets, *degrees)
@@ -528,17 +555,17 @@
         return call(
             local_products_kernel,
             shape((BR, WIDTH, TILE)),
-            [vmem, hbm, vmem, anywhere],
+            [vmem, vmem, hbm, vmem, anywhere],
             [
-                pltpu.VMEM((local_tiles, TILE, TILE), BF16),
-                pltpu.SemaphoreType.DMA((local_tiles // CHUNK,)),
+                pltpu.VMEM((local_tiles - HELD, TILE, TILE), BF16),
+                pltpu.SemaphoreType.DMA((local_tiles // CHUNK - HELD // CHUNK,)),
                 pltpu.SMEM(local_coords.shape, jnp.int32),
                 pltpu.SemaphoreType.DMA((1,)),
             ],
             flops=4 * local_tiles * TILE * TILE * WIDTH,
             moved=2 * local_tiles * TILE * TILE,
             name="local_products",
-        )(x, local_weights, local_gains, local_coords)
+        )(x, ready, local_weights, local_gains, local_coords)
 
     def product(x, sent, out_shape, whole):
         blocks = sent[0].shape[1]

time: 82.4 us -> 78.4 us (0.951)
  starting transfers between devices: 26.1 us -> 23.2 us
  Pallas kernels: 26.8 us -> 25.4 us
    ppermute x7 -> x8, starting transfers between devices: 13.6 us -> 10.7 us  [swap(): return lax.ppermute(value, 'cols', [(j, j ^ k) for j in range(splits)])]
    pallas_call x4, Pallas kernels: 16.6 us -> 13.9 us  [the longest x2 8.2 us: local_products(): call(local_products_kernel, shape((BR, WIDTH, TILE)), [vmem, vmem, hbm, v...]
    ppermute x7 -> x8, waiting for transfers between devices: 15.6 us -> 14.3 us  [swap(): return lax.ppermute(value, 'cols', [(j, j ^ k) for j in range(splits)])]
    pallas_call x1, Pallas kernels: 0.52 us -> 1.75 us  [scale(): pl.pallas_call(scale_kernel, out_shape=shape((count, TILE, TILE), BF16),...]
    ppermute x6, waiting for transfers between devices: 0.16 us -> 1.06 us  [product(): lax.ppermute(piece, 'rows', [(j, j ^ 2 * k) for j in range(groups)])]
  transfers between devices with their start and end apart: 16 -> 17, of which waited for: 9 -> 9; matrix products, arithmetic and copies ran while one was open for 0% -> 0% of each run, Pallas kernels for 21% -> 21%
where the time goes in v4:
time: 78.4 us; the launch traced here: 78.2 us
  Pallas kernels  25.4 us (32%)
  starting transfers between devices  23.2 us (30%)
  waiting for transfers between devices  18.3 us (23%)
  blocking collectives  10.9 us (14%)
    ppermute x8, waiting for transfers between devices, swap(): return lax.ppermute(value, 'cols', [(j, j ^ k) for j in range(splits)])  14.3 us
    all_to_all x1, blocking collectives, per_device(): lax.all_to_all(grams, ('rows', 'cols'), split_axis=0, concat_axis=0, tile...  10.9 us
    ppermute x8, starting transfers between devices, swap(): return lax.ppermute(value, 'cols', [(j, j ^ k) for j in range(splits)])  10.7 us
    pallas_call x2, Pallas kernels, local_products(): call(local_products_kernel, shape((BR, WIDTH, TILE)), [vmem, vmem, hbm, v...  8.2 us
    ppermute x6, starting transfers between devices, product(): lax.ppermute(piece, 'rows', [(j, j ^ 2 * k) for j in range(groups)])  7.11 us
    all_to_all x1, starting transfers between devices, trade(): lax.all_to_all(value, 'rows', split_axis=0, concat_axis=0, tiled=True)  5.21 us
    pallas_call x1, Pallas kernels, per_device(): call(local_degree_kernel, (shape((BR, TILE)), shape((HELD, TILE, TILE), B...  4.82 us
    ppermute x2, waiting for transfers between devices, product(): passed = lax.ppermute(far, 'rows', [(j, j ^ 1) for j in range(groups)])  2.72 us
  transfers between devices with their start and end apart: 17, of which 9 were waited for; matrix products, arithmetic and copies ran while one was open for 0% of the time, Pallas kernels for 21%

profile of v4, /device:TPU:0, one launch (start us, length us, event | category | flops | bytes accessed | tf_op | source)
XLA Modules:
  0.0 78.2 jit_solution(2562490904500391105)
XLA Ops:
  0.0 2.5 %remote_degree.1 = (f32[8,8,256]{2,1,0:T(8,128)}, f32[16,256]{1,0:T(8,128)S(1)}) custom-call(bf16[1,1,8,256,256]{4,3,2,1,0:T(8,128)(2,1)} %raw.1, f32[1,1,8,2,256]{4,3,2,1,0:T(2,128)} %gains.6, s32[1,1,8]{2,1,0:T(1,128)} %groups.9, s32[1,1,2,8]{3,2,1,0:T(2,128)} %bitcast.3), custom_call_target="tpu_custom_call" | custom-call | flops 1000000 | bytes 1000000 | tf_op jit(solution)/shard_map/remote_degree/pallas_call | solution.py:500
  2.5 5.2 %all-to-all-start = ((f32[8,8,256]{2,1,0:T(8,128)}), f32[8,8,256]{2,1,0:T(8,128)S(1)}, u32[]{:S(2)}, u32[]{:S(2)}) async-start(f32[8,8,256]{2,1,0:T(8,128)} %get-tuple-element.36), calls=%async_computation | async-start | bytes 131072 | tf_op jit(solution)/shard_map/all_to_all | solution.py:497
  7.8 4.8 %local_degree.1 = (f32[16,256]{1,0:T(8,128)S(1)}, bf16[16,256,256]{2,1,0:T(8,128)(2,1)S(1)}) custom-call(bf16[1,1,48,256,256]{4,3,2,1,0:T(8,128)(2,1)} %weights.7, f32[1,1,48,2,256]{4,3,2,1,0:T(2,128)} %gains.8, s32[1,1,2,48]{3,2,1,0:T(2,128)} %bitcast.8), custom_call_target="tpu_custom_call" | custom-call | flops 1000000 | bytes 10000000 | tf_op jit(solution)/shard_map/local_degree/pallas_call | solution.py:515
  12.8 3.7 %collective-permute-start.2 = (f32[16,256]{1,0:T(8,128)S(1)}, f32[16,256]{1,0:T(8,128)S(1)}, u32[]{:S(2)}, u32[]{:S(2)}) collective-permute-start(f32[16,256]{1,0:T(8,128)S(1)} %join_degree.1.refs_0_), channel_id=1, source_target_pairs={{0,3},{1,2},{2,1},{3,0},{4,7},{5,6},{6,5},{7,4},{8,11},{9,10},{10,... | collective-permute-start | bytes 49160 | tf_op jit(solution)/shard_map/ppermute | solution.py:494
  16.5 0.8 %collective-permute-start = (f32[16,256]{1,0:T(8,128)S(1)}, f32[16,256]{1,0:T(8,128)S(1)}, u32[]{:S(2)}, u32[]{:S(2)}) collective-permute-start(f32[16,256]{1,0:T(8,128)S(1)} %join_degree.1.refs_0_), channel_id=1, source_target_pairs={{0,1},{1,0},{2,3},{3,2},{4,5},{5,4},{6,7},{7,6},{8,9},{9,8},{10,11... | collective-permute-start | bytes 49160 | tf_op jit(solution)/shard_map/ppermute | solution.py:494
  17.5 1.7 %remote_scale.1.scaled = bf16[8,256,256]{2,1,0:T(8,128)(2,1)S(1)} custom-call(bf16[1,1,8,256,256]{4,3,2,1,0:T(8,128)(2,1)} %raw.1, f32[1,1,8,2,256]{4,3,2,1,0:T(2,128)S(1)} %copy-done.2), custom_call_target="tpu_custom_call" | custom-call | flops 1048576 | bytes 2097152 | tf_op jit(solution)/shard_map/remote_scale/pallas_call | solution.py:190
  19.2 1.9 %collective-permute-done.1.refs_2_ = f32[16,256]{1,0:T(8,128)S(1)} collective-permute-done((f32[16,256]{1,0:T(8,128)S(1)}, f32[16,256]{1,0:T(8,128)S(1)}, u32[]{:S(2)}, u32[]{:S(2)}) %collective-permute-start.1) | collective-permute-done | bytes 16416 | tf_op jit(solution)/shard_map/ppermute | solution.py:494
  21.1 0.9 %first_block.1 = (f32[16,256]{1,0:T(8,128)S(1)}, bf16[16,16,256]{2,1,0:T(8,128)(2,1)S(1)}, bf16[4,4,16,256]{3,2,1,0:T(8,128)(2,1)S(1)}, bf16[4,4,16,256]{3,2,1,0:T(8,128)(2,1)S(1)}) custom-call(f32[16,4096]{1,0:T(8,128)S(1)} %copy-done.1, bf16[8,256,256]{2,1,0:T(8,128)(2,1)S(1)} %remote_scale.1.scaled, s32[1,1,8]{2,1,0:T(1,128)S(1)} %copy-done.4, ...), custom_call_target="tpu_custom_call" | custom-call | flops 1000000 | bytes 1000000 | tf_op jit(solution)/shard_map/first_block/pallas_call | solution.py:546
  22.2 1.3 %collective-permute-done.3.passed = bf16[4,4,16,256]{3,2,1,0:T(8,128)(2,1)S(1)} collective-permute-done((bf16[4,4,16,256]{3,2,1,0:T(8,128)(2,1)S(1)}, bf16[4,4,16,256]{3,2,1,0:T(8,128)(2,1)S(1)}, u32[]{:S(2)}, u32[]{:S(2)}) %collective-permute-start.3) | collective-permute-done | bytes 131104 | tf_op jit(solution)/shard_map/ppermute | solution.py:574
  23.5 1.9 %collective-permute-start.4 = (bf16[2,4,16,256]{3,2,1,0:T(8,128)(2,1)S(1)}, bf16[2,4,16,256]{3,2,1,0:T(8,128)(2,1)S(1)}, u32[]{:S(2)}, u32[]{:S(2)}) collective-permute-start(bf16[2,4,16,256]{3,2,1,0:T(8,128)(2,1)S(1)} %get-tuple-element.47), channel_id=1, source_target_pairs={{0,8},{4,12},{8,0},{12,4},{16,24},{20,28},{24,16},{28,20},{1,9},{5... | collective-permute-start | bytes 196616 | tf_op jit(solution)/shard_map/ppermute | solution.py:582
  25.4 1.5 %collective-permute-start.5 = (bf16[2,4,16,256]{3,2,1,0:T(8,128)(2,1)S(1)}, bf16[2,4,16,256]{3,2,1,0:T(8,128)(2,1)S(1)}, u32[]{:S(2)}, u32[]{:S(2)}) collective-permute-start(bf16[2,4,16,256]{3,2,1,0:T(8,128)(2,1)S(1)} %get-tuple-element.48), channel_id=1, source_target_pairs={{0,16},{4,20},{8,24},{12,28},{16,0},{20,4},{24,8},{28,12},{1,17},{... | collective-permute-start | bytes 196616 | tf_op jit(solution)/shard_map/ppermute | solution.py:582
  27.1 4.1 %local_products.2.partial = f32[16,16,256]{2,1,0:T(8,128)S(1)} custom-call(bf16[16,16,256]{2,1,0:T(8,128)(2,1)S(1)} %get-tuple-element.42.x, bf16[16,256,256]{2,1,0:T(8,128)(2,1)S(1)} %get-tuple-element.43.ready, bf16[1,1,48,256,256]{4,3,2,1,0:T(8,128)(2,1)} %weights.7, f32[1,1,48,2,256]{4,3,2,1,0:T(2,128)S(1)} %copy-done, s32[1,1,2,48]{3,2,1,0:T(2,128)S(1)} %bitcast.9), custom_call_target="tpu_custom_call" | custom-call | flops 201326592 | bytes 6291456 | tf_op jit(solution)/shard_map/local_products/pallas_call | solution.py:555
  31.2 0.9 %collective-permute-done.6.refs_3_ = bf16[2,4,16,256]{3,2,1,0:T(8,128)(2,1)S(1)} collective-permute-done((bf16[2,4,16,256]{3,2,1,0:T(8,128)(2,1)S(1)}, bf16[2,4,16,256]{3,2,1,0:T(8,128)(2,1)S(1)}, u32[]{:S(2)}, u32[]{:S(2)}) %collective-permute-start.6) | collective-permute-done | bytes 65568 | tf_op jit(solution)/shard_map/ppermute | solution.py:582
  32.0 1.1 %remote_products.2 = (f32[16,16,256]{2,1,0:T(8,128)S(1)}, bf16[16,16,256]{2,1,0:T(8,128)(2,1)S(1)}) custom-call(bf16[8,256,256]{2,1,0:T(8,128)(2,1)S(1)} %remote_scale.1.scaled, f32[16,16,256]{2,1,0:T(8,128)S(1)} %local_products.2.partial, s32[1,1,8]{2,1,0:T(1,128)S(1)} %copy-done.4, s32[1,1,2,8]{3,2,1,0:T(2,128)S(1)} %bitcast.5, s32[8,2]{1,0:T(8,128)S(1)} %copy.15.targets, ...), custom_call_target="tpu_custom_call" | custom-call | flops 1000000 | bytes 1000000 | tf_op jit(solution)/shard_map/remote_products/pallas_call | solution.py:589
  33.3 5.0 %collective-permute-done.7.theirs = bf16[16,16,256]{2,1,0:T(8,128)(2,1)S(1)} collective-permute-done((bf16[16,16,256]{2,1,0:T(8,128)(2,1)S(1)}, bf16[16,16,256]{2,1,0:T(8,128)(2,1)S(1)}, u32[]{:S(2)}, u32[]{:S(2)}) %collective-permute-start.7) | collective-permute-done | bytes 131104 | tf_op jit(solution)/shard_map/ppermute | solution.py:494
  38.3 1.8 %collective-permute-start.8 = (bf16[16,16,256]{2,1,0:T(8,128)(2,1)S(1)}, bf16[16,16,256]{2,1,0:T(8,128)(2,1)S(1)}, u32[]{:S(2)}, u32[]{:S(2)}) collective-permute-start(bf16[16,16,256]{2,1,0:T(8,128)(2,1)S(1)} %get-tuple-element.53), channel_id=1, source_target_pairs={{0,3},{1,2},{2,1},{3,0},{4,7},{5,6},{6,5},{7,4},{8,11},{9,10},{10,... | collective-permute-start | bytes 393224 | tf_op jit(solution)/shard_map/ppermute | solution.py:494
  40.1 5.0 %collective-permute-done.8.theirs = bf16[16,16,256]{2,1,0:T(8,128)(2,1)S(1)} collective-permute-done((bf16[16,16,256]{2,1,0:T(8,128)(2,1)S(1)}, bf16[16,16,256]{2,1,0:T(8,128)(2,1)S(1)}, u32[]{:S(2)}, u32[]{:S(2)}) %collective-permute-start.8) | collective-permute-done | bytes 131104 | tf_op jit(solution)/shard_map/ppermute | solution.py:494
  45.1 1.0 %next_block.1 = (bf16[16,16,256]{2,1,0:T(8,128)(2,1)S(1)}, bf16[4,5,16,256]{3,2,1,0:T(8,128)(2,1)S(1)}, bf16[4,5,16,256]{3,2,1,0:T(8,128)(2,1)S(1)}) custom-call(bf16[8,256,256]{2,1,0:T(8,128)(2,1)S(1)} %remote_scale.1.scaled, f32[16,256]{1,0:T(8,128)S(1)} %get-tuple-element.41.inv_root, s32[1,1,8]{2,1,0:T(1,128)S(1)} %copy-done.4, ...), custom_call_target="tpu_custom_call" | custom-call | flops 1000000 | bytes 1000000 | tf_op jit(solution)/shard_map/next_block/pallas_call | solution.py:607
  46.2 1.4 %collective-permute-done.9.passed = bf16[4,5,16,256]{3,2,1,0:T(8,128)(2,1)S(1)} collective-permute-done((bf16[4,5,16,256]{3,2,1,0:T(8,128)(2,1)S(1)}, bf16[4,5,16,256]{3,2,1,0:T(8,128)(2,1)S(1)}, u32[]{:S(2)}, u32[]{:S(2)}) %collective-permute-start.9) | collective-permute-done | bytes 163872 | tf_op jit(solution)/shard_map/ppermute | solution.py:574
  47.6 1.1 %collective-permute-start.10 = (bf16[2,5,16,256]{3,2,1,0:T(8,128)(2,1)S(1)}, bf16[2,5,16,256]{3,2,1,0:T(8,128)(2,1)S(1)}, u32[]{:S(2)}, u32[]{:S(2)}) collective-permute-start(bf16[2,5,16,256]{3,2,1,0:T(8,128)(2,1)S(1)} %get-tuple-element.57), channel_id=1, source_target_pairs={{0,8},{4,12},{8,0},{12,4},{16,24},{20,28},{24,16},{28,20},{1,9},{5... | collective-permute-start | bytes 245768 | tf_op jit(solution)/shard_map/ppermute | solution.py:582
  48.7 1.5 %collective-permute-start.11 = (bf16[2,5,16,256]{3,2,1,0:T(8,128)(2,1)S(1)}, bf16[2,5,16,256]{3,2,1,0:T(8,128)(2,1)S(1)}, u32[]{:S(2)}, u32[]{:S(2)}) collective-permute-start(bf16[2,5,16,256]{3,2,1,0:T(8,128)(2,1)S(1)} %get-tuple-element.58), channel_id=1, source_target_pairs={{0,16},{4,20},{8,24},{12,28},{16,0},{20,4},{24,8},{28,12},{1,17},{... | collective-permute-start | bytes 245768 | tf_op jit(solution)/shard_map/ppermute | solution.py:582
  50.1 1.0 %collective-permute-start.12 = (bf16[2,5,16,256]{3,2,1,0:T(8,128)(2,1)S(1)}, bf16[2,5,16,256]{3,2,1,0:T(8,128)(2,1)S(1)}, u32[]{:S(2)}, u32[]{:S(2)}) collective-permute-start(bf16[2,5,16,256]{3,2,1,0:T(8,128)(2,1)S(1)} %get-tuple-element.59), channel_id=1, source_target_pairs={{0,24},{4,28},{8,16},{12,20},{16,8},{20,12},{24,0},{28,4},{1,25},{... | collective-permute-start | bytes 245768 | tf_op jit(solution)/shard_map/ppermute | solution.py:582
  51.2 4.1 %local_products.3.partial = f32[16,16,256]{2,1,0:T(8,128)S(1)} custom-call(bf16[16,16,256]{2,1,0:T(8,128)(2,1)S(1)} %get-tuple-element.60.x, bf16[16,256,256]{2,1,0:T(8,128)(2,1)S(1)} %get-tuple-element.43.ready, bf16[1,1,48,256,256]{4,3,2,1,0:T(8,128)(2,1)} %weights.7, f32[1,1,48,2,256]{4,3,2,1,0:T(2,128)S(1)} %copy-done, s32[1,1,2,48]{3,2,1,0:T(2,128)S(1)} %bitcast.10), custom_call_target="tpu_custom_call" | custom-call | flops 201326592 | bytes 6291456 | tf_op jit(solution)/shard_map/local_products/pallas_call | solution.py:555
  55.3 0.2 collective-permute-done.12.refs_3_
  55.5 1.1 %remote_products.3 = (f32[4,16,256]{2,1,0:T(8,128)S(1)}, bf16[4,16,256]{2,1,0:T(8,128)(2,1)S(1)}, bf16[4,16,256]{2,1,0:T(8,128)(2,1)S(1)}, bf16[4,16,256]{2,1,0:T(8,128)(2,1)S(1)}) custom-call(bf16[8,256,256]{2,1,0:T(8,128)(2,1)S(1)} %remote_scale.1.scaled, f32[16,16,256]{2,1,0:T(8,128)S(1)} %local_products.3.partial, s32[1,1,8]{2,1,0:T(1,128)S(1)} %copy-done.4, ...), custom_call_target="tpu_custom_call" | custom-call | flops 1000000 | bytes 1000000 | tf_op jit(solution)/shard_map/remote_products/pallas_call | solution.py:589
  56.7 2.4 %collective-permute-start.14 = (bf16[4,16,256]{2,1,0:T(8,128)(2,1)S(1)}, bf16[4,16,256]{2,1,0:T(8,128)(2,1)S(1)}, u32[]{:S(2)}, u32[]{:S(2)}) collective-permute-start(bf16[4,16,256]{2,1,0:T(8,128)(2,1)S(1)} %get-tuple-element.63), channel_id=1, source_target_pairs={{0,2},{1,3},{2,0},{3,1},{4,6},{5,7},{6,4},{7,5},{8,10},{9,11},{10,... | collective-permute-start | bytes 98312 | tf_op jit(solution)/shard_map/ppermute | solution.py:494
  59.1 2.0 %collective-permute-start.15 = (bf16[4,16,256]{2,1,0:T(8,128)(2,1)S(1)}, bf16[4,16,256]{2,1,0:T(8,128)(2,1)S(1)}, u32[]{:S(2)}, u32[]{:S(2)}) collective-permute-start(bf16[4,16,256]{2,1,0:T(8,128)(2,1)S(1)} %get-tuple-element.64), channel_id=1, source_target_pairs={{0,3},{1,2},{2,1},{3,0},{4,7},{5,6},{6,5},{7,4},{8,11},{9,10},{10,... | collective-permute-start | bytes 98312 | tf_op jit(solution)/shard_map/ppermute | solution.py:494
  61.1 1.3 %middle_factor.1.inverse = f32[16,16]{1,0:T(8,128)S(1)} custom-call(bf16[2,5,16,256]{3,2,1,0:T(8,128)(2,1)S(1)} %get-tuple-element.56.refs_0_, bf16[2,5,16,256]{3,2,1,0:T(8,128)(2,1)S(1)} %collective-permute-done.10.refs_1_, bf16[2,5,16,256]{3,2,1,0:T(8,128)(2,1)S(1)} %collective-permute-done.11.refs_2_, ...), custom_call_target="tpu_custom_call" | custom-call | flops 1000000 | bytes 1000000 | tf_op jit(solution)/shard_map/middle_factor/pallas_call | solution.py:629
  62.4 2.4 %collective-permute-done.15.refs_3_ = bf16[4,16,256]{2,1,0:T(8,128)(2,1)S(1)} collective-permute-done((bf16[4,16,256]{2,1,0:T(8,128)(2,1)S(1)}, bf16[4,16,256]{2,1,0:T(8,128)(2,1)S(1)}, u32[]{:S(2)}, u32[]{:S(2)}) %collective-permute-start.15) | collective-permute-done | bytes 32800 | tf_op jit(solution)/shard_map/ppermute | solution.py:494
  64.8 0.7 last_quarter.1
  65.5 10.9 %all_to_all.10.grams = f32[32,4,128]{2,1,0:T(4,128)S(1)} all-to-all(f32[32,4,128]{2,1,0:T(4,128)S(1)} %get-tuple-element.65), channel_id=1, replica_groups=mesh['rows'=8,'cols'=4] {'rows','cols'}, dimensions={0} | all-to-all | bytes 131072 | tf_op jit(solution)/shard_map/all_to_all | solution.py:641
  76.3 1.8 %finish.1 = f32[16,1024]{1,0:T(8,128)} custom-call(f32[32,4,128]{2,1,0:T(4,128)S(1)} %all_to_all.10.grams, f32[16,1024]{1,0:T(8,128)S(1)} %get-tuple-element.66.image), custom_call_target="tpu_custom_call" | custom-call | flops 1000000 | bytes 1000000 | tf_op jit(solution)/shard_map/finish/pallas_call | solution.py:644
  (34 shorter events, 1.0 us)
Async XLA Ops:
  0.0 21.1 %copy-start.4 = (s32[1,1,8]{2,1,0:T(1,128)S(1)}, s32[1,1,8]{2,1,0:T(1,128)}, u32[]{:S(2)}) copy-start(s32[1,1,8]{2,1,0:T(1,128)} %groups.9) | copy-start | bytes 100
  0.0 17.5 %copy-start.2 = (f32[1,1,8,2,256]{4,3,2,1,0:T(2,128)S(1)}, f32[1,1,8,2,256]{4,3,2,1,0:T(2,128)}, u32[]{:S(2)}) copy-start(f32[1,1,8,2,256]{4,3,2,1,0:T(2,128)} %gains.6) | copy-start | bytes 49156
  0.0 21.1 %copy-start.3 = (s32[1,1,8,2]{2,3,1,0:T(2,128)S(1)}, s32[1,1,8,2]{2,3,1,0:T(2,128)}, u32[]{:S(2)}) copy-start(s32[1,1,8,2]{2,3,1,0:T(2,128)} %param.14) | copy-start | bytes 196
  0.0 27.1 %copy-start = (f32[1,1,48,2,256]{4,3,2,1,0:T(2,128)S(1)}, f32[1,1,48,2,256]{4,3,2,1,0:T(2,128)}, u32[]{:S(2)}) copy-start(f32[1,1,48,2,256]{4,3,2,1,0:T(2,128)} %gains.8) | copy-start | bytes 294916
  0.0 27.1 %copy-start.5 = (s32[1,1,48,2]{2,3,1,0:T(2,128)S(1)}, s32[1,1,48,2]{2,3,1,0:T(2,128)}, u32[]{:S(2)}) copy-start(s32[1,1,48,2]{2,3,1,0:T(2,128)} %param.10) | copy-start | bytes 1156
  0.0 21.1 %copy-start.1 = (f32[16,4096]{1,0:T(8,128)S(1)}, f32[16,4096]{1,0:T(8,128)}, u32[]{:S(2)}) copy-start(f32[16,4096]{1,0:T(8,128)} %start.1) | copy-start | bytes 786436
  2.5 10.2 %all-to-all-start = ((f32[8,8,256]{2,1,0:T(8,128)}), f32[8,8,256]{2,1,0:T(8,128)S(1)}, u32[]{:S(2)}, u32[]{:S(2)}) async-start(f32[8,8,256]{2,1,0:T(8,128)} %get-tuple-element.36), calls=%async_computation | async-start | bytes 131072 | tf_op jit(solution)/shard_map/all_to_all | solution.py:497
  12.8 6.4 %collective-permute-start.2 = (f32[16,256]{1,0:T(8,128)S(1)}, f32[16,256]{1,0:T(8,128)S(1)}, u32[]{:S(2)}, u32[]{:S(2)}) collective-permute-start(f32[16,256]{1,0:T(8,128)S(1)} %join_degree.1.refs_0_), channel_id=1, source_target_pairs={{0,3},{1,2},{2,1},{3,0},{4,7},{5,6},{6,5},{7,4},{8,11},{9,10},{10,... | collective-permute-start | bytes 49160 | tf_op jit(solution)/shard_map/ppermute | solution.py:494
  16.5 4.6 %collective-permute-start.1 = (f32[16,256]{1,0:T(8,128)S(1)}, f32[16,256]{1,0:T(8,128)S(1)}, u32[]{:S(2)}, u32[]{:S(2)}) collective-permute-start(f32[16,256]{1,0:T(8,128)S(1)} %join_degree.1.refs_0_), channel_id=1, source_target_pairs={{0,2},{1,3},{2,0},{3,1},{4,6},{5,7},{6,4},{7,5},{8,10},{9,11},{10,... | collective-permute-start | bytes 49160 | tf_op jit(solution)/shard_map/ppermute | solution.py:494
  16.5 4.6 %collective-permute-start = (f32[16,256]{1,0:T(8,128)S(1)}, f32[16,256]{1,0:T(8,128)S(1)}, u32[]{:S(2)}, u32[]{:S(2)}) collective-permute-start(f32[16,256]{1,0:T(8,128)S(1)} %join_degree.1.refs_0_), channel_id=1, source_target_pairs={{0,1},{1,0},{2,3},{3,2},{4,5},{5,4},{6,7},{7,6},{8,9},{9,8},{10,11... | collective-permute-start | bytes 49160 | tf_op jit(solution)/shard_map/ppermute | solution.py:494
  22.1 1.4 %collective-permute-start.3 = (bf16[4,4,16,256]{3,2,1,0:T(8,128)(2,1)S(1)}, bf16[4,4,16,256]{3,2,1,0:T(8,128)(2,1)S(1)}, u32[]{:S(2)}, u32[]{:S(2)}) collective-permute-start(bf16[4,4,16,256]{3,2,1,0:T(8,128)(2,1)S(1)} %get-tuple-element.45), channel_id=1, source_target_pairs={{0,4},{4,0},{8,12},{12,8},{16,20},{20,16},{24,28},{28,24},{1,5},{5... | collective-permute-start | bytes 393224 | tf_op jit(solution)/shard_map/ppermute | solution.py:574
  23.5 7.7 %collective-permute-start.4 = (bf16[2,4,16,256]{3,2,1,0:T(8,128)(2,1)S(1)}, bf16[2,4,16,256]{3,2,1,0:T(8,128)(2,1)S(1)}, u32[]{:S(2)}, u32[]{:S(2)}) collective-permute-start(bf16[2,4,16,256]{3,2,1,0:T(8,128)(2,1)S(1)} %get-tuple-element.47), channel_id=1, source_target_pairs={{0,8},{4,12},{8,0},{12,4},{16,24},{20,28},{24,16},{28,20},{1,9},{5... | collective-permute-start | bytes 196616 | tf_op jit(solution)/shard_map/ppermute | solution.py:582
  25.4 5.8 %collective-permute-start.5 = (bf16[2,4,16,256]{3,2,1,0:T(8,128)(2,1)S(1)}, bf16[2,4,16,256]{3,2,1,0:T(8,128)(2,1)S(1)}, u32[]{:S(2)}, u32[]{:S(2)}) collective-permute-start(bf16[2,4,16,256]{3,2,1,0:T(8,128)(2,1)S(1)} %get-tuple-element.48), channel_id=1, source_target_pairs={{0,16},{4,20},{8,24},{12,28},{16,0},{20,4},{24,8},{28,12},{1,17},{... | collective-permute-start | bytes 196616 | tf_op jit(solution)/shard_map/ppermute | solution.py:582
  26.9 5.2 %collective-permute-start.6 = (bf16[2,4,16,256]{3,2,1,0:T(8,128)(2,1)S(1)}, bf16[2,4,16,256]{3,2,1,0:T(8,128)(2,1)S(1)}, u32[]{:S(2)}, u32[]{:S(2)}) collective-permute-start(bf16[2,4,16,256]{3,2,1,0:T(8,128)(2,1)S(1)} %get-tuple-element.49), channel_id=1, source_target_pairs={{0,24},{4,28},{8,16},{12,20},{16,8},{20,12},{24,0},{28,4},{1,25},{... | collective-permute-start | bytes 196616 | tf_op jit(solution)/shard_map/ppermute | solution.py:582
  33.2 5.0 %collective-permute-start.7 = (bf16[16,16,256]{2,1,0:T(8,128)(2,1)S(1)}, bf16[16,16,256]{2,1,0:T(8,128)(2,1)S(1)}, u32[]{:S(2)}, u32[]{:S(2)}) collective-permute-start(bf16[16,16,256]{2,1,0:T(8,128)(2,1)S(1)} %get-tuple-element.51), channel_id=1, source_target_pairs={{0,1},{1,0},{2,3},{3,2},{4,5},{5,4},{6,7},{7,6},{8,9},{9,8},{10,11... | collective-permute-start | bytes 393224 | tf_op jit(solution)/shard_map/ppermute | solution.py:494
  38.3 6.8 %collective-permute-start.8 = (bf16[16,16,256]{2,1,0:T(8,128)(2,1)S(1)}, bf16[16,16,256]{2,1,0:T(8,128)(2,1)S(1)}, u32[]{:S(2)}, u32[]{:S(2)}) collective-permute-start(bf16[16,16,256]{2,1,0:T(8,128)(2,1)S(1)} %get-tuple-element.53), channel_id=1, source_target_pairs={{0,3},{1,2},{2,1},{3,0},{4,7},{5,6},{6,5},{7,4},{8,11},{9,10},{10,... | collective-permute-start | bytes 393224 | tf_op jit(solution)/shard_map/ppermute | solution.py:494
  46.1 1.5 %collective-permute-start.9 = (bf16[4,5,16,256]{3,2,1,0:T(8,128)(2,1)S(1)}, bf16[4,5,16,256]{3,2,1,0:T(8,128)(2,1)S(1)}, u32[]{:S(2)}, u32[]{:S(2)}) collective-permute-start(bf16[4,5,16,256]{3,2,1,0:T(8,128)(2,1)S(1)} %get-tuple-element.55), channel_id=1, source_target_pairs={{0,4},{4,0},{8,12},{12,8},{16,20},{20,16},{24,28},{28,24},{1,5},{5... | collective-permute-start | bytes 491528 | tf_op jit(solution)/shard_map/ppermute | solution.py:574
  47.6 7.7 %collective-permute-start.10 = (bf16[2,5,16,256]{3,2,1,0:T(8,128)(2,1)S(1)}, bf16[2,5,16,256]{3,2,1,0:T(8,128)(2,1)S(1)}, u32[]{:S(2)}, u32[]{:S(2)}) collective-permute-start(bf16[2,5,16,256]{3,2,1,0:T(8,128)(2,1)S(1)} %get-tuple-element.57), channel_id=1, source_target_pairs={{0,8},{4,12},{8,0},{12,4},{16,24},{20,28},{24,16},{28,20},{1,9},{5... | collective-permute-start | bytes 245768 | tf_op jit(solution)/shard_map/ppermute | solution.py:582
  48.7 6.6 %collective-permute-start.11 = (bf16[2,5,16,256]{3,2,1,0:T(8,128)(2,1)S(1)}, bf16[2,5,16,256]{3,2,1,0:T(8,128)(2,1)S(1)}, u32[]{:S(2)}, u32[]{:S(2)}) collective-permute-start(bf16[2,5,16,256]{3,2,1,0:T(8,128)(2,1)S(1)} %get-tuple-element.58), channel_id=1, source_target_pairs={{0,16},{4,20},{8,24},{12,28},{16,0},{20,4},{24,8},{28,12},{1,17},{... | collective-permute-start | bytes 245768 | tf_op jit(solution)/shard_map/ppermute | solution.py:582
  50.1 5.3 %collective-permute-start.12 = (bf16[2,5,16,256]{3,2,1,0:T(8,128)(2,1)S(1)}, bf16[2,5,16,256]{3,2,1,0:T(8,128)(2,1)S(1)}, u32[]{:S(2)}, u32[]{:S(2)}) collective-permute-start(bf16[2,5,16,256]{3,2,1,0:T(8,128)(2,1)S(1)} %get-tuple-element.59), channel_id=1, source_target_pairs={{0,24},{4,28},{8,16},{12,20},{16,8},{20,12},{24,0},{28,4},{1,25},{... | collective-permute-start | bytes 245768 | tf_op jit(solution)/shard_map/ppermute | solution.py:582
  56.6 5.7 %collective-permute-start.13 = (bf16[4,16,256]{2,1,0:T(8,128)(2,1)S(1)}, bf16[4,16,256]{2,1,0:T(8,128)(2,1)S(1)}, u32[]{:S(2)}, u32[]{:S(2)}) collective-permute-start(bf16[4,16,256]{2,1,0:T(8,128)(2,1)S(1)} %get-tuple-element.62), channel_id=1, source_target_pairs={{0,1},{1,0},{2,3},{3,2},{4,5},{5,4},{6,7},{7,6},{8,9},{9,8},{10,11... | collective-permute-start | bytes 98312 | tf_op jit(solution)/shard_map/ppermute | solution.py:494
  56.7 5.7 %collective-permute-start.14 = (bf16[4,16,256]{2,1,0:T(8,128)(2,1)S(1)}, bf16[4,16,256]{2,1,0:T(8,128)(2,1)S(1)}, u32[]{:S(2)}, u32[]{:S(2)}) collective-permute-start(bf16[4,16,256]{2,1,0:T(8,128)(2,1)S(1)} %get-tuple-element.63), channel_id=1, source_target_pairs={{0,2},{1,3},{2,0},{3,1},{4,6},{5,7},{6,4},{7,5},{8,10},{9,11},{10,... | collective-permute-start | bytes 98312 | tf_op jit(solution)/shard_map/ppermute | solution.py:494
  59.1 5.7 %collective-permute-start.15 = (bf16[4,16,256]{2,1,0:T(8,128)(2,1)S(1)}, bf16[4,16,256]{2,1,0:T(8,128)(2,1)S(1)}, u32[]{:S(2)}, u32[]{:S(2)}) collective-permute-start(bf16[4,16,256]{2,1,0:T(8,128)(2,1)S(1)} %get-tuple-element.64), channel_id=1, source_target_pairs={{0,3},{1,2},{2,1},{3,0},{4,7},{5,6},{6,5},{7,4},{8,11},{9,10},{10,... | collective-permute-start | bytes 98312 | tf_op jit(solution)/shard_map/ppermute | solution.py:494

commit v5 on v4

--- a/solution.py
+++ b/solution.py
@@ -20,7 +20,6 @@
 VMEM_LIMIT = 48 * 1024 * 1024
 
 vmem = pl.BlockSpec(memory_space=pltpu.VMEM)
-smem = pl.BlockSpec(memory_space=pltpu.SMEM)
 hbm = pl.BlockSpec(memory_space=pltpu.HBM)
 anywhere = pl.BlockSpec(memory_space=pl.ANY)
 
@@ -267,9 +266,8 @@
 
 def first_block_kernel(splits, start, scaled, groups, coords, targets, *refs):
     parts, (inv_root, x, *refs) = refs[:splits], refs[splits:]
-    *outs, tile_groups, tile_coords, tile_targets, count, sems, staged = refs
-    routes = (tile_groups, tile_coords, tile_targets)
-    wait = fetch((groups, coords, targets), routes, sems)
+    *outs, count, staged = refs
+    routes = (groups, coords, targets)
     degree = parts[0][...]
     for part in parts[1:]:
         degree += part[...]
@@ -277,7 +275,6 @@
     inv_root[...] = inv
     for k in range(BR):
         x[k] = (start[:, k * TILE : (k + 1) * TILE] * inv[k : k + 1, :]).astype(BF16)
-    wait()
     outgoing(x, scaled, *routes, staged, count)
     split_out(staged, outs)
 
@@ -291,9 +288,8 @@
 def next_block_kernel(
     vertices, scaled, inv_root, groups, coords, targets, mine, theirs, x, *refs
 ):
-    *outs, tile_groups, tile_coords, tile_targets, count, sems, staged = refs
-    routes = (tile_groups, tile_coords, tile_targets)
-    wait = fetch((groups, coords, targets), routes, sems)
+    *outs, count, staged = refs
+    routes = (groups, coords, targets)
     gram = jnp.zeros((2 * WIDTH, 2 * WIDTH), F32)
     for k in range(BR):
         value = mine[k] + theirs[k].astype(F32)
@@ -311,7 +307,6 @@
     block = jnp.concatenate(
         [high, middle, low, jnp.zeros((WIDTH, TILE - 3 * WIDTH), BF16)], axis=1
     )
-    wait()
     outgoing(x, scaled, *routes, staged, count, block)
     split_out(staged, outs)
 
@@ -362,17 +357,15 @@
 
 def remote_products_kernel(splits, whole, pieces, scaled, partial, groups, coords, targets, *refs):
     arrived, refs = refs[:pieces], refs[pieces:]
-    *outs, total, tile_groups, tile_coords, tile_targets, count, sems, joined = refs
-    wait = fetch((groups, coords, targets), (tile_groups, tile_coords, tile_targets), sems)
+    *outs, total, count, joined = refs
     group_count = joined.shape[0]
     by_group(arrived, joined)
     total[...] = partial[...]
-    wait()
-    for t, g, m in slots_of(tile_groups, count, scaled.shape[0], group_count):
-        total[tile_coords[0, 0, 0, t]] += times_t(joined[g, m], scaled[t])
+    for t, g, m in slots_of(groups, count, scaled.shape[0], group_count):
+        total[coords[0, 0, 0, t]] += times_t(joined[g, m], scaled[t])
     for g in range(group_count):
         for m in range(MOST):
-            total[jnp.maximum(tile_targets[g, m], 0)] += joined[g, MOST + m].astype(F32)
+            total[jnp.maximum(targets[g, m], 0)] += joined[g, MOST + m].astype(F32)
     if whole:
         for out in outs:
             out[...] = total[...].astype(out.dtype)
@@ -480,13 +473,6 @@
     local_coords, remote_coords = jnp.swapaxes(local_coords, 2, 3), jnp.swapaxes(remote_coords, 2, 3)
     local_tiles, remote_tiles = local_weights.shape[2], remote_weights.shape[2]
     count = pltpu.SMEM((groups,), jnp.int32)
-    routes = [
-        pltpu.SMEM(remote_groups.shape, jnp.int32),
-        pltpu.SMEM(remote_coords.shape, jnp.int32),
-        pltpu.SMEM((groups, MOST), jnp.int32),
-        count,
-        pltpu.SemaphoreType.DMA((3,)),
-    ]
 
     partners = [2 * 2**k - 1 for k in range(splits.bit_length() - 1)]
 
@@ -529,6 +515,7 @@
         name="local_degree",
     )(*[in_hbm(value) for value in (local_weights, local_gains, local_coords)])
     targets = sums_in[:, MOST : 2 * MOST, 0].astype(jnp.int32)
+    far_scalars = [remote_groups, remote_coords, targets]
     joined = call(
         join_degree_kernel, shape((BR, TILE)), [vmem, vmem, vmem], name="join_degree"
     )(sums_in, row_degree, local_degree)
@@ -546,10 +533,10 @@
     inv_root, x, *sent = call(
         functools.partial(first_block_kernel, splits),
         (shape((BR, TILE)), shape((BR, WIDTH, TILE), BF16)) + sent_blocks(2 * MOST),
-        [vmem, vmem, anywhere, anywhere, anywhere] + [vmem] * splits,
-        routes + [staging(2 * MOST)],
+        [vmem, vmem, vmem, vmem, vmem] + [vmem] * splits,
+        [count, staging(2 * MOST)],
         name="first_block",
-    )(start_block, remote_scaled, remote_groups, remote_coords, targets, *degrees)
+    )(start_block, remote_scaled, *far_scalars, *degrees)
 
     def local_products(x):
         return call(
@@ -589,10 +576,10 @@
         return arrived, call(
             functools.partial(remote_products_kernel, splits, whole, len(arrived)),
             out_shape,
-            [vmem, vmem, anywhere, anywhere, anywhere] + [vmem] * len(arrived),
-            [pltpu.VMEM((BR, WIDTH, TILE), F32)] + routes + [staging(blocks)],
+            [vmem, vmem, vmem, vmem, vmem] + [vmem] * len(arrived),
+            [pltpu.VMEM((BR, WIDTH, TILE), F32), count, staging(blocks)],
             name="remote_products",
-        )(remote_scaled, partial, remote_groups, remote_coords, targets, *arrived)
+        )(remote_scaled, partial, *far_scalars, *arrived)
 
     _, (own, sent) = product(
         x, sent, (shape((BR, WIDTH, TILE)), shape((BR, WIDTH, TILE), BF16)), True
@@ -607,15 +594,13 @@
     x, *sent = call(
         functools.partial(next_block_kernel, vertices),
         (shape((BR, WIDTH, TILE), BF16),) + sent_blocks(2 * MOST + 1),
-        [vmem, vmem, anywhere, anywhere, anywhere, vmem, vmem],
-        routes + [staging(2 * MOST + 1)],
+        [vmem, vmem, vmem, vmem, vmem, vmem, vmem],
+        [count, staging(2 * MOST + 1)],
         name="next_block",
     )(
         remote_scaled,
         inv_root,
-        remote_groups,
-        remote_coords,
-        targets,
+        *far_scalars,
         own,
         swap(sent, partners[-1]),
     )

time: 78.4 us -> 76.2 us (0.972)
  Pallas kernels: 25.4 us -> 23.2 us
    pallas_call x2, Pallas kernels: 2.29 us -> 1.14 us  [product(): call(functools.partial(remote_products_kernel, splits, whole, len(arrived...]
where the time goes in v5:
time: 76.2 us; the launch traced here: 76 us
  Pallas kernels  23.2 us (30%)
  starting transfers between devices  23.2 us (30%)
  waiting for transfers between devices  18.3 us (24%)
  blocking collectives  10.8 us (14%)
    ppermute x8, waiting for transfers between devices, swap(): return lax.ppermute(value, 'cols', [(j, j ^ k) for j in range(splits)])  14.3 us
    all_to_all x1, blocking collectives, per_device(): lax.all_to_all(grams, ('rows', 'cols'), split_axis=0, concat_axis=0, tile...  10.8 us
    ppermute x8, starting transfers between devices, swap(): return lax.ppermute(value, 'cols', [(j, j ^ k) for j in range(splits)])  10.8 us
    pallas_call x2, Pallas kernels, local_products(): call(local_products_kernel, shape((BR, WIDTH, TILE)), [vmem, vmem, hbm, v...  8.2 us
    ppermute x6, starting transfers between devices, product(): lax.ppermute(piece, 'rows', [(j, j ^ 2 * k) for j in range(groups)])  7.11 us
    all_to_all x1, starting transfers between devices, trade(): lax.all_to_all(value, 'rows', split_axis=0, concat_axis=0, tiled=True)  5.21 us
    pallas_call x1, Pallas kernels, per_device(): call(local_degree_kernel, (shape((BR, TILE)), shape((HELD, TILE, TILE), B...  4.82 us
    ppermute x2, waiting for transfers between devices, product(): passed = lax.ppermute(far, 'rows', [(j, j ^ 1) for j in range(groups)])  2.72 us
  transfers between devices with their start and end apart: 17, of which 9 were waited for; matrix products, arithmetic and copies ran while one was open for 0% of the time, Pallas kernels for 21%

profile of v5, /device:TPU:0, one launch (start us, length us, event | category | flops | bytes accessed | tf_op | source)
XLA Modules:
  0.0 76.0 jit_solution(12247056928897948251)
XLA Ops:
  0.0 2.5 %remote_degree.1 = (f32[8,8,256]{2,1,0:T(8,128)}, f32[16,256]{1,0:T(8,128)S(1)}) custom-call(bf16[1,1,8,256,256]{4,3,2,1,0:T(8,128)(2,1)} %raw.1, f32[1,1,8,2,256]{4,3,2,1,0:T(2,128)} %gains.6, s32[1,1,8]{2,1,0:T(1,128)} %groups.9, s32[1,1,2,8]{3,2,1,0:T(2,128)} %bitcast.3), custom_call_target="tpu_custom_call" | custom-call | flops 1000000 | bytes 1000000 | tf_op jit(solution)/shard_map/remote_degree/pallas_call | solution.py:486
  2.5 5.2 %all-to-all-start = ((f32[8,8,256]{2,1,0:T(8,128)}), f32[8,8,256]{2,1,0:T(8,128)S(1)}, u32[]{:S(2)}, u32[]{:S(2)}) async-start(f32[8,8,256]{2,1,0:T(8,128)} %get-tuple-element.36), calls=%async_computation | async-start | bytes 131072 | tf_op jit(solution)/shard_map/all_to_all | solution.py:483
  7.8 4.8 %local_degree.1 = (f32[16,256]{1,0:T(8,128)S(1)}, bf16[16,256,256]{2,1,0:T(8,128)(2,1)S(1)}) custom-call(bf16[1,1,48,256,256]{4,3,2,1,0:T(8,128)(2,1)} %weights.7, f32[1,1,48,2,256]{4,3,2,1,0:T(2,128)} %gains.8, s32[1,1,2,48]{3,2,1,0:T(2,128)} %bitcast.8), custom_call_target="tpu_custom_call" | custom-call | flops 1000000 | bytes 10000000 | tf_op jit(solution)/shard_map/local_degree/pallas_call | solution.py:501
  12.8 3.7 %collective-permute-start.2 = (f32[16,256]{1,0:T(8,128)S(1)}, f32[16,256]{1,0:T(8,128)S(1)}, u32[]{:S(2)}, u32[]{:S(2)}) collective-permute-start(f32[16,256]{1,0:T(8,128)S(1)} %join_degree.1.refs_0_), channel_id=1, source_target_pairs={{0,3},{1,2},{2,1},{3,0},{4,7},{5,6},{6,5},{7,4},{8,11},{9,10},{10,... | collective-permute-start | bytes 49160 | tf_op jit(solution)/shard_map/ppermute | solution.py:480
  16.5 0.8 %collective-permute-start = (f32[16,256]{1,0:T(8,128)S(1)}, f32[16,256]{1,0:T(8,128)S(1)}, u32[]{:S(2)}, u32[]{:S(2)}) collective-permute-start(f32[16,256]{1,0:T(8,128)S(1)} %join_degree.1.refs_0_), channel_id=1, source_target_pairs={{0,1},{1,0},{2,3},{3,2},{4,5},{5,4},{6,7},{7,6},{8,9},{9,8},{10,11... | collective-permute-start | bytes 49160 | tf_op jit(solution)/shard_map/ppermute | solution.py:480
  17.5 1.7 %remote_scale.1.scaled = bf16[8,256,256]{2,1,0:T(8,128)(2,1)S(1)} custom-call(bf16[1,1,8,256,256]{4,3,2,1,0:T(8,128)(2,1)} %raw.1, f32[1,1,8,2,256]{4,3,2,1,0:T(2,128)S(1)} %copy-done.2), custom_call_target="tpu_custom_call" | custom-call | flops 1048576 | bytes 2097152 | tf_op jit(solution)/shard_map/remote_scale/pallas_call | solution.py:189
  19.2 1.9 %collective-permute-done.1.refs_2_ = f32[16,256]{1,0:T(8,128)S(1)} collective-permute-done((f32[16,256]{1,0:T(8,128)S(1)}, f32[16,256]{1,0:T(8,128)S(1)}, u32[]{:S(2)}, u32[]{:S(2)}) %collective-permute-start.1) | collective-permute-done | bytes 16416 | tf_op jit(solution)/shard_map/ppermute | solution.py:480
  21.1 0.4 first_block.1
  21.6 1.3 %collective-permute-done.3.passed = bf16[4,4,16,256]{3,2,1,0:T(8,128)(2,1)S(1)} collective-permute-done((bf16[4,4,16,256]{3,2,1,0:T(8,128)(2,1)S(1)}, bf16[4,4,16,256]{3,2,1,0:T(8,128)(2,1)S(1)}, u32[]{:S(2)}, u32[]{:S(2)}) %collective-permute-start.3) | collective-permute-done | bytes 131104 | tf_op jit(solution)/shard_map/ppermute | solution.py:561
  22.9 1.9 %collective-permute-start.4 = (bf16[2,4,16,256]{3,2,1,0:T(8,128)(2,1)S(1)}, bf16[2,4,16,256]{3,2,1,0:T(8,128)(2,1)S(1)}, u32[]{:S(2)}, u32[]{:S(2)}) collective-permute-start(bf16[2,4,16,256]{3,2,1,0:T(8,128)(2,1)S(1)} %get-tuple-element.47), channel_id=1, source_target_pairs={{0,8},{4,12},{8,0},{12,4},{16,24},{20,28},{24,16},{28,20},{1,9},{5... | collective-permute-start | bytes 196616 | tf_op jit(solution)/shard_map/ppermute | solution.py:569
  24.8 1.5 %collective-permute-start.5 = (bf16[2,4,16,256]{3,2,1,0:T(8,128)(2,1)S(1)}, bf16[2,4,16,256]{3,2,1,0:T(8,128)(2,1)S(1)}, u32[]{:S(2)}, u32[]{:S(2)}) collective-permute-start(bf16[2,4,16,256]{3,2,1,0:T(8,128)(2,1)S(1)} %get-tuple-element.48), channel_id=1, source_target_pairs={{0,16},{4,20},{8,24},{12,28},{16,0},{20,4},{24,8},{28,12},{1,17},{... | collective-permute-start | bytes 196616 | tf_op jit(solution)/shard_map/ppermute | solution.py:569
  26.5 4.1 %local_products.2.partial = f32[16,16,256]{2,1,0:T(8,128)S(1)} custom-call(bf16[16,16,256]{2,1,0:T(8,128)(2,1)S(1)} %get-tuple-element.42.x, bf16[16,256,256]{2,1,0:T(8,128)(2,1)S(1)} %get-tuple-element.43.ready, bf16[1,1,48,256,256]{4,3,2,1,0:T(8,128)(2,1)} %weights.7, f32[1,1,48,2,256]{4,3,2,1,0:T(2,128)S(1)} %copy-done, s32[1,1,2,48]{3,2,1,0:T(2,128)S(1)} %bitcast.9), custom_call_target="tpu_custom_call" | custom-call | flops 201326592 | bytes 6291456 | tf_op jit(solution)/shard_map/local_products/pallas_call | solution.py:542
  30.6 0.8 %collective-permute-done.6.refs_3_ = bf16[2,4,16,256]{3,2,1,0:T(8,128)(2,1)S(1)} collective-permute-done((bf16[2,4,16,256]{3,2,1,0:T(8,128)(2,1)S(1)}, bf16[2,4,16,256]{3,2,1,0:T(8,128)(2,1)S(1)}, u32[]{:S(2)}, u32[]{:S(2)}) %collective-permute-start.6) | collective-permute-done | bytes 65568 | tf_op jit(solution)/shard_map/ppermute | solution.py:569
  31.5 0.6 remote_products.2
  32.1 5.0 %collective-permute-done.7.theirs = bf16[16,16,256]{2,1,0:T(8,128)(2,1)S(1)} collective-permute-done((bf16[16,16,256]{2,1,0:T(8,128)(2,1)S(1)}, bf16[16,16,256]{2,1,0:T(8,128)(2,1)S(1)}, u32[]{:S(2)}, u32[]{:S(2)}) %collective-permute-start.7) | collective-permute-done | bytes 131104 | tf_op jit(solution)/shard_map/ppermute | solution.py:480
  37.1 1.8 %collective-permute-start.8 = (bf16[16,16,256]{2,1,0:T(8,128)(2,1)S(1)}, bf16[16,16,256]{2,1,0:T(8,128)(2,1)S(1)}, u32[]{:S(2)}, u32[]{:S(2)}) collective-permute-start(bf16[16,16,256]{2,1,0:T(8,128)(2,1)S(1)} %get-tuple-element.53), channel_id=1, source_target_pairs={{0,3},{1,2},{2,1},{3,0},{4,7},{5,6},{6,5},{7,4},{8,11},{9,10},{10,... | collective-permute-start | bytes 393224 | tf_op jit(solution)/shard_map/ppermute | solution.py:480
  38.9 5.0 %collective-permute-done.8.theirs = bf16[16,16,256]{2,1,0:T(8,128)(2,1)S(1)} collective-permute-done((bf16[16,16,256]{2,1,0:T(8,128)(2,1)S(1)}, bf16[16,16,256]{2,1,0:T(8,128)(2,1)S(1)}, u32[]{:S(2)}, u32[]{:S(2)}) %collective-permute-start.8) | collective-permute-done | bytes 131104 | tf_op jit(solution)/shard_map/ppermute | solution.py:480
  44.0 0.6 next_block.1
  44.6 1.4 %collective-permute-done.9.passed = bf16[4,5,16,256]{3,2,1,0:T(8,128)(2,1)S(1)} collective-permute-done((bf16[4,5,16,256]{3,2,1,0:T(8,128)(2,1)S(1)}, bf16[4,5,16,256]{3,2,1,0:T(8,128)(2,1)S(1)}, u32[]{:S(2)}, u32[]{:S(2)}) %collective-permute-start.9) | collective-permute-done | bytes 163872 | tf_op jit(solution)/shard_map/ppermute | solution.py:561
  46.0 1.1 %collective-permute-start.10 = (bf16[2,5,16,256]{3,2,1,0:T(8,128)(2,1)S(1)}, bf16[2,5,16,256]{3,2,1,0:T(8,128)(2,1)S(1)}, u32[]{:S(2)}, u32[]{:S(2)}) collective-permute-start(bf16[2,5,16,256]{3,2,1,0:T(8,128)(2,1)S(1)} %get-tuple-element.57), channel_id=1, source_target_pairs={{0,8},{4,12},{8,0},{12,4},{16,24},{20,28},{24,16},{28,20},{1,9},{5... | collective-permute-start | bytes 245768 | tf_op jit(solution)/shard_map/ppermute | solution.py:569
  47.1 1.5 %collective-permute-start.11 = (bf16[2,5,16,256]{3,2,1,0:T(8,128)(2,1)S(1)}, bf16[2,5,16,256]{3,2,1,0:T(8,128)(2,1)S(1)}, u32[]{:S(2)}, u32[]{:S(2)}) collective-permute-start(bf16[2,5,16,256]{3,2,1,0:T(8,128)(2,1)S(1)} %get-tuple-element.58), channel_id=1, source_target_pairs={{0,16},{4,20},{8,24},{12,28},{16,0},{20,4},{24,8},{28,12},{1,17},{... | collective-permute-start | bytes 245768 | tf_op jit(solution)/shard_map/ppermute | solution.py:569
  48.5 1.0 %collective-permute-start.12 = (bf16[2,5,16,256]{3,2,1,0:T(8,128)(2,1)S(1)}, bf16[2,5,16,256]{3,2,1,0:T(8,128)(2,1)S(1)}, u32[]{:S(2)}, u32[]{:S(2)}) collective-permute-start(bf16[2,5,16,256]{3,2,1,0:T(8,128)(2,1)S(1)} %get-tuple-element.59), channel_id=1, source_target_pairs={{0,24},{4,28},{8,16},{12,20},{16,8},{20,12},{24,0},{28,4},{1,25},{... | collective-permute-start | bytes 245768 | tf_op jit(solution)/shard_map/ppermute | solution.py:569
  49.6 4.1 %local_products.3.partial = f32[16,16,256]{2,1,0:T(8,128)S(1)} custom-call(bf16[16,16,256]{2,1,0:T(8,128)(2,1)S(1)} %get-tuple-element.60.x, bf16[16,256,256]{2,1,0:T(8,128)(2,1)S(1)} %get-tuple-element.43.ready, bf16[1,1,48,256,256]{4,3,2,1,0:T(8,128)(2,1)} %weights.7, f32[1,1,48,2,256]{4,3,2,1,0:T(2,128)S(1)} %copy-done, s32[1,1,2,48]{3,2,1,0:T(2,128)S(1)} %bitcast.10), custom_call_target="tpu_custom_call" | custom-call | flops 201326592 | bytes 6291456 | tf_op jit(solution)/shard_map/local_products/pallas_call | solution.py:542
  53.7 0.2 collective-permute-done.12.refs_3_
  53.9 0.6 remote_products.3
  54.5 2.4 %collective-permute-start.14 = (bf16[4,16,256]{2,1,0:T(8,128)(2,1)S(1)}, bf16[4,16,256]{2,1,0:T(8,128)(2,1)S(1)}, u32[]{:S(2)}, u32[]{:S(2)}) collective-permute-start(bf16[4,16,256]{2,1,0:T(8,128)(2,1)S(1)} %get-tuple-element.63), channel_id=1, source_target_pairs={{0,2},{1,3},{2,0},{3,1},{4,6},{5,7},{6,4},{7,5},{8,10},{9,11},{10,... | collective-permute-start | bytes 98312 | tf_op jit(solution)/shard_map/ppermute | solution.py:480
  56.9 2.0 %collective-permute-start.15 = (bf16[4,16,256]{2,1,0:T(8,128)(2,1)S(1)}, bf16[4,16,256]{2,1,0:T(8,128)(2,1)S(1)}, u32[]{:S(2)}, u32[]{:S(2)}) collective-permute-start(bf16[4,16,256]{2,1,0:T(8,128)(2,1)S(1)} %get-tuple-element.64), channel_id=1, source_target_pairs={{0,3},{1,2},{2,1},{3,0},{4,7},{5,6},{6,5},{7,4},{8,11},{9,10},{10,... | collective-permute-start | bytes 98312 | tf_op jit(solution)/shard_map/ppermute | solution.py:480
  58.9 1.3 %middle_factor.1.inverse = f32[16,16]{1,0:T(8,128)S(1)} custom-call(bf16[2,5,16,256]{3,2,1,0:T(8,128)(2,1)S(1)} %get-tuple-element.56.refs_0_, bf16[2,5,16,256]{3,2,1,0:T(8,128)(2,1)S(1)} %collective-permute-done.10.refs_1_, bf16[2,5,16,256]{3,2,1,0:T(8,128)(2,1)S(1)} %collective-permute-done.11.refs_2_, ...), custom_call_target="tpu_custom_call" | custom-call | flops 1000000 | bytes 1000000 | tf_op jit(solution)/shard_map/middle_factor/pallas_call | solution.py:614
  60.2 2.4 %collective-permute-done.15.refs_3_ = bf16[4,16,256]{2,1,0:T(8,128)(2,1)S(1)} collective-permute-done((bf16[4,16,256]{2,1,0:T(8,128)(2,1)S(1)}, bf16[4,16,256]{2,1,0:T(8,128)(2,1)S(1)}, u32[]{:S(2)}, u32[]{:S(2)}) %collective-permute-start.15) | collective-permute-done | bytes 32800 | tf_op jit(solution)/shard_map/ppermute | solution.py:480
  62.6 0.7 last_quarter.1
  63.3 10.8 %all_to_all.10.grams = f32[32,4,128]{2,1,0:T(4,128)S(1)} all-to-all(f32[32,4,128]{2,1,0:T(4,128)S(1)} %get-tuple-element.65), channel_id=1, replica_groups=mesh['rows'=8,'cols'=4] {'rows','cols'}, dimensions={0} | all-to-all | bytes 131072 | tf_op jit(solution)/shard_map/all_to_all | solution.py:626
  74.1 1.8 %finish.1 = f32[16,1024]{1,0:T(8,128)} custom-call(f32[32,4,128]{2,1,0:T(4,128)S(1)} %all_to_all.10.grams, f32[16,1024]{1,0:T(8,128)S(1)} %get-tuple-element.66.image), custom_call_target="tpu_custom_call" | custom-call | flops 1000000 | bytes 1000000 | tf_op jit(solution)/shard_map/finish/pallas_call | solution.py:629
  (34 shorter events, 1.0 us)
Async XLA Ops:
  0.0 21.1 %copy-start.4 = (s32[1,1,8]{2,1,0:T(1,128)S(1)}, s32[1,1,8]{2,1,0:T(1,128)}, u32[]{:S(2)}) copy-start(s32[1,1,8]{2,1,0:T(1,128)} %groups.9) | copy-start | bytes 100
  0.0 17.5 %copy-start.2 = (f32[1,1,8,2,256]{4,3,2,1,0:T(2,128)S(1)}, f32[1,1,8,2,256]{4,3,2,1,0:T(2,128)}, u32[]{:S(2)}) copy-start(f32[1,1,8,2,256]{4,3,2,1,0:T(2,128)} %gains.6) | copy-start | bytes 49156
  0.0 21.1 %copy-start.3 = (s32[1,1,8,2]{2,3,1,0:T(2,128)S(1)}, s32[1,1,8,2]{2,3,1,0:T(2,128)}, u32[]{:S(2)}) copy-start(s32[1,1,8,2]{2,3,1,0:T(2,128)} %param.14) | copy-start | bytes 196
  0.0 26.5 %copy-start = (f32[1,1,48,2,256]{4,3,2,1,0:T(2,128)S(1)}, f32[1,1,48,2,256]{4,3,2,1,0:T(2,128)}, u32[]{:S(2)}) copy-start(f32[1,1,48,2,256]{4,3,2,1,0:T(2,128)} %gains.8) | copy-start | bytes 294916
  0.0 26.5 %copy-start.5 = (s32[1,1,48,2]{2,3,1,0:T(2,128)S(1)}, s32[1,1,48,2]{2,3,1,0:T(2,128)}, u32[]{:S(2)}) copy-start(s32[1,1,48,2]{2,3,1,0:T(2,128)} %param.10) | copy-start | bytes 1156
  0.0 21.1 %copy-start.1 = (f32[16,4096]{1,0:T(8,128)S(1)}, f32[16,4096]{1,0:T(8,128)}, u32[]{:S(2)}) copy-start(f32[16,4096]{1,0:T(8,128)} %start.1) | copy-start | bytes 786436
  2.5 10.2 %all-to-all-start = ((f32[8,8,256]{2,1,0:T(8,128)}), f32[8,8,256]{2,1,0:T(8,128)S(1)}, u32[]{:S(2)}, u32[]{:S(2)}) async-start(f32[8,8,256]{2,1,0:T(8,128)} %get-tuple-element.36), calls=%async_computation | async-start | bytes 131072 | tf_op jit(solution)/shard_map/all_to_all | solution.py:483
  12.8 6.4 %collective-permute-start.2 = (f32[16,256]{1,0:T(8,128)S(1)}, f32[16,256]{1,0:T(8,128)S(1)}, u32[]{:S(2)}, u32[]{:S(2)}) collective-permute-start(f32[16,256]{1,0:T(8,128)S(1)} %join_degree.1.refs_0_), channel_id=1, source_target_pairs={{0,3},{1,2},{2,1},{3,0},{4,7},{5,6},{6,5},{7,4},{8,11},{9,10},{10,... | collective-permute-start | bytes 49160 | tf_op jit(solution)/shard_map/ppermute | solution.py:480
  16.5 4.6 %collective-permute-start.1 = (f32[16,256]{1,0:T(8,128)S(1)}, f32[16,256]{1,0:T(8,128)S(1)}, u32[]{:S(2)}, u32[]{:S(2)}) collective-permute-start(f32[16,256]{1,0:T(8,128)S(1)} %join_degree.1.refs_0_), channel_id=1, source_target_pairs={{0,2},{1,3},{2,0},{3,1},{4,6},{5,7},{6,4},{7,5},{8,10},{9,11},{10,... | collective-permute-start | bytes 49160 | tf_op jit(solution)/shard_map/ppermute | solution.py:480
  16.5 4.6 %collective-permute-start = (f32[16,256]{1,0:T(8,128)S(1)}, f32[16,256]{1,0:T(8,128)S(1)}, u32[]{:S(2)}, u32[]{:S(2)}) collective-permute-start(f32[16,256]{1,0:T(8,128)S(1)} %join_degree.1.refs_0_), channel_id=1, source_target_pairs={{0,1},{1,0},{2,3},{3,2},{4,5},{5,4},{6,7},{7,6},{8,9},{9,8},{10,11... | collective-permute-start | bytes 49160 | tf_op jit(solution)/shard_map/ppermute | solution.py:480
  21.5 1.4 %collective-permute-start.3 = (bf16[4,4,16,256]{3,2,1,0:T(8,128)(2,1)S(1)}, bf16[4,4,16,256]{3,2,1,0:T(8,128)(2,1)S(1)}, u32[]{:S(2)}, u32[]{:S(2)}) collective-permute-start(bf16[4,4,16,256]{3,2,1,0:T(8,128)(2,1)S(1)} %get-tuple-element.45), channel_id=1, source_target_pairs={{0,4},{4,0},{8,12},{12,8},{16,20},{20,16},{24,28},{28,24},{1,5},{5... | collective-permute-start | bytes 393224 | tf_op jit(solution)/shard_map/ppermute | solution.py:561
  22.9 7.7 %collective-permute-start.4 = (bf16[2,4,16,256]{3,2,1,0:T(8,128)(2,1)S(1)}, bf16[2,4,16,256]{3,2,1,0:T(8,128)(2,1)S(1)}, u32[]{:S(2)}, u32[]{:S(2)}) collective-permute-start(bf16[2,4,16,256]{3,2,1,0:T(8,128)(2,1)S(1)} %get-tuple-element.47), channel_id=1, source_target_pairs={{0,8},{4,12},{8,0},{12,4},{16,24},{20,28},{24,16},{28,20},{1,9},{5... | collective-permute-start | bytes 196616 | tf_op jit(solution)/shard_map/ppermute | solution.py:569
  24.8 5.8 %collective-permute-start.5 = (bf16[2,4,16,256]{3,2,1,0:T(8,128)(2,1)S(1)}, bf16[2,4,16,256]{3,2,1,0:T(8,128)(2,1)S(1)}, u32[]{:S(2)}, u32[]{:S(2)}) collective-permute-start(bf16[2,4,16,256]{3,2,1,0:T(8,128)(2,1)S(1)} %get-tuple-element.48), channel_id=1, source_target_pairs={{0,16},{4,20},{8,24},{12,28},{16,0},{20,4},{24,8},{28,12},{1,17},{... | collective-permute-start | bytes 196616 | tf_op jit(solution)/shard_map/ppermute | solution.py:569
  26.3 5.2 %collective-permute-start.6 = (bf16[2,4,16,256]{3,2,1,0:T(8,128)(2,1)S(1)}, bf16[2,4,16,256]{3,2,1,0:T(8,128)(2,1)S(1)}, u32[]{:S(2)}, u32[]{:S(2)}) collective-permute-start(bf16[2,4,16,256]{3,2,1,0:T(8,128)(2,1)S(1)} %get-tuple-element.49), channel_id=1, source_target_pairs={{0,24},{4,28},{8,16},{12,20},{16,8},{20,12},{24,0},{28,4},{1,25},{... | collective-permute-start | bytes 196616 | tf_op jit(solution)/shard_map/ppermute | solution.py:569
  32.1 5.0 %collective-permute-start.7 = (bf16[16,16,256]{2,1,0:T(8,128)(2,1)S(1)}, bf16[16,16,256]{2,1,0:T(8,128)(2,1)S(1)}, u32[]{:S(2)}, u32[]{:S(2)}) collective-permute-start(bf16[16,16,256]{2,1,0:T(8,128)(2,1)S(1)} %get-tuple-element.51), channel_id=1, source_target_pairs={{0,1},{1,0},{2,3},{3,2},{4,5},{5,4},{6,7},{7,6},{8,9},{9,8},{10,11... | collective-permute-start | bytes 393224 | tf_op jit(solution)/shard_map/ppermute | solution.py:480
  37.1 6.8 %collective-permute-start.8 = (bf16[16,16,256]{2,1,0:T(8,128)(2,1)S(1)}, bf16[16,16,256]{2,1,0:T(8,128)(2,1)S(1)}, u32[]{:S(2)}, u32[]{:S(2)}) collective-permute-start(bf16[16,16,256]{2,1,0:T(8,128)(2,1)S(1)} %get-tuple-element.53), channel_id=1, source_target_pairs={{0,3},{1,2},{2,1},{3,0},{4,7},{5,6},{6,5},{7,4},{8,11},{9,10},{10,... | collective-permute-start | bytes 393224 | tf_op jit(solution)/shard_map/ppermute | solution.py:480
  44.5 1.5 %collective-permute-start.9 = (bf16[4,5,16,256]{3,2,1,0:T(8,128)(2,1)S(1)}, bf16[4,5,16,256]{3,2,1,0:T(8,128)(2,1)S(1)}, u32[]{:S(2)}, u32[]{:S(2)}) collective-permute-start(bf16[4,5,16,256]{3,2,1,0:T(8,128)(2,1)S(1)} %get-tuple-element.55), channel_id=1, source_target_pairs={{0,4},{4,0},{8,12},{12,8},{16,20},{20,16},{24,28},{28,24},{1,5},{5... | collective-permute-start | bytes 491528 | tf_op jit(solution)/shard_map/ppermute | solution.py:561
  46.0 7.7 %collective-permute-start.10 = (bf16[2,5,16,256]{3,2,1,0:T(8,128)(2,1)S(1)}, bf16[2,5,16,256]{3,2,1,0:T(8,128)(2,1)S(1)}, u32[]{:S(2)}, u32[]{:S(2)}) collective-permute-start(bf16[2,5,16,256]{3,2,1,0:T(8,128)(2,1)S(1)} %get-tuple-element.57), channel_id=1, source_target_pairs={{0,8},{4,12},{8,0},{12,4},{16,24},{20,28},{24,16},{28,20},{1,9},{5... | collective-permute-start | bytes 245768 | tf_op jit(solution)/shard_map/ppermute | solution.py:569
  47.1 6.6 %collective-permute-start.11 = (bf16[2,5,16,256]{3,2,1,0:T(8,128)(2,1)S(1)}, bf16[2,5,16,256]{3,2,1,0:T(8,128)(2,1)S(1)}, u32[]{:S(2)}, u32[]{:S(2)}) collective-permute-start(bf16[2,5,16,256]{3,2,1,0:T(8,128)(2,1)S(1)} %get-tuple-element.58), channel_id=1, source_target_pairs={{0,16},{4,20},{8,24},{12,28},{16,0},{20,4},{24,8},{28,12},{1,17},{... | collective-permute-start | bytes 245768 | tf_op jit(solution)/shard_map/ppermute | solution.py:569
  48.5 5.3 %collective-permute-start.12 = (bf16[2,5,16,256]{3,2,1,0:T(8,128)(2,1)S(1)}, bf16[2,5,16,256]{3,2,1,0:T(8,128)(2,1)S(1)}, u32[]{:S(2)}, u32[]{:S(2)}) collective-permute-start(bf16[2,5,16,256]{3,2,1,0:T(8,128)(2,1)S(1)} %get-tuple-element.59), channel_id=1, source_target_pairs={{0,24},{4,28},{8,16},{12,20},{16,8},{20,12},{24,0},{28,4},{1,25},{... | collective-permute-start | bytes 245768 | tf_op jit(solution)/shard_map/ppermute | solution.py:569
  54.5 5.7 %collective-permute-start.13 = (bf16[4,16,256]{2,1,0:T(8,128)(2,1)S(1)}, bf16[4,16,256]{2,1,0:T(8,128)(2,1)S(1)}, u32[]{:S(2)}, u32[]{:S(2)}) collective-permute-start(bf16[4,16,256]{2,1,0:T(8,128)(2,1)S(1)} %get-tuple-element.62), channel_id=1, source_target_pairs={{0,1},{1,0},{2,3},{3,2},{4,5},{5,4},{6,7},{7,6},{8,9},{9,8},{10,11... | collective-permute-start | bytes 98312 | tf_op jit(solution)/shard_map/ppermute | solution.py:480
  54.5 5.7 %collective-permute-start.14 = (bf16[4,16,256]{2,1,0:T(8,128)(2,1)S(1)}, bf16[4,16,256]{2,1,0:T(8,128)(2,1)S(1)}, u32[]{:S(2)}, u32[]{:S(2)}) collective-permute-start(bf16[4,16,256]{2,1,0:T(8,128)(2,1)S(1)} %get-tuple-element.63), channel_id=1, source_target_pairs={{0,2},{1,3},{2,0},{3,1},{4,6},{5,7},{6,4},{7,5},{8,10},{9,11},{10,... | collective-permute-start | bytes 98312 | tf_op jit(solution)/shard_map/ppermute | solution.py:480
  56.9 5.7 %collective-permute-start.15 = (bf16[4,16,256]{2,1,0:T(8,128)(2,1)S(1)}, bf16[4,16,256]{2,1,0:T(8,128)(2,1)S(1)}, u32[]{:S(2)}, u32[]{:S(2)}) collective-permute-start(bf16[4,16,256]{2,1,0:T(8,128)(2,1)S(1)} %get-tuple-element.64), channel_id=1, source_target_pairs={{0,3},{1,2},{2,1},{3,0},{4,7},{5,6},{6,5},{7,4},{8,11},{9,10},{10,... | collective-permute-start | bytes 98312 | tf_op jit(solution)/shard_map/ppermute | solution.py:480

commit v6 on v5

--- a/solution.py
+++ b/solution.py
@@ -214,6 +214,10 @@
     joined[...] = total
 
 
+def offsets(count):
+    return [0] + list(range(count - 1, 0, -1))
+
+
 def by_chips(groups):
     return groups // 2 <= 4
 
@@ -250,7 +254,7 @@
     chips = near.shape[0]
     me = lax.axis_index("rows")
     chip, core = me // 2, me % 2
-    for k, piece in enumerate(pieces):
+    for k, piece in zip(offsets(chips), pieces):
         piece[core] = near[chip ^ k]
         piece[1 - core] = passed[chip ^ k]
 
@@ -260,7 +264,7 @@
         joined[...] = arrived[0][...]
         return
     chip = lax.axis_index("rows") // 2
-    for k, piece in enumerate(arrived):
+    for k, piece in zip(offsets(len(arrived)), arrived):
         joined[pl.ds((chip ^ k) * 2, 2)] = piece[...]
 
 
@@ -372,7 +376,7 @@
         return
     me = lax.axis_index("cols")
     quarter = BR // splits
-    for k, out in enumerate(outs):
+    for k, out in zip(offsets(splits), outs):
         base = pl.multiple_of((me ^ k) * quarter, quarter)
         out[...] = total[pl.ds(base, quarter)].astype(out.dtype)
 
@@ -439,9 +443,7 @@
             value, value, (((1,), (1,)), ((), ())), precision=HIGHEST, preferred_element_type=F32
         )
     gram = gram / vertices
-    block = jnp.concatenate(
-        [gram[4 * n : 4 * n + 4] for n in range(4)] + [jnp.zeros((4, LANES - 4 * WIDTH), F32)], axis=1
-    )
+    block = jnp.concatenate([gram[2 * n : 2 * n + 2] for n in range(WIDTH // 2)], axis=1)
     for n in range(grams.shape[0]):
         grams[n] = block
 
@@ -450,7 +452,9 @@
     block = grams[0]
     for n in range(1, grams.shape[0]):
         block = block + grams[n]
-    gram = jnp.concatenate([block[:, WIDTH * n : WIDTH * (n + 1)] for n in range(4)], axis=0)
+    gram = jnp.concatenate(
+        [block[:, WIDTH * n : WIDTH * (n + 1)] for n in range(WIDTH // 2)], axis=0
+    )
     starts = range(0, out.shape[1], LANES)
     for n, block in zip(starts, eliminate(gram, [image[:, n : n + LANES] for n in starts])):
         out[:, n : n + LANES] = block
@@ -567,7 +571,7 @@
             )(near, passed)
             arrived = [own] + [
                 lax.ppermute(piece, "rows", [(j, j ^ (2 * k)) for j in range(groups)])
-                for k, piece in enumerate(others, 1)
+                for k, piece in zip(offsets(groups // 2)[1:], others)
             ]
             partial = local_products(x)
         else:
@@ -610,7 +614,7 @@
         tuple(shape((quarter, WIDTH, TILE), BF16 if k else F32) for k in range(splits)),
         False,
     )
-    pieces = [sent[0]] + [swap(sent[k], k) for k in range(1, splits)]
+    pieces = [sent[0]] + [swap(part, k) for k, part in zip(offsets(splits)[1:], sent[1:])]
     inverse = call(
         middle_factor_kernel,
         shape((WIDTH, WIDTH)),
@@ -619,7 +623,7 @@
     )(*arrived)
     image, grams = call(
         functools.partial(last_quarter_kernel, splits, vertices),
-        (shape((WIDTH, quarter * TILE)), shape((groups * splits, 4, LANES))),
+        (shape((WIDTH, quarter * TILE)), shape((groups * splits, 2, LANES))),
         [vmem] * (2 + splits),
         name="last_quarter",
     )(inv_root, inverse, *pieces)

time: 76.2 us -> 74.8 us (0.982)
  waiting for transfers between devices: 18.3 us -> 16.2 us
    ppermute x8, waiting for transfers between devices: 14.3 us -> 13.2 us  [swap(): return lax.ppermute(value, 'cols', [(j, j ^ k) for j in range(splits)])]
    ppermute x6, waiting for transfers between devices: 1.06 us -> 0.06 us  [product(): lax.ppermute(piece, 'rows', [(j, j ^ 2 * k) for j in range(groups)])]
  transfers between devices with their start and end apart: 17 -> 17, of which waited for: 9 -> 9; matrix products, arithmetic and copies ran while one was open for 0% -> 0% of each run, Pallas kernels for 21% -> 22%
where the time goes in v6:
time: 74.8 us; the launch traced here: 74.5 us
  Pallas kernels  23.2 us (31%)
  starting transfers between devices  23.2 us (31%)
  waiting for transfers between devices  16.2 us (22%)
  blocking collectives  11.5 us (15%)
    ppermute x8, waiting for transfers between devices, swap(): return lax.ppermute(value, 'cols', [(j, j ^ k) for j in range(splits)])  13.2 us
    all_to_all x1, blocking collectives, per_device(): lax.all_to_all(grams, ('rows', 'cols'), split_axis=0, concat_axis=0, tile...  11.5 us
    ppermute x8, starting transfers between devices, swap(): return lax.ppermute(value, 'cols', [(j, j ^ k) for j in range(splits)])  10.8 us
    pallas_call x2, Pallas kernels, local_products(): call(local_products_kernel, shape((BR, WIDTH, TILE)), [vmem, vmem, hbm, v...  8.2 us
    ppermute x6, starting transfers between devices, product(): lax.ppermute(piece, 'rows', [(j, j ^ 2 * k) for j in range(groups)])  7.11 us
    all_to_all x1, starting transfers between devices, trade(): lax.all_to_all(value, 'rows', split_axis=0, concat_axis=0, tiled=True)  5.21 us
    pallas_call x1, Pallas kernels, per_device(): call(local_degree_kernel, (shape((BR, TILE)), shape((HELD, TILE, TILE), B...  4.82 us
    ppermute x2, waiting for transfers between devices, product(): passed = lax.ppermute(far, 'rows', [(j, j ^ 1) for j in range(groups)])  2.72 us
  transfers between devices with their start and end apart: 17, of which 9 were waited for; matrix products, arithmetic and copies ran while one was open for 0% of the time, Pallas kernels for 22%

profile of v6, /device:TPU:0, one launch (start us, length us, event | category | flops | bytes accessed | tf_op | source)
XLA Modules:
  0.0 74.5 jit_solution(5612772341870194551)
XLA Ops:
  0.0 2.5 %remote_degree.1 = (f32[8,8,256]{2,1,0:T(8,128)}, f32[16,256]{1,0:T(8,128)S(1)}) custom-call(bf16[1,1,8,256,256]{4,3,2,1,0:T(8,128)(2,1)} %raw.1, f32[1,1,8,2,256]{4,3,2,1,0:T(2,128)} %gains.6, s32[1,1,8]{2,1,0:T(1,128)} %groups.9, s32[1,1,2,8]{3,2,1,0:T(2,128)} %bitcast.3), custom_call_target="tpu_custom_call" | custom-call | flops 1000000 | bytes 1000000 | tf_op jit(solution)/shard_map/remote_degree/pallas_call | solution.py:490
  2.5 5.2 %all-to-all-start = ((f32[8,8,256]{2,1,0:T(8,128)}), f32[8,8,256]{2,1,0:T(8,128)S(1)}, u32[]{:S(2)}, u32[]{:S(2)}) async-start(f32[8,8,256]{2,1,0:T(8,128)} %get-tuple-element.36), calls=%async_computation | async-start | bytes 131072 | tf_op jit(solution)/shard_map/all_to_all | solution.py:487
  7.8 4.8 %local_degree.1 = (f32[16,256]{1,0:T(8,128)S(1)}, bf16[16,256,256]{2,1,0:T(8,128)(2,1)S(1)}) custom-call(bf16[1,1,48,256,256]{4,3,2,1,0:T(8,128)(2,1)} %weights.7, f32[1,1,48,2,256]{4,3,2,1,0:T(2,128)} %gains.8, s32[1,1,2,48]{3,2,1,0:T(2,128)} %bitcast.8), custom_call_target="tpu_custom_call" | custom-call | flops 1000000 | bytes 10000000 | tf_op jit(solution)/shard_map/local_degree/pallas_call | solution.py:505
  12.6 0.2 all-to-all-done.arrived
  12.8 3.7 %collective-permute-start.2 = (f32[16,256]{1,0:T(8,128)S(1)}, f32[16,256]{1,0:T(8,128)S(1)}, u32[]{:S(2)}, u32[]{:S(2)}) collective-permute-start(f32[16,256]{1,0:T(8,128)S(1)} %join_degree.1.refs_0_), channel_id=1, source_target_pairs={{0,3},{1,2},{2,1},{3,0},{4,7},{5,6},{6,5},{7,4},{8,11},{9,10},{10,... | collective-permute-start | bytes 49160 | tf_op jit(solution)/shard_map/ppermute | solution.py:484
  16.5 0.8 %collective-permute-start = (f32[16,256]{1,0:T(8,128)S(1)}, f32[16,256]{1,0:T(8,128)S(1)}, u32[]{:S(2)}, u32[]{:S(2)}) collective-permute-start(f32[16,256]{1,0:T(8,128)S(1)} %join_degree.1.refs_0_), channel_id=1, source_target_pairs={{0,1},{1,0},{2,3},{3,2},{4,5},{5,4},{6,7},{7,6},{8,9},{9,8},{10,11... | collective-permute-start | bytes 49160 | tf_op jit(solution)/shard_map/ppermute | solution.py:484
  17.5 1.7 %remote_scale.1.scaled = bf16[8,256,256]{2,1,0:T(8,128)(2,1)S(1)} custom-call(bf16[1,1,8,256,256]{4,3,2,1,0:T(8,128)(2,1)} %raw.1, f32[1,1,8,2,256]{4,3,2,1,0:T(2,128)S(1)} %copy-done.2), custom_call_target="tpu_custom_call" | custom-call | flops 1048576 | bytes 2097152 | tf_op jit(solution)/shard_map/remote_scale/pallas_call | solution.py:189
  19.2 1.9 %collective-permute-done.1.refs_2_ = f32[16,256]{1,0:T(8,128)S(1)} collective-permute-done((f32[16,256]{1,0:T(8,128)S(1)}, f32[16,256]{1,0:T(8,128)S(1)}, u32[]{:S(2)}, u32[]{:S(2)}) %collective-permute-start.1) | collective-permute-done | bytes 16416 | tf_op jit(solution)/shard_map/ppermute | solution.py:484
  21.1 0.4 first_block.1
  21.6 1.3 %collective-permute-done.3.passed = bf16[4,4,16,256]{3,2,1,0:T(8,128)(2,1)S(1)} collective-permute-done((bf16[4,4,16,256]{3,2,1,0:T(8,128)(2,1)S(1)}, bf16[4,4,16,256]{3,2,1,0:T(8,128)(2,1)S(1)}, u32[]{:S(2)}, u32[]{:S(2)}) %collective-permute-start.3) | collective-permute-done | bytes 131104 | tf_op jit(solution)/shard_map/ppermute | solution.py:565
  22.9 2.8 %collective-permute-start.4 = (bf16[2,4,16,256]{3,2,1,0:T(8,128)(2,1)S(1)}, bf16[2,4,16,256]{3,2,1,0:T(8,128)(2,1)S(1)}, u32[]{:S(2)}, u32[]{:S(2)}) collective-permute-start(bf16[2,4,16,256]{3,2,1,0:T(8,128)(2,1)S(1)} %get-tuple-element.47), channel_id=1, source_target_pairs={{0,24},{4,28},{8,16},{12,20},{16,8},{20,12},{24,0},{28,4},{1,25},{... | collective-permute-start | bytes 196616 | tf_op jit(solution)/shard_map/ppermute | solution.py:573
  25.7 0.6 collective-permute-start.5
  26.5 4.1 %local_products.2.partial = f32[16,16,256]{2,1,0:T(8,128)S(1)} custom-call(bf16[16,16,256]{2,1,0:T(8,128)(2,1)S(1)} %get-tuple-element.42.x, bf16[16,256,256]{2,1,0:T(8,128)(2,1)S(1)} %get-tuple-element.43.ready, bf16[1,1,48,256,256]{4,3,2,1,0:T(8,128)(2,1)} %weights.7, f32[1,1,48,2,256]{4,3,2,1,0:T(2,128)S(1)} %copy-done, s32[1,1,2,48]{3,2,1,0:T(2,128)S(1)} %bitcast.9), custom_call_target="tpu_custom_call" | custom-call | flops 201326592 | bytes 6291456 | tf_op jit(solution)/shard_map/local_products/pallas_call | solution.py:546
  30.6 0.5 remote_products.2
  31.3 5.0 %collective-permute-done.7.theirs = bf16[16,16,256]{2,1,0:T(8,128)(2,1)S(1)} collective-permute-done((bf16[16,16,256]{2,1,0:T(8,128)(2,1)S(1)}, bf16[16,16,256]{2,1,0:T(8,128)(2,1)S(1)}, u32[]{:S(2)}, u32[]{:S(2)}) %collective-permute-start.7) | collective-permute-done | bytes 131104 | tf_op jit(solution)/shard_map/ppermute | solution.py:484
  36.3 1.8 %collective-permute-start.8 = (bf16[16,16,256]{2,1,0:T(8,128)(2,1)S(1)}, bf16[16,16,256]{2,1,0:T(8,128)(2,1)S(1)}, u32[]{:S(2)}, u32[]{:S(2)}) collective-permute-start(bf16[16,16,256]{2,1,0:T(8,128)(2,1)S(1)} %get-tuple-element.53), channel_id=1, source_target_pairs={{0,3},{1,2},{2,1},{3,0},{4,7},{5,6},{6,5},{7,4},{8,11},{9,10},{10,... | collective-permute-start | bytes 393224 | tf_op jit(solution)/shard_map/ppermute | solution.py:484
  38.1 5.1 %collective-permute-done.8.theirs = bf16[16,16,256]{2,1,0:T(8,128)(2,1)S(1)} collective-permute-done((bf16[16,16,256]{2,1,0:T(8,128)(2,1)S(1)}, bf16[16,16,256]{2,1,0:T(8,128)(2,1)S(1)}, u32[]{:S(2)}, u32[]{:S(2)}) %collective-permute-start.8) | collective-permute-done | bytes 131104 | tf_op jit(solution)/shard_map/ppermute | solution.py:484
  43.2 0.6 next_block.1
  43.8 1.4 %collective-permute-done.9.passed = bf16[4,5,16,256]{3,2,1,0:T(8,128)(2,1)S(1)} collective-permute-done((bf16[4,5,16,256]{3,2,1,0:T(8,128)(2,1)S(1)}, bf16[4,5,16,256]{3,2,1,0:T(8,128)(2,1)S(1)}, u32[]{:S(2)}, u32[]{:S(2)}) %collective-permute-start.9) | collective-permute-done | bytes 163872 | tf_op jit(solution)/shard_map/ppermute | solution.py:565
  45.2 2.8 %collective-permute-start.10 = (bf16[2,5,16,256]{3,2,1,0:T(8,128)(2,1)S(1)}, bf16[2,5,16,256]{3,2,1,0:T(8,128)(2,1)S(1)}, u32[]{:S(2)}, u32[]{:S(2)}) collective-permute-start(bf16[2,5,16,256]{3,2,1,0:T(8,128)(2,1)S(1)} %get-tuple-element.57), channel_id=1, source_target_pairs={{0,24},{4,28},{8,16},{12,20},{16,8},{20,12},{24,0},{28,4},{1,25},{... | collective-permute-start | bytes 245768 | tf_op jit(solution)/shard_map/ppermute | solution.py:573
  48.0 0.5 collective-permute-start.11
  48.5 0.3 collective-permute-start.12
  48.8 4.1 %local_products.3.partial = f32[16,16,256]{2,1,0:T(8,128)S(1)} custom-call(bf16[16,16,256]{2,1,0:T(8,128)(2,1)S(1)} %get-tuple-element.60.x, bf16[16,256,256]{2,1,0:T(8,128)(2,1)S(1)} %get-tuple-element.43.ready, bf16[1,1,48,256,256]{4,3,2,1,0:T(8,128)(2,1)} %weights.7, f32[1,1,48,2,256]{4,3,2,1,0:T(2,128)S(1)} %copy-done, s32[1,1,2,48]{3,2,1,0:T(2,128)S(1)} %bitcast.10), custom_call_target="tpu_custom_call" | custom-call | flops 201326592 | bytes 6291456 | tf_op jit(solution)/shard_map/local_products/pallas_call | solution.py:546
  53.0 0.5 remote_products.3
  53.5 1.9 %collective-permute-start.13 = (bf16[4,16,256]{2,1,0:T(8,128)(2,1)S(1)}, bf16[4,16,256]{2,1,0:T(8,128)(2,1)S(1)}, u32[]{:S(2)}, u32[]{:S(2)}) collective-permute-start(bf16[4,16,256]{2,1,0:T(8,128)(2,1)S(1)} %get-tuple-element.62), channel_id=1, source_target_pairs={{0,3},{1,2},{2,1},{3,0},{4,7},{5,6},{6,5},{7,4},{8,11},{9,10},{10,... | collective-permute-start | bytes 98312 | tf_op jit(solution)/shard_map/ppermute | solution.py:484
  55.4 0.2 collective-permute-start.14
  55.7 2.3 %collective-permute-start.15 = (bf16[4,16,256]{2,1,0:T(8,128)(2,1)S(1)}, bf16[4,16,256]{2,1,0:T(8,128)(2,1)S(1)}, u32[]{:S(2)}, u32[]{:S(2)}) collective-permute-start(bf16[4,16,256]{2,1,0:T(8,128)(2,1)S(1)} %get-tuple-element.64), channel_id=1, source_target_pairs={{0,1},{1,0},{2,3},{3,2},{4,5},{5,4},{6,7},{7,6},{8,9},{9,8},{10,11... | collective-permute-start | bytes 98312 | tf_op jit(solution)/shard_map/ppermute | solution.py:484
  58.0 1.3 %middle_factor.1.inverse = f32[16,16]{1,0:T(8,128)S(1)} custom-call(bf16[2,5,16,256]{3,2,1,0:T(8,128)(2,1)S(1)} %get-tuple-element.56.refs_0_, bf16[2,5,16,256]{3,2,1,0:T(8,128)(2,1)S(1)} %collective-permute-done.10.refs_1_, bf16[2,5,16,256]{3,2,1,0:T(8,128)(2,1)S(1)} %collective-permute-done.11.refs_2_, ...), custom_call_target="tpu_custom_call" | custom-call | flops 1000000 | bytes 1000000 | tf_op jit(solution)/shard_map/middle_factor/pallas_call | solution.py:618
  59.4 1.1 %collective-permute-done.14.refs_2_ = bf16[4,16,256]{2,1,0:T(8,128)(2,1)S(1)} collective-permute-done((bf16[4,16,256]{2,1,0:T(8,128)(2,1)S(1)}, bf16[4,16,256]{2,1,0:T(8,128)(2,1)S(1)}, u32[]{:S(2)}, u32[]{:S(2)}) %collective-permute-start.14) | collective-permute-done | bytes 32800 | tf_op jit(solution)/shard_map/ppermute | solution.py:484
  60.4 0.7 last_quarter.1
  61.1 11.5 %all_to_all.10.grams = f32[32,2,128]{2,1,0:T(2,128)S(1)} all-to-all(f32[32,2,128]{2,1,0:T(2,128)S(1)} %get-tuple-element.65), channel_id=1, replica_groups=mesh['rows'=8,'cols'=4] {'rows','cols'}, dimensions={0} | all-to-all | bytes 65536 | tf_op jit(solution)/shard_map/all_to_all | solution.py:630
  72.6 1.9 %finish.1 = f32[16,1024]{1,0:T(8,128)} custom-call(f32[32,2,128]{2,1,0:T(2,128)S(1)} %all_to_all.10.grams, f32[16,1024]{1,0:T(8,128)S(1)} %get-tuple-element.66.image), custom_call_target="tpu_custom_call" | custom-call | flops 1000000 | bytes 1000000 | tf_op jit(solution)/shard_map/finish/pallas_call | solution.py:633
  (34 shorter events, 0.9 us)
Async XLA Ops:
  0.0 21.1 %copy-start.4 = (s32[1,1,8]{2,1,0:T(1,128)S(1)}, s32[1,1,8]{2,1,0:T(1,128)}, u32[]{:S(2)}) copy-start(s32[1,1,8]{2,1,0:T(1,128)} %groups.9) | copy-start | bytes 100
  0.0 17.5 %copy-start.2 = (f32[1,1,8,2,256]{4,3,2,1,0:T(2,128)S(1)}, f32[1,1,8,2,256]{4,3,2,1,0:T(2,128)}, u32[]{:S(2)}) copy-start(f32[1,1,8,2,256]{4,3,2,1,0:T(2,128)} %gains.6) | copy-start | bytes 49156
  0.0 21.1 %copy-start.3 = (s32[1,1,8,2]{2,3,1,0:T(2,128)S(1)}, s32[1,1,8,2]{2,3,1,0:T(2,128)}, u32[]{:S(2)}) copy-start(s32[1,1,8,2]{2,3,1,0:T(2,128)} %param.14) | copy-start | bytes 196
  0.0 26.5 %copy-start = (f32[1,1,48,2,256]{4,3,2,1,0:T(2,128)S(1)}, f32[1,1,48,2,256]{4,3,2,1,0:T(2,128)}, u32[]{:S(2)}) copy-start(f32[1,1,48,2,256]{4,3,2,1,0:T(2,128)} %gains.8) | copy-start | bytes 294916
  0.0 26.5 %copy-start.5 = (s32[1,1,48,2]{2,3,1,0:T(2,128)S(1)}, s32[1,1,48,2]{2,3,1,0:T(2,128)}, u32[]{:S(2)}) copy-start(s32[1,1,48,2]{2,3,1,0:T(2,128)} %param.10) | copy-start | bytes 1156
  0.0 21.1 %copy-start.1 = (f32[16,4096]{1,0:T(8,128)S(1)}, f32[16,4096]{1,0:T(8,128)}, u32[]{:S(2)}) copy-start(f32[16,4096]{1,0:T(8,128)} %start.1) | copy-start | bytes 786436
  2.5 10.2 %all-to-all-start = ((f32[8,8,256]{2,1,0:T(8,128)}), f32[8,8,256]{2,1,0:T(8,128)S(1)}, u32[]{:S(2)}, u32[]{:S(2)}) async-start(f32[8,8,256]{2,1,0:T(8,128)} %get-tuple-element.36), calls=%async_computation | async-start | bytes 131072 | tf_op jit(solution)/shard_map/all_to_all | solution.py:487
  12.8 6.4 %collective-permute-start.2 = (f32[16,256]{1,0:T(8,128)S(1)}, f32[16,256]{1,0:T(8,128)S(1)}, u32[]{:S(2)}, u32[]{:S(2)}) collective-permute-start(f32[16,256]{1,0:T(8,128)S(1)} %join_degree.1.refs_0_), channel_id=1, source_target_pairs={{0,3},{1,2},{2,1},{3,0},{4,7},{5,6},{6,5},{7,4},{8,11},{9,10},{10,... | collective-permute-start | bytes 49160 | tf_op jit(solution)/shard_map/ppermute | solution.py:484
  16.5 4.6 %collective-permute-start.1 = (f32[16,256]{1,0:T(8,128)S(1)}, f32[16,256]{1,0:T(8,128)S(1)}, u32[]{:S(2)}, u32[]{:S(2)}) collective-permute-start(f32[16,256]{1,0:T(8,128)S(1)} %join_degree.1.refs_0_), channel_id=1, source_target_pairs={{0,2},{1,3},{2,0},{3,1},{4,6},{5,7},{6,4},{7,5},{8,10},{9,11},{10,... | collective-permute-start | bytes 49160 | tf_op jit(solution)/shard_map/ppermute | solution.py:484
  16.5 4.6 %collective-permute-start = (f32[16,256]{1,0:T(8,128)S(1)}, f32[16,256]{1,0:T(8,128)S(1)}, u32[]{:S(2)}, u32[]{:S(2)}) collective-permute-start(f32[16,256]{1,0:T(8,128)S(1)} %join_degree.1.refs_0_), channel_id=1, source_target_pairs={{0,1},{1,0},{2,3},{3,2},{4,5},{5,4},{6,7},{7,6},{8,9},{9,8},{10,11... | collective-permute-start | bytes 49160 | tf_op jit(solution)/shard_map/ppermute | solution.py:484
  21.5 1.4 %collective-permute-start.3 = (bf16[4,4,16,256]{3,2,1,0:T(8,128)(2,1)S(1)}, bf16[4,4,16,256]{3,2,1,0:T(8,128)(2,1)S(1)}, u32[]{:S(2)}, u32[]{:S(2)}) collective-permute-start(bf16[4,4,16,256]{3,2,1,0:T(8,128)(2,1)S(1)} %get-tuple-element.45), channel_id=1, source_target_pairs={{0,4},{4,0},{8,12},{12,8},{16,20},{20,16},{24,28},{28,24},{1,5},{5... | collective-permute-start | bytes 393224 | tf_op jit(solution)/shard_map/ppermute | solution.py:565
  22.9 7.7 %collective-permute-start.4 = (bf16[2,4,16,256]{3,2,1,0:T(8,128)(2,1)S(1)}, bf16[2,4,16,256]{3,2,1,0:T(8,128)(2,1)S(1)}, u32[]{:S(2)}, u32[]{:S(2)}) collective-permute-start(bf16[2,4,16,256]{3,2,1,0:T(8,128)(2,1)S(1)} %get-tuple-element.47), channel_id=1, source_target_pairs={{0,24},{4,28},{8,16},{12,20},{16,8},{20,12},{24,0},{28,4},{1,25},{... | collective-permute-start | bytes 196616 | tf_op jit(solution)/shard_map/ppermute | solution.py:573
  25.7 4.9 %collective-permute-start.5 = (bf16[2,4,16,256]{3,2,1,0:T(8,128)(2,1)S(1)}, bf16[2,4,16,256]{3,2,1,0:T(8,128)(2,1)S(1)}, u32[]{:S(2)}, u32[]{:S(2)}) collective-permute-start(bf16[2,4,16,256]{3,2,1,0:T(8,128)(2,1)S(1)} %get-tuple-element.48), channel_id=1, source_target_pairs={{0,16},{4,20},{8,24},{12,28},{16,0},{20,4},{24,8},{28,12},{1,17},{... | collective-permute-start | bytes 196616 | tf_op jit(solution)/shard_map/ppermute | solution.py:573
  26.3 4.3 %collective-permute-start.6 = (bf16[2,4,16,256]{3,2,1,0:T(8,128)(2,1)S(1)}, bf16[2,4,16,256]{3,2,1,0:T(8,128)(2,1)S(1)}, u32[]{:S(2)}, u32[]{:S(2)}) collective-permute-start(bf16[2,4,16,256]{3,2,1,0:T(8,128)(2,1)S(1)} %get-tuple-element.49), channel_id=1, source_target_pairs={{0,8},{4,12},{8,0},{12,4},{16,24},{20,28},{24,16},{28,20},{1,9},{5... | collective-permute-start | bytes 196616 | tf_op jit(solution)/shard_map/ppermute | solution.py:573
  31.2 5.0 %collective-permute-start.7 = (bf16[16,16,256]{2,1,0:T(8,128)(2,1)S(1)}, bf16[16,16,256]{2,1,0:T(8,128)(2,1)S(1)}, u32[]{:S(2)}, u32[]{:S(2)}) collective-permute-start(bf16[16,16,256]{2,1,0:T(8,128)(2,1)S(1)} %get-tuple-element.51), channel_id=1, source_target_pairs={{0,1},{1,0},{2,3},{3,2},{4,5},{5,4},{6,7},{7,6},{8,9},{9,8},{10,11... | collective-permute-start | bytes 393224 | tf_op jit(solution)/shard_map/ppermute | solution.py:484
  36.3 6.9 %collective-permute-start.8 = (bf16[16,16,256]{2,1,0:T(8,128)(2,1)S(1)}, bf16[16,16,256]{2,1,0:T(8,128)(2,1)S(1)}, u32[]{:S(2)}, u32[]{:S(2)}) collective-permute-start(bf16[16,16,256]{2,1,0:T(8,128)(2,1)S(1)} %get-tuple-element.53), channel_id=1, source_target_pairs={{0,3},{1,2},{2,1},{3,0},{4,7},{5,6},{6,5},{7,4},{8,11},{9,10},{10,... | collective-permute-start | bytes 393224 | tf_op jit(solution)/shard_map/ppermute | solution.py:484
  43.8 1.5 %collective-permute-start.9 = (bf16[4,5,16,256]{3,2,1,0:T(8,128)(2,1)S(1)}, bf16[4,5,16,256]{3,2,1,0:T(8,128)(2,1)S(1)}, u32[]{:S(2)}, u32[]{:S(2)}) collective-permute-start(bf16[4,5,16,256]{3,2,1,0:T(8,128)(2,1)S(1)} %get-tuple-element.55), channel_id=1, source_target_pairs={{0,4},{4,0},{8,12},{12,8},{16,20},{20,16},{24,28},{28,24},{1,5},{5... | collective-permute-start | bytes 491528 | tf_op jit(solution)/shard_map/ppermute | solution.py:565
  45.2 7.7 %collective-permute-start.10 = (bf16[2,5,16,256]{3,2,1,0:T(8,128)(2,1)S(1)}, bf16[2,5,16,256]{3,2,1,0:T(8,128)(2,1)S(1)}, u32[]{:S(2)}, u32[]{:S(2)}) collective-permute-start(bf16[2,5,16,256]{3,2,1,0:T(8,128)(2,1)S(1)} %get-tuple-element.57), channel_id=1, source_target_pairs={{0,24},{4,28},{8,16},{12,20},{16,8},{20,12},{24,0},{28,4},{1,25},{... | collective-permute-start | bytes 245768 | tf_op jit(solution)/shard_map/ppermute | solution.py:573
  48.0 4.9 %collective-permute-start.11 = (bf16[2,5,16,256]{3,2,1,0:T(8,128)(2,1)S(1)}, bf16[2,5,16,256]{3,2,1,0:T(8,128)(2,1)S(1)}, u32[]{:S(2)}, u32[]{:S(2)}) collective-permute-start(bf16[2,5,16,256]{3,2,1,0:T(8,128)(2,1)S(1)} %get-tuple-element.58), channel_id=1, source_target_pairs={{0,16},{4,20},{8,24},{12,28},{16,0},{20,4},{24,8},{28,12},{1,17},{... | collective-permute-start | bytes 245768 | tf_op jit(solution)/shard_map/ppermute | solution.py:573
  48.5 4.4 %collective-permute-start.12 = (bf16[2,5,16,256]{3,2,1,0:T(8,128)(2,1)S(1)}, bf16[2,5,16,256]{3,2,1,0:T(8,128)(2,1)S(1)}, u32[]{:S(2)}, u32[]{:S(2)}) collective-permute-start(bf16[2,5,16,256]{3,2,1,0:T(8,128)(2,1)S(1)} %get-tuple-element.59), channel_id=1, source_target_pairs={{0,8},{4,12},{8,0},{12,4},{16,24},{20,28},{24,16},{28,20},{1,9},{5... | collective-permute-start | bytes 245768 | tf_op jit(solution)/shard_map/ppermute | solution.py:573
  53.5 5.9 %collective-permute-start.13 = (bf16[4,16,256]{2,1,0:T(8,128)(2,1)S(1)}, bf16[4,16,256]{2,1,0:T(8,128)(2,1)S(1)}, u32[]{:S(2)}, u32[]{:S(2)}) collective-permute-start(bf16[4,16,256]{2,1,0:T(8,128)(2,1)S(1)} %get-tuple-element.62), channel_id=1, source_target_pairs={{0,3},{1,2},{2,1},{3,0},{4,7},{5,6},{6,5},{7,4},{8,11},{9,10},{10,... | collective-permute-start | bytes 98312 | tf_op jit(solution)/shard_map/ppermute | solution.py:484
  55.4 5.0 %collective-permute-start.14 = (bf16[4,16,256]{2,1,0:T(8,128)(2,1)S(1)}, bf16[4,16,256]{2,1,0:T(8,128)(2,1)S(1)}, u32[]{:S(2)}, u32[]{:S(2)}) collective-permute-start(bf16[4,16,256]{2,1,0:T(8,128)(2,1)S(1)} %get-tuple-element.63), channel_id=1, source_target_pairs={{0,2},{1,3},{2,0},{3,1},{4,6},{5,7},{6,4},{7,5},{8,10},{9,11},{10,... | collective-permute-start | bytes 98312 | tf_op jit(solution)/shard_map/ppermute | solution.py:484
  55.7 4.8 %collective-permute-start.15 = (bf16[4,16,256]{2,1,0:T(8,128)(2,1)S(1)}, bf16[4,16,256]{2,1,0:T(8,128)(2,1)S(1)}, u32[]{:S(2)}, u32[]{:S(2)}) collective-permute-start(bf16[4,16,256]{2,1,0:T(8,128)(2,1)S(1)} %get-tuple-element.64), channel_id=1, source_target_pairs={{0,1},{1,0},{2,3},{3,2},{4,5},{5,4},{6,7},{7,6},{8,9},{9,8},{10,11... | collective-permute-start | bytes 98312 | tf_op jit(solution)/shard_map/ppermute | solution.py:484

commit v7 on v6

--- a/solution.py
+++ b/solution.py
@@ -12,12 +12,12 @@
 BR = 16
 MOST = 2
 CHUNK = 8
-HELD = 16
+HEAD = 16
 LANES = 128
 F32 = jnp.float32
 BF16 = jnp.bfloat16
 HIGHEST = lax.Precision.HIGHEST
-VMEM_LIMIT = 48 * 1024 * 1024
+VMEM_LIMIT = 16 * 1024 * 1024
 
 vmem = pl.BlockSpec(memory_space=pltpu.VMEM)
 hbm = pl.BlockSpec(memory_space=pltpu.HBM)
@@ -88,37 +88,33 @@
     return (rows[1:2] + rows[9:10]) * gains[0:1, :], (cols[0:1] + cols[8:9]) * gains[1:2, :]
 
 
-def remote_degree_kernel(
-    group_count,
-    weights,
-    gains,
-    groups,
-    coords,
-    payload,
-    row_degree,
-    tiles,
-    tile_gains,
-    tile_groups,
-    tile_coords,
-    count,
-    sems,
-):
+def remote_degree_kernel(weights, gains, groups, coords, near_weights, row_degree, tiles, held, *refs):
+    *outs, tile_gains, tile_groups, tile_coords, staged, count, sems = refs
+    group_count = staged.shape[0]
     wait = fetch(
-        (groups, coords, gains, weights), (tile_groups, tile_coords, tile_gains, tiles), sems
+        (groups, coords, gains, weights.at[0, 0]),
+        (tile_groups, tile_coords, tile_gains, tiles),
+        sems.at[pl.ds(0, 4)],
+    )
+    wait_held = fetch(
+        (near_weights.at[0, 0, pl.ds(0, held.shape[0])],), (held,), sems.at[pl.ds(4, 1)]
     )
     sub = lax.broadcasted_iota(jnp.int32, (8, TILE), 0)
     blank = jnp.where((sub >= MOST) & (sub < 2 * MOST), -1.0, 0.0).astype(F32)
     for g in range(group_count):
-        payload[g] = blank
+        staged[g] = blank
     row_degree[...] = jnp.zeros(row_degree.shape, F32)
+    core = lax.axis_index("rows") % 2
     wait()
-    places = slots_of(tile_groups, count, weights.shape[2], group_count)
-    for t, g, m in places:
+    for t, g, m in slots_of(tile_groups, count, tiles.shape[0], group_count):
+        place = place_of(g, group_count, core)
         r, c = tile_coords[0, 0, 0, t], tile_coords[0, 0, 1, t]
-        by_row, by_col = weighted_sums(jnp.abs(tiles[0, 0, t]), tile_gains[0, 0, t])
+        by_row, by_col = weighted_sums(jnp.abs(tiles[t]), tile_gains[0, 0, t])
         row_degree[pl.ds(r, 1), :] += by_row
-        payload[g, pl.ds(m, 1), :] = by_col
-        payload[g, pl.ds(MOST + m, 1), :] = jnp.full((1, TILE), c, jnp.int32).astype(F32)
+        staged[place, pl.ds(m, 1), :] = by_col
+        staged[place, pl.ds(MOST + m, 1), :] = jnp.full((1, TILE), c, jnp.int32).astype(F32)
+    split_out(staged, outs)
+    wait_held()
 
 
 def halves_of(value):
@@ -134,80 +130,77 @@
 
 
 def local_degree_kernel(
-    weights, gains, coords, degree, ready, tiles, tile_gains, places, by_row, by_col, sems, small_sems
+    held, weights, gains, coords, degree, tiles, by_row, by_col, sems
 ):
-    count, held = weights.shape[2], ready.shape[0]
-
-    def copy_of(n, base, target):
-        source = weights.at[0, 0, pl.ds(base + n * CHUNK, CHUNK)]
-        return pltpu.make_async_copy(
-            source, target.at[pl.ds(n * CHUNK, CHUNK)], sems.at[base // CHUNK + n]
-        )
-
-    wait = fetch((gains, coords), (tile_gains, places), small_sems)
-    parts = ((0, ready), (held, tiles))
-    for base, target in parts:
-        for n in range(target.shape[0] // CHUNK):
-            copy_of(n, base, target).start()
+    first, count = held.shape[0], weights.shape[2]
+
+    def copy_of(n):
+        source = weights.at[0, 0, pl.ds(first + n * CHUNK, CHUNK)]
+        return pltpu.make_async_copy(source, tiles.at[pl.ds(n * CHUNK, CHUNK)], sems.at[n])
+
+    for n in range((count - first) // CHUNK):
+        copy_of(n).start()
     by_row[...] = jnp.zeros(by_row.shape, F32)
-    first = lax.broadcasted_iota(jnp.int32, (8, TILE), 0) == 0
+    top = lax.broadcasted_iota(jnp.int32, (8, TILE), 0) == 0
     lane = lax.broadcasted_iota(jnp.int32, by_row.shape, 1)
-    wait()
-
-    def step(base, target, n, _):
-        copy_of(n, base, target).wait()
+
+    def add(t, size):
+        pair = jnp.abs(gains[0, 0, t])
+        left = jnp.where(top, pair[0:1, :], 0.0)
+        high = left.astype(BF16).astype(F32)
+        sums = times(jnp.concatenate([high, left - high], axis=0).astype(BF16), size)
+        by_col[pl.ds(t, 1), :] = (sums[0:1] + sums[8:9]) * pair[1:2, :]
+        sums = jnp.sum(size.astype(F32) * pair[1:2, :], axis=1, keepdims=True)
+        by_row[...] = jnp.where(lane == t, sums, by_row[...])
+
+    def held_step(n, _):
         for k in range(CHUNK):
-            t = base + n * CHUNK + k
-            size = jnp.abs(target[n * CHUNK + k])
-            pair = jnp.abs(tile_gains[0, 0, t])
-            left = jnp.where(first, pair[0:1, :], 0.0)
-            high = left.astype(BF16).astype(F32)
-            sums = times(jnp.concatenate([high, left - high], axis=0).astype(BF16), size)
-            by_col[pl.ds(t, 1), :] = (sums[0:1] + sums[8:9]) * pair[1:2, :]
-            sums = jnp.sum(size.astype(F32) * pair[1:2, :], axis=1, keepdims=True)
-            by_row[...] = jnp.where(lane == t, sums, by_row[...])
+            add(n * CHUNK + k, jnp.abs(held[n * CHUNK + k]))
         return 0
 
-    for base, target in parts:
-        lax.fori_loop(0, target.shape[0] // CHUNK, functools.partial(step, base, target), 0)
-    row_sums = jnp.transpose(by_row[...])[:count] * jnp.abs(tile_gains[0, 0, :, 0, :])
-    degree[...] = add_by_place(places[0, 0, 0:1, :], row_sums) + add_by_place(
-        places[0, 0, 1:2, :], by_col[...]
+    def step(n, _):
+        copy_of(n).wait()
+        for k in range(CHUNK):
+            add(first + n * CHUNK + k, jnp.abs(tiles[n * CHUNK + k]))
+        return 0
+
+    lax.fori_loop(0, first // CHUNK, held_step, 0)
+    lax.fori_loop(0, (count - first) // CHUNK, step, 0)
+    row_sums = jnp.transpose(by_row[...])[:count] * jnp.abs(gains[0, 0, :, 0, :])
+    degree[...] = add_by_place(coords[0, 0, 0:1, :], row_sums) + add_by_place(
+        coords[0, 0, 1:2, :], by_col[...]
     )
 
 
 def scale_kernel(raw, gains, scaled):
-    row_gain = jnp.transpose(gains[0, 0, :, 0, :])
-    for k in range(raw.shape[2]):
-        scaled[k] = (
-            row_gain[:, k : k + 1] * raw[0, 0, k].astype(F32) * gains[0, 0, k, 1:2, :]
-        ).astype(BF16)
-
-
-def scale(weights, gains, name):
-    count = weights.shape[2]
-    return pl.pallas_call(
-        scale_kernel,
-        out_shape=shape((count, TILE, TILE), BF16),
-        grid=(count // CHUNK,),
-        in_specs=[
-            pl.BlockSpec((1, 1, CHUNK, TILE, TILE), lambda n: (0, 0, n, 0, 0)),
-            pl.BlockSpec((1, 1, CHUNK, 2, TILE), lambda n: (0, 0, n, 0, 0)),
-        ],
-        out_specs=pl.BlockSpec((CHUNK, TILE, TILE), lambda n: (n, 0, 0)),
-        cost_estimate=pl.CostEstimate(
-            flops=2 * count * TILE * TILE, bytes_accessed=4 * count * TILE * TILE, transcendentals=0
-        ),
-        compiler_params=pltpu.CompilerParams(vmem_limit_bytes=VMEM_LIMIT),
-        name=name,
-    )(in_hbm(weights), gains)
-
-
-def join_degree_kernel(arrived, row_degree, local_degree, joined):
+    def step(n, _):
+        base = n * CHUNK
+        row_gain = jnp.transpose(gains[0, 0, pl.ds(base, CHUNK), 0, :])
+        for k in range(CHUNK):
+            scaled[base + k] = (
+                row_gain[:, k : k + 1]
+                * raw[base + k].astype(F32)
+                * gains[0, 0, base + k, 1:2, :]
+            ).astype(BF16)
+        return 0
+
+    lax.fori_loop(0, scaled.shape[0] // CHUNK, step, 0)
+
+
+def scale(raw, gains, name):
+    return call(
+        scale_kernel, shape(raw.shape, BF16), [vmem, vmem], flops=2 * raw.size, name=name
+    )(raw, gains)
+
+
+def join_degree_kernel(row_degree, local_degree, *refs):
+    *arrived, joined, targets, sums = refs
+    by_group(arrived, sums)
+    targets[...] = sums[...].astype(jnp.int32)
     total = row_degree[...] + local_degree[...]
     sub = lax.broadcasted_iota(jnp.int32, total.shape, 0).astype(F32)
-    for g in range(arrived.shape[0]):
-        block = arrived[g]
+    for g in range(sums.shape[0]):
+        block = sums[g]
         for m in range(MOST):
             hit = sub == block[MOST + m : MOST + m + 1, :]
             total += jnp.where(hit, block[m : m + 1, :], 0.0)
@@ -241,7 +234,7 @@
     for g in range(group_count):
         place = place_of(g, group_count, core)
         for m in range(MOST):
-            staged[place, m] = x[jnp.maximum(targets[g, m], 0)]
+            staged[place, m] = x[jnp.maximum(targets[g, MOST + m, 0], 0)]
 
 
 def split_out(staged, outs):
@@ -250,8 +243,9 @@
         out[...] = staged[k * size : (k + 1) * size]
 
 
-def forward_kernel(near, passed, *pieces):
+def forward_kernel(near, passed, *refs):
     chips = near.shape[0]
+    pieces = refs[-chips:]
     me = lax.axis_index("rows")
     chip, core = me // 2, me % 2
     for k, piece in zip(offsets(chips), pieces):
@@ -268,7 +262,7 @@
         joined[pl.ds((chip ^ k) * 2, 2)] = piece[...]
 
 
-def first_block_kernel(splits, start, scaled, groups, coords, targets, *refs):
+def first_block_kernel(splits, start, scaled, groups, coords, targets, later, *refs):
     parts, (inv_root, x, *refs) = refs[:splits], refs[splits:]
     *outs, count, staged = refs
     routes = (groups, coords, targets)
@@ -315,45 +309,35 @@
     split_out(staged, outs)
 
 
-def local_products_kernel(
-    x, ready, weights, gains, coords, partial, tiles, sems, tile_coords, coord_sems
-):
-    held, count, chunk = ready.shape[0], tiles.shape[0], CHUNK
-    batch = 2 * chunk if count % (2 * chunk) == 0 else chunk
-
-    def copy_of(n):
-        source = weights.at[0, 0, pl.ds(held + n * chunk, chunk)]
-        return pltpu.make_async_copy(source, tiles.at[pl.ds(n * chunk, chunk)], sems.at[n])
-
-    wait = fetch((coords,), (tile_coords,), coord_sems)
-    for n in range(count // chunk):
-        copy_of(n).start()
-    partial[...] = jnp.zeros(partial.shape, F32)
+def local_products_kernel(first, x, tiles, coords, *refs):
+    *refs, partial, tile_coords, sems = refs
+    gains, earlier = refs or (None, None)
+    count = tiles.shape[0]
+    batch = 2 * CHUNK if count % (2 * CHUNK) == 0 else CHUNK
+    wait = fetch((coords,), (tile_coords,), sems)
+    partial[...] = earlier[...] if refs else jnp.zeros(partial.shape, F32)
     wait()
 
-    def add(base, raw):
-        row_gains = [
-            jnp.transpose(gains[0, 0, pl.ds(base + k, CHUNK), 0, :])
-            for k in range(0, len(raw), CHUNK)
-        ]
+    def step(n, _):
+        base = first + n * batch
+        if refs:
+            row_gains = [
+                jnp.transpose(gains[0, 0, pl.ds(base + k, CHUNK), 0, :])
+                for k in range(0, batch, CHUNK)
+            ]
         places, results = [], []
-        for k, tile in enumerate(raw):
+        for k in range(batch):
             t = base + k
             r, c = tile_coords[0, 0, 0, t], tile_coords[0, 0, 1, t]
-            row_gain = row_gains[k // CHUNK][:, k % CHUNK : k % CHUNK + 1]
-            tile = (row_gain * tile().astype(F32) * gains[0, 0, t, 1:2, :]).astype(BF16)
+            tile = tiles[n * batch + k]
+            if refs:
+                row_gain = row_gains[k // CHUNK][:, k % CHUNK : k % CHUNK + 1]
+                tile = (row_gain * tile.astype(F32) * gains[0, 0, t, 1:2, :]).astype(BF16)
             results.append((times_t(x[c], tile), times(x[r], tile)))
             places.append((r, c))
         for (r, c), (forward, backward) in zip(places, results):
             partial[r] += forward
             partial[c] += backward
-
-    add(0, [lambda k=k: ready[k] for k in range(held)])
-
-    def step(n, _):
-        for k in range(batch // chunk):
-            copy_of(n * (batch // chunk) + k).wait()
-        add(held + n * batch, [lambda k=k: tiles[n * batch + k] for k in range(batch)])
         return 0
 
     lax.fori_loop(0, count // batch, step, 0)
@@ -369,7 +353,7 @@
         total[coords[0, 0, 0, t]] += times_t(joined[g, m], scaled[t])
     for g in range(group_count):
         for m in range(MOST):
-            total[jnp.maximum(targets[g, m], 0)] += joined[g, MOST + m].astype(F32)
+            total[jnp.maximum(targets[g, MOST + m, 0], 0)] += joined[g, MOST + m].astype(F32)
     if whole:
         for out in outs:
             out[...] = total[...].astype(out.dtype)
@@ -486,102 +470,110 @@
     def trade(value):
         return lax.all_to_all(value, "rows", split_axis=0, concat_axis=0, tiled=True)
 
-    listing = (remote_weights, remote_gains, remote_groups, remote_coords)
-    sums, row_degree = call(
-        functools.partial(remote_degree_kernel, groups),
-        (shape((groups, 8, TILE)), shape((BR, TILE))),
-        [hbm, hbm, hbm, hbm],
+    def sent_blocks(block, dtype):
+        if by_chips(groups):
+            return (shape((groups // 2,) + block, dtype),) * 2
+        return (shape((groups,) + block, dtype),)
+
+    def exchange(sent, before=()):
+        if not by_chips(groups):
+            return [trade(sent[0])]
+        near, far = sent
+        passed = lax.ppermute(far, "rows", [(j, j ^ 1) for j in range(groups)])
+        own, *others = call(
+            forward_kernel,
+            (shape((2,) + near.shape[1:], near.dtype),) * (groups // 2),
+            [vmem, vmem] + [anywhere] * len(before),
+            name="forward",
+        )(near, passed, *before)
+        return [own] + [
+            lax.ppermute(piece, "rows", [(j, j ^ (2 * k)) for j in range(groups)])
+            for k, piece in zip(offsets(groups // 2)[1:], others)
+        ]
+
+    listing = (remote_weights, remote_gains, remote_groups, remote_coords, local_weights)
+    row_degree, remote_raw, held, *sent = call(
+        remote_degree_kernel,
+        (
+            shape((BR, TILE)),
+            shape((remote_tiles, TILE, TILE), BF16),
+            shape((HEAD, TILE, TILE), BF16),
+        )
+        + sent_blocks((8, TILE), F32),
+        [hbm] * len(listing),
         [
-            pltpu.VMEM(remote_weights.shape, BF16),
             pltpu.VMEM(remote_gains.shape, F32),
             pltpu.SMEM(remote_groups.shape, jnp.int32),
             pltpu.SMEM(remote_coords.shape, jnp.int32),
+            pltpu.VMEM((groups, 8, TILE), F32),
             count,
-            pltpu.SemaphoreType.DMA((4,)),
+            pltpu.SemaphoreType.DMA((5,)),
         ],
         name="remote_degree",
     )(*[in_hbm(value) for value in listing])
-    sums_in = trade(sums)
-    local_degree, ready = call(
+    sums_in = exchange(sent)
+    local_degree, local_raw = call(
         local_degree_kernel,
-        (shape((BR, TILE)), shape((HELD, TILE, TILE), BF16)),
-        [hbm, hbm, hbm],
+        (shape((BR, TILE)), shape((local_tiles - HEAD, TILE, TILE), BF16)),
+        [vmem, hbm, vmem, vmem],
         [
-            pltpu.VMEM((local_tiles - HELD, TILE, TILE), BF16),
-            pltpu.VMEM(local_gains.shape, F32),
-            pltpu.VMEM(local_coords.shape, jnp.int32),
             pltpu.VMEM((TILE, -(-local_tiles // LANES) * LANES), F32),
             pltpu.VMEM((local_tiles, TILE), F32),
-            pltpu.SemaphoreType.DMA((local_tiles // CHUNK,)),
-            pltpu.SemaphoreType.DMA((2,)),
+            pltpu.SemaphoreType.DMA(((local_tiles - HEAD) // CHUNK,)),
         ],
         moved=10**7,
         name="local_degree",
-    )(*[in_hbm(value) for value in (local_weights, local_gains, local_coords)])
-    targets = sums_in[:, MOST : 2 * MOST, 0].astype(jnp.int32)
+    )(held, in_hbm(local_weights), local_gains, local_coords)
+    joined, targets = call(
+        join_degree_kernel,
+        (shape((BR, TILE)), shape((groups, 8, TILE), jnp.int32)),
+        [vmem] * (2 + len(sums_in)),
+        [pltpu.VMEM((groups, 8, TILE), F32)],
+        name="join_degree",
+    )(row_degree, local_degree, *sums_in)
     far_scalars = [remote_groups, remote_coords, targets]
-    joined = call(
-        join_degree_kernel, shape((BR, TILE)), [vmem, vmem, vmem], name="join_degree"
-    )(sums_in, row_degree, local_degree)
-    joined, remote_gains = lax.optimization_barrier((joined, remote_gains))
+    joined, remote_gains, local_gains = lax.optimization_barrier(
+        (joined, remote_gains, local_gains)
+    )
     degrees = [joined] + [swap(joined, k) for k in range(1, splits)]
-    remote_scaled = scale(remote_weights, remote_gains, "remote_scale")
-    def sent_blocks(blocks):
-        if by_chips(groups):
-            return (shape((groups // 2, blocks, WIDTH, TILE), BF16),) * 2
-        return (shape((groups, blocks, WIDTH, TILE), BF16),)
+    remote_scaled = scale(remote_raw, remote_gains, "remote_scale")
+    local_scaled = scale(held, local_gains, "local_scale")
 
     def staging(blocks):
         return pltpu.VMEM((groups, blocks, WIDTH, TILE), BF16)
 
     inv_root, x, *sent = call(
         functools.partial(first_block_kernel, splits),
-        (shape((BR, TILE)), shape((BR, WIDTH, TILE), BF16)) + sent_blocks(2 * MOST),
-        [vmem, vmem, vmem, vmem, vmem] + [vmem] * splits,
+        (shape((BR, TILE)), shape((BR, WIDTH, TILE), BF16))
+        + sent_blocks((2 * MOST, WIDTH, TILE), BF16),
+        [vmem, vmem, vmem, vmem, vmem, anywhere] + [vmem] * splits,
         [count, staging(2 * MOST)],
         name="first_block",
-    )(start_block, remote_scaled, *far_scalars, *degrees)
-
-    def local_products(x):
+    )(start_block, remote_scaled, *far_scalars, local_scaled, *degrees)
+
+    def local_products(first, number, x, tiles, *more):
         return call(
-            local_products_kernel,
+            functools.partial(local_products_kernel, first),
             shape((BR, WIDTH, TILE)),
-            [vmem, vmem, hbm, vmem, anywhere],
+            [vmem, vmem, anywhere] + [vmem] * len(more),
             [
-                pltpu.VMEM((local_tiles - HELD, TILE, TILE), BF16),
-                pltpu.SemaphoreType.DMA((local_tiles // CHUNK - HELD // CHUNK,)),
                 pltpu.SMEM(local_coords.shape, jnp.int32),
                 pltpu.SemaphoreType.DMA((1,)),
             ],
-            flops=4 * local_tiles * TILE * TILE * WIDTH,
-            moved=2 * local_tiles * TILE * TILE,
+            flops=4 * number * TILE * TILE * WIDTH,
+            moved=2 * number * TILE * TILE,
             name="local_products",
-        )(x, ready, local_weights, local_gains, local_coords)
+        )(x, tiles, local_coords, *more)
 
     def product(x, sent, out_shape, whole):
-        blocks = sent[0].shape[1]
-        if by_chips(groups):
-            near, far = sent
-            passed = lax.ppermute(far, "rows", [(j, j ^ 1) for j in range(groups)])
-            own, *others = call(
-                forward_kernel,
-                (shape((2, blocks, WIDTH, TILE), BF16),) * (groups // 2),
-                [vmem, vmem],
-                name="forward",
-            )(near, passed)
-            arrived = [own] + [
-                lax.ppermute(piece, "rows", [(j, j ^ (2 * k)) for j in range(groups)])
-                for k, piece in zip(offsets(groups // 2)[1:], others)
-            ]
-            partial = local_products(x)
-        else:
-            arrived = [trade(sent[0])]
-            partial = local_products(x)
+        partial = local_products(0, HEAD, x, local_scaled)
+        arrived = exchange(sent, (partial,))
+        partial = local_products(HEAD, local_tiles - HEAD, x, local_raw, local_gains, partial)
         return arrived, call(
             functools.partial(remote_products_kernel, splits, whole, len(arrived)),
             out_shape,
             [vmem, vmem, vmem, vmem, vmem] + [vmem] * len(arrived),
-            [pltpu.VMEM((BR, WIDTH, TILE), F32), count, staging(blocks)],
+            [pltpu.VMEM((BR, WIDTH, TILE), F32), count, staging(sent[0].shape[1])],
             name="remote_products",
         )(remote_scaled, partial, *far_scalars, *arrived)
 
@@ -597,7 +589,7 @@
         )(own, swap(sent, k))
     x, *sent = call(
         functools.partial(next_block_kernel, vertices),
-        (shape((BR, WIDTH, TILE), BF16),) + sent_blocks(2 * MOST + 1),
+        (shape((BR, WIDTH, TILE), BF16),) + sent_blocks((2 * MOST + 1, WIDTH, TILE), BF16),
         [vmem, vmem, vmem, vmem, vmem, vmem, vmem],
         [count, staging(2 * MOST + 1)],
         name="next_block",

time: 74.8 us -> 72.5 us (0.969)
  Pallas kernels: 23.2 us -> 21.5 us
  waiting for transfers between devices: 16.2 us -> 17.1 us
  blocking collectives: 11.5 us -> 10.7 us
    all_to_all x1 -> x0, starting transfers between devices: 5.21 us -> none  [trade(): lax.all_to_all(value, 'rows', split_axis=0, concat_axis=0, tiled=True)]
    ppermute x8 -> x12, starting transfers between devices: 7.25 us -> 12.2 us  [the longest x9 11.5 us: exchange(): lax.ppermute(piece, 'rows', [(j, j ^ 2 * k) for j in range(groups)])]
    pallas_call x8 -> x12, Pallas kernels: 17.4 us -> 15.6 us  [the longest x4 8.87 us: local_products(): call(functools.partial(local_products_kernel, first), shape((BR, WIDTH, T...]
    all_to_all x1, blocking collectives: 11.5 us -> 10.7 us  [per_device(): lax.all_to_all(grams, ('rows', 'cols'), split_axis=0, concat_axis=0, tile...]
    ppermute x8 -> x12, waiting for transfers between devices: 2.78 us -> 3.46 us  [the longest x9 2.59 us: exchange(): lax.ppermute(piece, 'rows', [(j, j ^ 2 * k) for j in range(groups)])]
  transfers between devices with their start and end apart: 17 -> 20, of which waited for: 9 -> 12; matrix products, arithmetic and copies ran while one was open for 0% -> 0% of each run, Pallas kernels for 22% -> 20%
where the time goes in v7:
time: 72.5 us; the launch traced here: 72.3 us
  starting transfers between devices  22.7 us (31%)
  Pallas kernels  21.5 us (30%)
  waiting for transfers between devices  17.1 us (24%)
  blocking collectives  10.7 us (15%)
    ppermute x8, waiting for transfers between devices, swap(): return lax.ppermute(value, 'cols', [(j, j ^ k) for j in range(splits)])  13.7 us
    ppermute x9, starting transfers between devices, exchange(): lax.ppermute(piece, 'rows', [(j, j ^ 2 * k) for j in range(groups)])  11.5 us
    all_to_all x1, blocking collectives, per_device(): lax.all_to_all(grams, ('rows', 'cols'), split_axis=0, concat_axis=0, tile...  10.7 us
    ppermute x8, starting transfers between devices, swap(): return lax.ppermute(value, 'cols', [(j, j ^ k) for j in range(splits)])  10.5 us
    pallas_call x4, Pallas kernels, local_products(): call(functools.partial(local_products_kernel, first), shape((BR, WIDTH, T...  8.87 us
    pallas_call x1, Pallas kernels, per_device(): call(local_degree_kernel, (shape((BR, TILE)), shape((local_tiles - HEAD,...  3.01 us
    ppermute x9, waiting for transfers between devices, exchange(): lax.ppermute(piece, 'rows', [(j, j ^ 2 * k) for j in range(groups)])  2.59 us
    pallas_call x1, Pallas kernels, per_device(): call(remote_degree_kernel, (shape((BR, TILE)), shape((remote_tiles, TILE,...  2 us
  transfers between devices with their start and end apart: 20, of which 12 were waited for; matrix products, arithmetic and copies ran while one was open for 0% of the time, Pallas kernels for 20%

profile of v7, /device:TPU:0, one launch (start us, length us, event | category | flops | bytes accessed | tf_op | source)
XLA Modules:
  0.0 72.3 jit_solution(10394786329643624172)
XLA Ops:
  0.0 2.0 %remote_degree.1 = (f32[16,256]{1,0:T(8,128)S(1)}, bf16[8,256,256]{2,1,0:T(8,128)(2,1)S(1)}, bf16[16,256,256]{2,1,0:T(8,128)(2,1)S(1)}, f32[4,8,256]{2,1,0:T(8,128)S(1)}, f32[4,8,256]{2,1,0:T(8,128)S(1)}) custom-call(bf16[1,1,8,256,256]{4,3,2,1,0:T(8,128)(2,1)} %weights.2, f32[1,1,8,2,256]{4,3,2,1,0:T(2,128)} %gains.4, s32[1,1,8]{2,1,0:T(1,128)} %groups.9, ...), custom_call_target="tpu_custom_call" | custom-call | flops 1000000 | bytes 1000000 | tf_op jit(solution)/shard_map/remote_degree/pallas_call | solution.py:495
  2.5 0.9 %collective-permute-done.passed = f32[4,8,256]{2,1,0:T(8,128)S(1)} collective-permute-done((f32[4,8,256]{2,1,0:T(8,128)S(1)}, f32[4,8,256]{2,1,0:T(8,128)S(1)}, u32[]{:S(2)}, u32[]{:S(2)}) %collective-permute-start) | collective-permute-done | bytes 32800 | tf_op jit(solution)/shard_map/ppermute | solution.py:482
  3.4 3.8 %collective-permute-start.1 = (f32[2,8,256]{2,1,0:T(8,128)S(1)}, f32[2,8,256]{2,1,0:T(8,128)S(1)}, u32[]{:S(2)}, u32[]{:S(2)}) collective-permute-start(f32[2,8,256]{2,1,0:T(8,128)S(1)} %get-tuple-element.53), channel_id=1, source_target_pairs={{0,24},{4,28},{8,16},{12,20},{16,8},{20,12},{24,0},{28,4},{1,25},{... | collective-permute-start | bytes 49160 | tf_op jit(solution)/shard_map/ppermute | solution.py:490
  7.8 3.0 %local_degree.1 = (f32[16,256]{1,0:T(8,128)S(1)}, bf16[32,256,256]{2,1,0:T(8,128)(2,1)S(1)}) custom-call(bf16[16,256,256]{2,1,0:T(8,128)(2,1)S(1)} %get-tuple-element.48.held.raw, bf16[1,1,48,256,256]{4,3,2,1,0:T(8,128)(2,1)} %weights.3, f32[1,1,48,2,256]{4,3,2,1,0:T(2,128)S(1)} %copy-done, s32[1,1,2,48]{3,2,1,0:T(2,128)S(1)} %bitcast.7), custom_call_target="tpu_custom_call" | custom-call | flops 1000000 | bytes 10000000 | tf_op jit(solution)/shard_map/local_degree/pallas_call | solution.py:515
  11.5 3.7 %collective-permute-start.6 = (f32[16,256]{1,0:T(8,128)S(1)}, f32[16,256]{1,0:T(8,128)S(1)}, u32[]{:S(2)}, u32[]{:S(2)}) collective-permute-start(f32[16,256]{1,0:T(8,128)S(1)} %get-tuple-element.60.refs_0_), channel_id=1, source_target_pairs={{0,3},{1,2},{2,1},{3,0},{4,7},{5,6},{6,5},{7,4},{8,11},{9,10},{10,... | collective-permute-start | bytes 49160 | tf_op jit(solution)/shard_map/ppermute | solution.py:468
  15.2 0.8 %collective-permute-start.4 = (f32[16,256]{1,0:T(8,128)S(1)}, f32[16,256]{1,0:T(8,128)S(1)}, u32[]{:S(2)}, u32[]{:S(2)}) collective-permute-start(f32[16,256]{1,0:T(8,128)S(1)} %get-tuple-element.60.refs_0_), channel_id=1, source_target_pairs={{0,1},{1,0},{2,3},{3,2},{4,5},{5,4},{6,7},{7,6},{8,9},{9,8},{10,11... | collective-permute-start | bytes 49160 | tf_op jit(solution)/shard_map/ppermute | solution.py:468
  15.9 0.5 remote_scale.1.scaled
  16.5 1.1 %local_scale.1.later.tiles = bf16[16,256,256]{2,1,0:T(8,128)(2,1)S(1)} custom-call(bf16[16,256,256]{2,1,0:T(8,128)(2,1)S(1)} %get-tuple-element.48.held.raw, f32[1,1,48,2,256]{4,3,2,1,0:T(2,128)S(1)} %copy-done), custom_call_target="tpu_custom_call" | custom-call | flops 2097152 | bytes 1000000 | tf_op jit(solution)/shard_map/local_scale/pallas_call | solution.py:191
  17.5 2.3 %collective-permute-done.5.refs_2_ = f32[16,256]{1,0:T(8,128)S(1)} collective-permute-done((f32[16,256]{1,0:T(8,128)S(1)}, f32[16,256]{1,0:T(8,128)S(1)}, u32[]{:S(2)}, u32[]{:S(2)}) %collective-permute-start.5) | collective-permute-done | bytes 16416 | tf_op jit(solution)/shard_map/ppermute | solution.py:468
  20.3 1.5 %local_products.4.refs_1_.refs_0_ = f32[16,16,256]{2,1,0:T(8,128)S(1)} custom-call(bf16[16,16,256]{2,1,0:T(8,128)(2,1)S(1)} %get-tuple-element.62.x, bf16[16,256,256]{2,1,0:T(8,128)(2,1)S(1)} %local_scale.1.later.tiles, s32[1,1,2,48]{3,2,1,0:T(2,128)S(1)} %bitcast.8), custom_call_target="tpu_custom_call" | custom-call | flops 67108864 | bytes 2097152 | tf_op jit(solution)/shard_map/local_products/pallas_call | solution.py:555
  21.8 2.4 %collective-permute-start.8 = (bf16[2,4,16,256]{3,2,1,0:T(8,128)(2,1)S(1)}, bf16[2,4,16,256]{3,2,1,0:T(8,128)(2,1)S(1)}, u32[]{:S(2)}, u32[]{:S(2)}) collective-permute-start(bf16[2,4,16,256]{3,2,1,0:T(8,128)(2,1)S(1)} %get-tuple-element.67), channel_id=1, source_target_pairs={{0,24},{4,28},{8,16},{12,20},{16,8},{20,12},{24,0},{28,4},{1,25},{... | collective-permute-start | bytes 196616 | tf_op jit(solution)/shard_map/ppermute | solution.py:490
  24.8 0.6 collective-permute-start.10
  25.4 2.9 %local_products.5.partial = f32[16,16,256]{2,1,0:T(8,128)S(1)} custom-call(bf16[16,16,256]{2,1,0:T(8,128)(2,1)S(1)} %get-tuple-element.62.x, bf16[32,256,256]{2,1,0:T(8,128)(2,1)S(1)} %get-tuple-element.63.tiles, s32[1,1,2,48]{3,2,1,0:T(2,128)S(1)} %bitcast.9, f32[1,1,48,2,256]{4,3,2,1,0:T(2,128)S(1)} %copy-done, ...), custom_call_target="tpu_custom_call" | custom-call | flops 134217728 | bytes 4194304 | tf_op jit(solution)/shard_map/local_products/pallas_call | solution.py:555
  29.0 0.6 remote_products.2
  29.7 5.0 %collective-permute-done.11.theirs = bf16[16,16,256]{2,1,0:T(8,128)(2,1)S(1)} collective-permute-done((bf16[16,16,256]{2,1,0:T(8,128)(2,1)S(1)}, bf16[16,16,256]{2,1,0:T(8,128)(2,1)S(1)}, u32[]{:S(2)}, u32[]{:S(2)}) %collective-permute-start.11) | collective-permute-done | bytes 131104 | tf_op jit(solution)/shard_map/ppermute | solution.py:468
  34.7 1.5 %collective-permute-start.12 = (bf16[16,16,256]{2,1,0:T(8,128)(2,1)S(1)}, bf16[16,16,256]{2,1,0:T(8,128)(2,1)S(1)}, u32[]{:S(2)}, u32[]{:S(2)}) collective-permute-start(bf16[16,16,256]{2,1,0:T(8,128)(2,1)S(1)} %get-tuple-element.73), channel_id=1, source_target_pairs={{0,3},{1,2},{2,1},{3,0},{4,7},{5,6},{6,5},{7,4},{8,11},{9,10},{10,... | collective-permute-start | bytes 393224 | tf_op jit(solution)/shard_map/ppermute | solution.py:468
  36.2 5.3 %collective-permute-done.12.theirs = bf16[16,16,256]{2,1,0:T(8,128)(2,1)S(1)} collective-permute-done((bf16[16,16,256]{2,1,0:T(8,128)(2,1)S(1)}, bf16[16,16,256]{2,1,0:T(8,128)(2,1)S(1)}, u32[]{:S(2)}, u32[]{:S(2)}) %collective-permute-start.12) | collective-permute-done | bytes 131104 | tf_op jit(solution)/shard_map/ppermute | solution.py:468
  41.5 0.5 next_block.1
  42.2 1.5 %local_products.6.refs_0_.refs_1_ = f32[16,16,256]{2,1,0:T(8,128)S(1)} custom-call(bf16[16,16,256]{2,1,0:T(8,128)(2,1)S(1)} %get-tuple-element.76.x, bf16[16,256,256]{2,1,0:T(8,128)(2,1)S(1)} %local_scale.1.later.tiles, s32[1,1,2,48]{3,2,1,0:T(2,128)S(1)} %bitcast.10), custom_call_target="tpu_custom_call" | custom-call | flops 67108864 | bytes 2097152 | tf_op jit(solution)/shard_map/local_products/pallas_call | solution.py:555
  43.8 1.9 %collective-permute-start.14 = (bf16[2,5,16,256]{3,2,1,0:T(8,128)(2,1)S(1)}, bf16[2,5,16,256]{3,2,1,0:T(8,128)(2,1)S(1)}, u32[]{:S(2)}, u32[]{:S(2)}) collective-permute-start(bf16[2,5,16,256]{3,2,1,0:T(8,128)(2,1)S(1)} %get-tuple-element.78), channel_id=1, source_target_pairs={{0,24},{4,28},{8,16},{12,20},{16,8},{20,12},{24,0},{28,4},{1,25},{... | collective-permute-start | bytes 245768 | tf_op jit(solution)/shard_map/ppermute | solution.py:490
  45.7 1.2 %collective-permute-start.15 = (bf16[2,5,16,256]{3,2,1,0:T(8,128)(2,1)S(1)}, bf16[2,5,16,256]{3,2,1,0:T(8,128)(2,1)S(1)}, u32[]{:S(2)}, u32[]{:S(2)}) collective-permute-start(bf16[2,5,16,256]{3,2,1,0:T(8,128)(2,1)S(1)} %get-tuple-element.79), channel_id=1, source_target_pairs={{0,16},{4,20},{8,24},{12,28},{16,0},{20,4},{24,8},{28,12},{1,17},{... | collective-permute-start | bytes 245768 | tf_op jit(solution)/shard_map/ppermute | solution.py:490
  47.3 2.9 %local_products.7.partial = f32[16,16,256]{2,1,0:T(8,128)S(1)} custom-call(bf16[16,16,256]{2,1,0:T(8,128)(2,1)S(1)} %get-tuple-element.76.x, bf16[32,256,256]{2,1,0:T(8,128)(2,1)S(1)} %get-tuple-element.63.tiles, s32[1,1,2,48]{3,2,1,0:T(2,128)S(1)} %bitcast.11, f32[1,1,48,2,256]{4,3,2,1,0:T(2,128)S(1)} %copy-done, ...), custom_call_target="tpu_custom_call" | custom-call | flops 134217728 | bytes 4194304 | tf_op jit(solution)/shard_map/local_products/pallas_call | solution.py:555
  50.2 1.1 %collective-permute-done.15.refs_2_ = bf16[2,5,16,256]{3,2,1,0:T(8,128)(2,1)S(1)} collective-permute-done((bf16[2,5,16,256]{3,2,1,0:T(8,128)(2,1)S(1)}, bf16[2,5,16,256]{3,2,1,0:T(8,128)(2,1)S(1)}, u32[]{:S(2)}, u32[]{:S(2)}) %collective-permute-start.15) | collective-permute-done | bytes 81952 | tf_op jit(solution)/shard_map/ppermute | solution.py:490
  51.6 0.6 remote_products.3
  52.2 1.7 %collective-permute-start.17 = (bf16[4,16,256]{2,1,0:T(8,128)(2,1)S(1)}, bf16[4,16,256]{2,1,0:T(8,128)(2,1)S(1)}, u32[]{:S(2)}, u32[]{:S(2)}) collective-permute-start(bf16[4,16,256]{2,1,0:T(8,128)(2,1)S(1)} %get-tuple-element.82), channel_id=1, source_target_pairs={{0,3},{1,2},{2,1},{3,0},{4,7},{5,6},{6,5},{7,4},{8,11},{9,10},{10,... | collective-permute-start | bytes 98312 | tf_op jit(solution)/shard_map/ppermute | solution.py:468
  53.9 0.9 %collective-permute-start.18 = (bf16[4,16,256]{2,1,0:T(8,128)(2,1)S(1)}, bf16[4,16,256]{2,1,0:T(8,128)(2,1)S(1)}, u32[]{:S(2)}, u32[]{:S(2)}) collective-permute-start(bf16[4,16,256]{2,1,0:T(8,128)(2,1)S(1)} %get-tuple-element.83), channel_id=1, source_target_pairs={{0,2},{1,3},{2,0},{3,1},{4,6},{5,7},{6,4},{7,5},{8,10},{9,11},{10,... | collective-permute-start | bytes 98312 | tf_op jit(solution)/shard_map/ppermute | solution.py:468
  54.8 1.8 %collective-permute-start.19 = (bf16[4,16,256]{2,1,0:T(8,128)(2,1)S(1)}, bf16[4,16,256]{2,1,0:T(8,128)(2,1)S(1)}, u32[]{:S(2)}, u32[]{:S(2)}) collective-permute-start(bf16[4,16,256]{2,1,0:T(8,128)(2,1)S(1)} %get-tuple-element.84), channel_id=1, source_target_pairs={{0,1},{1,0},{2,3},{3,2},{4,5},{5,4},{6,7},{7,6},{8,9},{9,8},{10,11... | collective-permute-start | bytes 98312 | tf_op jit(solution)/shard_map/ppermute | solution.py:468
  56.6 1.3 %middle_factor.1.inverse = f32[16,16]{1,0:T(8,128)S(1)} custom-call(bf16[2,5,16,256]{3,2,1,0:T(8,128)(2,1)S(1)} %get-tuple-element.77.refs_0_, bf16[2,5,16,256]{3,2,1,0:T(8,128)(2,1)S(1)} %collective-permute-done.14.refs_1_, bf16[2,5,16,256]{3,2,1,0:T(8,128)(2,1)S(1)} %collective-permute-done.15.refs_2_, ...), custom_call_target="tpu_custom_call" | custom-call | flops 1000000 | bytes 1000000 | tf_op jit(solution)/shard_map/middle_factor/pallas_call | solution.py:610
  58.0 0.8 %collective-permute-done.18.refs_2_ = bf16[4,16,256]{2,1,0:T(8,128)(2,1)S(1)} collective-permute-done((bf16[4,16,256]{2,1,0:T(8,128)(2,1)S(1)}, bf16[4,16,256]{2,1,0:T(8,128)(2,1)S(1)}, u32[]{:S(2)}, u32[]{:S(2)}) %collective-permute-start.18) | collective-permute-done | bytes 32800 | tf_op jit(solution)/shard_map/ppermute | solution.py:468
  59.1 0.7 last_quarter.1
  59.7 10.7 %all_to_all.5.grams = f32[32,2,128]{2,1,0:T(2,128)S(1)} all-to-all(f32[32,2,128]{2,1,0:T(2,128)S(1)} %get-tuple-element.85), channel_id=1, replica_groups=mesh['rows'=8,'cols'=4] {'rows','cols'}, dimensions={0} | all-to-all | bytes 65536 | tf_op jit(solution)/shard_map/all_to_all | solution.py:622
  70.5 1.9 %finish.1 = f32[16,1024]{1,0:T(8,128)} custom-call(f32[32,2,128]{2,1,0:T(2,128)S(1)} %all_to_all.5.grams, f32[16,1024]{1,0:T(8,128)S(1)} %get-tuple-element.86.image), custom_call_target="tpu_custom_call" | custom-call | flops 1000000 | bytes 1000000 | tf_op jit(solution)/shard_map/finish/pallas_call | solution.py:625
  (41 shorter events, 4.8 us)
Async XLA Ops:
  0.0 7.8 %copy-start = (f32[1,1,48,2,256]{4,3,2,1,0:T(2,128)S(1)}, f32[1,1,48,2,256]{4,3,2,1,0:T(2,128)}, u32[]{:S(2)}) copy-start(f32[1,1,48,2,256]{4,3,2,1,0:T(2,128)} %refs_0_.1) | copy-start | bytes 294916
  0.0 7.8 %copy-start.4 = (s32[1,1,48,2]{2,3,1,0:T(2,128)S(1)}, s32[1,1,48,2]{2,3,1,0:T(2,128)}, u32[]{:S(2)}) copy-start(s32[1,1,48,2]{2,3,1,0:T(2,128)} %param.10) | copy-start | bytes 1156
  2.0 1.4 %collective-permute-start = (f32[4,8,256]{2,1,0:T(8,128)S(1)}, f32[4,8,256]{2,1,0:T(8,128)S(1)}, u32[]{:S(2)}, u32[]{:S(2)}) collective-permute-start(f32[4,8,256]{2,1,0:T(8,128)S(1)} %get-tuple-element.51), channel_id=1, source_target_pairs={{0,4},{4,0},{8,12},{12,8},{16,20},{20,16},{24,28},{28,24},{1,5},{5... | collective-permute-start | bytes 98312 | tf_op jit(solution)/shard_map/ppermute | solution.py:482
  3.4 7.5 %collective-permute-start.1 = (f32[2,8,256]{2,1,0:T(8,128)S(1)}, f32[2,8,256]{2,1,0:T(8,128)S(1)}, u32[]{:S(2)}, u32[]{:S(2)}) collective-permute-start(f32[2,8,256]{2,1,0:T(8,128)S(1)} %get-tuple-element.53), channel_id=1, source_target_pairs={{0,24},{4,28},{8,16},{12,20},{16,8},{20,12},{24,0},{28,4},{1,25},{... | collective-permute-start | bytes 49160 | tf_op jit(solution)/shard_map/ppermute | solution.py:490
  7.2 3.7 %collective-permute-start.2 = (f32[2,8,256]{2,1,0:T(8,128)S(1)}, f32[2,8,256]{2,1,0:T(8,128)S(1)}, u32[]{:S(2)}, u32[]{:S(2)}) collective-permute-start(f32[2,8,256]{2,1,0:T(8,128)S(1)} %get-tuple-element.54), channel_id=1, source_target_pairs={{0,16},{4,20},{8,24},{12,28},{16,0},{20,4},{24,8},{28,12},{1,17},{... | collective-permute-start | bytes 49160 | tf_op jit(solution)/shard_map/ppermute | solution.py:490
  7.7 3.7 %collective-permute-start.3 = (f32[2,8,256]{2,1,0:T(8,128)S(1)}, f32[2,8,256]{2,1,0:T(8,128)S(1)}, u32[]{:S(2)}, u32[]{:S(2)}) collective-permute-start(f32[2,8,256]{2,1,0:T(8,128)S(1)} %get-tuple-element.55), channel_id=1, source_target_pairs={{0,8},{4,12},{8,0},{12,4},{16,24},{20,28},{24,16},{28,20},{1,9},{5... | collective-permute-start | bytes 49160 | tf_op jit(solution)/shard_map/ppermute | solution.py:490
  7.8 8.1 %copy-start.2 = (f32[1,1,8,2,256]{4,3,2,1,0:T(2,128)S(1)}, f32[1,1,8,2,256]{4,3,2,1,0:T(2,128)}, u32[]{:S(2)}) copy-start(f32[1,1,8,2,256]{4,3,2,1,0:T(2,128)} %gains.4) | copy-start | bytes 49156
  10.9 8.9 %copy-start.1 = (f32[16,4096]{1,0:T(8,128)S(1)}, f32[16,4096]{1,0:T(8,128)}, u32[]{:S(2)}) copy-start(f32[16,4096]{1,0:T(8,128)} %start.1) | copy-start | bytes 786436
  10.9 8.9 %copy-start.3 = (s32[1,1,8,2]{2,3,1,0:T(2,128)S(1)}, s32[1,1,8,2]{2,3,1,0:T(2,128)}, u32[]{:S(2)}) copy-start(s32[1,1,8,2]{2,3,1,0:T(2,128)} %param.14) | copy-start | bytes 196
  10.9 8.9 %copy-start.5 = (s32[1,1,8]{2,1,0:T(1,128)S(1)}, s32[1,1,8]{2,1,0:T(1,128)}, u32[]{:S(2)}) copy-start(s32[1,1,8]{2,1,0:T(1,128)} %groups.9) | copy-start | bytes 100
  11.5 6.0 %collective-permute-start.6 = (f32[16,256]{1,0:T(8,128)S(1)}, f32[16,256]{1,0:T(8,128)S(1)}, u32[]{:S(2)}, u32[]{:S(2)}) collective-permute-start(f32[16,256]{1,0:T(8,128)S(1)} %get-tuple-element.60.refs_0_), channel_id=1, source_target_pairs={{0,3},{1,2},{2,1},{3,0},{4,7},{5,6},{6,5},{7,4},{8,11},{9,10},{10,... | collective-permute-start | bytes 49160 | tf_op jit(solution)/shard_map/ppermute | solution.py:468
  15.2 4.6 %collective-permute-start.5 = (f32[16,256]{1,0:T(8,128)S(1)}, f32[16,256]{1,0:T(8,128)S(1)}, u32[]{:S(2)}, u32[]{:S(2)}) collective-permute-start(f32[16,256]{1,0:T(8,128)S(1)} %get-tuple-element.60.refs_0_), channel_id=1, source_target_pairs={{0,2},{1,3},{2,0},{3,1},{4,6},{5,7},{6,4},{7,5},{8,10},{9,11},{10,... | collective-permute-start | bytes 49160 | tf_op jit(solution)/shard_map/ppermute | solution.py:468
  15.2 4.6 %collective-permute-start.4 = (f32[16,256]{1,0:T(8,128)S(1)}, f32[16,256]{1,0:T(8,128)S(1)}, u32[]{:S(2)}, u32[]{:S(2)}) collective-permute-start(f32[16,256]{1,0:T(8,128)S(1)} %get-tuple-element.60.refs_0_), channel_id=1, source_target_pairs={{0,1},{1,0},{2,3},{3,2},{4,5},{5,4},{6,7},{7,6},{8,9},{9,8},{10,11... | collective-permute-start | bytes 49160 | tf_op jit(solution)/shard_map/ppermute | solution.py:468
  20.2 1.6 %collective-permute-start.7 = (bf16[4,4,16,256]{3,2,1,0:T(8,128)(2,1)S(1)}, bf16[4,4,16,256]{3,2,1,0:T(8,128)(2,1)S(1)}, u32[]{:S(2)}, u32[]{:S(2)}) collective-permute-start(bf16[4,4,16,256]{3,2,1,0:T(8,128)(2,1)S(1)} %get-tuple-element.65), channel_id=1, source_target_pairs={{0,4},{4,0},{8,12},{12,8},{16,20},{20,16},{24,28},{28,24},{1,5},{5... | collective-permute-start | bytes 393224 | tf_op jit(solution)/shard_map/ppermute | solution.py:482
  21.8 6.5 %collective-permute-start.8 = (bf16[2,4,16,256]{3,2,1,0:T(8,128)(2,1)S(1)}, bf16[2,4,16,256]{3,2,1,0:T(8,128)(2,1)S(1)}, u32[]{:S(2)}, u32[]{:S(2)}) collective-permute-start(bf16[2,4,16,256]{3,2,1,0:T(8,128)(2,1)S(1)} %get-tuple-element.67), channel_id=1, source_target_pairs={{0,24},{4,28},{8,16},{12,20},{16,8},{20,12},{24,0},{28,4},{1,25},{... | collective-permute-start | bytes 196616 | tf_op jit(solution)/shard_map/ppermute | solution.py:490
  24.3 4.4 %collective-permute-start.9 = (bf16[2,4,16,256]{3,2,1,0:T(8,128)(2,1)S(1)}, bf16[2,4,16,256]{3,2,1,0:T(8,128)(2,1)S(1)}, u32[]{:S(2)}, u32[]{:S(2)}) collective-permute-start(bf16[2,4,16,256]{3,2,1,0:T(8,128)(2,1)S(1)} %get-tuple-element.68), channel_id=1, source_target_pairs={{0,16},{4,20},{8,24},{12,28},{16,0},{20,4},{24,8},{28,12},{1,17},{... | collective-permute-start | bytes 196616 | tf_op jit(solution)/shard_map/ppermute | solution.py:490
  24.8 4.3 %collective-permute-start.10 = (bf16[2,4,16,256]{3,2,1,0:T(8,128)(2,1)S(1)}, bf16[2,4,16,256]{3,2,1,0:T(8,128)(2,1)S(1)}, u32[]{:S(2)}, u32[]{:S(2)}) collective-permute-start(bf16[2,4,16,256]{3,2,1,0:T(8,128)(2,1)S(1)} %get-tuple-element.69), channel_id=1, source_target_pairs={{0,8},{4,12},{8,0},{12,4},{16,24},{20,28},{24,16},{28,20},{1,9},{5... | collective-permute-start | bytes 196616 | tf_op jit(solution)/shard_map/ppermute | solution.py:490
  29.6 5.0 %collective-permute-start.11 = (bf16[16,16,256]{2,1,0:T(8,128)(2,1)S(1)}, bf16[16,16,256]{2,1,0:T(8,128)(2,1)S(1)}, u32[]{:S(2)}, u32[]{:S(2)}) collective-permute-start(bf16[16,16,256]{2,1,0:T(8,128)(2,1)S(1)} %get-tuple-element.71), channel_id=1, source_target_pairs={{0,1},{1,0},{2,3},{3,2},{4,5},{5,4},{6,7},{7,6},{8,9},{9,8},{10,11... | collective-permute-start | bytes 393224 | tf_op jit(solution)/shard_map/ppermute | solution.py:468
  34.7 6.8 %collective-permute-start.12 = (bf16[16,16,256]{2,1,0:T(8,128)(2,1)S(1)}, bf16[16,16,256]{2,1,0:T(8,128)(2,1)S(1)}, u32[]{:S(2)}, u32[]{:S(2)}) collective-permute-start(bf16[16,16,256]{2,1,0:T(8,128)(2,1)S(1)} %get-tuple-element.73), channel_id=1, source_target_pairs={{0,3},{1,2},{2,1},{3,0},{4,7},{5,6},{6,5},{7,4},{8,11},{9,10},{10,... | collective-permute-start | bytes 393224 | tf_op jit(solution)/shard_map/ppermute | solution.py:468
  42.1 1.6 %collective-permute-start.13 = (bf16[4,5,16,256]{3,2,1,0:T(8,128)(2,1)S(1)}, bf16[4,5,16,256]{3,2,1,0:T(8,128)(2,1)S(1)}, u32[]{:S(2)}, u32[]{:S(2)}) collective-permute-start(bf16[4,5,16,256]{3,2,1,0:T(8,128)(2,1)S(1)} %get-tuple-element.75), channel_id=1, source_target_pairs={{0,4},{4,0},{8,12},{12,8},{16,20},{20,16},{24,28},{28,24},{1,5},{5... | collective-permute-start | bytes 491528 | tf_op jit(solution)/shard_map/ppermute | solution.py:482
  43.8 6.5 %collective-permute-start.14 = (bf16[2,5,16,256]{3,2,1,0:T(8,128)(2,1)S(1)}, bf16[2,5,16,256]{3,2,1,0:T(8,128)(2,1)S(1)}, u32[]{:S(2)}, u32[]{:S(2)}) collective-permute-start(bf16[2,5,16,256]{3,2,1,0:T(8,128)(2,1)S(1)} %get-tuple-element.78), channel_id=1, source_target_pairs={{0,24},{4,28},{8,16},{12,20},{16,8},{20,12},{24,0},{28,4},{1,25},{... | collective-permute-start | bytes 245768 | tf_op jit(solution)/shard_map/ppermute | solution.py:490
  45.7 5.7 %collective-permute-start.15 = (bf16[2,5,16,256]{3,2,1,0:T(8,128)(2,1)S(1)}, bf16[2,5,16,256]{3,2,1,0:T(8,128)(2,1)S(1)}, u32[]{:S(2)}, u32[]{:S(2)}) collective-permute-start(bf16[2,5,16,256]{3,2,1,0:T(8,128)(2,1)S(1)} %get-tuple-element.79), channel_id=1, source_target_pairs={{0,16},{4,20},{8,24},{12,28},{16,0},{20,4},{24,8},{28,12},{1,17},{... | collective-permute-start | bytes 245768 | tf_op jit(solution)/shard_map/ppermute | solution.py:490
  46.8 4.8 %collective-permute-start.16 = (bf16[2,5,16,256]{3,2,1,0:T(8,128)(2,1)S(1)}, bf16[2,5,16,256]{3,2,1,0:T(8,128)(2,1)S(1)}, u32[]{:S(2)}, u32[]{:S(2)}) collective-permute-start(bf16[2,5,16,256]{3,2,1,0:T(8,128)(2,1)S(1)} %get-tuple-element.80), channel_id=1, source_target_pairs={{0,8},{4,12},{8,0},{12,4},{16,24},{20,28},{24,16},{28,20},{1,9},{5... | collective-permute-start | bytes 245768 | tf_op jit(solution)/shard_map/ppermute | solution.py:490
  52.2 5.8 %collective-permute-start.17 = (bf16[4,16,256]{2,1,0:T(8,128)(2,1)S(1)}, bf16[4,16,256]{2,1,0:T(8,128)(2,1)S(1)}, u32[]{:S(2)}, u32[]{:S(2)}) collective-permute-start(bf16[4,16,256]{2,1,0:T(8,128)(2,1)S(1)} %get-tuple-element.82), channel_id=1, source_target_pairs={{0,3},{1,2},{2,1},{3,0},{4,7},{5,6},{6,5},{7,4},{8,11},{9,10},{10,... | collective-permute-start | bytes 98312 | tf_op jit(solution)/shard_map/ppermute | solution.py:468
  53.9 4.9 %collective-permute-start.18 = (bf16[4,16,256]{2,1,0:T(8,128)(2,1)S(1)}, bf16[4,16,256]{2,1,0:T(8,128)(2,1)S(1)}, u32[]{:S(2)}, u32[]{:S(2)}) collective-permute-start(bf16[4,16,256]{2,1,0:T(8,128)(2,1)S(1)} %get-tuple-element.83), channel_id=1, source_target_pairs={{0,2},{1,3},{2,0},{3,1},{4,6},{5,7},{6,4},{7,5},{8,10},{9,11},{10,... | collective-permute-start | bytes 98312 | tf_op jit(solution)/shard_map/ppermute | solution.py:468
  54.8 4.3 %collective-permute-start.19 = (bf16[4,16,256]{2,1,0:T(8,128)(2,1)S(1)}, bf16[4,16,256]{2,1,0:T(8,128)(2,1)S(1)}, u32[]{:S(2)}, u32[]{:S(2)}) collective-permute-start(bf16[4,16,256]{2,1,0:T(8,128)(2,1)S(1)} %get-tuple-element.84), channel_id=1, source_target_pairs={{0,1},{1,0},{2,3},{3,2},{4,5},{5,4},{6,7},{7,6},{8,9},{9,8},{10,11... | collective-permute-start | bytes 98312 | tf_op jit(solution)/shard_map/ppermute | solution.py:468

commit v8 on v7

--- a/solution.py
+++ b/solution.py
@@ -12,7 +12,7 @@
 BR = 16
 MOST = 2
 CHUNK = 8
-HEAD = 16
+HEAD = 8
 LANES = 128
 F32 = jnp.float32
 BF16 = jnp.bfloat16
@@ -313,7 +313,7 @@
     *refs, partial, tile_coords, sems = refs
     gains, earlier = refs or (None, None)
     count = tiles.shape[0]
-    batch = 2 * CHUNK if count % (2 * CHUNK) == 0 else CHUNK
+    batch = next(size for size in (20, 16, CHUNK) if count % size == 0)
     wait = fetch((coords,), (tile_coords,), sems)
     partial[...] = earlier[...] if refs else jnp.zeros(partial.shape, F32)
     wait()
@@ -322,7 +322,7 @@
         base = first + n * batch
         if refs:
             row_gains = [
-                jnp.transpose(gains[0, 0, pl.ds(base + k, CHUNK), 0, :])
+                jnp.transpose(gains[0, 0, pl.ds(base + k, min(CHUNK, batch - k)), 0, :])
                 for k in range(0, batch, CHUNK)
             ]
         places, results = [], []
@@ -381,24 +381,16 @@
 def eliminate(gram, right):
     shape = (WIDTH, LANES)
     row = lax.broadcasted_iota(jnp.int32, shape, 0)
-    lane = lax.broadcasted_iota(jnp.int32, shape, 1)
-    gram = jnp.concatenate([gram, jnp.zeros((WIDTH, LANES - WIDTH), F32)], axis=1)
-    for k in range(0, WIDTH, 2):
-        first = jnp.broadcast_to(gram[:, k : k + 1], shape)
-        second = jnp.broadcast_to(gram[:, k + 1 : k + 2], shape)
-        factor = first / first[k : k + 1]
-        second = second - factor * second[k : k + 1]
-        then = jnp.where(row > k + 1, second / second[k + 1 : k + 2], 0.0)
-        link = factor[k + 1 : k + 2]
-        factor = jnp.where(row > k, factor, 0.0)
-
-        def step(work):
-            top = work[k : k + 1, :]
-            return work - factor * top - then * (work[k + 1 : k + 2, :] - link * top)
-
-        gram, right = step(gram), [step(block) for block in right]
-    pivots = jnp.sum(jnp.where(row == lane, gram, 0.0), axis=1, keepdims=True)
-    root = jnp.broadcast_to(1.0 / jnp.sqrt(pivots), shape)
+    columns = [jnp.broadcast_to(gram[:, k : k + 1], shape) for k in range(WIDTH)]
+    pivots = jnp.zeros(shape, F32)
+    for k in range(WIDTH):
+        pivot = columns[k][k : k + 1]
+        pivots = jnp.where(row == k, pivot, pivots)
+        factor = jnp.where(row > k, columns[k] * (1.0 / pivot), 0.0)
+        for n in range(k + 1, WIDTH):
+            columns[n] = columns[n] - factor * columns[n][k : k + 1]
+        right = [block - factor * block[k : k + 1] for block in right]
+    root = 1.0 / jnp.sqrt(pivots)
     return [block * root for block in right]
 
 

time: 72.5 us -> 71.3 us (0.983)
  Pallas kernels: 21.5 us -> 19.7 us
    ppermute x9, waiting for transfers between devices: 2.59 us -> 0.87 us  [exchange(): lax.ppermute(piece, 'rows', [(j, j ^ 2 * k) for j in range(groups)])]
    ppermute x8, waiting for transfers between devices: 13.7 us -> 15.2 us  [swap(): return lax.ppermute(value, 'cols', [(j, j ^ k) for j in range(splits)])]
    pallas_call x1, Pallas kernels: 1.28 us -> 0.38 us  [per_device(): call(middle_factor_kernel, shape((WIDTH, WIDTH)), [vmem] * len(arrived),...]
    pallas_call x1, Pallas kernels: 1.88 us -> 1.11 us  [per_device(): call(finish_kernel, shape((WIDTH, quarter * TILE)), [vmem, vmem], name='f...]
  transfers between devices with their start and end apart: 20 -> 20, of which waited for: 12 -> 14; matrix products, arithmetic and copies ran while one was open for 0% -> 0% of each run, Pallas kernels for 20% -> 20%
where the time goes in v8:
time: 71.3 us; the launch traced here: 71.1 us
  starting transfers between devices  22.8 us (32%)
  Pallas kernels  19.7 us (28%)
  waiting for transfers between devices  17.4 us (24%)
  blocking collectives  10.9 us (15%)
    ppermute x8, waiting for transfers between devices, swap(): return lax.ppermute(value, 'cols', [(j, j ^ k) for j in range(splits)])  15.2 us
    ppermute x9, starting transfers between devices, exchange(): lax.ppermute(piece, 'rows', [(j, j ^ 2 * k) for j in range(groups)])  11.5 us
    all_to_all x1, blocking collectives, per_device(): lax.all_to_all(grams, ('rows', 'cols'), split_axis=0, concat_axis=0, tile...  10.9 us
    ppermute x8, starting transfers between devices, swap(): return lax.ppermute(value, 'cols', [(j, j ^ k) for j in range(splits)])  10.6 us
    pallas_call x4, Pallas kernels, local_products(): call(functools.partial(local_products_kernel, first), shape((BR, WIDTH, T...  9.05 us
    pallas_call x1, Pallas kernels, per_device(): call(local_degree_kernel, (shape((BR, TILE)), shape((local_tiles - HEAD,...  3.43 us
    pallas_call x1, Pallas kernels, per_device(): call(remote_degree_kernel, (shape((BR, TILE)), shape((remote_tiles, TILE,...  1.87 us
  transfers between devices with their start and end apart: 20, of which 14 were waited for; matrix products, arithmetic and copies ran while one was open for 0% of the time, Pallas kernels for 20%

profile of v8, /device:TPU:0, one launch (start us, length us, event | category | flops | bytes accessed | tf_op | source)
XLA Modules:
  0.0 71.1 jit_solution(3432601702648597620)
XLA Ops:
  0.0 1.9 %remote_degree.1 = (f32[16,256]{1,0:T(8,128)S(1)}, bf16[8,256,256]{2,1,0:T(8,128)(2,1)S(1)}, bf16[8,256,256]{2,1,0:T(8,128)(2,1)S(1)}, f32[4,8,256]{2,1,0:T(8,128)S(1)}, f32[4,8,256]{2,1,0:T(8,128)S(1)}) custom-call(bf16[1,1,8,256,256]{4,3,2,1,0:T(8,128)(2,1)} %weights.2, f32[1,1,8,2,256]{4,3,2,1,0:T(2,128)} %gains.4, s32[1,1,8]{2,1,0:T(1,128)} %groups.9, ...), custom_call_target="tpu_custom_call" | custom-call | flops 1000000 | bytes 1000000 | tf_op jit(solution)/shard_map/remote_degree/pallas_call | solution.py:487
  2.4 0.9 %collective-permute-done.passed = f32[4,8,256]{2,1,0:T(8,128)S(1)} collective-permute-done((f32[4,8,256]{2,1,0:T(8,128)S(1)}, f32[4,8,256]{2,1,0:T(8,128)S(1)}, u32[]{:S(2)}, u32[]{:S(2)}) %collective-permute-start) | collective-permute-done | bytes 32800 | tf_op jit(solution)/shard_map/ppermute | solution.py:474
  3.3 3.8 %collective-permute-start.1 = (f32[2,8,256]{2,1,0:T(8,128)S(1)}, f32[2,8,256]{2,1,0:T(8,128)S(1)}, u32[]{:S(2)}, u32[]{:S(2)}) collective-permute-start(f32[2,8,256]{2,1,0:T(8,128)S(1)} %get-tuple-element.53), channel_id=1, source_target_pairs={{0,24},{4,28},{8,16},{12,20},{16,8},{20,12},{24,0},{28,4},{1,25},{... | collective-permute-start | bytes 49160 | tf_op jit(solution)/shard_map/ppermute | solution.py:482
  7.7 3.4 %local_degree.1 = (f32[16,256]{1,0:T(8,128)S(1)}, bf16[40,256,256]{2,1,0:T(8,128)(2,1)S(1)}) custom-call(bf16[8,256,256]{2,1,0:T(8,128)(2,1)S(1)} %get-tuple-element.48.held.raw, bf16[1,1,48,256,256]{4,3,2,1,0:T(8,128)(2,1)} %weights.3, f32[1,1,48,2,256]{4,3,2,1,0:T(2,128)S(1)} %copy-done, s32[1,1,2,48]{3,2,1,0:T(2,128)S(1)} %bitcast.7), custom_call_target="tpu_custom_call" | custom-call | flops 1000000 | bytes 10000000 | tf_op jit(solution)/shard_map/local_degree/pallas_call | solution.py:507
  11.4 3.9 %collective-permute-start.6 = (f32[16,256]{1,0:T(8,128)S(1)}, f32[16,256]{1,0:T(8,128)S(1)}, u32[]{:S(2)}, u32[]{:S(2)}) collective-permute-start(f32[16,256]{1,0:T(8,128)S(1)} %get-tuple-element.60.refs_0_), channel_id=1, source_target_pairs={{0,3},{1,2},{2,1},{3,0},{4,7},{5,6},{6,5},{7,4},{8,11},{9,10},{10,... | collective-permute-start | bytes 49160 | tf_op jit(solution)/shard_map/ppermute | solution.py:460
  15.4 0.6 collective-permute-start.4
  16.0 0.5 local_scale.1.later.tiles
  16.5 0.5 remote_scale.1.scaled
  17.3 2.7 %collective-permute-done.5.refs_2_ = f32[16,256]{1,0:T(8,128)S(1)} collective-permute-done((f32[16,256]{1,0:T(8,128)S(1)}, f32[16,256]{1,0:T(8,128)S(1)}, u32[]{:S(2)}, u32[]{:S(2)}) %collective-permute-start.5) | collective-permute-done | bytes 16416 | tf_op jit(solution)/shard_map/ppermute | solution.py:460
  20.5 1.1 %local_products.4.refs_1_.refs_0_ = f32[16,16,256]{2,1,0:T(8,128)S(1)} custom-call(bf16[16,16,256]{2,1,0:T(8,128)(2,1)S(1)} %get-tuple-element.62.x, bf16[8,256,256]{2,1,0:T(8,128)(2,1)S(1)} %local_scale.1.later.tiles, s32[1,1,2,48]{3,2,1,0:T(2,128)S(1)} %bitcast.8), custom_call_target="tpu_custom_call" | custom-call | flops 33554432 | bytes 1048576 | tf_op jit(solution)/shard_map/local_products/pallas_call | solution.py:547
  21.8 2.5 %collective-permute-start.8 = (bf16[2,4,16,256]{3,2,1,0:T(8,128)(2,1)S(1)}, bf16[2,4,16,256]{3,2,1,0:T(8,128)(2,1)S(1)}, u32[]{:S(2)}, u32[]{:S(2)}) collective-permute-start(bf16[2,4,16,256]{3,2,1,0:T(8,128)(2,1)S(1)} %get-tuple-element.67), channel_id=1, source_target_pairs={{0,24},{4,28},{8,16},{12,20},{16,8},{20,12},{24,0},{28,4},{1,25},{... | collective-permute-start | bytes 196616 | tf_op jit(solution)/shard_map/ppermute | solution.py:482
  24.8 0.5 collective-permute-start.10
  25.4 3.4 %local_products.5.partial = f32[16,16,256]{2,1,0:T(8,128)S(1)} custom-call(bf16[16,16,256]{2,1,0:T(8,128)(2,1)S(1)} %get-tuple-element.62.x, bf16[40,256,256]{2,1,0:T(8,128)(2,1)S(1)} %get-tuple-element.63.tiles, s32[1,1,2,48]{3,2,1,0:T(2,128)S(1)} %bitcast.9, f32[1,1,48,2,256]{4,3,2,1,0:T(2,128)S(1)} %copy-done, ...), custom_call_target="tpu_custom_call" | custom-call | flops 167772160 | bytes 5242880 | tf_op jit(solution)/shard_map/local_products/pallas_call | solution.py:547
  29.1 0.6 remote_products.2
  29.7 5.0 %collective-permute-done.11.theirs = bf16[16,16,256]{2,1,0:T(8,128)(2,1)S(1)} collective-permute-done((bf16[16,16,256]{2,1,0:T(8,128)(2,1)S(1)}, bf16[16,16,256]{2,1,0:T(8,128)(2,1)S(1)}, u32[]{:S(2)}, u32[]{:S(2)}) %collective-permute-start.11) | collective-permute-done | bytes 131104 | tf_op jit(solution)/shard_map/ppermute | solution.py:460
  34.7 1.5 %collective-permute-start.12 = (bf16[16,16,256]{2,1,0:T(8,128)(2,1)S(1)}, bf16[16,16,256]{2,1,0:T(8,128)(2,1)S(1)}, u32[]{:S(2)}, u32[]{:S(2)}) collective-permute-start(bf16[16,16,256]{2,1,0:T(8,128)(2,1)S(1)} %get-tuple-element.73), channel_id=1, source_target_pairs={{0,3},{1,2},{2,1},{3,0},{4,7},{5,6},{6,5},{7,4},{8,11},{9,10},{10,... | collective-permute-start | bytes 393224 | tf_op jit(solution)/shard_map/ppermute | solution.py:460
  36.3 5.3 %collective-permute-done.12.theirs = bf16[16,16,256]{2,1,0:T(8,128)(2,1)S(1)} collective-permute-done((bf16[16,16,256]{2,1,0:T(8,128)(2,1)S(1)}, bf16[16,16,256]{2,1,0:T(8,128)(2,1)S(1)}, u32[]{:S(2)}, u32[]{:S(2)}) %collective-permute-start.12) | collective-permute-done | bytes 131104 | tf_op jit(solution)/shard_map/ppermute | solution.py:460
  41.6 0.5 next_block.1
  42.2 1.1 %local_products.6.refs_0_.refs_1_ = f32[16,16,256]{2,1,0:T(8,128)S(1)} custom-call(bf16[16,16,256]{2,1,0:T(8,128)(2,1)S(1)} %get-tuple-element.76.x, bf16[8,256,256]{2,1,0:T(8,128)(2,1)S(1)} %local_scale.1.later.tiles, s32[1,1,2,48]{3,2,1,0:T(2,128)S(1)} %bitcast.10), custom_call_target="tpu_custom_call" | custom-call | flops 33554432 | bytes 1048576 | tf_op jit(solution)/shard_map/local_products/pallas_call | solution.py:547
  43.6 2.3 %collective-permute-start.14 = (bf16[2,5,16,256]{3,2,1,0:T(8,128)(2,1)S(1)}, bf16[2,5,16,256]{3,2,1,0:T(8,128)(2,1)S(1)}, u32[]{:S(2)}, u32[]{:S(2)}) collective-permute-start(bf16[2,5,16,256]{3,2,1,0:T(8,128)(2,1)S(1)} %get-tuple-element.78), channel_id=1, source_target_pairs={{0,24},{4,28},{8,16},{12,20},{16,8},{20,12},{24,0},{28,4},{1,25},{... | collective-permute-start | bytes 245768 | tf_op jit(solution)/shard_map/ppermute | solution.py:482
  46.0 0.6 collective-permute-start.15
  46.6 0.6 collective-permute-start.16
  47.2 3.4 %local_products.7.partial = f32[16,16,256]{2,1,0:T(8,128)S(1)} custom-call(bf16[16,16,256]{2,1,0:T(8,128)(2,1)S(1)} %get-tuple-element.76.x, bf16[40,256,256]{2,1,0:T(8,128)(2,1)S(1)} %get-tuple-element.63.tiles, s32[1,1,2,48]{3,2,1,0:T(2,128)S(1)} %bitcast.11, f32[1,1,48,2,256]{4,3,2,1,0:T(2,128)S(1)} %copy-done, ...), custom_call_target="tpu_custom_call" | custom-call | flops 167772160 | bytes 5242880 | tf_op jit(solution)/shard_map/local_products/pallas_call | solution.py:547
  51.1 0.5 remote_products.3
  51.6 1.7 %collective-permute-start.17 = (bf16[4,16,256]{2,1,0:T(8,128)(2,1)S(1)}, bf16[4,16,256]{2,1,0:T(8,128)(2,1)S(1)}, u32[]{:S(2)}, u32[]{:S(2)}) collective-permute-start(bf16[4,16,256]{2,1,0:T(8,128)(2,1)S(1)} %get-tuple-element.82), channel_id=1, source_target_pairs={{0,3},{1,2},{2,1},{3,0},{4,7},{5,6},{6,5},{7,4},{8,11},{9,10},{10,... | collective-permute-start | bytes 98312 | tf_op jit(solution)/shard_map/ppermute | solution.py:460
  53.4 0.8 %collective-permute-start.18 = (bf16[4,16,256]{2,1,0:T(8,128)(2,1)S(1)}, bf16[4,16,256]{2,1,0:T(8,128)(2,1)S(1)}, u32[]{:S(2)}, u32[]{:S(2)}) collective-permute-start(bf16[4,16,256]{2,1,0:T(8,128)(2,1)S(1)} %get-tuple-element.83), channel_id=1, source_target_pairs={{0,2},{1,3},{2,0},{3,1},{4,6},{5,7},{6,4},{7,5},{8,10},{9,11},{10,... | collective-permute-start | bytes 98312 | tf_op jit(solution)/shard_map/ppermute | solution.py:460
  54.2 1.9 %collective-permute-start.19 = (bf16[4,16,256]{2,1,0:T(8,128)(2,1)S(1)}, bf16[4,16,256]{2,1,0:T(8,128)(2,1)S(1)}, u32[]{:S(2)}, u32[]{:S(2)}) collective-permute-start(bf16[4,16,256]{2,1,0:T(8,128)(2,1)S(1)} %get-tuple-element.84), channel_id=1, source_target_pairs={{0,1},{1,0},{2,3},{3,2},{4,5},{5,4},{6,7},{7,6},{8,9},{9,8},{10,11... | collective-permute-start | bytes 98312 | tf_op jit(solution)/shard_map/ppermute | solution.py:460
  56.5 1.1 %collective-permute-done.17.refs_1_ = bf16[4,16,256]{2,1,0:T(8,128)(2,1)S(1)} collective-permute-done((bf16[4,16,256]{2,1,0:T(8,128)(2,1)S(1)}, bf16[4,16,256]{2,1,0:T(8,128)(2,1)S(1)}, u32[]{:S(2)}, u32[]{:S(2)}) %collective-permute-start.17) | collective-permute-done | bytes 32800 | tf_op jit(solution)/shard_map/ppermute | solution.py:460
  57.6 0.7 collective-permute-done.18.refs_2_
  58.4 0.7 last_quarter.1
  59.1 10.9 %all_to_all.5.grams = f32[32,2,128]{2,1,0:T(2,128)S(1)} all-to-all(f32[32,2,128]{2,1,0:T(2,128)S(1)} %get-tuple-element.85), channel_id=1, replica_groups=mesh['rows'=8,'cols'=4] {'rows','cols'}, dimensions={0} | all-to-all | bytes 65536 | tf_op jit(solution)/shard_map/all_to_all | solution.py:614
  70.0 1.1 %finish.1 = f32[16,1024]{1,0:T(8,128)} custom-call(f32[32,2,128]{2,1,0:T(2,128)S(1)} %all_to_all.5.grams, f32[16,1024]{1,0:T(8,128)S(1)} %get-tuple-element.86.image), custom_call_target="tpu_custom_call" | custom-call | flops 1000000 | bytes 1000000 | tf_op jit(solution)/shard_map/finish/pallas_call | solution.py:617
  (41 shorter events, 4.6 us)
Async XLA Ops:
  0.0 7.7 %copy-start = (f32[1,1,48,2,256]{4,3,2,1,0:T(2,128)S(1)}, f32[1,1,48,2,256]{4,3,2,1,0:T(2,128)}, u32[]{:S(2)}) copy-start(f32[1,1,48,2,256]{4,3,2,1,0:T(2,128)} %refs_0_.1) | copy-start | bytes 294916
  0.0 7.7 %copy-start.4 = (s32[1,1,48,2]{2,3,1,0:T(2,128)S(1)}, s32[1,1,48,2]{2,3,1,0:T(2,128)}, u32[]{:S(2)}) copy-start(s32[1,1,48,2]{2,3,1,0:T(2,128)} %param.10) | copy-start | bytes 1156
  1.9 14.6 %copy-start.2 = (f32[1,1,8,2,256]{4,3,2,1,0:T(2,128)S(1)}, f32[1,1,8,2,256]{4,3,2,1,0:T(2,128)}, u32[]{:S(2)}) copy-start(f32[1,1,8,2,256]{4,3,2,1,0:T(2,128)} %gains.4) | copy-start | bytes 49156
  1.9 18.1 %copy-start.1 = (f32[16,4096]{1,0:T(8,128)S(1)}, f32[16,4096]{1,0:T(8,128)}, u32[]{:S(2)}) copy-start(f32[16,4096]{1,0:T(8,128)} %start.1) | copy-start | bytes 786436
  1.9 18.1 %copy-start.3 = (s32[1,1,8,2]{2,3,1,0:T(2,128)S(1)}, s32[1,1,8,2]{2,3,1,0:T(2,128)}, u32[]{:S(2)}) copy-start(s32[1,1,8,2]{2,3,1,0:T(2,128)} %param.14) | copy-start | bytes 196
  1.9 18.1 %copy-start.5 = (s32[1,1,8]{2,1,0:T(1,128)S(1)}, s32[1,1,8]{2,1,0:T(1,128)}, u32[]{:S(2)}) copy-start(s32[1,1,8]{2,1,0:T(1,128)} %groups.9) | copy-start | bytes 100
  1.9 1.4 %collective-permute-start = (f32[4,8,256]{2,1,0:T(8,128)S(1)}, f32[4,8,256]{2,1,0:T(8,128)S(1)}, u32[]{:S(2)}, u32[]{:S(2)}) collective-permute-start(f32[4,8,256]{2,1,0:T(8,128)S(1)} %get-tuple-element.51), channel_id=1, source_target_pairs={{0,4},{4,0},{8,12},{12,8},{16,20},{20,16},{24,28},{28,24},{1,5},{5... | collective-permute-start | bytes 98312 | tf_op jit(solution)/shard_map/ppermute | solution.py:474
  3.3 7.9 %collective-permute-start.1 = (f32[2,8,256]{2,1,0:T(8,128)S(1)}, f32[2,8,256]{2,1,0:T(8,128)S(1)}, u32[]{:S(2)}, u32[]{:S(2)}) collective-permute-start(f32[2,8,256]{2,1,0:T(8,128)S(1)} %get-tuple-element.53), channel_id=1, source_target_pairs={{0,24},{4,28},{8,16},{12,20},{16,8},{20,12},{24,0},{28,4},{1,25},{... | collective-permute-start | bytes 49160 | tf_op jit(solution)/shard_map/ppermute | solution.py:482
  7.1 4.1 %collective-permute-start.2 = (f32[2,8,256]{2,1,0:T(8,128)S(1)}, f32[2,8,256]{2,1,0:T(8,128)S(1)}, u32[]{:S(2)}, u32[]{:S(2)}) collective-permute-start(f32[2,8,256]{2,1,0:T(8,128)S(1)} %get-tuple-element.54), channel_id=1, source_target_pairs={{0,16},{4,20},{8,24},{12,28},{16,0},{20,4},{24,8},{28,12},{1,17},{... | collective-permute-start | bytes 49160 | tf_op jit(solution)/shard_map/ppermute | solution.py:482
  7.6 3.7 %collective-permute-start.3 = (f32[2,8,256]{2,1,0:T(8,128)S(1)}, f32[2,8,256]{2,1,0:T(8,128)S(1)}, u32[]{:S(2)}, u32[]{:S(2)}) collective-permute-start(f32[2,8,256]{2,1,0:T(8,128)S(1)} %get-tuple-element.55), channel_id=1, source_target_pairs={{0,8},{4,12},{8,0},{12,4},{16,24},{20,28},{24,16},{28,20},{1,9},{5... | collective-permute-start | bytes 49160 | tf_op jit(solution)/shard_map/ppermute | solution.py:482
  11.4 5.9 %collective-permute-start.6 = (f32[16,256]{1,0:T(8,128)S(1)}, f32[16,256]{1,0:T(8,128)S(1)}, u32[]{:S(2)}, u32[]{:S(2)}) collective-permute-start(f32[16,256]{1,0:T(8,128)S(1)} %get-tuple-element.60.refs_0_), channel_id=1, source_target_pairs={{0,3},{1,2},{2,1},{3,0},{4,7},{5,6},{6,5},{7,4},{8,11},{9,10},{10,... | collective-permute-start | bytes 49160 | tf_op jit(solution)/shard_map/ppermute | solution.py:460
  15.3 4.6 %collective-permute-start.5 = (f32[16,256]{1,0:T(8,128)S(1)}, f32[16,256]{1,0:T(8,128)S(1)}, u32[]{:S(2)}, u32[]{:S(2)}) collective-permute-start(f32[16,256]{1,0:T(8,128)S(1)} %get-tuple-element.60.refs_0_), channel_id=1, source_target_pairs={{0,2},{1,3},{2,0},{3,1},{4,6},{5,7},{6,4},{7,5},{8,10},{9,11},{10,... | collective-permute-start | bytes 49160 | tf_op jit(solution)/shard_map/ppermute | solution.py:460
  15.4 4.6 %collective-permute-start.4 = (f32[16,256]{1,0:T(8,128)S(1)}, f32[16,256]{1,0:T(8,128)S(1)}, u32[]{:S(2)}, u32[]{:S(2)}) collective-permute-start(f32[16,256]{1,0:T(8,128)S(1)} %get-tuple-element.60.refs_0_), channel_id=1, source_target_pairs={{0,1},{1,0},{2,3},{3,2},{4,5},{5,4},{6,7},{7,6},{8,9},{9,8},{10,11... | collective-permute-start | bytes 49160 | tf_op jit(solution)/shard_map/ppermute | solution.py:460
  20.4 1.4 %collective-permute-start.7 = (bf16[4,4,16,256]{3,2,1,0:T(8,128)(2,1)S(1)}, bf16[4,4,16,256]{3,2,1,0:T(8,128)(2,1)S(1)}, u32[]{:S(2)}, u32[]{:S(2)}) collective-permute-start(bf16[4,4,16,256]{3,2,1,0:T(8,128)(2,1)S(1)} %get-tuple-element.65), channel_id=1, source_target_pairs={{0,4},{4,0},{8,12},{12,8},{16,20},{20,16},{24,28},{28,24},{1,5},{5... | collective-permute-start | bytes 393224 | tf_op jit(solution)/shard_map/ppermute | solution.py:474
  21.8 7.0 %collective-permute-start.8 = (bf16[2,4,16,256]{3,2,1,0:T(8,128)(2,1)S(1)}, bf16[2,4,16,256]{3,2,1,0:T(8,128)(2,1)S(1)}, u32[]{:S(2)}, u32[]{:S(2)}) collective-permute-start(bf16[2,4,16,256]{3,2,1,0:T(8,128)(2,1)S(1)} %get-tuple-element.67), channel_id=1, source_target_pairs={{0,24},{4,28},{8,16},{12,20},{16,8},{20,12},{24,0},{28,4},{1,25},{... | collective-permute-start | bytes 196616 | tf_op jit(solution)/shard_map/ppermute | solution.py:482
  24.3 4.5 %collective-permute-start.9 = (bf16[2,4,16,256]{3,2,1,0:T(8,128)(2,1)S(1)}, bf16[2,4,16,256]{3,2,1,0:T(8,128)(2,1)S(1)}, u32[]{:S(2)}, u32[]{:S(2)}) collective-permute-start(bf16[2,4,16,256]{3,2,1,0:T(8,128)(2,1)S(1)} %get-tuple-element.68), channel_id=1, source_target_pairs={{0,16},{4,20},{8,24},{12,28},{16,0},{20,4},{24,8},{28,12},{1,17},{... | collective-permute-start | bytes 196616 | tf_op jit(solution)/shard_map/ppermute | solution.py:482
  24.8 4.3 %collective-permute-start.10 = (bf16[2,4,16,256]{3,2,1,0:T(8,128)(2,1)S(1)}, bf16[2,4,16,256]{3,2,1,0:T(8,128)(2,1)S(1)}, u32[]{:S(2)}, u32[]{:S(2)}) collective-permute-start(bf16[2,4,16,256]{3,2,1,0:T(8,128)(2,1)S(1)} %get-tuple-element.69), channel_id=1, source_target_pairs={{0,8},{4,12},{8,0},{12,4},{16,24},{20,28},{24,16},{28,20},{1,9},{5... | collective-permute-start | bytes 196616 | tf_op jit(solution)/shard_map/ppermute | solution.py:482
  29.7 5.0 %collective-permute-start.11 = (bf16[16,16,256]{2,1,0:T(8,128)(2,1)S(1)}, bf16[16,16,256]{2,1,0:T(8,128)(2,1)S(1)}, u32[]{:S(2)}, u32[]{:S(2)}) collective-permute-start(bf16[16,16,256]{2,1,0:T(8,128)(2,1)S(1)} %get-tuple-element.71), channel_id=1, source_target_pairs={{0,1},{1,0},{2,3},{3,2},{4,5},{5,4},{6,7},{7,6},{8,9},{9,8},{10,11... | collective-permute-start | bytes 393224 | tf_op jit(solution)/shard_map/ppermute | solution.py:460
  34.7 6.8 %collective-permute-start.12 = (bf16[16,16,256]{2,1,0:T(8,128)(2,1)S(1)}, bf16[16,16,256]{2,1,0:T(8,128)(2,1)S(1)}, u32[]{:S(2)}, u32[]{:S(2)}) collective-permute-start(bf16[16,16,256]{2,1,0:T(8,128)(2,1)S(1)} %get-tuple-element.73), channel_id=1, source_target_pairs={{0,3},{1,2},{2,1},{3,0},{4,7},{5,6},{6,5},{7,4},{8,11},{9,10},{10,... | collective-permute-start | bytes 393224 | tf_op jit(solution)/shard_map/ppermute | solution.py:460
  42.1 1.5 %collective-permute-start.13 = (bf16[4,5,16,256]{3,2,1,0:T(8,128)(2,1)S(1)}, bf16[4,5,16,256]{3,2,1,0:T(8,128)(2,1)S(1)}, u32[]{:S(2)}, u32[]{:S(2)}) collective-permute-start(bf16[4,5,16,256]{3,2,1,0:T(8,128)(2,1)S(1)} %get-tuple-element.75), channel_id=1, source_target_pairs={{0,4},{4,0},{8,12},{12,8},{16,20},{20,16},{24,28},{28,24},{1,5},{5... | collective-permute-start | bytes 491528 | tf_op jit(solution)/shard_map/ppermute | solution.py:474
  43.6 7.0 %collective-permute-start.14 = (bf16[2,5,16,256]{3,2,1,0:T(8,128)(2,1)S(1)}, bf16[2,5,16,256]{3,2,1,0:T(8,128)(2,1)S(1)}, u32[]{:S(2)}, u32[]{:S(2)}) collective-permute-start(bf16[2,5,16,256]{3,2,1,0:T(8,128)(2,1)S(1)} %get-tuple-element.78), channel_id=1, source_target_pairs={{0,24},{4,28},{8,16},{12,20},{16,8},{20,12},{24,0},{28,4},{1,25},{... | collective-permute-start | bytes 245768 | tf_op jit(solution)/shard_map/ppermute | solution.py:482
  46.0 5.0 %collective-permute-start.15 = (bf16[2,5,16,256]{3,2,1,0:T(8,128)(2,1)S(1)}, bf16[2,5,16,256]{3,2,1,0:T(8,128)(2,1)S(1)}, u32[]{:S(2)}, u32[]{:S(2)}) collective-permute-start(bf16[2,5,16,256]{3,2,1,0:T(8,128)(2,1)S(1)} %get-tuple-element.79), channel_id=1, source_target_pairs={{0,16},{4,20},{8,24},{12,28},{16,0},{20,4},{24,8},{28,12},{1,17},{... | collective-permute-start | bytes 245768 | tf_op jit(solution)/shard_map/ppermute | solution.py:482
  46.6 4.5 %collective-permute-start.16 = (bf16[2,5,16,256]{3,2,1,0:T(8,128)(2,1)S(1)}, bf16[2,5,16,256]{3,2,1,0:T(8,128)(2,1)S(1)}, u32[]{:S(2)}, u32[]{:S(2)}) collective-permute-start(bf16[2,5,16,256]{3,2,1,0:T(8,128)(2,1)S(1)} %get-tuple-element.80), channel_id=1, source_target_pairs={{0,8},{4,12},{8,0},{12,4},{16,24},{20,28},{24,16},{28,20},{1,9},{5... | collective-permute-start | bytes 245768 | tf_op jit(solution)/shard_map/ppermute | solution.py:482
  51.6 5.9 %collective-permute-start.17 = (bf16[4,16,256]{2,1,0:T(8,128)(2,1)S(1)}, bf16[4,16,256]{2,1,0:T(8,128)(2,1)S(1)}, u32[]{:S(2)}, u32[]{:S(2)}) collective-permute-start(bf16[4,16,256]{2,1,0:T(8,128)(2,1)S(1)} %get-tuple-element.82), channel_id=1, source_target_pairs={{0,3},{1,2},{2,1},{3,0},{4,7},{5,6},{6,5},{7,4},{8,11},{9,10},{10,... | collective-permute-start | bytes 98312 | tf_op jit(solution)/shard_map/ppermute | solution.py:460
  53.4 4.9 %collective-permute-start.18 = (bf16[4,16,256]{2,1,0:T(8,128)(2,1)S(1)}, bf16[4,16,256]{2,1,0:T(8,128)(2,1)S(1)}, u32[]{:S(2)}, u32[]{:S(2)}) collective-permute-start(bf16[4,16,256]{2,1,0:T(8,128)(2,1)S(1)} %get-tuple-element.83), channel_id=1, source_target_pairs={{0,2},{1,3},{2,0},{3,1},{4,6},{5,7},{6,4},{7,5},{8,10},{9,11},{10,... | collective-permute-start | bytes 98312 | tf_op jit(solution)/shard_map/ppermute | solution.py:460
  54.2 4.3 %collective-permute-start.19 = (bf16[4,16,256]{2,1,0:T(8,128)(2,1)S(1)}, bf16[4,16,256]{2,1,0:T(8,128)(2,1)S(1)}, u32[]{:S(2)}, u32[]{:S(2)}) collective-permute-start(bf16[4,16,256]{2,1,0:T(8,128)(2,1)S(1)} %get-tuple-element.84), channel_id=1, source_target_pairs={{0,1},{1,0},{2,3},{3,2},{4,5},{5,4},{6,7},{7,6},{8,9},{9,8},{10,11... | collective-permute-start | bytes 98312 | tf_op jit(solution)/shard_map/ppermute | solution.py:460

commit v9 on v8

--- a/solution.py
+++ b/solution.py
@@ -78,17 +78,7 @@
         yield t, g, m
 
 
-def weighted_sums(size, gains):
-    sub = lax.broadcasted_iota(jnp.int32, (8, TILE), 0)
-    gains = jnp.abs(gains)
-    left = jnp.where(sub == 0, gains[0:1, :], jnp.where(sub == 1, gains[1:2, :], 0.0))
-    high = left.astype(BF16).astype(F32)
-    halves = jnp.concatenate([high, left - high], axis=0).astype(BF16)
-    rows, cols = times_t(halves, size), times(halves, size)
-    return (rows[1:2] + rows[9:10]) * gains[0:1, :], (cols[0:1] + cols[8:9]) * gains[1:2, :]
-
-
-def remote_degree_kernel(weights, gains, groups, coords, near_weights, row_degree, tiles, held, *refs):
+def remote_degree_kernel(weights, gains, groups, coords, near_weights, tiles, held, *refs):
     *outs, tile_gains, tile_groups, tile_coords, staged, count, sems = refs
     group_count = staged.shape[0]
     wait = fetch(
@@ -103,15 +93,12 @@
     blank = jnp.where((sub >= MOST) & (sub < 2 * MOST), -1.0, 0.0).astype(F32)
     for g in range(group_count):
         staged[g] = blank
-    row_degree[...] = jnp.zeros(row_degree.shape, F32)
     core = lax.axis_index("rows") % 2
     wait()
     for t, g, m in slots_of(tile_groups, count, tiles.shape[0], group_count):
         place = place_of(g, group_count, core)
-        r, c = tile_coords[0, 0, 0, t], tile_coords[0, 0, 1, t]
-        by_row, by_col = weighted_sums(jnp.abs(tiles[t]), tile_gains[0, 0, t])
-        row_degree[pl.ds(r, 1), :] += by_row
-        staged[place, pl.ds(m, 1), :] = by_col
+        c = tile_coords[0, 0, 1, t]
+        staged[place, pl.ds(m, 1), :] = column_sums(jnp.abs(tiles[t]), jnp.abs(tile_gains[0, 0, t]))
         staged[place, pl.ds(MOST + m, 1), :] = jnp.full((1, TILE), c, jnp.int32).astype(F32)
     split_out(staged, outs)
     wait_held()
@@ -129,47 +116,75 @@
     return times(chosen, high) + times(chosen, low)
 
 
-def local_degree_kernel(
-    held, weights, gains, coords, degree, tiles, by_row, by_col, sems
+def column_sums(size, pair):
+    top = lax.broadcasted_iota(jnp.int32, (8, TILE), 0) == 0
+    left = jnp.where(top, pair[0:1, :], 0.0)
+    high = left.astype(BF16).astype(F32)
+    sums = times(jnp.concatenate([high, left - high], axis=0).astype(BF16), size)
+    return (sums[0:1] + sums[8:9]) * pair[1:2, :]
+
+
+def spread_row_sums(by_row, t, size, pair):
+    sums = jnp.sum(size.astype(F32) * pair[1:2, :], axis=1, keepdims=True)
+    lane = lax.broadcasted_iota(jnp.int32, by_row.shape, 1)
+    by_row[...] = jnp.where(lane == t, sums, by_row[...])
+
+
+def rows_by_place(by_row, gains, places):
+    count = gains.shape[0]
+    return add_by_place(places, jnp.transpose(by_row[...])[:count] * jnp.abs(gains))
+
+
+def early_degree_kernel(
+    remote, remote_gains, remote_coords, held, gains, coords, degree, remote_row, by_row, by_col
 ):
-    first, count = held.shape[0], weights.shape[2]
+    remote_row[...] = jnp.zeros(remote_row.shape, F32)
+    by_row[...] = jnp.zeros(by_row.shape, F32)
+
+    def remote_step(n, _):
+        for k in range(CHUNK):
+            t = n * CHUNK + k
+            pair = jnp.abs(remote_gains[0, 0, t])
+            spread_row_sums(remote_row, t, jnp.abs(remote[t]), pair)
+        return 0
+
+    lax.fori_loop(0, remote.shape[0] // CHUNK, remote_step, 0)
+    count = held.shape[0]
+    for t in range(count):
+        size, pair = jnp.abs(held[t]), jnp.abs(gains[0, 0, t])
+        by_col[t : t + 1, :] = column_sums(size, pair)
+        spread_row_sums(by_row, t, size, pair)
+    degree[...] = (
+        rows_by_place(remote_row, remote_gains[0, 0, :, 0, :], remote_coords[0, 0, 0:1, :])
+        + rows_by_place(by_row, gains[0, 0, :count, 0, :], coords[0, 0, 0:1, :count])
+        + add_by_place(coords[0, 0, 1:2, :count], by_col[...])
+    )
+
+
+def local_degree_kernel(first, weights, gains, coords, degree, tiles, by_row, by_col, sems):
+    count = tiles.shape[0]
 
     def copy_of(n):
         source = weights.at[0, 0, pl.ds(first + n * CHUNK, CHUNK)]
         return pltpu.make_async_copy(source, tiles.at[pl.ds(n * CHUNK, CHUNK)], sems.at[n])
 
-    for n in range((count - first) // CHUNK):
+    for n in range(count // CHUNK):
         copy_of(n).start()
     by_row[...] = jnp.zeros(by_row.shape, F32)
-    top = lax.broadcasted_iota(jnp.int32, (8, TILE), 0) == 0
-    lane = lax.broadcasted_iota(jnp.int32, by_row.shape, 1)
-
-    def add(t, size):
-        pair = jnp.abs(gains[0, 0, t])
-        left = jnp.where(top, pair[0:1, :], 0.0)
-        high = left.astype(BF16).astype(F32)
-        sums = times(jnp.concatenate([high, left - high], axis=0).astype(BF16), size)
-        by_col[pl.ds(t, 1), :] = (sums[0:1] + sums[8:9]) * pair[1:2, :]
-        sums = jnp.sum(size.astype(F32) * pair[1:2, :], axis=1, keepdims=True)
-        by_row[...] = jnp.where(lane == t, sums, by_row[...])
-
-    def held_step(n, _):
-        for k in range(CHUNK):
-            add(n * CHUNK + k, jnp.abs(held[n * CHUNK + k]))
-        return 0
 
     def step(n, _):
         copy_of(n).wait()
         for k in range(CHUNK):
-            add(first + n * CHUNK + k, jnp.abs(tiles[n * CHUNK + k]))
+            t = n * CHUNK + k
+            size, pair = jnp.abs(tiles[t]), jnp.abs(gains[0, 0, first + t])
+            by_col[pl.ds(t, 1), :] = column_sums(size, pair)
+            spread_row_sums(by_row, t, size, pair)
         return 0
 
-    lax.fori_loop(0, first // CHUNK, held_step, 0)
-    lax.fori_loop(0, (count - first) // CHUNK, step, 0)
-    row_sums = jnp.transpose(by_row[...])[:count] * jnp.abs(gains[0, 0, :, 0, :])
-    degree[...] = add_by_place(coords[0, 0, 0:1, :], row_sums) + add_by_place(
-        coords[0, 0, 1:2, :], by_col[...]
-    )
+    lax.fori_loop(0, count // CHUNK, step, 0)
+    degree[...] = rows_by_place(
+        by_row, gains[0, 0, first:, 0, :], coords[0, 0, 0:1, first:]
+    ) + add_by_place(coords[0, 0, 1:2, first:], by_col[...])
 
 
 def scale_kernel(raw, gains, scaled):
@@ -193,11 +208,11 @@
     )(raw, gains)
 
 
-def join_degree_kernel(row_degree, local_degree, *refs):
+def join_degree_kernel(early, late, *refs):
     *arrived, joined, targets, sums = refs
     by_group(arrived, sums)
     targets[...] = sums[...].astype(jnp.int32)
-    total = row_degree[...] + local_degree[...]
+    total = early[...] + late[...]
     sub = lax.broadcasted_iota(jnp.int32, total.shape, 0).astype(F32)
     for g in range(sums.shape[0]):
         block = sums[g]
@@ -410,14 +425,13 @@
 def last_quarter_kernel(splits, vertices, inv_root, inverse, *refs):
     pieces, (image_out, grams) = refs[:splits], refs[splits:]
     images, _ = quarter_sum(pieces, inv_root, lax.axis_index("cols"))
-    first = inverse[...]
-    gram = jnp.zeros((WIDTH, WIDTH), F32)
-    for k, image in enumerate(images):
-        value = jnp.dot(first, image, precision=HIGHEST, preferred_element_type=F32)
-        image_out[:, k * TILE : (k + 1) * TILE] = value
-        gram += lax.dot_general(
-            value, value, (((1,), (1,)), ((), ())), precision=HIGHEST, preferred_element_type=F32
-        )
+    image = jnp.dot(
+        inverse[...], jnp.concatenate(images, axis=1), precision=HIGHEST, preferred_element_type=F32
+    )
+    image_out[...] = image
+    gram = lax.dot_general(
+        image, image, (((1,), (1,)), ((), ())), precision=HIGHEST, preferred_element_type=F32
+    )
     gram = gram / vertices
     block = jnp.concatenate([gram[2 * n : 2 * n + 2] for n in range(WIDTH // 2)], axis=1)
     for n in range(grams.shape[0]):
@@ -484,10 +498,9 @@
         ]
 
     listing = (remote_weights, remote_gains, remote_groups, remote_coords, local_weights)
-    row_degree, remote_raw, held, *sent = call(
+    remote_raw, held, *sent = call(
         remote_degree_kernel,
         (
-            shape((BR, TILE)),
             shape((remote_tiles, TILE, TILE), BF16),
             shape((HEAD, TILE, TILE), BF16),
         )
@@ -503,26 +516,34 @@
         ],
         name="remote_degree",
     )(*[in_hbm(value) for value in listing])
-    sums_in = exchange(sent)
-    local_degree, local_raw = call(
-        local_degree_kernel,
+    lanes = pltpu.VMEM((TILE, LANES), F32)
+    early_degree = call(
+        early_degree_kernel,
+        shape((BR, TILE)),
+        [vmem] * 6,
+        [lanes, lanes, pltpu.VMEM((HEAD, TILE), F32)],
+        name="early_degree",
+    )(remote_raw, remote_gains, remote_coords, held, local_gains, local_coords)
+    sums_in = exchange(sent, (early_degree,))
+    late_degree, local_raw = call(
+        functools.partial(local_degree_kernel, HEAD),
         (shape((BR, TILE)), shape((local_tiles - HEAD, TILE, TILE), BF16)),
-        [vmem, hbm, vmem, vmem],
+        [hbm, vmem, vmem],
         [
-            pltpu.VMEM((TILE, -(-local_tiles // LANES) * LANES), F32),
-            pltpu.VMEM((local_tiles, TILE), F32),
+            lanes,
+            pltpu.VMEM((local_tiles - HEAD, TILE), F32),
             pltpu.SemaphoreType.DMA(((local_tiles - HEAD) // CHUNK,)),
         ],
         moved=10**7,
         name="local_degree",
-    )(held, in_hbm(local_weights), local_gains, local_coords)
+    )(in_hbm(local_weights), local_gains, local_coords)
     joined, targets = call(
         join_degree_kernel,
         (shape((BR, TILE)), shape((groups, 8, TILE), jnp.int32)),
         [vmem] * (2 + len(sums_in)),
         [pltpu.VMEM((groups, 8, TILE), F32)],
         name="join_degree",
-    )(row_degree, local_degree, *sums_in)
+    )(early_degree, late_degree, *sums_in)
     far_scalars = [remote_groups, remote_coords, targets]
     joined, remote_gains, local_gains = lax.optimization_barrier(
         (joined, remote_gains, local_gains)

time: 71.3 us -> 70.9 us (level)
  waiting for transfers between devices: 17.4 us -> 16.6 us
    ppermute x3, waiting for transfers between devices: 1.37 us -> 0.51 us  [exchange(): passed = lax.ppermute(far, 'rows', [(j, j ^ 1) for j in range(groups)])]
    pallas_call x2 -> x3, Pallas kernels: 5.3 us -> 5.89 us  [the longest x1 3.44 us: per_device(): call(functools.partial(local_degree_kernel, HEAD), (shape((BR, TILE)), sh...]
  transfers between devices with their start and end apart: 20 -> 20, of which waited for: 14 -> 13; matrix products, arithmetic and copies ran while one was open for 0% -> 0% of each run, Pallas kernels for 20% -> 21%
where the time goes in v9:
time: 70.9 us; the launch traced here: 70.8 us
  starting transfers between devices  22.9 us (32%)
  Pallas kernels  20.2 us (28%)
  waiting for transfers between devices  16.6 us (23%)
  blocking collectives  10.8 us (15%)
    ppermute x8, waiting for transfers between devices, swap(): return lax.ppermute(value, 'cols', [(j, j ^ k) for j in range(splits)])  15.2 us
    ppermute x9, starting transfers between devices, exchange(): lax.ppermute(piece, 'rows', [(j, j ^ 2 * k) for j in range(groups)])  11.5 us
    all_to_all x1, blocking collectives, per_device(): lax.all_to_all(grams, ('rows', 'cols'), split_axis=0, concat_axis=0, tile...  10.8 us
    ppermute x8, starting transfers between devices, swap(): return lax.ppermute(value, 'cols', [(j, j ^ k) for j in range(splits)])  10.7 us
    pallas_call x4, Pallas kernels, local_products(): call(functools.partial(local_products_kernel, first), shape((BR, WIDTH, T...  9.05 us
    pallas_call x1, Pallas kernels, per_device(): call(functools.partial(local_degree_kernel, HEAD), (shape((BR, TILE)), sh...  3.44 us
    pallas_call x1, Pallas kernels, per_device(): call(remote_degree_kernel, (shape((remote_tiles, TILE, TILE), BF16), shap...  1.64 us
  transfers between devices with their start and end apart: 20, of which 13 were waited for; matrix products, arithmetic and copies ran while one was open for 0% of the time, Pallas kernels for 21%

profile of v9, /device:TPU:0, one launch (start us, length us, event | category | flops | bytes accessed | tf_op | source)
XLA Modules:
  0.0 70.8 jit_solution(653013415186084101)
XLA Ops:
  0.0 1.6 %remote_degree.1 = (bf16[8,256,256]{2,1,0:T(8,128)(2,1)S(1)}, bf16[8,256,256]{2,1,0:T(8,128)(2,1)S(1)}, f32[4,8,256]{2,1,0:T(8,128)S(1)}, f32[4,8,256]{2,1,0:T(8,128)S(1)}) custom-call(bf16[1,1,8,256,256]{4,3,2,1,0:T(8,128)(2,1)} %weights.2, f32[1,1,8,2,256]{4,3,2,1,0:T(2,128)} %gains.6, s32[1,1,8]{2,1,0:T(1,128)} %groups.9, s32[1,1,2,8]{3,2,1,0:T(2,128)} %bitcast.2, ...), custom_call_target="tpu_custom_call" | custom-call | flops 1000000 | bytes 1000000 | tf_op jit(solution)/shard_map/remote_degree/pallas_call | solution.py:501
  1.7 0.6 collective-permute-start
  2.3 0.8 %early_degree.1.refs_0_.early = f32[16,256]{1,0:T(8,128)S(1)} custom-call(bf16[8,256,256]{2,1,0:T(8,128)(2,1)S(1)} %get-tuple-element.45.remote.raw, f32[1,1,8,2,256]{4,3,2,1,0:T(2,128)S(1)} %copy-done.2, s32[1,1,2,8]{3,2,1,0:T(2,128)S(1)} %bitcast.3, bf16[8,256,256]{2,1,0:T(8,128)(2,1)S(1)} %get-tuple-element.46.held.raw, ...), custom_call_target="tpu_custom_call" | custom-call | flops 1000000 | bytes 1000000 | tf_op jit(solution)/shard_map/early_degree/pallas_call | solution.py:520
  3.1 3.8 %collective-permute-start.1 = (f32[2,8,256]{2,1,0:T(8,128)S(1)}, f32[2,8,256]{2,1,0:T(8,128)S(1)}, u32[]{:S(2)}, u32[]{:S(2)}) collective-permute-start(f32[2,8,256]{2,1,0:T(8,128)S(1)} %get-tuple-element.51), channel_id=1, source_target_pairs={{0,24},{4,28},{8,16},{12,20},{16,8},{20,12},{24,0},{28,4},{1,25},{... | collective-permute-start | bytes 49160 | tf_op jit(solution)/shard_map/ppermute | solution.py:496
  7.5 3.4 %local_degree.1 = (f32[16,256]{1,0:T(8,128)S(1)}, bf16[40,256,256]{2,1,0:T(8,128)(2,1)S(1)}) custom-call(bf16[1,1,48,256,256]{4,3,2,1,0:T(8,128)(2,1)} %weights.3, f32[1,1,48,2,256]{4,3,2,1,0:T(2,128)S(1)} %copy-done, s32[1,1,2,48]{3,2,1,0:T(2,128)S(1)} %bitcast.9), custom_call_target="tpu_custom_call" | custom-call | flops 1000000 | bytes 10000000 | tf_op jit(solution)/shard_map/local_degree/pallas_call | solution.py:528
  11.2 4.0 %collective-permute-start.6 = (f32[16,256]{1,0:T(8,128)S(1)}, f32[16,256]{1,0:T(8,128)S(1)}, u32[]{:S(2)}, u32[]{:S(2)}) collective-permute-start(f32[16,256]{1,0:T(8,128)S(1)} %get-tuple-element.58.refs_0_), channel_id=1, source_target_pairs={{0,3},{1,2},{2,1},{3,0},{4,7},{5,6},{6,5},{7,4},{8,11},{9,10},{10,... | collective-permute-start | bytes 49160 | tf_op jit(solution)/shard_map/ppermute | solution.py:474
  15.1 0.6 collective-permute-start.4
  16.3 0.5 local_scale.1.later.tiles
  17.0 2.8 %collective-permute-done.5.refs_2_ = f32[16,256]{1,0:T(8,128)S(1)} collective-permute-done((f32[16,256]{1,0:T(8,128)S(1)}, f32[16,256]{1,0:T(8,128)S(1)}, u32[]{:S(2)}, u32[]{:S(2)}) %collective-permute-start.5) | collective-permute-done | bytes 16416 | tf_op jit(solution)/shard_map/ppermute | solution.py:474
  20.2 1.1 %local_products.4.refs_1_.refs_0_ = f32[16,16,256]{2,1,0:T(8,128)S(1)} custom-call(bf16[16,16,256]{2,1,0:T(8,128)(2,1)S(1)} %get-tuple-element.60.x, bf16[8,256,256]{2,1,0:T(8,128)(2,1)S(1)} %local_scale.1.later.tiles, s32[1,1,2,48]{3,2,1,0:T(2,128)S(1)} %bitcast.10), custom_call_target="tpu_custom_call" | custom-call | flops 33554432 | bytes 1048576 | tf_op jit(solution)/shard_map/local_products/pallas_call | solution.py:568
  21.6 2.5 %collective-permute-start.8 = (bf16[2,4,16,256]{3,2,1,0:T(8,128)(2,1)S(1)}, bf16[2,4,16,256]{3,2,1,0:T(8,128)(2,1)S(1)}, u32[]{:S(2)}, u32[]{:S(2)}) collective-permute-start(bf16[2,4,16,256]{3,2,1,0:T(8,128)(2,1)S(1)} %get-tuple-element.65), channel_id=1, source_target_pairs={{0,24},{4,28},{8,16},{12,20},{16,8},{20,12},{24,0},{28,4},{1,25},{... | collective-permute-start | bytes 196616 | tf_op jit(solution)/shard_map/ppermute | solution.py:496
  24.6 0.5 collective-permute-start.10
  25.1 3.4 %local_products.5.partial = f32[16,16,256]{2,1,0:T(8,128)S(1)} custom-call(bf16[16,16,256]{2,1,0:T(8,128)(2,1)S(1)} %get-tuple-element.60.x, bf16[40,256,256]{2,1,0:T(8,128)(2,1)S(1)} %get-tuple-element.61.tiles, s32[1,1,2,48]{3,2,1,0:T(2,128)S(1)} %bitcast.11, f32[1,1,48,2,256]{4,3,2,1,0:T(2,128)S(1)} %copy-done, ...), custom_call_target="tpu_custom_call" | custom-call | flops 167772160 | bytes 5242880 | tf_op jit(solution)/shard_map/local_products/pallas_call | solution.py:568
  28.9 0.5 remote_products.2
  29.5 5.0 %collective-permute-done.11.theirs = bf16[16,16,256]{2,1,0:T(8,128)(2,1)S(1)} collective-permute-done((bf16[16,16,256]{2,1,0:T(8,128)(2,1)S(1)}, bf16[16,16,256]{2,1,0:T(8,128)(2,1)S(1)}, u32[]{:S(2)}, u32[]{:S(2)}) %collective-permute-start.11) | collective-permute-done | bytes 131104 | tf_op jit(solution)/shard_map/ppermute | solution.py:474
  34.5 1.5 %collective-permute-start.12 = (bf16[16,16,256]{2,1,0:T(8,128)(2,1)S(1)}, bf16[16,16,256]{2,1,0:T(8,128)(2,1)S(1)}, u32[]{:S(2)}, u32[]{:S(2)}) collective-permute-start(bf16[16,16,256]{2,1,0:T(8,128)(2,1)S(1)} %get-tuple-element.71), channel_id=1, source_target_pairs={{0,3},{1,2},{2,1},{3,0},{4,7},{5,6},{6,5},{7,4},{8,11},{9,10},{10,... | collective-permute-start | bytes 393224 | tf_op jit(solution)/shard_map/ppermute | solution.py:474
  36.0 5.3 %collective-permute-done.12.theirs = bf16[16,16,256]{2,1,0:T(8,128)(2,1)S(1)} collective-permute-done((bf16[16,16,256]{2,1,0:T(8,128)(2,1)S(1)}, bf16[16,16,256]{2,1,0:T(8,128)(2,1)S(1)}, u32[]{:S(2)}, u32[]{:S(2)}) %collective-permute-start.12) | collective-permute-done | bytes 131104 | tf_op jit(solution)/shard_map/ppermute | solution.py:474
  41.3 0.5 next_block.1
  42.0 1.1 %local_products.6.refs_0_.refs_1_ = f32[16,16,256]{2,1,0:T(8,128)S(1)} custom-call(bf16[16,16,256]{2,1,0:T(8,128)(2,1)S(1)} %get-tuple-element.74.x, bf16[8,256,256]{2,1,0:T(8,128)(2,1)S(1)} %local_scale.1.later.tiles, s32[1,1,2,48]{3,2,1,0:T(2,128)S(1)} %bitcast.12), custom_call_target="tpu_custom_call" | custom-call | flops 33554432 | bytes 1048576 | tf_op jit(solution)/shard_map/local_products/pallas_call | solution.py:568
  43.4 2.3 %collective-permute-start.14 = (bf16[2,5,16,256]{3,2,1,0:T(8,128)(2,1)S(1)}, bf16[2,5,16,256]{3,2,1,0:T(8,128)(2,1)S(1)}, u32[]{:S(2)}, u32[]{:S(2)}) collective-permute-start(bf16[2,5,16,256]{3,2,1,0:T(8,128)(2,1)S(1)} %get-tuple-element.76), channel_id=1, source_target_pairs={{0,24},{4,28},{8,16},{12,20},{16,8},{20,12},{24,0},{28,4},{1,25},{... | collective-permute-start | bytes 245768 | tf_op jit(solution)/shard_map/ppermute | solution.py:496
  45.7 0.7 collective-permute-start.15
  46.4 0.6 collective-permute-start.16
  46.9 3.4 %local_products.7.partial = f32[16,16,256]{2,1,0:T(8,128)S(1)} custom-call(bf16[16,16,256]{2,1,0:T(8,128)(2,1)S(1)} %get-tuple-element.74.x, bf16[40,256,256]{2,1,0:T(8,128)(2,1)S(1)} %get-tuple-element.61.tiles, s32[1,1,2,48]{3,2,1,0:T(2,128)S(1)} %bitcast.13, f32[1,1,48,2,256]{4,3,2,1,0:T(2,128)S(1)} %copy-done, ...), custom_call_target="tpu_custom_call" | custom-call | flops 167772160 | bytes 5242880 | tf_op jit(solution)/shard_map/local_products/pallas_call | solution.py:568
  50.9 0.5 remote_products.3
  51.4 1.7 %collective-permute-start.17 = (bf16[4,16,256]{2,1,0:T(8,128)(2,1)S(1)}, bf16[4,16,256]{2,1,0:T(8,128)(2,1)S(1)}, u32[]{:S(2)}, u32[]{:S(2)}) collective-permute-start(bf16[4,16,256]{2,1,0:T(8,128)(2,1)S(1)} %get-tuple-element.80), channel_id=1, source_target_pairs={{0,3},{1,2},{2,1},{3,0},{4,7},{5,6},{6,5},{7,4},{8,11},{9,10},{10,... | collective-permute-start | bytes 98312 | tf_op jit(solution)/shard_map/ppermute | solution.py:474
  53.1 0.9 %collective-permute-start.18 = (bf16[4,16,256]{2,1,0:T(8,128)(2,1)S(1)}, bf16[4,16,256]{2,1,0:T(8,128)(2,1)S(1)}, u32[]{:S(2)}, u32[]{:S(2)}) collective-permute-start(bf16[4,16,256]{2,1,0:T(8,128)(2,1)S(1)} %get-tuple-element.81), channel_id=1, source_target_pairs={{0,2},{1,3},{2,0},{3,1},{4,6},{5,7},{6,4},{7,5},{8,10},{9,11},{10,... | collective-permute-start | bytes 98312 | tf_op jit(solution)/shard_map/ppermute | solution.py:474
  54.0 1.9 %collective-permute-start.19 = (bf16[4,16,256]{2,1,0:T(8,128)(2,1)S(1)}, bf16[4,16,256]{2,1,0:T(8,128)(2,1)S(1)}, u32[]{:S(2)}, u32[]{:S(2)}) collective-permute-start(bf16[4,16,256]{2,1,0:T(8,128)(2,1)S(1)} %get-tuple-element.82), channel_id=1, source_target_pairs={{0,1},{1,0},{2,3},{3,2},{4,5},{5,4},{6,7},{7,6},{8,9},{9,8},{10,11... | collective-permute-start | bytes 98312 | tf_op jit(solution)/shard_map/ppermute | solution.py:474
  56.2 1.1 %collective-permute-done.17.refs_1_ = bf16[4,16,256]{2,1,0:T(8,128)(2,1)S(1)} collective-permute-done((bf16[4,16,256]{2,1,0:T(8,128)(2,1)S(1)}, bf16[4,16,256]{2,1,0:T(8,128)(2,1)S(1)}, u32[]{:S(2)}, u32[]{:S(2)}) %collective-permute-start.17) | collective-permute-done | bytes 32800 | tf_op jit(solution)/shard_map/ppermute | solution.py:474
  57.4 0.6 collective-permute-done.18.refs_2_
  58.2 0.6 last_quarter.1
  58.8 10.8 %all_to_all.5.grams = f32[32,2,128]{2,1,0:T(2,128)S(1)} all-to-all(f32[32,2,128]{2,1,0:T(2,128)S(1)} %get-tuple-element.83), channel_id=1, replica_groups=mesh['rows'=8,'cols'=4] {'rows','cols'}, dimensions={0} | all-to-all | bytes 65536 | tf_op jit(solution)/shard_map/all_to_all | solution.py:635
  69.7 1.1 %finish.1 = f32[16,1024]{1,0:T(8,128)} custom-call(f32[32,2,128]{2,1,0:T(2,128)S(1)} %all_to_all.5.grams, f32[16,1024]{1,0:T(8,128)S(1)} %get-tuple-element.84.image), custom_call_target="tpu_custom_call" | custom-call | flops 1000000 | bytes 1000000 | tf_op jit(solution)/shard_map/finish/pallas_call | solution.py:638
  (42 shorter events, 4.7 us)
Async XLA Ops:
  0.0 2.2 %copy-start.2 = (f32[1,1,8,2,256]{4,3,2,1,0:T(2,128)S(1)}, f32[1,1,8,2,256]{4,3,2,1,0:T(2,128)}, u32[]{:S(2)}) copy-start(f32[1,1,8,2,256]{4,3,2,1,0:T(2,128)} %gains.6) | copy-start | bytes 49156
  0.0 2.2 %copy-start.3 = (s32[1,1,8,2]{2,3,1,0:T(2,128)S(1)}, s32[1,1,8,2]{2,3,1,0:T(2,128)}, u32[]{:S(2)}) copy-start(s32[1,1,8,2]{2,3,1,0:T(2,128)} %param.14) | copy-start | bytes 196
  0.0 2.2 %copy-start = (f32[1,1,48,2,256]{4,3,2,1,0:T(2,128)S(1)}, f32[1,1,48,2,256]{4,3,2,1,0:T(2,128)}, u32[]{:S(2)}) copy-start(f32[1,1,48,2,256]{4,3,2,1,0:T(2,128)} %refs_0_.1) | copy-start | bytes 294916
  0.0 2.2 %copy-start.4 = (s32[1,1,48,2]{2,3,1,0:T(2,128)S(1)}, s32[1,1,48,2]{2,3,1,0:T(2,128)}, u32[]{:S(2)}) copy-start(s32[1,1,48,2]{2,3,1,0:T(2,128)} %param.10) | copy-start | bytes 1156
  1.7 1.4 %collective-permute-start = (f32[4,8,256]{2,1,0:T(8,128)S(1)}, f32[4,8,256]{2,1,0:T(8,128)S(1)}, u32[]{:S(2)}, u32[]{:S(2)}) collective-permute-start(f32[4,8,256]{2,1,0:T(8,128)S(1)} %get-tuple-element.49), channel_id=1, source_target_pairs={{0,4},{4,0},{8,12},{12,8},{16,20},{20,16},{24,28},{28,24},{1,5},{5... | collective-permute-start | bytes 98312 | tf_op jit(solution)/shard_map/ppermute | solution.py:488
  2.2 17.5 %copy-start.1 = (f32[16,4096]{1,0:T(8,128)S(1)}, f32[16,4096]{1,0:T(8,128)}, u32[]{:S(2)}) copy-start(f32[16,4096]{1,0:T(8,128)} %start.1) | copy-start | bytes 786436
  2.2 17.5 %copy-start.5 = (s32[1,1,8]{2,1,0:T(1,128)S(1)}, s32[1,1,8]{2,1,0:T(1,128)}, u32[]{:S(2)}) copy-start(s32[1,1,8]{2,1,0:T(1,128)} %groups.9) | copy-start | bytes 100
  3.1 7.9 %collective-permute-start.1 = (f32[2,8,256]{2,1,0:T(8,128)S(1)}, f32[2,8,256]{2,1,0:T(8,128)S(1)}, u32[]{:S(2)}, u32[]{:S(2)}) collective-permute-start(f32[2,8,256]{2,1,0:T(8,128)S(1)} %get-tuple-element.51), channel_id=1, source_target_pairs={{0,24},{4,28},{8,16},{12,20},{16,8},{20,12},{24,0},{28,4},{1,25},{... | collective-permute-start | bytes 49160 | tf_op jit(solution)/shard_map/ppermute | solution.py:496
  6.9 4.1 %collective-permute-start.2 = (f32[2,8,256]{2,1,0:T(8,128)S(1)}, f32[2,8,256]{2,1,0:T(8,128)S(1)}, u32[]{:S(2)}, u32[]{:S(2)}) collective-permute-start(f32[2,8,256]{2,1,0:T(8,128)S(1)} %get-tuple-element.52), channel_id=1, source_target_pairs={{0,16},{4,20},{8,24},{12,28},{16,0},{20,4},{24,8},{28,12},{1,17},{... | collective-permute-start | bytes 49160 | tf_op jit(solution)/shard_map/ppermute | solution.py:496
  7.4 3.7 %collective-permute-start.3 = (f32[2,8,256]{2,1,0:T(8,128)S(1)}, f32[2,8,256]{2,1,0:T(8,128)S(1)}, u32[]{:S(2)}, u32[]{:S(2)}) collective-permute-start(f32[2,8,256]{2,1,0:T(8,128)S(1)} %get-tuple-element.53), channel_id=1, source_target_pairs={{0,8},{4,12},{8,0},{12,4},{16,24},{20,28},{24,16},{28,20},{1,9},{5... | collective-permute-start | bytes 49160 | tf_op jit(solution)/shard_map/ppermute | solution.py:496
  11.2 5.8 %collective-permute-start.6 = (f32[16,256]{1,0:T(8,128)S(1)}, f32[16,256]{1,0:T(8,128)S(1)}, u32[]{:S(2)}, u32[]{:S(2)}) collective-permute-start(f32[16,256]{1,0:T(8,128)S(1)} %get-tuple-element.58.refs_0_), channel_id=1, source_target_pairs={{0,3},{1,2},{2,1},{3,0},{4,7},{5,6},{6,5},{7,4},{8,11},{9,10},{10,... | collective-permute-start | bytes 49160 | tf_op jit(solution)/shard_map/ppermute | solution.py:474
  15.1 4.6 %collective-permute-start.5 = (f32[16,256]{1,0:T(8,128)S(1)}, f32[16,256]{1,0:T(8,128)S(1)}, u32[]{:S(2)}, u32[]{:S(2)}) collective-permute-start(f32[16,256]{1,0:T(8,128)S(1)} %get-tuple-element.58.refs_0_), channel_id=1, source_target_pairs={{0,2},{1,3},{2,0},{3,1},{4,6},{5,7},{6,4},{7,5},{8,10},{9,11},{10,... | collective-permute-start | bytes 49160 | tf_op jit(solution)/shard_map/ppermute | solution.py:474
  15.1 4.6 %collective-permute-start.4 = (f32[16,256]{1,0:T(8,128)S(1)}, f32[16,256]{1,0:T(8,128)S(1)}, u32[]{:S(2)}, u32[]{:S(2)}) collective-permute-start(f32[16,256]{1,0:T(8,128)S(1)} %get-tuple-element.58.refs_0_), channel_id=1, source_target_pairs={{0,1},{1,0},{2,3},{3,2},{4,5},{5,4},{6,7},{7,6},{8,9},{9,8},{10,11... | collective-permute-start | bytes 49160 | tf_op jit(solution)/shard_map/ppermute | solution.py:474
  20.1 1.4 %collective-permute-start.7 = (bf16[4,4,16,256]{3,2,1,0:T(8,128)(2,1)S(1)}, bf16[4,4,16,256]{3,2,1,0:T(8,128)(2,1)S(1)}, u32[]{:S(2)}, u32[]{:S(2)}) collective-permute-start(bf16[4,4,16,256]{3,2,1,0:T(8,128)(2,1)S(1)} %get-tuple-element.63), channel_id=1, source_target_pairs={{0,4},{4,0},{8,12},{12,8},{16,20},{20,16},{24,28},{28,24},{1,5},{5... | collective-permute-start | bytes 393224 | tf_op jit(solution)/shard_map/ppermute | solution.py:488
  21.6 7.0 %collective-permute-start.8 = (bf16[2,4,16,256]{3,2,1,0:T(8,128)(2,1)S(1)}, bf16[2,4,16,256]{3,2,1,0:T(8,128)(2,1)S(1)}, u32[]{:S(2)}, u32[]{:S(2)}) collective-permute-start(bf16[2,4,16,256]{3,2,1,0:T(8,128)(2,1)S(1)} %get-tuple-element.65), channel_id=1, source_target_pairs={{0,24},{4,28},{8,16},{12,20},{16,8},{20,12},{24,0},{28,4},{1,25},{... | collective-permute-start | bytes 196616 | tf_op jit(solution)/shard_map/ppermute | solution.py:496
  24.1 4.5 %collective-permute-start.9 = (bf16[2,4,16,256]{3,2,1,0:T(8,128)(2,1)S(1)}, bf16[2,4,16,256]{3,2,1,0:T(8,128)(2,1)S(1)}, u32[]{:S(2)}, u32[]{:S(2)}) collective-permute-start(bf16[2,4,16,256]{3,2,1,0:T(8,128)(2,1)S(1)} %get-tuple-element.66), channel_id=1, source_target_pairs={{0,16},{4,20},{8,24},{12,28},{16,0},{20,4},{24,8},{28,12},{1,17},{... | collective-permute-start | bytes 196616 | tf_op jit(solution)/shard_map/ppermute | solution.py:496
  24.6 4.3 %collective-permute-start.10 = (bf16[2,4,16,256]{3,2,1,0:T(8,128)(2,1)S(1)}, bf16[2,4,16,256]{3,2,1,0:T(8,128)(2,1)S(1)}, u32[]{:S(2)}, u32[]{:S(2)}) collective-permute-start(bf16[2,4,16,256]{3,2,1,0:T(8,128)(2,1)S(1)} %get-tuple-element.67), channel_id=1, source_target_pairs={{0,8},{4,12},{8,0},{12,4},{16,24},{20,28},{24,16},{28,20},{1,9},{5... | collective-permute-start | bytes 196616 | tf_op jit(solution)/shard_map/ppermute | solution.py:496
  29.4 5.0 %collective-permute-start.11 = (bf16[16,16,256]{2,1,0:T(8,128)(2,1)S(1)}, bf16[16,16,256]{2,1,0:T(8,128)(2,1)S(1)}, u32[]{:S(2)}, u32[]{:S(2)}) collective-permute-start(bf16[16,16,256]{2,1,0:T(8,128)(2,1)S(1)} %get-tuple-element.69), channel_id=1, source_target_pairs={{0,1},{1,0},{2,3},{3,2},{4,5},{5,4},{6,7},{7,6},{8,9},{9,8},{10,11... | collective-permute-start | bytes 393224 | tf_op jit(solution)/shard_map/ppermute | solution.py:474
  34.5 6.8 %collective-permute-start.12 = (bf16[16,16,256]{2,1,0:T(8,128)(2,1)S(1)}, bf16[16,16,256]{2,1,0:T(8,128)(2,1)S(1)}, u32[]{:S(2)}, u32[]{:S(2)}) collective-permute-start(bf16[16,16,256]{2,1,0:T(8,128)(2,1)S(1)} %get-tuple-element.71), channel_id=1, source_target_pairs={{0,3},{1,2},{2,1},{3,0},{4,7},{5,6},{6,5},{7,4},{8,11},{9,10},{10,... | collective-permute-start | bytes 393224 | tf_op jit(solution)/shard_map/ppermute | solution.py:474
  41.9 1.5 %collective-permute-start.13 = (bf16[4,5,16,256]{3,2,1,0:T(8,128)(2,1)S(1)}, bf16[4,5,16,256]{3,2,1,0:T(8,128)(2,1)S(1)}, u32[]{:S(2)}, u32[]{:S(2)}) collective-permute-start(bf16[4,5,16,256]{3,2,1,0:T(8,128)(2,1)S(1)} %get-tuple-element.73), channel_id=1, source_target_pairs={{0,4},{4,0},{8,12},{12,8},{16,20},{20,16},{24,28},{28,24},{1,5},{5... | collective-permute-start | bytes 491528 | tf_op jit(solution)/shard_map/ppermute | solution.py:488
  43.4 7.0 %collective-permute-start.14 = (bf16[2,5,16,256]{3,2,1,0:T(8,128)(2,1)S(1)}, bf16[2,5,16,256]{3,2,1,0:T(8,128)(2,1)S(1)}, u32[]{:S(2)}, u32[]{:S(2)}) collective-permute-start(bf16[2,5,16,256]{3,2,1,0:T(8,128)(2,1)S(1)} %get-tuple-element.76), channel_id=1, source_target_pairs={{0,24},{4,28},{8,16},{12,20},{16,8},{20,12},{24,0},{28,4},{1,25},{... | collective-permute-start | bytes 245768 | tf_op jit(solution)/shard_map/ppermute | solution.py:496
  45.7 5.0 %collective-permute-start.15 = (bf16[2,5,16,256]{3,2,1,0:T(8,128)(2,1)S(1)}, bf16[2,5,16,256]{3,2,1,0:T(8,128)(2,1)S(1)}, u32[]{:S(2)}, u32[]{:S(2)}) collective-permute-start(bf16[2,5,16,256]{3,2,1,0:T(8,128)(2,1)S(1)} %get-tuple-element.77), channel_id=1, source_target_pairs={{0,16},{4,20},{8,24},{12,28},{16,0},{20,4},{24,8},{28,12},{1,17},{... | collective-permute-start | bytes 245768 | tf_op jit(solution)/shard_map/ppermute | solution.py:496
  46.4 4.5 %collective-permute-start.16 = (bf16[2,5,16,256]{3,2,1,0:T(8,128)(2,1)S(1)}, bf16[2,5,16,256]{3,2,1,0:T(8,128)(2,1)S(1)}, u32[]{:S(2)}, u32[]{:S(2)}) collective-permute-start(bf16[2,5,16,256]{3,2,1,0:T(8,128)(2,1)S(1)} %get-tuple-element.78), channel_id=1, source_target_pairs={{0,8},{4,12},{8,0},{12,4},{16,24},{20,28},{24,16},{28,20},{1,9},{5... | collective-permute-start | bytes 245768 | tf_op jit(solution)/shard_map/ppermute | solution.py:496
  51.4 6.0 %collective-permute-start.17 = (bf16[4,16,256]{2,1,0:T(8,128)(2,1)S(1)}, bf16[4,16,256]{2,1,0:T(8,128)(2,1)S(1)}, u32[]{:S(2)}, u32[]{:S(2)}) collective-permute-start(bf16[4,16,256]{2,1,0:T(8,128)(2,1)S(1)} %get-tuple-element.80), channel_id=1, source_target_pairs={{0,3},{1,2},{2,1},{3,0},{4,7},{5,6},{6,5},{7,4},{8,11},{9,10},{10,... | collective-permute-start | bytes 98312 | tf_op jit(solution)/shard_map/ppermute | solution.py:474
  53.1 4.9 %collective-permute-start.18 = (bf16[4,16,256]{2,1,0:T(8,128)(2,1)S(1)}, bf16[4,16,256]{2,1,0:T(8,128)(2,1)S(1)}, u32[]{:S(2)}, u32[]{:S(2)}) collective-permute-start(bf16[4,16,256]{2,1,0:T(8,128)(2,1)S(1)} %get-tuple-element.81), channel_id=1, source_target_pairs={{0,2},{1,3},{2,0},{3,1},{4,6},{5,7},{6,4},{7,5},{8,10},{9,11},{10,... | collective-permute-start | bytes 98312 | tf_op jit(solution)/shard_map/ppermute | solution.py:474
  54.0 4.3 %collective-permute-start.19 = (bf16[4,16,256]{2,1,0:T(8,128)(2,1)S(1)}, bf16[4,16,256]{2,1,0:T(8,128)(2,1)S(1)}, u32[]{:S(2)}, u32[]{:S(2)}) collective-permute-start(bf16[4,16,256]{2,1,0:T(8,128)(2,1)S(1)} %get-tuple-element.82), channel_id=1, source_target_pairs={{0,1},{1,0},{2,3},{3,2},{4,5},{5,4},{6,7},{7,6},{8,9},{9,8},{10,11... | collective-permute-start | bytes 98312 | tf_op jit(solution)/shard_map/ppermute | solution.py:474

commit v10 on v9

--- a/solution.py
+++ b/solution.py
@@ -325,13 +325,14 @@
 
 
 def local_products_kernel(first, x, tiles, coords, *refs):
-    *refs, partial, tile_coords, sems = refs
+    *refs, partial, table = refs
     gains, earlier = refs or (None, None)
     count = tiles.shape[0]
     batch = next(size for size in (20, 16, CHUNK) if count % size == 0)
-    wait = fetch((coords,), (tile_coords,), sems)
     partial[...] = earlier[...] if refs else jnp.zeros(partial.shape, F32)
-    wait()
+    for t in range(first, first + count):
+        for side in range(2):
+            table[side, t] = coords[0, 0, side, t]
 
     def step(n, _):
         base = first + n * batch
@@ -343,7 +344,7 @@
         places, results = [], []
         for k in range(batch):
             t = base + k
-            r, c = tile_coords[0, 0, 0, t], tile_coords[0, 0, 1, t]
+            r, c = table[0, t], table[1, t]
             tile = tiles[n * batch + k]
             if refs:
                 row_gain = row_gains[k // CHUNK][:, k % CHUNK : k % CHUNK + 1]
@@ -568,11 +569,8 @@
         return call(
             functools.partial(local_products_kernel, first),
             shape((BR, WIDTH, TILE)),
-            [vmem, vmem, anywhere] + [vmem] * len(more),
-            [
-                pltpu.SMEM(local_coords.shape, jnp.int32),
-                pltpu.SemaphoreType.DMA((1,)),
-            ],
+            [vmem, vmem, vmem] + [vmem] * len(more),
+            [pltpu.SMEM((2, local_tiles), jnp.int32)],
             flops=4 * number * TILE * TILE * WIDTH,
             moved=2 * number * TILE * TILE,
             name="local_products",

time: 70.9 us -> 70.7 us (level)
  Pallas kernels: 20.2 us -> 18.4 us
  waiting for transfers between devices: 16.6 us -> 18.2 us
    pallas_call x4, Pallas kernels: 9.05 us -> 7.21 us  [local_products(): call(functools.partial(local_products_kernel, first), shape((BR, WIDTH, T...]
    ppermute x3, waiting for transfers between devices: 0.51 us -> 1.6 us  [exchange(): passed = lax.ppermute(far, 'rows', [(j, j ^ 1) for j in range(groups)])]
  transfers between devices with their start and end apart: 20 -> 20, of which waited for: 13 -> 14; matrix products, arithmetic and copies ran while one was open for 0% -> 0% of each run, Pallas kernels for 21% -> 18%
where the time goes in v10:
time: 70.7 us; the launch traced here: 70.5 us
  starting transfers between devices  22.9 us (32%)
  Pallas kernels  18.4 us (26%)
  waiting for transfers between devices  18.2 us (26%)
  blocking collectives  10.8 us (15%)
    ppermute x8, waiting for transfers between devices, swap(): return lax.ppermute(value, 'cols', [(j, j ^ k) for j in range(splits)])  15.1 us
    ppermute x9, starting transfers between devices, exchange(): lax.ppermute(piece, 'rows', [(j, j ^ 2 * k) for j in range(groups)])  11.5 us
    all_to_all x1, blocking collectives, per_device(): lax.all_to_all(grams, ('rows', 'cols'), split_axis=0, concat_axis=0, tile...  10.8 us
    ppermute x8, starting transfers between devices, swap(): return lax.ppermute(value, 'cols', [(j, j ^ k) for j in range(splits)])  10.6 us
    pallas_call x4, Pallas kernels, local_products(): call(functools.partial(local_products_kernel, first), shape((BR, WIDTH, T...  7.21 us
    pallas_call x1, Pallas kernels, per_device(): call(functools.partial(local_degree_kernel, HEAD), (shape((BR, TILE)), sh...  3.44 us
    pallas_call x1, Pallas kernels, per_device(): call(remote_degree_kernel, (shape((remote_tiles, TILE, TILE), BF16), shap...  1.64 us
    ppermute x3, waiting for transfers between devices, exchange(): passed = lax.ppermute(far, 'rows', [(j, j ^ 1) for j in range(groups)])  1.6 us
  transfers between devices with their start and end apart: 20, of which 14 were waited for; matrix products, arithmetic and copies ran while one was open for 0% of the time, Pallas kernels for 18%

profile of v10, /device:TPU:0, one launch (start us, length us, event | category | flops | bytes accessed | tf_op | source)
XLA Modules:
  0.0 70.5 jit_solution(16533087043876972148)
XLA Ops:
  0.0 1.6 %remote_degree.1 = (bf16[8,256,256]{2,1,0:T(8,128)(2,1)S(1)}, bf16[8,256,256]{2,1,0:T(8,128)(2,1)S(1)}, f32[4,8,256]{2,1,0:T(8,128)S(1)}, f32[4,8,256]{2,1,0:T(8,128)S(1)}) custom-call(bf16[1,1,8,256,256]{4,3,2,1,0:T(8,128)(2,1)} %weights.2, f32[1,1,8,2,256]{4,3,2,1,0:T(2,128)} %gains.6, s32[1,1,8]{2,1,0:T(1,128)} %groups.9, s32[1,1,2,8]{3,2,1,0:T(2,128)} %bitcast.2, ...), custom_call_target="tpu_custom_call" | custom-call | flops 1000000 | bytes 1000000 | tf_op jit(solution)/shard_map/remote_degree/pallas_call | solution.py:502
  1.7 0.6 collective-permute-start
  2.3 0.8 %early_degree.1.refs_0_.early = f32[16,256]{1,0:T(8,128)S(1)} custom-call(bf16[8,256,256]{2,1,0:T(8,128)(2,1)S(1)} %get-tuple-element.45.remote.raw, f32[1,1,8,2,256]{4,3,2,1,0:T(2,128)S(1)} %copy-done.2, s32[1,1,2,8]{3,2,1,0:T(2,128)S(1)} %bitcast.3, bf16[8,256,256]{2,1,0:T(8,128)(2,1)S(1)} %get-tuple-element.46.held.raw, ...), custom_call_target="tpu_custom_call" | custom-call | flops 1000000 | bytes 1000000 | tf_op jit(solution)/shard_map/early_degree/pallas_call | solution.py:521
  3.1 3.8 %collective-permute-start.1 = (f32[2,8,256]{2,1,0:T(8,128)S(1)}, f32[2,8,256]{2,1,0:T(8,128)S(1)}, u32[]{:S(2)}, u32[]{:S(2)}) collective-permute-start(f32[2,8,256]{2,1,0:T(8,128)S(1)} %get-tuple-element.51), channel_id=1, source_target_pairs={{0,24},{4,28},{8,16},{12,20},{16,8},{20,12},{24,0},{28,4},{1,25},{... | collective-permute-start | bytes 49160 | tf_op jit(solution)/shard_map/ppermute | solution.py:497
  7.5 3.4 %local_degree.1 = (f32[16,256]{1,0:T(8,128)S(1)}, bf16[40,256,256]{2,1,0:T(8,128)(2,1)S(1)}) custom-call(bf16[1,1,48,256,256]{4,3,2,1,0:T(8,128)(2,1)} %weights.3, f32[1,1,48,2,256]{4,3,2,1,0:T(2,128)S(1)} %copy-done, s32[1,1,2,48]{3,2,1,0:T(2,128)S(1)} %bitcast.9), custom_call_target="tpu_custom_call" | custom-call | flops 1000000 | bytes 10000000 | tf_op jit(solution)/shard_map/local_degree/pallas_call | solution.py:529
  11.2 4.0 %collective-permute-start.6 = (f32[16,256]{1,0:T(8,128)S(1)}, f32[16,256]{1,0:T(8,128)S(1)}, u32[]{:S(2)}, u32[]{:S(2)}) collective-permute-start(f32[16,256]{1,0:T(8,128)S(1)} %get-tuple-element.58.refs_0_), channel_id=1, source_target_pairs={{0,3},{1,2},{2,1},{3,0},{4,7},{5,6},{6,5},{7,4},{8,11},{9,10},{10,... | collective-permute-start | bytes 49160 | tf_op jit(solution)/shard_map/ppermute | solution.py:475
  15.1 0.6 collective-permute-start.4
  17.0 2.8 %collective-permute-done.5.refs_2_ = f32[16,256]{1,0:T(8,128)S(1)} collective-permute-done((f32[16,256]{1,0:T(8,128)S(1)}, f32[16,256]{1,0:T(8,128)S(1)}, u32[]{:S(2)}, u32[]{:S(2)}) %collective-permute-start.5) | collective-permute-done | bytes 16416 | tf_op jit(solution)/shard_map/ppermute | solution.py:475
  20.2 0.5 local_products.4.refs_1_.refs_0_
  20.8 0.8 %collective-permute-done.7.passed = bf16[4,4,16,256]{3,2,1,0:T(8,128)(2,1)S(1)} collective-permute-done((bf16[4,4,16,256]{3,2,1,0:T(8,128)(2,1)S(1)}, bf16[4,4,16,256]{3,2,1,0:T(8,128)(2,1)S(1)}, u32[]{:S(2)}, u32[]{:S(2)}) %collective-permute-start.7) | collective-permute-done | bytes 131104 | tf_op jit(solution)/shard_map/ppermute | solution.py:489
  21.6 2.5 %collective-permute-start.8 = (bf16[2,4,16,256]{3,2,1,0:T(8,128)(2,1)S(1)}, bf16[2,4,16,256]{3,2,1,0:T(8,128)(2,1)S(1)}, u32[]{:S(2)}, u32[]{:S(2)}) collective-permute-start(bf16[2,4,16,256]{3,2,1,0:T(8,128)(2,1)S(1)} %get-tuple-element.65), channel_id=1, source_target_pairs={{0,24},{4,28},{8,16},{12,20},{16,8},{20,12},{24,0},{28,4},{1,25},{... | collective-permute-start | bytes 196616 | tf_op jit(solution)/shard_map/ppermute | solution.py:497
  25.1 3.1 %local_products.5.partial = f32[16,16,256]{2,1,0:T(8,128)S(1)} custom-call(bf16[16,16,256]{2,1,0:T(8,128)(2,1)S(1)} %get-tuple-element.60.x, bf16[40,256,256]{2,1,0:T(8,128)(2,1)S(1)} %get-tuple-element.61.tiles, s32[1,1,2,48]{3,2,1,0:T(2,128)S(1)} %bitcast.11, f32[1,1,48,2,256]{4,3,2,1,0:T(2,128)S(1)} %copy-done, ...), custom_call_target="tpu_custom_call" | custom-call | flops 167772160 | bytes 5242880 | tf_op jit(solution)/shard_map/local_products/pallas_call | solution.py:569
  28.9 0.6 remote_products.2
  29.5 5.0 %collective-permute-done.11.theirs = bf16[16,16,256]{2,1,0:T(8,128)(2,1)S(1)} collective-permute-done((bf16[16,16,256]{2,1,0:T(8,128)(2,1)S(1)}, bf16[16,16,256]{2,1,0:T(8,128)(2,1)S(1)}, u32[]{:S(2)}, u32[]{:S(2)}) %collective-permute-start.11) | collective-permute-done | bytes 131104 | tf_op jit(solution)/shard_map/ppermute | solution.py:475
  34.5 1.5 %collective-permute-start.12 = (bf16[16,16,256]{2,1,0:T(8,128)(2,1)S(1)}, bf16[16,16,256]{2,1,0:T(8,128)(2,1)S(1)}, u32[]{:S(2)}, u32[]{:S(2)}) collective-permute-start(bf16[16,16,256]{2,1,0:T(8,128)(2,1)S(1)} %get-tuple-element.71), channel_id=1, source_target_pairs={{0,3},{1,2},{2,1},{3,0},{4,7},{5,6},{6,5},{7,4},{8,11},{9,10},{10,... | collective-permute-start | bytes 393224 | tf_op jit(solution)/shard_map/ppermute | solution.py:475
  36.0 5.3 %collective-permute-done.12.theirs = bf16[16,16,256]{2,1,0:T(8,128)(2,1)S(1)} collective-permute-done((bf16[16,16,256]{2,1,0:T(8,128)(2,1)S(1)}, bf16[16,16,256]{2,1,0:T(8,128)(2,1)S(1)}, u32[]{:S(2)}, u32[]{:S(2)}) %collective-permute-start.12) | collective-permute-done | bytes 131104 | tf_op jit(solution)/shard_map/ppermute | solution.py:475
  42.0 0.6 local_products.6.refs_0_.refs_1_
  42.5 0.8 %collective-permute-done.13.passed = bf16[4,5,16,256]{3,2,1,0:T(8,128)(2,1)S(1)} collective-permute-done((bf16[4,5,16,256]{3,2,1,0:T(8,128)(2,1)S(1)}, bf16[4,5,16,256]{3,2,1,0:T(8,128)(2,1)S(1)}, u32[]{:S(2)}, u32[]{:S(2)}) %collective-permute-start.13) | collective-permute-done | bytes 163872 | tf_op jit(solution)/shard_map/ppermute | solution.py:489
  43.4 1.9 %collective-permute-start.14 = (bf16[2,5,16,256]{3,2,1,0:T(8,128)(2,1)S(1)}, bf16[2,5,16,256]{3,2,1,0:T(8,128)(2,1)S(1)}, u32[]{:S(2)}, u32[]{:S(2)}) collective-permute-start(bf16[2,5,16,256]{3,2,1,0:T(8,128)(2,1)S(1)} %get-tuple-element.76), channel_id=1, source_target_pairs={{0,24},{4,28},{8,16},{12,20},{16,8},{20,12},{24,0},{28,4},{1,25},{... | collective-permute-start | bytes 245768 | tf_op jit(solution)/shard_map/ppermute | solution.py:497
  45.3 0.9 %collective-permute-start.15 = (bf16[2,5,16,256]{3,2,1,0:T(8,128)(2,1)S(1)}, bf16[2,5,16,256]{3,2,1,0:T(8,128)(2,1)S(1)}, u32[]{:S(2)}, u32[]{:S(2)}) collective-permute-start(bf16[2,5,16,256]{3,2,1,0:T(8,128)(2,1)S(1)} %get-tuple-element.77), channel_id=1, source_target_pairs={{0,16},{4,20},{8,24},{12,28},{16,0},{20,4},{24,8},{28,12},{1,17},{... | collective-permute-start | bytes 245768 | tf_op jit(solution)/shard_map/ppermute | solution.py:497
  46.1 0.8 %collective-permute-start.16 = (bf16[2,5,16,256]{3,2,1,0:T(8,128)(2,1)S(1)}, bf16[2,5,16,256]{3,2,1,0:T(8,128)(2,1)S(1)}, u32[]{:S(2)}, u32[]{:S(2)}) collective-permute-start(bf16[2,5,16,256]{3,2,1,0:T(8,128)(2,1)S(1)} %get-tuple-element.78), channel_id=1, source_target_pairs={{0,8},{4,12},{8,0},{12,4},{16,24},{20,28},{24,16},{28,20},{1,9},{5... | collective-permute-start | bytes 245768 | tf_op jit(solution)/shard_map/ppermute | solution.py:497
  47.0 3.1 %local_products.7.partial = f32[16,16,256]{2,1,0:T(8,128)S(1)} custom-call(bf16[16,16,256]{2,1,0:T(8,128)(2,1)S(1)} %get-tuple-element.74.x, bf16[40,256,256]{2,1,0:T(8,128)(2,1)S(1)} %get-tuple-element.61.tiles, s32[1,1,2,48]{3,2,1,0:T(2,128)S(1)} %bitcast.13, f32[1,1,48,2,256]{4,3,2,1,0:T(2,128)S(1)} %copy-done, ...), custom_call_target="tpu_custom_call" | custom-call | flops 167772160 | bytes 5242880 | tf_op jit(solution)/shard_map/local_products/pallas_call | solution.py:569
  50.0 0.6 collective-permute-done.15.refs_2_
  50.7 0.6 remote_products.3
  51.3 1.6 %collective-permute-start.17 = (bf16[4,16,256]{2,1,0:T(8,128)(2,1)S(1)}, bf16[4,16,256]{2,1,0:T(8,128)(2,1)S(1)}, u32[]{:S(2)}, u32[]{:S(2)}) collective-permute-start(bf16[4,16,256]{2,1,0:T(8,128)(2,1)S(1)} %get-tuple-element.80), channel_id=1, source_target_pairs={{0,3},{1,2},{2,1},{3,0},{4,7},{5,6},{6,5},{7,4},{8,11},{9,10},{10,... | collective-permute-start | bytes 98312 | tf_op jit(solution)/shard_map/ppermute | solution.py:475
  52.9 1.0 %collective-permute-start.18 = (bf16[4,16,256]{2,1,0:T(8,128)(2,1)S(1)}, bf16[4,16,256]{2,1,0:T(8,128)(2,1)S(1)}, u32[]{:S(2)}, u32[]{:S(2)}) collective-permute-start(bf16[4,16,256]{2,1,0:T(8,128)(2,1)S(1)} %get-tuple-element.81), channel_id=1, source_target_pairs={{0,2},{1,3},{2,0},{3,1},{4,6},{5,7},{6,4},{7,5},{8,10},{9,11},{10,... | collective-permute-start | bytes 98312 | tf_op jit(solution)/shard_map/ppermute | solution.py:475
  53.9 1.9 %collective-permute-start.19 = (bf16[4,16,256]{2,1,0:T(8,128)(2,1)S(1)}, bf16[4,16,256]{2,1,0:T(8,128)(2,1)S(1)}, u32[]{:S(2)}, u32[]{:S(2)}) collective-permute-start(bf16[4,16,256]{2,1,0:T(8,128)(2,1)S(1)} %get-tuple-element.82), channel_id=1, source_target_pairs={{0,1},{1,0},{2,3},{3,2},{4,5},{5,4},{6,7},{7,6},{8,9},{9,8},{10,11... | collective-permute-start | bytes 98312 | tf_op jit(solution)/shard_map/ppermute | solution.py:475
  56.1 0.9 %collective-permute-done.17.refs_1_ = bf16[4,16,256]{2,1,0:T(8,128)(2,1)S(1)} collective-permute-done((bf16[4,16,256]{2,1,0:T(8,128)(2,1)S(1)}, bf16[4,16,256]{2,1,0:T(8,128)(2,1)S(1)}, u32[]{:S(2)}, u32[]{:S(2)}) %collective-permute-start.17) | collective-permute-done | bytes 32800 | tf_op jit(solution)/shard_map/ppermute | solution.py:475
  57.1 0.7 collective-permute-done.18.refs_2_
  58.0 0.6 last_quarter.1
  58.6 10.8 %all_to_all.5.grams = f32[32,2,128]{2,1,0:T(2,128)S(1)} all-to-all(f32[32,2,128]{2,1,0:T(2,128)S(1)} %get-tuple-element.83), channel_id=1, replica_groups=mesh['rows'=8,'cols'=4] {'rows','cols'}, dimensions={0} | all-to-all | bytes 65536 | tf_op jit(solution)/shard_map/all_to_all | solution.py:633
  69.4 1.1 %finish.1 = f32[16,1024]{1,0:T(8,128)} custom-call(f32[32,2,128]{2,1,0:T(2,128)S(1)} %all_to_all.5.grams, f32[16,1024]{1,0:T(8,128)S(1)} %get-tuple-element.84.image), custom_call_target="tpu_custom_call" | custom-call | flops 1000000 | bytes 1000000 | tf_op jit(solution)/shard_map/finish/pallas_call | solution.py:636
  (42 shorter events, 5.8 us)
Async XLA Ops:
  0.0 2.2 %copy-start.2 = (f32[1,1,8,2,256]{4,3,2,1,0:T(2,128)S(1)}, f32[1,1,8,2,256]{4,3,2,1,0:T(2,128)}, u32[]{:S(2)}) copy-start(f32[1,1,8,2,256]{4,3,2,1,0:T(2,128)} %gains.6) | copy-start | bytes 49156
  0.0 2.2 %copy-start.3 = (s32[1,1,8,2]{2,3,1,0:T(2,128)S(1)}, s32[1,1,8,2]{2,3,1,0:T(2,128)}, u32[]{:S(2)}) copy-start(s32[1,1,8,2]{2,3,1,0:T(2,128)} %param.14) | copy-start | bytes 196
  0.0 2.2 %copy-start = (f32[1,1,48,2,256]{4,3,2,1,0:T(2,128)S(1)}, f32[1,1,48,2,256]{4,3,2,1,0:T(2,128)}, u32[]{:S(2)}) copy-start(f32[1,1,48,2,256]{4,3,2,1,0:T(2,128)} %refs_0_.1) | copy-start | bytes 294916
  0.0 2.2 %copy-start.4 = (s32[1,1,48,2]{2,3,1,0:T(2,128)S(1)}, s32[1,1,48,2]{2,3,1,0:T(2,128)}, u32[]{:S(2)}) copy-start(s32[1,1,48,2]{2,3,1,0:T(2,128)} %param.10) | copy-start | bytes 1156
  1.7 1.4 %collective-permute-start = (f32[4,8,256]{2,1,0:T(8,128)S(1)}, f32[4,8,256]{2,1,0:T(8,128)S(1)}, u32[]{:S(2)}, u32[]{:S(2)}) collective-permute-start(f32[4,8,256]{2,1,0:T(8,128)S(1)} %get-tuple-element.49), channel_id=1, source_target_pairs={{0,4},{4,0},{8,12},{12,8},{16,20},{20,16},{24,28},{28,24},{1,5},{5... | collective-permute-start | bytes 98312 | tf_op jit(solution)/shard_map/ppermute | solution.py:489
  2.2 17.5 %copy-start.1 = (f32[16,4096]{1,0:T(8,128)S(1)}, f32[16,4096]{1,0:T(8,128)}, u32[]{:S(2)}) copy-start(f32[16,4096]{1,0:T(8,128)} %start.1) | copy-start | bytes 786436
  2.2 17.5 %copy-start.5 = (s32[1,1,8]{2,1,0:T(1,128)S(1)}, s32[1,1,8]{2,1,0:T(1,128)}, u32[]{:S(2)}) copy-start(s32[1,1,8]{2,1,0:T(1,128)} %groups.9) | copy-start | bytes 100
  3.1 7.9 %collective-permute-start.1 = (f32[2,8,256]{2,1,0:T(8,128)S(1)}, f32[2,8,256]{2,1,0:T(8,128)S(1)}, u32[]{:S(2)}, u32[]{:S(2)}) collective-permute-start(f32[2,8,256]{2,1,0:T(8,128)S(1)} %get-tuple-element.51), channel_id=1, source_target_pairs={{0,24},{4,28},{8,16},{12,20},{16,8},{20,12},{24,0},{28,4},{1,25},{... | collective-permute-start | bytes 49160 | tf_op jit(solution)/shard_map/ppermute | solution.py:497
  6.9 4.1 %collective-permute-start.2 = (f32[2,8,256]{2,1,0:T(8,128)S(1)}, f32[2,8,256]{2,1,0:T(8,128)S(1)}, u32[]{:S(2)}, u32[]{:S(2)}) collective-permute-start(f32[2,8,256]{2,1,0:T(8,128)S(1)} %get-tuple-element.52), channel_id=1, source_target_pairs={{0,16},{4,20},{8,24},{12,28},{16,0},{20,4},{24,8},{28,12},{1,17},{... | collective-permute-start | bytes 49160 | tf_op jit(solution)/shard_map/ppermute | solution.py:497
  7.4 3.7 %collective-permute-start.3 = (f32[2,8,256]{2,1,0:T(8,128)S(1)}, f32[2,8,256]{2,1,0:T(8,128)S(1)}, u32[]{:S(2)}, u32[]{:S(2)}) collective-permute-start(f32[2,8,256]{2,1,0:T(8,128)S(1)} %get-tuple-element.53), channel_id=1, source_target_pairs={{0,8},{4,12},{8,0},{12,4},{16,24},{20,28},{24,16},{28,20},{1,9},{5... | collective-permute-start | bytes 49160 | tf_op jit(solution)/shard_map/ppermute | solution.py:497
  11.2 5.8 %collective-permute-start.6 = (f32[16,256]{1,0:T(8,128)S(1)}, f32[16,256]{1,0:T(8,128)S(1)}, u32[]{:S(2)}, u32[]{:S(2)}) collective-permute-start(f32[16,256]{1,0:T(8,128)S(1)} %get-tuple-element.58.refs_0_), channel_id=1, source_target_pairs={{0,3},{1,2},{2,1},{3,0},{4,7},{5,6},{6,5},{7,4},{8,11},{9,10},{10,... | collective-permute-start | bytes 49160 | tf_op jit(solution)/shard_map/ppermute | solution.py:475
  15.1 4.6 %collective-permute-start.5 = (f32[16,256]{1,0:T(8,128)S(1)}, f32[16,256]{1,0:T(8,128)S(1)}, u32[]{:S(2)}, u32[]{:S(2)}) collective-permute-start(f32[16,256]{1,0:T(8,128)S(1)} %get-tuple-element.58.refs_0_), channel_id=1, source_target_pairs={{0,2},{1,3},{2,0},{3,1},{4,6},{5,7},{6,4},{7,5},{8,10},{9,11},{10,... | collective-permute-start | bytes 49160 | tf_op jit(solution)/shard_map/ppermute | solution.py:475
  15.1 4.6 %collective-permute-start.4 = (f32[16,256]{1,0:T(8,128)S(1)}, f32[16,256]{1,0:T(8,128)S(1)}, u32[]{:S(2)}, u32[]{:S(2)}) collective-permute-start(f32[16,256]{1,0:T(8,128)S(1)} %get-tuple-element.58.refs_0_), channel_id=1, source_target_pairs={{0,1},{1,0},{2,3},{3,2},{4,5},{5,4},{6,7},{7,6},{8,9},{9,8},{10,11... | collective-permute-start | bytes 49160 | tf_op jit(solution)/shard_map/ppermute | solution.py:475
  20.1 1.4 %collective-permute-start.7 = (bf16[4,4,16,256]{3,2,1,0:T(8,128)(2,1)S(1)}, bf16[4,4,16,256]{3,2,1,0:T(8,128)(2,1)S(1)}, u32[]{:S(2)}, u32[]{:S(2)}) collective-permute-start(bf16[4,4,16,256]{3,2,1,0:T(8,128)(2,1)S(1)} %get-tuple-element.63), channel_id=1, source_target_pairs={{0,4},{4,0},{8,12},{12,8},{16,20},{20,16},{24,28},{28,24},{1,5},{5... | collective-permute-start | bytes 393224 | tf_op jit(solution)/shard_map/ppermute | solution.py:489
  21.6 6.6 %collective-permute-start.8 = (bf16[2,4,16,256]{3,2,1,0:T(8,128)(2,1)S(1)}, bf16[2,4,16,256]{3,2,1,0:T(8,128)(2,1)S(1)}, u32[]{:S(2)}, u32[]{:S(2)}) collective-permute-start(bf16[2,4,16,256]{3,2,1,0:T(8,128)(2,1)S(1)} %get-tuple-element.65), channel_id=1, source_target_pairs={{0,24},{4,28},{8,16},{12,20},{16,8},{20,12},{24,0},{28,4},{1,25},{... | collective-permute-start | bytes 196616 | tf_op jit(solution)/shard_map/ppermute | solution.py:497
  24.1 4.3 %collective-permute-start.9 = (bf16[2,4,16,256]{3,2,1,0:T(8,128)(2,1)S(1)}, bf16[2,4,16,256]{3,2,1,0:T(8,128)(2,1)S(1)}, u32[]{:S(2)}, u32[]{:S(2)}) collective-permute-start(bf16[2,4,16,256]{3,2,1,0:T(8,128)(2,1)S(1)} %get-tuple-element.66), channel_id=1, source_target_pairs={{0,16},{4,20},{8,24},{12,28},{16,0},{20,4},{24,8},{28,12},{1,17},{... | collective-permute-start | bytes 196616 | tf_op jit(solution)/shard_map/ppermute | solution.py:497
  24.6 4.3 %collective-permute-start.10 = (bf16[2,4,16,256]{3,2,1,0:T(8,128)(2,1)S(1)}, bf16[2,4,16,256]{3,2,1,0:T(8,128)(2,1)S(1)}, u32[]{:S(2)}, u32[]{:S(2)}) collective-permute-start(bf16[2,4,16,256]{3,2,1,0:T(8,128)(2,1)S(1)} %get-tuple-element.67), channel_id=1, source_target_pairs={{0,8},{4,12},{8,0},{12,4},{16,24},{20,28},{24,16},{28,20},{1,9},{5... | collective-permute-start | bytes 196616 | tf_op jit(solution)/shard_map/ppermute | solution.py:497
  29.4 5.0 %collective-permute-start.11 = (bf16[16,16,256]{2,1,0:T(8,128)(2,1)S(1)}, bf16[16,16,256]{2,1,0:T(8,128)(2,1)S(1)}, u32[]{:S(2)}, u32[]{:S(2)}) collective-permute-start(bf16[16,16,256]{2,1,0:T(8,128)(2,1)S(1)} %get-tuple-element.69), channel_id=1, source_target_pairs={{0,1},{1,0},{2,3},{3,2},{4,5},{5,4},{6,7},{7,6},{8,9},{9,8},{10,11... | collective-permute-start | bytes 393224 | tf_op jit(solution)/shard_map/ppermute | solution.py:475
  34.5 6.8 %collective-permute-start.12 = (bf16[16,16,256]{2,1,0:T(8,128)(2,1)S(1)}, bf16[16,16,256]{2,1,0:T(8,128)(2,1)S(1)}, u32[]{:S(2)}, u32[]{:S(2)}) collective-permute-start(bf16[16,16,256]{2,1,0:T(8,128)(2,1)S(1)} %get-tuple-element.71), channel_id=1, source_target_pairs={{0,3},{1,2},{2,1},{3,0},{4,7},{5,6},{6,5},{7,4},{8,11},{9,10},{10,... | collective-permute-start | bytes 393224 | tf_op jit(solution)/shard_map/ppermute | solution.py:475
  41.9 1.5 %collective-permute-start.13 = (bf16[4,5,16,256]{3,2,1,0:T(8,128)(2,1)S(1)}, bf16[4,5,16,256]{3,2,1,0:T(8,128)(2,1)S(1)}, u32[]{:S(2)}, u32[]{:S(2)}) collective-permute-start(bf16[4,5,16,256]{3,2,1,0:T(8,128)(2,1)S(1)} %get-tuple-element.73), channel_id=1, source_target_pairs={{0,4},{4,0},{8,12},{12,8},{16,20},{20,16},{24,28},{28,24},{1,5},{5... | collective-permute-start | bytes 491528 | tf_op jit(solution)/shard_map/ppermute | solution.py:489
  43.4 6.6 %collective-permute-start.14 = (bf16[2,5,16,256]{3,2,1,0:T(8,128)(2,1)S(1)}, bf16[2,5,16,256]{3,2,1,0:T(8,128)(2,1)S(1)}, u32[]{:S(2)}, u32[]{:S(2)}) collective-permute-start(bf16[2,5,16,256]{3,2,1,0:T(8,128)(2,1)S(1)} %get-tuple-element.76), channel_id=1, source_target_pairs={{0,24},{4,28},{8,16},{12,20},{16,8},{20,12},{24,0},{28,4},{1,25},{... | collective-permute-start | bytes 245768 | tf_op jit(solution)/shard_map/ppermute | solution.py:497
  45.3 5.3 %collective-permute-start.15 = (bf16[2,5,16,256]{3,2,1,0:T(8,128)(2,1)S(1)}, bf16[2,5,16,256]{3,2,1,0:T(8,128)(2,1)S(1)}, u32[]{:S(2)}, u32[]{:S(2)}) collective-permute-start(bf16[2,5,16,256]{3,2,1,0:T(8,128)(2,1)S(1)} %get-tuple-element.77), channel_id=1, source_target_pairs={{0,16},{4,20},{8,24},{12,28},{16,0},{20,4},{24,8},{28,12},{1,17},{... | collective-permute-start | bytes 245768 | tf_op jit(solution)/shard_map/ppermute | solution.py:497
  46.1 4.6 %collective-permute-start.16 = (bf16[2,5,16,256]{3,2,1,0:T(8,128)(2,1)S(1)}, bf16[2,5,16,256]{3,2,1,0:T(8,128)(2,1)S(1)}, u32[]{:S(2)}, u32[]{:S(2)}) collective-permute-start(bf16[2,5,16,256]{3,2,1,0:T(8,128)(2,1)S(1)} %get-tuple-element.78), channel_id=1, source_target_pairs={{0,8},{4,12},{8,0},{12,4},{16,24},{20,28},{24,16},{28,20},{1,9},{5... | collective-permute-start | bytes 245768 | tf_op jit(solution)/shard_map/ppermute | solution.py:497
  51.3 5.8 %collective-permute-start.17 = (bf16[4,16,256]{2,1,0:T(8,128)(2,1)S(1)}, bf16[4,16,256]{2,1,0:T(8,128)(2,1)S(1)}, u32[]{:S(2)}, u32[]{:S(2)}) collective-permute-start(bf16[4,16,256]{2,1,0:T(8,128)(2,1)S(1)} %get-tuple-element.80), channel_id=1, source_target_pairs={{0,3},{1,2},{2,1},{3,0},{4,7},{5,6},{6,5},{7,4},{8,11},{9,10},{10,... | collective-permute-start | bytes 98312 | tf_op jit(solution)/shard_map/ppermute | solution.py:475
  52.9 4.8 %collective-permute-start.18 = (bf16[4,16,256]{2,1,0:T(8,128)(2,1)S(1)}, bf16[4,16,256]{2,1,0:T(8,128)(2,1)S(1)}, u32[]{:S(2)}, u32[]{:S(2)}) collective-permute-start(bf16[4,16,256]{2,1,0:T(8,128)(2,1)S(1)} %get-tuple-element.81), channel_id=1, source_target_pairs={{0,2},{1,3},{2,0},{3,1},{4,6},{5,7},{6,4},{7,5},{8,10},{9,11},{10,... | collective-permute-start | bytes 98312 | tf_op jit(solution)/shard_map/ppermute | solution.py:475
  53.9 4.2 %collective-permute-start.19 = (bf16[4,16,256]{2,1,0:T(8,128)(2,1)S(1)}, bf16[4,16,256]{2,1,0:T(8,128)(2,1)S(1)}, u32[]{:S(2)}, u32[]{:S(2)}) collective-permute-start(bf16[4,16,256]{2,1,0:T(8,128)(2,1)S(1)} %get-tuple-element.82), channel_id=1, source_target_pairs={{0,1},{1,0},{2,3},{3,2},{4,5},{5,4},{6,7},{7,6},{8,9},{9,8},{10,11... | collective-permute-start | bytes 98312 | tf_op jit(solution)/shard_map/ppermute | solution.py:475

commit v11 on v10

--- a/solution.py
+++ b/solution.py
@@ -69,12 +69,11 @@
 
 
 def slots_of(groups_ref, count_ref, tile_count, group_count):
-    for g in range(group_count):
-        count_ref[g] = 0
+    seen = []
     for t in range(tile_count):
         g = groups_ref[0, 0, t]
-        m = count_ref[g]
-        count_ref[g] = m + 1
+        m = sum((earlier == g).astype(jnp.int32) for earlier in seen) if seen else 0
+        seen.append(g)
         yield t, g, m
 
 

time: 70.7 us -> 70.6 us (level)
  no operation moved by 1% of the time
where the time goes in v11:
time: 70.6 us; the launch traced here: 70.5 us
  starting transfers between devices  22.9 us (32%)
  Pallas kernels  18.4 us (26%)
  waiting for transfers between devices  18.2 us (26%)
  blocking collectives  10.7 us (15%)
    ppermute x8, waiting for transfers between devices, swap(): return lax.ppermute(value, 'cols', [(j, j ^ k) for j in range(splits)])  15.1 us
    ppermute x9, starting transfers between devices, exchange(): lax.ppermute(piece, 'rows', [(j, j ^ 2 * k) for j in range(groups)])  11.5 us
    all_to_all x1, blocking collectives, per_device(): lax.all_to_all(grams, ('rows', 'cols'), split_axis=0, concat_axis=0, tile...  10.7 us
    ppermute x8, starting transfers between devices, swap(): return lax.ppermute(value, 'cols', [(j, j ^ k) for j in range(splits)])  10.7 us
    pallas_call x4, Pallas kernels, local_products(): call(functools.partial(local_products_kernel, first), shape((BR, WIDTH, T...  7.21 us
    pallas_call x1, Pallas kernels, per_device(): call(functools.partial(local_degree_kernel, HEAD), (shape((BR, TILE)), sh...  3.44 us
    pallas_call x1, Pallas kernels, per_device(): call(remote_degree_kernel, (shape((remote_tiles, TILE, TILE), BF16), shap...  1.64 us
    ppermute x3, waiting for transfers between devices, exchange(): passed = lax.ppermute(far, 'rows', [(j, j ^ 1) for j in range(groups)])  1.61 us
  transfers between devices with their start and end apart: 20, of which 14 were waited for; matrix products, arithmetic and copies ran while one was open for 0% of the time, Pallas kernels for 18%

profile of v11, /device:TPU:0, one launch (start us, length us, event | category | flops | bytes accessed | tf_op | source)
XLA Modules:
  0.0 70.5 jit_solution(13748081175938053323)
XLA Ops:
  0.0 1.6 %remote_degree.1 = (bf16[8,256,256]{2,1,0:T(8,128)(2,1)S(1)}, bf16[8,256,256]{2,1,0:T(8,128)(2,1)S(1)}, f32[4,8,256]{2,1,0:T(8,128)S(1)}, f32[4,8,256]{2,1,0:T(8,128)S(1)}) custom-call(bf16[1,1,8,256,256]{4,3,2,1,0:T(8,128)(2,1)} %weights.2, f32[1,1,8,2,256]{4,3,2,1,0:T(2,128)} %gains.6, s32[1,1,8]{2,1,0:T(1,128)} %groups.9, s32[1,1,2,8]{3,2,1,0:T(2,128)} %bitcast.2, ...), custom_call_target="tpu_custom_call" | custom-call | flops 1000000 | bytes 1000000 | tf_op jit(solution)/shard_map/remote_degree/pallas_call | solution.py:501
  1.7 0.6 collective-permute-start
  2.3 0.8 %early_degree.1.refs_0_.early = f32[16,256]{1,0:T(8,128)S(1)} custom-call(bf16[8,256,256]{2,1,0:T(8,128)(2,1)S(1)} %get-tuple-element.45.remote.raw, f32[1,1,8,2,256]{4,3,2,1,0:T(2,128)S(1)} %copy-done.2, s32[1,1,2,8]{3,2,1,0:T(2,128)S(1)} %bitcast.3, bf16[8,256,256]{2,1,0:T(8,128)(2,1)S(1)} %get-tuple-element.46.held.raw, ...), custom_call_target="tpu_custom_call" | custom-call | flops 1000000 | bytes 1000000 | tf_op jit(solution)/shard_map/early_degree/pallas_call | solution.py:520
  3.1 3.8 %collective-permute-start.1 = (f32[2,8,256]{2,1,0:T(8,128)S(1)}, f32[2,8,256]{2,1,0:T(8,128)S(1)}, u32[]{:S(2)}, u32[]{:S(2)}) collective-permute-start(f32[2,8,256]{2,1,0:T(8,128)S(1)} %get-tuple-element.51), channel_id=1, source_target_pairs={{0,24},{4,28},{8,16},{12,20},{16,8},{20,12},{24,0},{28,4},{1,25},{... | collective-permute-start | bytes 49160 | tf_op jit(solution)/shard_map/ppermute | solution.py:496
  7.5 3.4 %local_degree.1 = (f32[16,256]{1,0:T(8,128)S(1)}, bf16[40,256,256]{2,1,0:T(8,128)(2,1)S(1)}) custom-call(bf16[1,1,48,256,256]{4,3,2,1,0:T(8,128)(2,1)} %weights.3, f32[1,1,48,2,256]{4,3,2,1,0:T(2,128)S(1)} %copy-done, s32[1,1,2,48]{3,2,1,0:T(2,128)S(1)} %bitcast.9), custom_call_target="tpu_custom_call" | custom-call | flops 1000000 | bytes 10000000 | tf_op jit(solution)/shard_map/local_degree/pallas_call | solution.py:528
  11.2 4.0 %collective-permute-start.6 = (f32[16,256]{1,0:T(8,128)S(1)}, f32[16,256]{1,0:T(8,128)S(1)}, u32[]{:S(2)}, u32[]{:S(2)}) collective-permute-start(f32[16,256]{1,0:T(8,128)S(1)} %get-tuple-element.58.refs_0_), channel_id=1, source_target_pairs={{0,3},{1,2},{2,1},{3,0},{4,7},{5,6},{6,5},{7,4},{8,11},{9,10},{10,... | collective-permute-start | bytes 49160 | tf_op jit(solution)/shard_map/ppermute | solution.py:474
  15.1 0.6 collective-permute-start.4
  17.0 2.8 %collective-permute-done.5.refs_2_ = f32[16,256]{1,0:T(8,128)S(1)} collective-permute-done((f32[16,256]{1,0:T(8,128)S(1)}, f32[16,256]{1,0:T(8,128)S(1)}, u32[]{:S(2)}, u32[]{:S(2)}) %collective-permute-start.5) | collective-permute-done | bytes 16416 | tf_op jit(solution)/shard_map/ppermute | solution.py:474
  20.2 0.5 local_products.4.refs_1_.refs_0_
  20.8 0.8 %collective-permute-done.7.passed = bf16[4,4,16,256]{3,2,1,0:T(8,128)(2,1)S(1)} collective-permute-done((bf16[4,4,16,256]{3,2,1,0:T(8,128)(2,1)S(1)}, bf16[4,4,16,256]{3,2,1,0:T(8,128)(2,1)S(1)}, u32[]{:S(2)}, u32[]{:S(2)}) %collective-permute-start.7) | collective-permute-done | bytes 131104 | tf_op jit(solution)/shard_map/ppermute | solution.py:488
  21.6 2.5 %collective-permute-start.8 = (bf16[2,4,16,256]{3,2,1,0:T(8,128)(2,1)S(1)}, bf16[2,4,16,256]{3,2,1,0:T(8,128)(2,1)S(1)}, u32[]{:S(2)}, u32[]{:S(2)}) collective-permute-start(bf16[2,4,16,256]{3,2,1,0:T(8,128)(2,1)S(1)} %get-tuple-element.65), channel_id=1, source_target_pairs={{0,24},{4,28},{8,16},{12,20},{16,8},{20,12},{24,0},{28,4},{1,25},{... | collective-permute-start | bytes 196616 | tf_op jit(solution)/shard_map/ppermute | solution.py:496
  25.1 3.1 %local_products.5.partial = f32[16,16,256]{2,1,0:T(8,128)S(1)} custom-call(bf16[16,16,256]{2,1,0:T(8,128)(2,1)S(1)} %get-tuple-element.60.x, bf16[40,256,256]{2,1,0:T(8,128)(2,1)S(1)} %get-tuple-element.61.tiles, s32[1,1,2,48]{3,2,1,0:T(2,128)S(1)} %bitcast.11, f32[1,1,48,2,256]{4,3,2,1,0:T(2,128)S(1)} %copy-done, ...), custom_call_target="tpu_custom_call" | custom-call | flops 167772160 | bytes 5242880 | tf_op jit(solution)/shard_map/local_products/pallas_call | solution.py:568
  28.9 0.6 remote_products.2
  29.5 5.0 %collective-permute-done.11.theirs = bf16[16,16,256]{2,1,0:T(8,128)(2,1)S(1)} collective-permute-done((bf16[16,16,256]{2,1,0:T(8,128)(2,1)S(1)}, bf16[16,16,256]{2,1,0:T(8,128)(2,1)S(1)}, u32[]{:S(2)}, u32[]{:S(2)}) %collective-permute-start.11) | collective-permute-done | bytes 131104 | tf_op jit(solution)/shard_map/ppermute | solution.py:474
  34.5 1.5 %collective-permute-start.12 = (bf16[16,16,256]{2,1,0:T(8,128)(2,1)S(1)}, bf16[16,16,256]{2,1,0:T(8,128)(2,1)S(1)}, u32[]{:S(2)}, u32[]{:S(2)}) collective-permute-start(bf16[16,16,256]{2,1,0:T(8,128)(2,1)S(1)} %get-tuple-element.71), channel_id=1, source_target_pairs={{0,3},{1,2},{2,1},{3,0},{4,7},{5,6},{6,5},{7,4},{8,11},{9,10},{10,... | collective-permute-start | bytes 393224 | tf_op jit(solution)/shard_map/ppermute | solution.py:474
  36.0 5.3 %collective-permute-done.12.theirs = bf16[16,16,256]{2,1,0:T(8,128)(2,1)S(1)} collective-permute-done((bf16[16,16,256]{2,1,0:T(8,128)(2,1)S(1)}, bf16[16,16,256]{2,1,0:T(8,128)(2,1)S(1)}, u32[]{:S(2)}, u32[]{:S(2)}) %collective-permute-start.12) | collective-permute-done | bytes 131104 | tf_op jit(solution)/shard_map/ppermute | solution.py:474
  42.0 0.5 local_products.6.refs_0_.refs_1_
  42.5 0.8 %collective-permute-done.13.passed = bf16[4,5,16,256]{3,2,1,0:T(8,128)(2,1)S(1)} collective-permute-done((bf16[4,5,16,256]{3,2,1,0:T(8,128)(2,1)S(1)}, bf16[4,5,16,256]{3,2,1,0:T(8,128)(2,1)S(1)}, u32[]{:S(2)}, u32[]{:S(2)}) %collective-permute-start.13) | collective-permute-done | bytes 163872 | tf_op jit(solution)/shard_map/ppermute | solution.py:488
  43.4 1.9 %collective-permute-start.14 = (bf16[2,5,16,256]{3,2,1,0:T(8,128)(2,1)S(1)}, bf16[2,5,16,256]{3,2,1,0:T(8,128)(2,1)S(1)}, u32[]{:S(2)}, u32[]{:S(2)}) collective-permute-start(bf16[2,5,16,256]{3,2,1,0:T(8,128)(2,1)S(1)} %get-tuple-element.76), channel_id=1, source_target_pairs={{0,24},{4,28},{8,16},{12,20},{16,8},{20,12},{24,0},{28,4},{1,25},{... | collective-permute-start | bytes 245768 | tf_op jit(solution)/shard_map/ppermute | solution.py:496
  45.3 0.9 %collective-permute-start.15 = (bf16[2,5,16,256]{3,2,1,0:T(8,128)(2,1)S(1)}, bf16[2,5,16,256]{3,2,1,0:T(8,128)(2,1)S(1)}, u32[]{:S(2)}, u32[]{:S(2)}) collective-permute-start(bf16[2,5,16,256]{3,2,1,0:T(8,128)(2,1)S(1)} %get-tuple-element.77), channel_id=1, source_target_pairs={{0,16},{4,20},{8,24},{12,28},{16,0},{20,4},{24,8},{28,12},{1,17},{... | collective-permute-start | bytes 245768 | tf_op jit(solution)/shard_map/ppermute | solution.py:496
  46.1 0.8 %collective-permute-start.16 = (bf16[2,5,16,256]{3,2,1,0:T(8,128)(2,1)S(1)}, bf16[2,5,16,256]{3,2,1,0:T(8,128)(2,1)S(1)}, u32[]{:S(2)}, u32[]{:S(2)}) collective-permute-start(bf16[2,5,16,256]{3,2,1,0:T(8,128)(2,1)S(1)} %get-tuple-element.78), channel_id=1, source_target_pairs={{0,8},{4,12},{8,0},{12,4},{16,24},{20,28},{24,16},{28,20},{1,9},{5... | collective-permute-start | bytes 245768 | tf_op jit(solution)/shard_map/ppermute | solution.py:496
  46.9 3.1 %local_products.7.partial = f32[16,16,256]{2,1,0:T(8,128)S(1)} custom-call(bf16[16,16,256]{2,1,0:T(8,128)(2,1)S(1)} %get-tuple-element.74.x, bf16[40,256,256]{2,1,0:T(8,128)(2,1)S(1)} %get-tuple-element.61.tiles, s32[1,1,2,48]{3,2,1,0:T(2,128)S(1)} %bitcast.13, f32[1,1,48,2,256]{4,3,2,1,0:T(2,128)S(1)} %copy-done, ...), custom_call_target="tpu_custom_call" | custom-call | flops 167772160 | bytes 5242880 | tf_op jit(solution)/shard_map/local_products/pallas_call | solution.py:568
  50.0 0.6 collective-permute-done.15.refs_2_
  50.7 0.5 remote_products.3
  51.2 1.6 %collective-permute-start.17 = (bf16[4,16,256]{2,1,0:T(8,128)(2,1)S(1)}, bf16[4,16,256]{2,1,0:T(8,128)(2,1)S(1)}, u32[]{:S(2)}, u32[]{:S(2)}) collective-permute-start(bf16[4,16,256]{2,1,0:T(8,128)(2,1)S(1)} %get-tuple-element.80), channel_id=1, source_target_pairs={{0,3},{1,2},{2,1},{3,0},{4,7},{5,6},{6,5},{7,4},{8,11},{9,10},{10,... | collective-permute-start | bytes 98312 | tf_op jit(solution)/shard_map/ppermute | solution.py:474
  52.9 1.0 %collective-permute-start.18 = (bf16[4,16,256]{2,1,0:T(8,128)(2,1)S(1)}, bf16[4,16,256]{2,1,0:T(8,128)(2,1)S(1)}, u32[]{:S(2)}, u32[]{:S(2)}) collective-permute-start(bf16[4,16,256]{2,1,0:T(8,128)(2,1)S(1)} %get-tuple-element.81), channel_id=1, source_target_pairs={{0,2},{1,3},{2,0},{3,1},{4,6},{5,7},{6,4},{7,5},{8,10},{9,11},{10,... | collective-permute-start | bytes 98312 | tf_op jit(solution)/shard_map/ppermute | solution.py:474
  53.8 1.9 %collective-permute-start.19 = (bf16[4,16,256]{2,1,0:T(8,128)(2,1)S(1)}, bf16[4,16,256]{2,1,0:T(8,128)(2,1)S(1)}, u32[]{:S(2)}, u32[]{:S(2)}) collective-permute-start(bf16[4,16,256]{2,1,0:T(8,128)(2,1)S(1)} %get-tuple-element.82), channel_id=1, source_target_pairs={{0,1},{1,0},{2,3},{3,2},{4,5},{5,4},{6,7},{7,6},{8,9},{9,8},{10,11... | collective-permute-start | bytes 98312 | tf_op jit(solution)/shard_map/ppermute | solution.py:474
  56.1 1.0 %collective-permute-done.17.refs_1_ = bf16[4,16,256]{2,1,0:T(8,128)(2,1)S(1)} collective-permute-done((bf16[4,16,256]{2,1,0:T(8,128)(2,1)S(1)}, bf16[4,16,256]{2,1,0:T(8,128)(2,1)S(1)}, u32[]{:S(2)}, u32[]{:S(2)}) %collective-permute-start.17) | collective-permute-done | bytes 32800 | tf_op jit(solution)/shard_map/ppermute | solution.py:474
  57.0 0.7 collective-permute-done.18.refs_2_
  58.0 0.6 last_quarter.1
  58.6 10.7 %all_to_all.5.grams = f32[32,2,128]{2,1,0:T(2,128)S(1)} all-to-all(f32[32,2,128]{2,1,0:T(2,128)S(1)} %get-tuple-element.83), channel_id=1, replica_groups=mesh['rows'=8,'cols'=4] {'rows','cols'}, dimensions={0} | all-to-all | bytes 65536 | tf_op jit(solution)/shard_map/all_to_all | solution.py:632
  69.4 1.1 %finish.1 = f32[16,1024]{1,0:T(8,128)} custom-call(f32[32,2,128]{2,1,0:T(2,128)S(1)} %all_to_all.5.grams, f32[16,1024]{1,0:T(8,128)S(1)} %get-tuple-element.84.image), custom_call_target="tpu_custom_call" | custom-call | flops 1000000 | bytes 1000000 | tf_op jit(solution)/shard_map/finish/pallas_call | solution.py:635
  (42 shorter events, 5.8 us)
Async XLA Ops:
  0.0 2.2 %copy-start.2 = (f32[1,1,8,2,256]{4,3,2,1,0:T(2,128)S(1)}, f32[1,1,8,2,256]{4,3,2,1,0:T(2,128)}, u32[]{:S(2)}) copy-start(f32[1,1,8,2,256]{4,3,2,1,0:T(2,128)} %gains.6) | copy-start | bytes 49156
  0.0 2.2 %copy-start.3 = (s32[1,1,8,2]{2,3,1,0:T(2,128)S(1)}, s32[1,1,8,2]{2,3,1,0:T(2,128)}, u32[]{:S(2)}) copy-start(s32[1,1,8,2]{2,3,1,0:T(2,128)} %param.14) | copy-start | bytes 196
  0.0 2.2 %copy-start = (f32[1,1,48,2,256]{4,3,2,1,0:T(2,128)S(1)}, f32[1,1,48,2,256]{4,3,2,1,0:T(2,128)}, u32[]{:S(2)}) copy-start(f32[1,1,48,2,256]{4,3,2,1,0:T(2,128)} %refs_0_.1) | copy-start | bytes 294916
  0.0 2.2 %copy-start.4 = (s32[1,1,48,2]{2,3,1,0:T(2,128)S(1)}, s32[1,1,48,2]{2,3,1,0:T(2,128)}, u32[]{:S(2)}) copy-start(s32[1,1,48,2]{2,3,1,0:T(2,128)} %param.10) | copy-start | bytes 1156
  1.7 1.4 %collective-permute-start = (f32[4,8,256]{2,1,0:T(8,128)S(1)}, f32[4,8,256]{2,1,0:T(8,128)S(1)}, u32[]{:S(2)}, u32[]{:S(2)}) collective-permute-start(f32[4,8,256]{2,1,0:T(8,128)S(1)} %get-tuple-element.49), channel_id=1, source_target_pairs={{0,4},{4,0},{8,12},{12,8},{16,20},{20,16},{24,28},{28,24},{1,5},{5... | collective-permute-start | bytes 98312 | tf_op jit(solution)/shard_map/ppermute | solution.py:488
  2.2 17.5 %copy-start.1 = (f32[16,4096]{1,0:T(8,128)S(1)}, f32[16,4096]{1,0:T(8,128)}, u32[]{:S(2)}) copy-start(f32[16,4096]{1,0:T(8,128)} %start.1) | copy-start | bytes 786436
  2.2 17.5 %copy-start.5 = (s32[1,1,8]{2,1,0:T(1,128)S(1)}, s32[1,1,8]{2,1,0:T(1,128)}, u32[]{:S(2)}) copy-start(s32[1,1,8]{2,1,0:T(1,128)} %groups.9) | copy-start | bytes 100
  3.1 7.9 %collective-permute-start.1 = (f32[2,8,256]{2,1,0:T(8,128)S(1)}, f32[2,8,256]{2,1,0:T(8,128)S(1)}, u32[]{:S(2)}, u32[]{:S(2)}) collective-permute-start(f32[2,8,256]{2,1,0:T(8,128)S(1)} %get-tuple-element.51), channel_id=1, source_target_pairs={{0,24},{4,28},{8,16},{12,20},{16,8},{20,12},{24,0},{28,4},{1,25},{... | collective-permute-start | bytes 49160 | tf_op jit(solution)/shard_map/ppermute | solution.py:496
  6.9 4.1 %collective-permute-start.2 = (f32[2,8,256]{2,1,0:T(8,128)S(1)}, f32[2,8,256]{2,1,0:T(8,128)S(1)}, u32[]{:S(2)}, u32[]{:S(2)}) collective-permute-start(f32[2,8,256]{2,1,0:T(8,128)S(1)} %get-tuple-element.52), channel_id=1, source_target_pairs={{0,16},{4,20},{8,24},{12,28},{16,0},{20,4},{24,8},{28,12},{1,17},{... | collective-permute-start | bytes 49160 | tf_op jit(solution)/shard_map/ppermute | solution.py:496
  7.4 3.7 %collective-permute-start.3 = (f32[2,8,256]{2,1,0:T(8,128)S(1)}, f32[2,8,256]{2,1,0:T(8,128)S(1)}, u32[]{:S(2)}, u32[]{:S(2)}) collective-permute-start(f32[2,8,256]{2,1,0:T(8,128)S(1)} %get-tuple-element.53), channel_id=1, source_target_pairs={{0,8},{4,12},{8,0},{12,4},{16,24},{20,28},{24,16},{28,20},{1,9},{5... | collective-permute-start | bytes 49160 | tf_op jit(solution)/shard_map/ppermute | solution.py:496
  11.2 5.8 %collective-permute-start.6 = (f32[16,256]{1,0:T(8,128)S(1)}, f32[16,256]{1,0:T(8,128)S(1)}, u32[]{:S(2)}, u32[]{:S(2)}) collective-permute-start(f32[16,256]{1,0:T(8,128)S(1)} %get-tuple-element.58.refs_0_), channel_id=1, source_target_pairs={{0,3},{1,2},{2,1},{3,0},{4,7},{5,6},{6,5},{7,4},{8,11},{9,10},{10,... | collective-permute-start | bytes 49160 | tf_op jit(solution)/shard_map/ppermute | solution.py:474
  15.1 4.6 %collective-permute-start.5 = (f32[16,256]{1,0:T(8,128)S(1)}, f32[16,256]{1,0:T(8,128)S(1)}, u32[]{:S(2)}, u32[]{:S(2)}) collective-permute-start(f32[16,256]{1,0:T(8,128)S(1)} %get-tuple-element.58.refs_0_), channel_id=1, source_target_pairs={{0,2},{1,3},{2,0},{3,1},{4,6},{5,7},{6,4},{7,5},{8,10},{9,11},{10,... | collective-permute-start | bytes 49160 | tf_op jit(solution)/shard_map/ppermute | solution.py:474
  15.1 4.6 %collective-permute-start.4 = (f32[16,256]{1,0:T(8,128)S(1)}, f32[16,256]{1,0:T(8,128)S(1)}, u32[]{:S(2)}, u32[]{:S(2)}) collective-permute-start(f32[16,256]{1,0:T(8,128)S(1)} %get-tuple-element.58.refs_0_), channel_id=1, source_target_pairs={{0,1},{1,0},{2,3},{3,2},{4,5},{5,4},{6,7},{7,6},{8,9},{9,8},{10,11... | collective-permute-start | bytes 49160 | tf_op jit(solution)/shard_map/ppermute | solution.py:474
  20.1 1.4 %collective-permute-start.7 = (bf16[4,4,16,256]{3,2,1,0:T(8,128)(2,1)S(1)}, bf16[4,4,16,256]{3,2,1,0:T(8,128)(2,1)S(1)}, u32[]{:S(2)}, u32[]{:S(2)}) collective-permute-start(bf16[4,4,16,256]{3,2,1,0:T(8,128)(2,1)S(1)} %get-tuple-element.63), channel_id=1, source_target_pairs={{0,4},{4,0},{8,12},{12,8},{16,20},{20,16},{24,28},{28,24},{1,5},{5... | collective-permute-start | bytes 393224 | tf_op jit(solution)/shard_map/ppermute | solution.py:488
  21.6 6.6 %collective-permute-start.8 = (bf16[2,4,16,256]{3,2,1,0:T(8,128)(2,1)S(1)}, bf16[2,4,16,256]{3,2,1,0:T(8,128)(2,1)S(1)}, u32[]{:S(2)}, u32[]{:S(2)}) collective-permute-start(bf16[2,4,16,256]{3,2,1,0:T(8,128)(2,1)S(1)} %get-tuple-element.65), channel_id=1, source_target_pairs={{0,24},{4,28},{8,16},{12,20},{16,8},{20,12},{24,0},{28,4},{1,25},{... | collective-permute-start | bytes 196616 | tf_op jit(solution)/shard_map/ppermute | solution.py:496
  24.1 4.3 %collective-permute-start.9 = (bf16[2,4,16,256]{3,2,1,0:T(8,128)(2,1)S(1)}, bf16[2,4,16,256]{3,2,1,0:T(8,128)(2,1)S(1)}, u32[]{:S(2)}, u32[]{:S(2)}) collective-permute-start(bf16[2,4,16,256]{3,2,1,0:T(8,128)(2,1)S(1)} %get-tuple-element.66), channel_id=1, source_target_pairs={{0,16},{4,20},{8,24},{12,28},{16,0},{20,4},{24,8},{28,12},{1,17},{... | collective-permute-start | bytes 196616 | tf_op jit(solution)/shard_map/ppermute | solution.py:496
  24.6 4.3 %collective-permute-start.10 = (bf16[2,4,16,256]{3,2,1,0:T(8,128)(2,1)S(1)}, bf16[2,4,16,256]{3,2,1,0:T(8,128)(2,1)S(1)}, u32[]{:S(2)}, u32[]{:S(2)}) collective-permute-start(bf16[2,4,16,256]{3,2,1,0:T(8,128)(2,1)S(1)} %get-tuple-element.67), channel_id=1, source_target_pairs={{0,8},{4,12},{8,0},{12,4},{16,24},{20,28},{24,16},{28,20},{1,9},{5... | collective-permute-start | bytes 196616 | tf_op jit(solution)/shard_map/ppermute | solution.py:496
  29.4 5.0 %collective-permute-start.11 = (bf16[16,16,256]{2,1,0:T(8,128)(2,1)S(1)}, bf16[16,16,256]{2,1,0:T(8,128)(2,1)S(1)}, u32[]{:S(2)}, u32[]{:S(2)}) collective-permute-start(bf16[16,16,256]{2,1,0:T(8,128)(2,1)S(1)} %get-tuple-element.69), channel_id=1, source_target_pairs={{0,1},{1,0},{2,3},{3,2},{4,5},{5,4},{6,7},{7,6},{8,9},{9,8},{10,11... | collective-permute-start | bytes 393224 | tf_op jit(solution)/shard_map/ppermute | solution.py:474
  34.5 6.8 %collective-permute-start.12 = (bf16[16,16,256]{2,1,0:T(8,128)(2,1)S(1)}, bf16[16,16,256]{2,1,0:T(8,128)(2,1)S(1)}, u32[]{:S(2)}, u32[]{:S(2)}) collective-permute-start(bf16[16,16,256]{2,1,0:T(8,128)(2,1)S(1)} %get-tuple-element.71), channel_id=1, source_target_pairs={{0,3},{1,2},{2,1},{3,0},{4,7},{5,6},{6,5},{7,4},{8,11},{9,10},{10,... | collective-permute-start | bytes 393224 | tf_op jit(solution)/shard_map/ppermute | solution.py:474
  41.9 1.5 %collective-permute-start.13 = (bf16[4,5,16,256]{3,2,1,0:T(8,128)(2,1)S(1)}, bf16[4,5,16,256]{3,2,1,0:T(8,128)(2,1)S(1)}, u32[]{:S(2)}, u32[]{:S(2)}) collective-permute-start(bf16[4,5,16,256]{3,2,1,0:T(8,128)(2,1)S(1)} %get-tuple-element.73), channel_id=1, source_target_pairs={{0,4},{4,0},{8,12},{12,8},{16,20},{20,16},{24,28},{28,24},{1,5},{5... | collective-permute-start | bytes 491528 | tf_op jit(solution)/shard_map/ppermute | solution.py:488
  43.4 6.6 %collective-permute-start.14 = (bf16[2,5,16,256]{3,2,1,0:T(8,128)(2,1)S(1)}, bf16[2,5,16,256]{3,2,1,0:T(8,128)(2,1)S(1)}, u32[]{:S(2)}, u32[]{:S(2)}) collective-permute-start(bf16[2,5,16,256]{3,2,1,0:T(8,128)(2,1)S(1)} %get-tuple-element.76), channel_id=1, source_target_pairs={{0,24},{4,28},{8,16},{12,20},{16,8},{20,12},{24,0},{28,4},{1,25},{... | collective-permute-start | bytes 245768 | tf_op jit(solution)/shard_map/ppermute | solution.py:496
  45.3 5.3 %collective-permute-start.15 = (bf16[2,5,16,256]{3,2,1,0:T(8,128)(2,1)S(1)}, bf16[2,5,16,256]{3,2,1,0:T(8,128)(2,1)S(1)}, u32[]{:S(2)}, u32[]{:S(2)}) collective-permute-start(bf16[2,5,16,256]{3,2,1,0:T(8,128)(2,1)S(1)} %get-tuple-element.77), channel_id=1, source_target_pairs={{0,16},{4,20},{8,24},{12,28},{16,0},{20,4},{24,8},{28,12},{1,17},{... | collective-permute-start | bytes 245768 | tf_op jit(solution)/shard_map/ppermute | solution.py:496
  46.1 4.6 %collective-permute-start.16 = (bf16[2,5,16,256]{3,2,1,0:T(8,128)(2,1)S(1)}, bf16[2,5,16,256]{3,2,1,0:T(8,128)(2,1)S(1)}, u32[]{:S(2)}, u32[]{:S(2)}) collective-permute-start(bf16[2,5,16,256]{3,2,1,0:T(8,128)(2,1)S(1)} %get-tuple-element.78), channel_id=1, source_target_pairs={{0,8},{4,12},{8,0},{12,4},{16,24},{20,28},{24,16},{28,20},{1,9},{5... | collective-permute-start | bytes 245768 | tf_op jit(solution)/shard_map/ppermute | solution.py:496
  51.2 5.8 %collective-permute-start.17 = (bf16[4,16,256]{2,1,0:T(8,128)(2,1)S(1)}, bf16[4,16,256]{2,1,0:T(8,128)(2,1)S(1)}, u32[]{:S(2)}, u32[]{:S(2)}) collective-permute-start(bf16[4,16,256]{2,1,0:T(8,128)(2,1)S(1)} %get-tuple-element.80), channel_id=1, source_target_pairs={{0,3},{1,2},{2,1},{3,0},{4,7},{5,6},{6,5},{7,4},{8,11},{9,10},{10,... | collective-permute-start | bytes 98312 | tf_op jit(solution)/shard_map/ppermute | solution.py:474
  52.9 4.8 %collective-permute-start.18 = (bf16[4,16,256]{2,1,0:T(8,128)(2,1)S(1)}, bf16[4,16,256]{2,1,0:T(8,128)(2,1)S(1)}, u32[]{:S(2)}, u32[]{:S(2)}) collective-permute-start(bf16[4,16,256]{2,1,0:T(8,128)(2,1)S(1)} %get-tuple-element.81), channel_id=1, source_target_pairs={{0,2},{1,3},{2,0},{3,1},{4,6},{5,7},{6,4},{7,5},{8,10},{9,11},{10,... | collective-permute-start | bytes 98312 | tf_op jit(solution)/shard_map/ppermute | solution.py:474
  53.8 4.2 %collective-permute-start.19 = (bf16[4,16,256]{2,1,0:T(8,128)(2,1)S(1)}, bf16[4,16,256]{2,1,0:T(8,128)(2,1)S(1)}, u32[]{:S(2)}, u32[]{:S(2)}) collective-permute-start(bf16[4,16,256]{2,1,0:T(8,128)(2,1)S(1)} %get-tuple-element.82), channel_id=1, source_target_pairs={{0,1},{1,0},{2,3},{3,2},{4,5},{5,4},{6,7},{7,6},{8,9},{9,8},{10,11... | collective-permute-start | bytes 98312 | tf_op jit(solution)/shard_map/ppermute | solution.py:474
